TPU v7x, 32 devices: a whole 2x2x4 slice. The times are simulated.
32 devices in a mesh: group: 2 (over x), gx: 16 (over z, y, core).
Axes of the slice: x: 2, y: 2, z: 4, core: 2. Of those that a mesh axis runs over, the one named last changes fastest.
Arguments:
- out_grad: bfloat16 [1024, 24576], P('group', 'gx'), parts along dimension 0, may hold values from -6 to 6
- pre_act: bfloat16 [1024, 24576], P('group', 'gx'), parts along dimension 0, may hold values from -6 to 6
- layer_input: bfloat16 [1024, 6144], P(('group', 'gx')), parts along dimension 0, may hold values from -0.3984375 to 0.3984375
- weight: bfloat16 [6144, 24576], P(None, 'gx'), may hold values from -0.078125 to 0.078125
Outputs:
- grad_input: bfloat16 [1024, 6144], P(('group', 'gx')), parts along dimension 0
- grad_weight: bfloat16 [6144, 49152], P(None, ('group', 'gx')), parts along dimension 1
There are 2 independent parts, one for each index of `group`. A program takes and returns all parts, laid end to end along the dimension named above; an argument that names none is the same for every part. Nothing has to cross between parts.
All inputs are finite; a program needn't handle non-finite values.
Results may differ from a plain program's by a relative error of at most 0.005.
Values may be sent and summed in bfloat16 or wider, within the bound.
No kernel may reach another device: no remote copies, remote signals or barrier semaphores. Data moves between devices by JAX's collectives and lax.ppermute only.
A program may use at most 192 MiB of HBM per device.

v0:
```python
import math

import jax
import jax.numpy as jnp
from jax import lax
from jax.sharding import PartitionSpec as P


def gelu_slope(pre):
    coeff = math.sqrt(2.0 / math.pi)
    inner = coeff * (pre + 0.044715 * pre * pre * pre)
    tanh_value = jnp.tanh(inner)
    return 0.5 * (1.0 + tanh_value) + 0.5 * pre * (1.0 - tanh_value * tanh_value) * coeff * (
        1.0 + 3.0 * 0.044715 * pre * pre
    )


def on_device(out_grad, pre_act, layer_input, weight):
    slope = gelu_slope(pre_act.astype(jnp.float32))
    grad_hidden = (out_grad.astype(jnp.float32) * slope).astype(jnp.bfloat16)
    block = grad_hidden
    local_grad = lax.dot_general(
        lax.all_gather(layer_input, "gx", axis=0, tiled=True),
        block,
        (((0,), (0,)), ((), ())),
        preferred_element_type=jnp.float32,
    )
    block = grad_hidden
    grad_input = lax.psum_scatter(
        lax.dot_general(
            block, weight, (((1,), (1,)), ((), ())), preferred_element_type=jnp.float32
        ),
        "gx",
        scatter_dimension=0,
        tiled=True,
    ).astype(jnp.bfloat16)
    grad_weight = local_grad.astype(jnp.bfloat16)
    return (grad_input, grad_weight)


def solution(mesh):
    placed = (P("group", "gx"), P("group", "gx"), P(("group", "gx"), None), P(None, "gx"))
    return jax.shard_map(
        on_device,
        mesh=mesh,
        in_specs=placed,
        out_specs=(P(("group", "gx"), None), P(None, ("group", "gx"))),
        check_vma=False,
    )
```

profile of v0, /device:TPU:0, one launch (start us, length us, event | category | flops | bytes accessed | tf_op | source)
XLA Modules:
  0.0 220.9 jit_solution(7072647559357630344)
XLA Ops:
  7.2 0.0 all-gather.2.cloned.1.call-start
  7.2 0.7 all-gather.2.cloned.1.call-update
  7.9 0.0 reduce-scatter.2.cloned.1.call-start
  7.9 20.2 %fusion.11 = f32[512,6144]{1,0:T(8,128)} fusion(bf16[6144,1536]{1,0:T(8,128)(2,1)} %param.7, bf16[512,1536]{1,0:T(8,128)(2,1)} %param.5, bf16[512,1536]{1,0:T(8,128)(2,1)} %param.4), kind=kOutput, calls=%fused_computation.18 | convolution fusion | flops 9680191488 | bytes 34603008 | tf_op jit(solution)/shard_map/dot_general | solution.py:30
  28.2 0.0 copy-start
  28.2 0.0 copy-start.1
  28.2 0.0 reduce-scatter.2.cloned.1.call-update
  28.2 46.7 %all-gather.2.cloned.1.call-done = bf16[512,6144]{1,0:T(8,128)(2,1)} async-done(((bf16[32,6144]{1,0:T(8,128)(2,1)}), bf16[512,6144]{1,0:T(8,128)(2,1)}) %all-gather.2.cloned.1.call-update) | async-done | bytes 6291472 | tf_op jit(solution)/shard_map/all_gather | solution.py:23
  74.9 0.0 copy-done
  74.9 0.0 copy-done.1
  74.9 18.0 %fusion = bf16[6144,1536]{0,1:T(8,128)(2,1)} fusion(bf16[512,6144]{1,0:T(8,128)(2,1)} %all-gather.2.cloned.1.call-done, bf16[512,1536]{1,0:T(8,128)(2,1)S(1)} %copy-done, bf16[512,1536]{1,0:T(8,128)(2,1)S(1)} %copy-done.1), kind=kOutput, calls=%fused_computation.1 | convolution fusion | flops 9689628672 | bytes 28311552 | tf_op jit(solution)/shard_map/dot_general | solution.py:22
  92.9 25.0 %copy.6 = bf16[6144,1536]{1,0:T(8,128)(2,1)} copy(bf16[6144,1536]{0,1:T(8,128)(2,1)} %fusion) | data formatting | bytes 37748736
  117.9 94.3 %reduce-scatter.2.cloned.1.call-done = f32[32,6144]{1,0:T(8,128)} async-done(((f32[512,6144]{1,0:T(8,128)}), f32[32,6144]{1,0:T(8,128)}) %reduce-scatter.2.cloned.1.call-update) | async-done | bytes 786448 | tf_op jit(solution)/shard_map/reduce_scatter | solution.py:29
  212.2 1.9 convert_element_type.21
Async XLA Ops:
  7.2 67.7 %all-gather.2.cloned.1.call-start = ((), (), s32[]{:S(2)}) async-start(), calls=%async_computation.2 | async-start | bytes 6684672 | tf_op jit(solution)/shard_map/all_gather | solution.py:23
  7.9 204.3 %reduce-scatter.2.cloned.1.call-start = ((), (), s32[]{:S(2)}) async-start(), calls=%async_computation.1 | async-start | bytes 13369344 | tf_op jit(solution)/shard_map/reduce_scatter | solution.py:29
  28.2 46.7 %copy-start = (bf16[512,1536]{1,0:T(8,128)(2,1)S(1)}, bf16[512,1536]{1,0:T(8,128)(2,1)}, u32[]{:S(2)}) copy-start(bf16[512,1536]{1,0:T(8,128)(2,1)} %param.5) | copy-start | bytes 4718596
  28.2 46.7 %copy-start.1 = (bf16[512,1536]{1,0:T(8,128)(2,1)S(1)}, bf16[512,1536]{1,0:T(8,128)(2,1)}, u32[]{:S(2)}) copy-start(bf16[512,1536]{1,0:T(8,128)(2,1)} %param.4) | copy-start | bytes 4718596
Sparse Core Ops, SparseCore 0:
  10.3 64.5 all-gather.1
  78.9 133.2 reduce-scatter.1
where the time goes:
time: 222 us; the launch traced here: 221 us
  waiting for transfers between devices  142 us (64%)
  matrix products  38.2 us (17%)
  local copies, waits for them, and re-layouts  25 us (11%)
  between operations  14 us (6%)
    reduce_scatter x1, waiting for transfers between devices, on_device(): lax.psum_scatter(lax.dot_general(block, weight, (((1,), (1,)), ((), ())),...  94.3 us
    all_gather x1, waiting for transfers between devices, on_device(): lax.all_gather(layer_input, 'gx', axis=0, tiled=True)  46.7 us
    unnamed x5, local copies, waits for them, and re-layouts  25 us
    dot_general x1, matrix products, on_device(): lax.dot_general(block, weight, (((1,), (1,)), ((), ())), preferred_elemen...  20.2 us
    dot_general x1, matrix products, on_device(): lax.dot_general(lax.all_gather(layer_input, 'gx', axis=0, tiled=True), bl...  18 us
  transfers between devices with their start and end apart: 2, of which 2 were waited for; matrix products, arithmetic and copies ran while one was open for 29% of the time, Pallas kernels for 0%

commit v1 on v0

--- a/solution.py
+++ b/solution.py
@@ -3,7 +3,13 @@
 import jax
 import jax.numpy as jnp
 from jax import lax
+from jax.experimental import pallas as pl
+from jax.experimental.pallas import tpu as pltpu
 from jax.sharding import PartitionSpec as P
+
+CHUNKS = 4
+ROWS_BLOCK = 256
+VMEM = 48 * 1024 * 1024
 
 
 def gelu_slope(pre):
@@ -15,26 +21,174 @@
     )
 
 
-def on_device(out_grad, pre_act, layer_input, weight):
+def plain(out_grad, pre_act, layer_input, weight):
     slope = gelu_slope(pre_act.astype(jnp.float32))
     grad_hidden = (out_grad.astype(jnp.float32) * slope).astype(jnp.bfloat16)
-    block = grad_hidden
     local_grad = lax.dot_general(
         lax.all_gather(layer_input, "gx", axis=0, tiled=True),
-        block,
+        grad_hidden,
         (((0,), (0,)), ((), ())),
         preferred_element_type=jnp.float32,
     )
-    block = grad_hidden
     grad_input = lax.psum_scatter(
         lax.dot_general(
-            block, weight, (((1,), (1,)), ((), ())), preferred_element_type=jnp.float32
+            grad_hidden, weight, (((1,), (1,)), ((), ())), preferred_element_type=jnp.float32
         ),
         "gx",
         scatter_dimension=0,
         tiled=True,
     ).astype(jnp.bfloat16)
-    grad_weight = local_grad.astype(jnp.bfloat16)
+    return (grad_input, local_grad.astype(jnp.bfloat16))
+
+
+def distance(p):
+    return ((p & 3) << 2) | (((p >> 2) & 1) << 1) | (p >> 3)
+
+
+def hidden_kernel(me_ref, og_ref, pre_ref, dh_ref, *, n, rows):
+    me = me_ref[0]
+    for p in range(n):
+        block = me ^ distance(p)
+        at = pl.ds(pl.multiple_of(block * rows, rows), rows)
+        pre = pre_ref[at, :].astype(jnp.float32)
+        og = og_ref[at, :].astype(jnp.float32)
+        dh_ref[pl.ds(p * rows, rows), :] = (og * gelu_slope(pre)).astype(jnp.bfloat16)
+
+
+def hidden(me, out_grad, pre_act, n):
+    tokens, ff = out_grad.shape
+    step = 256
+    spec = pl.BlockSpec((tokens, step), lambda i, me: (0, i))
+    return pl.pallas_call(
+        lambda *refs: hidden_kernel(*refs, n=n, rows=tokens // n),
+        out_shape=jax.ShapeDtypeStruct((tokens, ff), jnp.bfloat16),
+        grid_spec=pltpu.PrefetchScalarGridSpec(
+            num_scalar_prefetch=1, grid=(ff // step,), in_specs=[spec, spec], out_specs=spec
+        ),
+        compiler_params=pltpu.CompilerParams(vmem_limit_bytes=VMEM),
+        cost_estimate=pl.CostEstimate(
+            flops=tokens * ff * 20, bytes_accessed=tokens * ff * 6, transcendentals=tokens * ff
+        ),
+        name="hidden",
+    )(me, out_grad, pre_act)
+
+
+def input_kernel(dh_ref, w_ref, keep_ref, send_ref):
+    part = lax.dot_general(
+        dh_ref[...], w_ref[...], (((1,), (1,)), ((), ())), preferred_element_type=jnp.float32
+    ).astype(jnp.bfloat16)
+    half = keep_ref.shape[0]
+    keep_ref[...] = part[:half]
+    send_ref[...] = part[half:]
+
+
+def input_part(dh, weight, first, count):
+    tokens, ff = dh.shape
+    out = jax.ShapeDtypeStruct((tokens // 2, count * ROWS_BLOCK), jnp.bfloat16)
+    out_spec = pl.BlockSpec((tokens // 2, ROWS_BLOCK), lambda i: (0, i))
+    return pl.pallas_call(
+        input_kernel,
+        out_shape=(out, out),
+        grid=(count,),
+        in_specs=[
+            pl.BlockSpec((tokens, ff), lambda i: (0, 0)),
+            pl.BlockSpec((ROWS_BLOCK, ff), lambda i: (first + i, 0)),
+        ],
+        out_specs=(out_spec, out_spec),
+        compiler_params=pltpu.CompilerParams(vmem_limit_bytes=VMEM),
+        cost_estimate=pl.CostEstimate(
+            flops=2 * tokens * ff * count * ROWS_BLOCK,
+            bytes_accessed=2 * (tokens * ff + ff * count * ROWS_BLOCK + tokens * count * ROWS_BLOCK),
+            transcendentals=0,
+        ),
+        name="input_part",
+    )(dh, weight)
+
+
+def weight_kernel(dh_ref, a_ref, b_ref, c_ref, *rest):
+    out_ref = rest[-1]
+    x = jnp.concatenate([a_ref[...], b_ref[...], c_ref[...]], axis=0)
+    out_ref[...] = lax.dot_general(
+        x, dh_ref[...], (((0,), (0,)), ((), ())), preferred_element_type=jnp.float32
+    ).astype(jnp.bfloat16)
+
+
+def weight_part(dh, a, b, c, first, total, before):
+    tokens, ff = dh.shape
+    count = a.shape[1] // ROWS_BLOCK
+
+    def piece(x):
+        return pl.BlockSpec((x.shape[0], ROWS_BLOCK), lambda i: (0, i))
+
+    more = () if before is None else (before,)
+    return pl.pallas_call(
+        weight_kernel,
+        out_shape=jax.ShapeDtypeStruct((total, ff), jnp.bfloat16),
+        grid=(count,),
+        in_specs=[pl.BlockSpec((tokens, ff), lambda i: (0, 0)), piece(a), piece(b), piece(c)]
+        + [pl.BlockSpec(memory_space=pl.ANY)] * len(more),
+        out_specs=pl.BlockSpec((ROWS_BLOCK, ff), lambda i: (first + i, 0)),
+        input_output_aliases={4: 0} if more else {},
+        compiler_params=pltpu.CompilerParams(vmem_limit_bytes=VMEM),
+        cost_estimate=pl.CostEstimate(
+            flops=2 * tokens * ff * count * ROWS_BLOCK,
+            bytes_accessed=2 * (tokens * ff + ff * count * ROWS_BLOCK + tokens * count * ROWS_BLOCK),
+            transcendentals=0,
+        ),
+        name="weight_part",
+    )(dh, a, b, c, *more)
+
+
+def add(x, y):
+    return (x.astype(jnp.float32) + y.astype(jnp.float32)).astype(jnp.bfloat16)
+
+
+def after(x, *others):
+    return lax.optimization_barrier((x, *others))[0]
+
+
+def on_device(out_grad, pre_act, layer_input, weight):
+    n = lax.axis_size("gx")
+    rows, width = layer_input.shape
+    if n != 16 or rows % 16:
+        return plain(out_grad, pre_act, layer_input, weight)
+
+    def swap(x, bits):
+        return lax.ppermute(x, "gx", [(i, i ^ bits) for i in range(n)])
+
+    me = lax.axis_index("gx").astype(jnp.int32).reshape(1)
+    wide = width // CHUNKS
+    blocks = wide // ROWS_BLOCK
+
+    gathered = []
+    last = None
+    for j in range(CHUNKS):
+        mine = layer_input[:, j * wide : (j + 1) * wide]
+        if last is not None:
+            mine = after(mine, *last)
+        along = [swap(mine, k << 2) for k in (1, 2, 3)]
+        last = along
+        a = jnp.concatenate([mine] + along, axis=0)
+        b = swap(a, 2)
+        c = swap(jnp.concatenate([a, b], axis=0), 1)
+        gathered.append((a, b, c))
+
+    dh = hidden(me, out_grad, pre_act, n)
+    outs = []
+    for j in range(CHUNKS):
+        keep, send = input_part(dh, weight, j * blocks, blocks)
+        part = add(keep, swap(send, 1))
+        half = part.shape[0] // 2
+        part = add(part[:half], swap(part[half:], 2))
+        total = part[:rows].astype(jnp.float32)
+        for k in (1, 2, 3):
+            total = total + swap(part[k * rows : (k + 1) * rows], k << 2).astype(jnp.float32)
+        outs.append(total.astype(jnp.bfloat16))
+    grad_input = jnp.concatenate(outs, axis=1)
+
+    grad_weight = None
+    for j, (a, b, c) in enumerate(gathered):
+        grad_weight = weight_part(dh, a, b, c, j * blocks, width, grad_weight)
     return (grad_input, grad_weight)
 
 

time: 222 us -> 191 us (0.86)
  waiting for transfers between devices: 142 us -> 87.7 us
  starting transfers between devices: 0.08 us -> 47.5 us
  Pallas kernels: 0 us -> 47.4 us
  matrix products: 38.2 us -> 0 us
  local copies, waits for them, and re-layouts: 25 us -> 4.4 us
  between operations: 14 us -> 1.05 us
    reduce_scatter x1 -> x0, waiting for transfers between devices: 94.3 us -> none  [on_device(): lax.psum_scatter(lax.dot_general(block, weight, (((1,), (1,)), ((), ())),...]
    ppermute x0 -> x40, waiting for transfers between devices: none -> 87.7 us  [swap(): return lax.ppermute(x, 'gx', [(i, i ^ bits) for i in range(n)])]
    ppermute x0 -> x40, starting transfers between devices: none -> 47.5 us  [swap(): return lax.ppermute(x, 'gx', [(i, i ^ bits) for i in range(n)])]
    pallas_call x0 -> x9, Pallas kernels: none -> 47.4 us  [the longest x4 24.2 us: input_part(): pl.pallas_call(input_kernel, out_shape=(out, out), grid=(count,), in_spec...]
    all_gather x1 -> x0, waiting for transfers between devices: 46.7 us -> none  [on_device(): lax.all_gather(layer_input, 'gx', axis=0, tiled=True)]
    dot_general x2 -> x0, matrix products: 38.2 us -> none  [the longest x1 20.2 us: on_device(): lax.dot_general(block, weight, (((1,), (1,)), ((), ())), preferred_elemen...]
    unnamed x5 -> x24, local copies, waits for them, and re-layouts: 25 us -> 4.1 us
  transfers between devices with their start and end apart: 2 -> 40, of which waited for: 2 -> 20; matrix products, arithmetic and copies ran while one was open for 29% -> 1% of each run, Pallas kernels for 0% -> 22%
where the time goes in v1:
time: 191 us; the launch traced here: 190 us
  waiting for transfers between devices  87.7 us (46%)
  starting transfers between devices  47.5 us (25%)
  Pallas kernels  47.4 us (25%)
  local copies, waits for them, and re-layouts  4.4 us (2%)
  other arithmetic  2.15 us (1%)
    ppermute x40, waiting for transfers between devices, swap(): return lax.ppermute(x, 'gx', [(i, i ^ bits) for i in range(n)])  87.7 us
    ppermute x40, starting transfers between devices, swap(): return lax.ppermute(x, 'gx', [(i, i ^ bits) for i in range(n)])  47.5 us
    pallas_call x4, Pallas kernels, input_part(): pl.pallas_call(input_kernel, out_shape=(out, out), grid=(count,), in_spec...  24.2 us
    pallas_call x4, Pallas kernels, weight_part(): pl.pallas_call(weight_kernel, out_shape=jax.ShapeDtypeStruct((total, ff),...  20.6 us
    unnamed x24, local copies, waits for them, and re-layouts  4.1 us
  transfers between devices with their start and end apart: 40, of which 20 were waited for; matrix products, arithmetic and copies ran while one was open for 1% of the time, Pallas kernels for 22%

profile of v1, /device:TPU:0, one launch (start us, length us, event | category | flops | bytes accessed | tf_op | source)
XLA Modules:
  0.0 190.1 jit_solution(12679822850892767383)
XLA Ops:
  0.6 1.1 constant_dynamic-update-slice_fusion.31
  1.7 3.1 %collective-permute-start.20 = (bf16[32,1536]{1,0:T(8,128)(2,1)S(1)}, bf16[32,1536]{1,0:T(8,128)(2,1)S(1)}, u32[]{:S(2)}, u32[]{:S(2)}) collective-permute-start(bf16[32,1536]{1,0:T(8,128)(2,1)S(1)} %get-tuple-element.27), channel_id=1, source_target_pairs={{0,4},{1,5},{2,6},{3,7},{4,0},{5,1},{6,2},{7,3},{8,12},{9,13},{10,... | collective-permute-start | bytes 294920 | tf_op jit(solution)/shard_map/ppermute | solution.py:157
  4.8 2.6 %collective-permute-start.21 = (bf16[32,1536]{1,0:T(8,128)(2,1)S(1)}, bf16[32,1536]{1,0:T(8,128)(2,1)S(1)}, u32[]{:S(2)}, u32[]{:S(2)}) collective-permute-start(bf16[32,1536]{1,0:T(8,128)(2,1)S(1)} %get-tuple-element.27), channel_id=1, source_target_pairs={{0,8},{1,9},{2,10},{3,11},{4,12},{5,13},{6,14},{7,15},{8,0},{9,1},... | collective-permute-start | bytes 294920 | tf_op jit(solution)/shard_map/ppermute | solution.py:157
  7.4 1.4 copy-done
  8.8 1.4 copy-done.1
  10.2 2.6 %hidden.1.dh_ref = bf16[512,1536]{1,0:T(8,128)(2,1)S(1)} custom-call(s32[1]{0:T(128)} %bitcast.refs_0_, bf16[512,1536]{1,0:T(8,128)(2,1)S(1)} %copy-done, bf16[512,1536]{1,0:T(8,128)(2,1)S(1)} %copy-done.1), custom_call_target="tpu_custom_call" | custom-call | flops 15728640 | bytes 4718592 | tf_op jit(solution)/shard_map/hidden/pallas_call | solution.py:62
  12.8 6.0 %input_part.4 = (bf16[256,1536]{1,0:T(8,128)(2,1)S(1)}, bf16[256,1536]{1,0:T(8,128)(2,1)S(1)}) custom-call(bf16[512,1536]{1,0:T(8,128)(2,1)S(1)} %hidden.1.dh_ref, bf16[6144,1536]{1,0:T(8,128)(2,1)} %w_ref.7), custom_call_target="tpu_custom_call" | custom-call | flops 2415919104 | bytes 7864320 | tf_op jit(solution)/shard_map/input_part/pallas_call | solution.py:89
  18.9 6.1 %input_part.5 = (bf16[256,1536]{1,0:T(8,128)(2,1)S(1)}, bf16[256,1536]{1,0:T(8,128)(2,1)S(1)}) custom-call(bf16[512,1536]{1,0:T(8,128)(2,1)S(1)} %hidden.1.dh_ref, bf16[6144,1536]{1,0:T(8,128)(2,1)} %w_ref.7), custom_call_target="tpu_custom_call" | custom-call | flops 2415919104 | bytes 7864320 | tf_op jit(solution)/shard_map/input_part/pallas_call | solution.py:89
  25.0 0.6 collective-permute-start.5
  25.5 6.1 %input_part.6 = (bf16[256,1536]{1,0:T(8,128)(2,1)S(1)}, bf16[256,1536]{1,0:T(8,128)(2,1)S(1)}) custom-call(bf16[512,1536]{1,0:T(8,128)(2,1)S(1)} %hidden.1.dh_ref, bf16[6144,1536]{1,0:T(8,128)(2,1)} %w_ref.7), custom_call_target="tpu_custom_call" | custom-call | flops 2415919104 | bytes 7864320 | tf_op jit(solution)/shard_map/input_part/pallas_call | solution.py:89
  31.6 6.0 %input_part.7 = (bf16[256,1536]{1,0:T(8,128)(2,1)S(1)}, bf16[256,1536]{1,0:T(8,128)(2,1)S(1)}) custom-call(bf16[512,1536]{1,0:T(8,128)(2,1)S(1)} %hidden.1.dh_ref, bf16[6144,1536]{1,0:T(8,128)(2,1)} %w_ref.7), custom_call_target="tpu_custom_call" | custom-call | flops 2415919104 | bytes 7864320 | tf_op jit(solution)/shard_map/input_part/pallas_call | solution.py:89
  37.7 1.0 collective-permute-start.23
  38.7 3.5 %collective-permute-start.24 = (bf16[32,1536]{1,0:T(8,128)(2,1)S(1)}, bf16[32,1536]{1,0:T(8,128)(2,1)S(1)}, u32[]{:S(2)}, u32[]{:S(2)}) collective-permute-start(bf16[32,1536]{1,0:T(8,128)(2,1)S(1)} %get-tuple-element.21), channel_id=1, source_target_pairs={{0,8},{1,9},{2,10},{3,11},{4,12},{5,13},{6,14},{7,15},{8,0},{9,1},... | collective-permute-start | bytes 294920 | tf_op jit(solution)/shard_map/ppermute | solution.py:157
  42.2 0.2 collective-permute-done.23
  42.5 7.4 %collective-permute-done.24 = bf16[32,1536]{1,0:T(8,128)(2,1)S(1)} collective-permute-done((bf16[32,1536]{1,0:T(8,128)(2,1)S(1)}, bf16[32,1536]{1,0:T(8,128)(2,1)S(1)}, u32[]{:S(2)}, u32[]{:S(2)}) %collective-permute-start.24) | collective-permute-done | bytes 98336 | tf_op jit(solution)/shard_map/ppermute | solution.py:157
  50.0 1.9 collective-permute-start.26
  51.8 1.3 collective-permute-start.27
  53.1 1.3 collective-permute-start.28
  54.5 1.1 collective-permute-done.26
  55.6 6.1 %collective-permute-done.27 = bf16[32,1536]{1,0:T(8,128)(2,1)S(1)} collective-permute-done((bf16[32,1536]{1,0:T(8,128)(2,1)S(1)}, bf16[32,1536]{1,0:T(8,128)(2,1)S(1)}, u32[]{:S(2)}, u32[]{:S(2)}) %collective-permute-start.27) | collective-permute-done | bytes 98336 | tf_op jit(solution)/shard_map/ppermute | solution.py:157
  61.6 1.5 collective-permute-start.38
  63.2 0.2 collective-permute-start.29
  63.4 4.5 %collective-permute-done.29 = bf16[32,1536]{1,0:T(8,128)(2,1)S(1)} collective-permute-done((bf16[32,1536]{1,0:T(8,128)(2,1)S(1)}, bf16[32,1536]{1,0:T(8,128)(2,1)S(1)}, u32[]{:S(2)}, u32[]{:S(2)}) %collective-permute-start.29) | collective-permute-done | bytes 98336 | tf_op jit(solution)/shard_map/ppermute | solution.py:157
  67.9 0.9 collective-permute-start.30
  68.7 7.3 %collective-permute-done.30 = bf16[32,1536]{1,0:T(8,128)(2,1)S(1)} collective-permute-done((bf16[32,1536]{1,0:T(8,128)(2,1)S(1)}, bf16[32,1536]{1,0:T(8,128)(2,1)S(1)}, u32[]{:S(2)}, u32[]{:S(2)}) %collective-permute-start.30) | collective-permute-done | bytes 98336 | tf_op jit(solution)/shard_map/ppermute | solution.py:157
  76.1 2.2 %collective-permute-start.31 = (bf16[32,1536]{1,0:T(8,128)(2,1)S(1)}, bf16[32,1536]{1,0:T(8,128)(2,1)S(1)}, u32[]{:S(2)}, u32[]{:S(2)}) collective-permute-start(bf16[32,1536]{1,0:T(8,128)(2,1)S(1)} %get-tuple-element.23), channel_id=1, source_target_pairs={{0,12},{1,13},{2,14},{3,15},{4,8},{5,9},{6,10},{7,11},{8,4},{9,5},... | collective-permute-start | bytes 294920 | tf_op jit(solution)/shard_map/ppermute | solution.py:157
  78.3 4.2 %collective-permute-done.31 = bf16[32,1536]{1,0:T(8,128)(2,1)S(1)} collective-permute-done((bf16[32,1536]{1,0:T(8,128)(2,1)S(1)}, bf16[32,1536]{1,0:T(8,128)(2,1)S(1)}, u32[]{:S(2)}, u32[]{:S(2)}) %collective-permute-start.31) | collective-permute-done | bytes 98336 | tf_op jit(solution)/shard_map/ppermute | solution.py:157
  82.5 2.1 %collective-permute-start.34 = (bf16[128,1536]{1,0:T(8,128)(2,1)S(1)}, bf16[128,1536]{1,0:T(8,128)(2,1)S(1)}, u32[]{:S(2)}, u32[]{:S(2)}) collective-permute-start(bf16[128,1536]{1,0:T(8,128)(2,1)S(1)} %get-tuple-element.50.a_ref), channel_id=1, source_target_pairs={{0,2},{1,3},{2,0},{3,1},{4,6},{5,7},{6,4},{7,5},{8,10},{9,11},{10,... | collective-permute-start | bytes 1179656 | tf_op jit(solution)/shard_map/ppermute | solution.py:157
  84.6 5.9 %collective-permute-done.36.b_ref = bf16[128,1536]{1,0:T(8,128)(2,1)S(1)} collective-permute-done((bf16[128,1536]{1,0:T(8,128)(2,1)S(1)}, bf16[128,1536]{1,0:T(8,128)(2,1)S(1)}, u32[]{:S(2)}, u32[]{:S(2)}) %collective-permute-start.36) | collective-permute-done | bytes 393248 | tf_op jit(solution)/shard_map/ppermute | solution.py:157
  90.6 5.1 %collective-permute-done.34.b_ref = bf16[128,1536]{1,0:T(8,128)(2,1)S(1)} collective-permute-done((bf16[128,1536]{1,0:T(8,128)(2,1)S(1)}, bf16[128,1536]{1,0:T(8,128)(2,1)S(1)}, u32[]{:S(2)}, u32[]{:S(2)}) %collective-permute-start.34) | collective-permute-done | bytes 393248 | tf_op jit(solution)/shard_map/ppermute | solution.py:157
  95.7 1.5 collective-permute-start.32
  97.3 0.2 add_convert_fusion.3
  97.5 0.6 collective-permute-start.37
  98.1 0.2 add_convert_fusion.2
  98.4 0.2 add_convert_fusion.1
  98.6 0.6 collective-permute-start.1
  99.2 0.2 add_convert_fusion
  99.5 5.7 %collective-permute-done.32.b_ref = bf16[128,1536]{1,0:T(8,128)(2,1)S(1)} collective-permute-done((bf16[128,1536]{1,0:T(8,128)(2,1)S(1)}, bf16[128,1536]{1,0:T(8,128)(2,1)S(1)}, u32[]{:S(2)}, u32[]{:S(2)}) %collective-permute-start.32) | collective-permute-done | bytes 393248 | tf_op jit(solution)/shard_map/ppermute | solution.py:157
  105.1 2.5 %collective-permute-start.6 = (bf16[128,1536]{1,0:T(8,128)(2,1)S(1)}, bf16[128,1536]{1,0:T(8,128)(2,1)S(1)}, u32[]{:S(2)}, u32[]{:S(2)}) collective-permute-start(bf16[128,1536]{1,0:T(8,128)(2,1)S(1)} %slice.119), channel_id=1, source_target_pairs={{0,2},{1,3},{2,0},{3,1},{4,6},{5,7},{6,4},{7,5},{8,10},{9,11},{10,... | collective-permute-start | bytes 1179656 | tf_op jit(solution)/shard_map/ppermute | solution.py:157
  107.7 5.9 %collective-permute-done.1 = bf16[128,1536]{1,0:T(8,128)(2,1)S(1)} collective-permute-done((bf16[128,1536]{1,0:T(8,128)(2,1)S(1)}, bf16[128,1536]{1,0:T(8,128)(2,1)S(1)}, u32[]{:S(2)}, u32[]{:S(2)}) %collective-permute-start.1) | collective-permute-done | bytes 393248 | tf_op jit(solution)/shard_map/ppermute | solution.py:157
  113.6 2.5 %collective-permute-start.11 = (bf16[128,1536]{1,0:T(8,128)(2,1)S(1)}, bf16[128,1536]{1,0:T(8,128)(2,1)S(1)}, u32[]{:S(2)}, u32[]{:S(2)}) collective-permute-start(bf16[128,1536]{1,0:T(8,128)(2,1)S(1)} %slice.125), channel_id=1, source_target_pairs={{0,2},{1,3},{2,0},{3,1},{4,6},{5,7},{6,4},{7,5},{8,10},{9,11},{10,... | collective-permute-start | bytes 1179656 | tf_op jit(solution)/shard_map/ppermute | solution.py:157
  116.1 5.8 %collective-permute-done.6 = bf16[128,1536]{1,0:T(8,128)(2,1)S(1)} collective-permute-done((bf16[128,1536]{1,0:T(8,128)(2,1)S(1)}, bf16[128,1536]{1,0:T(8,128)(2,1)S(1)}, u32[]{:S(2)}, u32[]{:S(2)}) %collective-permute-start.6) | collective-permute-done | bytes 393248 | tf_op jit(solution)/shard_map/ppermute | solution.py:157
  122.0 2.5 %collective-permute-start.16 = (bf16[128,1536]{1,0:T(8,128)(2,1)S(1)}, bf16[128,1536]{1,0:T(8,128)(2,1)S(1)}, u32[]{:S(2)}, u32[]{:S(2)}) collective-permute-start(bf16[128,1536]{1,0:T(8,128)(2,1)S(1)} %slice.131), channel_id=1, source_target_pairs={{0,2},{1,3},{2,0},{3,1},{4,6},{5,7},{6,4},{7,5},{8,10},{9,11},{10,... | collective-permute-start | bytes 1179656 | tf_op jit(solution)/shard_map/ppermute | solution.py:157
  124.6 5.8 %collective-permute-done.11 = bf16[128,1536]{1,0:T(8,128)(2,1)S(1)} collective-permute-done((bf16[128,1536]{1,0:T(8,128)(2,1)S(1)}, bf16[128,1536]{1,0:T(8,128)(2,1)S(1)}, u32[]{:S(2)}, u32[]{:S(2)}) %collective-permute-start.11) | collective-permute-done | bytes 393248 | tf_op jit(solution)/shard_map/ppermute | solution.py:157
  130.4 1.7 collective-permute-start.2
  132.2 4.9 %collective-permute-done.16 = bf16[128,1536]{1,0:T(8,128)(2,1)S(1)} collective-permute-done((bf16[128,1536]{1,0:T(8,128)(2,1)S(1)}, bf16[128,1536]{1,0:T(8,128)(2,1)S(1)}, u32[]{:S(2)}, u32[]{:S(2)}) %collective-permute-start.16) | collective-permute-done | bytes 393248 | tf_op jit(solution)/shard_map/ppermute | solution.py:157
  137.2 2.1 %collective-permute-start.3 = (bf16[32,1536]{1,0:T(8,128)(2,1)S(1)}, bf16[32,1536]{1,0:T(8,128)(2,1)S(1)}, u32[]{:S(2)}, u32[]{:S(2)}) collective-permute-start(bf16[32,1536]{1,0:T(8,128)(2,1)S(1)} %get-tuple-element.31), channel_id=1, source_target_pairs={{0,8},{1,9},{2,10},{3,11},{4,12},{5,13},{6,14},{7,15},{8,0},{9,1},... | collective-permute-start | bytes 294920 | tf_op jit(solution)/shard_map/ppermute | solution.py:157
  139.5 1.5 collective-permute-start.4
  140.9 5.1 %weight_part.4.rest_0_ = bf16[6144,1536]{1,0:T(8,128)(2,1)} custom-call(bf16[512,1536]{1,0:T(8,128)(2,1)S(1)} %hidden.1.dh_ref, bf16[128,1536]{1,0:T(8,128)(2,1)S(1)} %pad_maximum_fusion.1.a_ref, bf16[128,1536]{1,0:T(8,128)(2,1)S(1)} %collective-permute-done.38.b_ref, bf16[256,1536]{1,0:T(8,128)(2,1)S(1)} %collective-permute-done.39.c_ref), custom_call_target="tpu_custom_call" | custom-call | flops 2415919104 | bytes 7864320 | tf_op jit(solution)/shard_map/weight_part/pallas_call | solution.py:124
  146.1 0.4 collective-permute-done.3
  146.4 2.6 %collective-permute-start.8 = (bf16[32,1536]{1,0:T(8,128)(2,1)S(1)}, bf16[32,1536]{1,0:T(8,128)(2,1)S(1)}, u32[]{:S(2)}, u32[]{:S(2)}) collective-permute-start(bf16[32,1536]{1,0:T(8,128)(2,1)S(1)} %get-tuple-element.34), channel_id=1, source_target_pairs={{0,8},{1,9},{2,10},{3,11},{4,12},{5,13},{6,14},{7,15},{8,0},{9,1},... | collective-permute-start | bytes 294920 | tf_op jit(solution)/shard_map/ppermute | solution.py:157
  149.1 1.4 collective-permute-start.9
  150.5 3.5 %collective-permute-done.7 = bf16[32,1536]{1,0:T(8,128)(2,1)S(1)} collective-permute-done((bf16[32,1536]{1,0:T(8,128)(2,1)S(1)}, bf16[32,1536]{1,0:T(8,128)(2,1)S(1)}, u32[]{:S(2)}, u32[]{:S(2)}) %collective-permute-start.7) | collective-permute-done | bytes 98336 | tf_op jit(solution)/shard_map/ppermute | solution.py:157
  154.0 3.3 %collective-permute-done.8 = bf16[32,1536]{1,0:T(8,128)(2,1)S(1)} collective-permute-done((bf16[32,1536]{1,0:T(8,128)(2,1)S(1)}, bf16[32,1536]{1,0:T(8,128)(2,1)S(1)}, u32[]{:S(2)}, u32[]{:S(2)}) %collective-permute-start.8) | collective-permute-done | bytes 98336 | tf_op jit(solution)/shard_map/ppermute | solution.py:157
  157.3 2.4 %collective-permute-start.14 = (bf16[32,1536]{1,0:T(8,128)(2,1)S(1)}, bf16[32,1536]{1,0:T(8,128)(2,1)S(1)}, u32[]{:S(2)}, u32[]{:S(2)}) collective-permute-start(bf16[32,1536]{1,0:T(8,128)(2,1)S(1)} %get-tuple-element.36), channel_id=1, source_target_pairs={{0,12},{1,13},{2,14},{3,15},{4,8},{5,9},{6,10},{7,11},{8,4},{9,5},... | collective-permute-start | bytes 294920 | tf_op jit(solution)/shard_map/ppermute | solution.py:157
  159.7 0.5 collective-permute-done.12
  160.2 1.2 collective-permute-start.17
  161.4 5.4 %collective-permute-done.13 = bf16[32,1536]{1,0:T(8,128)(2,1)S(1)} collective-permute-done((bf16[32,1536]{1,0:T(8,128)(2,1)S(1)}, bf16[32,1536]{1,0:T(8,128)(2,1)S(1)}, u32[]{:S(2)}, u32[]{:S(2)}) %collective-permute-start.13) | collective-permute-done | bytes 98336 | tf_op jit(solution)/shard_map/ppermute | solution.py:157
  166.9 2.2 %collective-permute-start.19 = (bf16[32,1536]{1,0:T(8,128)(2,1)S(1)}, bf16[32,1536]{1,0:T(8,128)(2,1)S(1)}, u32[]{:S(2)}, u32[]{:S(2)}) collective-permute-start(bf16[32,1536]{1,0:T(8,128)(2,1)S(1)} %get-tuple-element.39), channel_id=1, source_target_pairs={{0,12},{1,13},{2,14},{3,15},{4,8},{5,9},{6,10},{7,11},{8,4},{9,5},... | collective-permute-start | bytes 294920 | tf_op jit(solution)/shard_map/ppermute | solution.py:157
  169.3 4.5 %collective-permute-done.18 = bf16[32,1536]{1,0:T(8,128)(2,1)S(1)} collective-permute-done((bf16[32,1536]{1,0:T(8,128)(2,1)S(1)}, bf16[32,1536]{1,0:T(8,128)(2,1)S(1)}, u32[]{:S(2)}, u32[]{:S(2)}) %collective-permute-start.18) | collective-permute-done | bytes 98336 | tf_op jit(solution)/shard_map/ppermute | solution.py:157
  173.9 0.8 pad_maximum_fusion
  174.6 5.1 %weight_part.5.rest_0_ = bf16[6144,1536]{1,0:T(8,128)(2,1)} custom-call(bf16[512,1536]{1,0:T(8,128)(2,1)S(1)} %hidden.1.dh_ref, bf16[128,1536]{1,0:T(8,128)(2,1)S(1)} %get-tuple-element.42.a_ref, bf16[128,1536]{1,0:T(8,128)(2,1)S(1)} %collective-permute-done.36.b_ref, ...), custom_call_target="tpu_custom_call", output_to_operand_aliasing={{}: (4, {})} | custom-call | flops 2415919104 | bytes 7864320 | tf_op jit(solution)/shard_map/weight_part/pallas_call | solution.py:124
  179.8 5.1 %weight_part.6.rest_0_ = bf16[6144,1536]{1,0:T(8,128)(2,1)} custom-call(bf16[512,1536]{1,0:T(8,128)(2,1)S(1)} %hidden.1.dh_ref, bf16[128,1536]{1,0:T(8,128)(2,1)S(1)} %get-tuple-element.50.a_ref, bf16[128,1536]{1,0:T(8,128)(2,1)S(1)} %collective-permute-done.34.b_ref, ...), custom_call_target="tpu_custom_call", output_to_operand_aliasing={{}: (4, {})} | custom-call | flops 2415919104 | bytes 7864320 | tf_op jit(solution)/shard_map/weight_part/pallas_call | solution.py:124
  184.9 5.1 %weight_part.7 = bf16[6144,1536]{1,0:T(8,128)(2,1)} custom-call(bf16[512,1536]{1,0:T(8,128)(2,1)S(1)} %hidden.1.dh_ref, bf16[128,1536]{1,0:T(8,128)(2,1)S(1)} %get-tuple-element.58.a_ref, bf16[128,1536]{1,0:T(8,128)(2,1)S(1)} %collective-permute-done.32.b_ref, bf16[256,1536]{1,0:T(8,128)(2,1)S(1)} %collective-permute-done.33.c_ref, ...), custom_call_target="tpu_custom_call", output_to_operand_aliasing={{}: (4, {})} | custom-call | flops 2415919104 | bytes 7864320 | tf_op jit(solution)/shard_map/weight_part/pallas_call | solution.py:124
  (75 shorter events, 1.5 us)
Async XLA Ops:
  1.7 36.0 %collective-permute-start.20 = (bf16[32,1536]{1,0:T(8,128)(2,1)S(1)}, bf16[32,1536]{1,0:T(8,128)(2,1)S(1)}, u32[]{:S(2)}, u32[]{:S(2)}) collective-permute-start(bf16[32,1536]{1,0:T(8,128)(2,1)S(1)} %get-tuple-element.27), channel_id=1, source_target_pairs={{0,4},{1,5},{2,6},{3,7},{4,0},{5,1},{6,2},{7,3},{8,12},{9,13},{10,... | collective-permute-start | bytes 294920 | tf_op jit(solution)/shard_map/ppermute | solution.py:157
  4.8 32.9 %collective-permute-start.21 = (bf16[32,1536]{1,0:T(8,128)(2,1)S(1)}, bf16[32,1536]{1,0:T(8,128)(2,1)S(1)}, u32[]{:S(2)}, u32[]{:S(2)}) collective-permute-start(bf16[32,1536]{1,0:T(8,128)(2,1)S(1)} %get-tuple-element.27), channel_id=1, source_target_pairs={{0,8},{1,9},{2,10},{3,11},{4,12},{5,13},{6,14},{7,15},{8,0},{9,1},... | collective-permute-start | bytes 294920 | tf_op jit(solution)/shard_map/ppermute | solution.py:157
  7.4 30.3 %collective-permute-start.22 = (bf16[32,1536]{1,0:T(8,128)(2,1)S(1)}, bf16[32,1536]{1,0:T(8,128)(2,1)S(1)}, u32[]{:S(2)}, u32[]{:S(2)}) collective-permute-start(bf16[32,1536]{1,0:T(8,128)(2,1)S(1)} %get-tuple-element.27), channel_id=1, source_target_pairs={{0,12},{1,13},{2,14},{3,15},{4,8},{5,9},{6,10},{7,11},{8,4},{9,5},... | collective-permute-start | bytes 294920 | tf_op jit(solution)/shard_map/ppermute | solution.py:157
  7.4 1.4 copy-start
  8.8 1.4 copy-start.1
  18.9 78.4 %collective-permute-start = (bf16[256,1536]{1,0:T(8,128)(2,1)S(1)}, bf16[256,1536]{1,0:T(8,128)(2,1)S(1)}, u32[]{:S(2)}, u32[]{:S(2)}) collective-permute-start(bf16[256,1536]{1,0:T(8,128)(2,1)S(1)} %get-tuple-element.14), channel_id=1, source_target_pairs={{0,1},{1,0},{2,3},{3,2},{4,5},{5,4},{6,7},{7,6},{8,9},{9,8},{10,11... | collective-permute-start | bytes 2359304 | tf_op jit(solution)/shard_map/ppermute | solution.py:157
  25.0 72.5 %collective-permute-start.5 = (bf16[256,1536]{1,0:T(8,128)(2,1)S(1)}, bf16[256,1536]{1,0:T(8,128)(2,1)S(1)}, u32[]{:S(2)}, u32[]{:S(2)}) collective-permute-start(bf16[256,1536]{1,0:T(8,128)(2,1)S(1)} %get-tuple-element.16), channel_id=1, source_target_pairs={{0,1},{1,0},{2,3},{3,2},{4,5},{5,4},{6,7},{7,6},{8,9},{9,8},{10,11... | collective-permute-start | bytes 2359304 | tf_op jit(solution)/shard_map/ppermute | solution.py:157
  37.7 4.8 %collective-permute-start.23 = (bf16[32,1536]{1,0:T(8,128)(2,1)S(1)}, bf16[32,1536]{1,0:T(8,128)(2,1)S(1)}, u32[]{:S(2)}, u32[]{:S(2)}) collective-permute-start(bf16[32,1536]{1,0:T(8,128)(2,1)S(1)} %get-tuple-element.21), channel_id=1, source_target_pairs={{0,4},{1,5},{2,6},{3,7},{4,0},{5,1},{6,2},{7,3},{8,12},{9,13},{10,... | collective-permute-start | bytes 294920 | tf_op jit(solution)/shard_map/ppermute | solution.py:157
  38.7 11.3 %collective-permute-start.24 = (bf16[32,1536]{1,0:T(8,128)(2,1)S(1)}, bf16[32,1536]{1,0:T(8,128)(2,1)S(1)}, u32[]{:S(2)}, u32[]{:S(2)}) collective-permute-start(bf16[32,1536]{1,0:T(8,128)(2,1)S(1)} %get-tuple-element.21), channel_id=1, source_target_pairs={{0,8},{1,9},{2,10},{3,11},{4,12},{5,13},{6,14},{7,15},{8,0},{9,1},... | collective-permute-start | bytes 294920 | tf_op jit(solution)/shard_map/ppermute | solution.py:157
  42.1 7.8 %collective-permute-start.25 = (bf16[32,1536]{1,0:T(8,128)(2,1)S(1)}, bf16[32,1536]{1,0:T(8,128)(2,1)S(1)}, u32[]{:S(2)}, u32[]{:S(2)}) collective-permute-start(bf16[32,1536]{1,0:T(8,128)(2,1)S(1)} %get-tuple-element.21), channel_id=1, source_target_pairs={{0,12},{1,13},{2,14},{3,15},{4,8},{5,9},{6,10},{7,11},{8,4},{9,5},... | collective-permute-start | bytes 294920 | tf_op jit(solution)/shard_map/ppermute | solution.py:157
  50.0 5.6 %collective-permute-start.26 = (bf16[32,1536]{1,0:T(8,128)(2,1)S(1)}, bf16[32,1536]{1,0:T(8,128)(2,1)S(1)}, u32[]{:S(2)}, u32[]{:S(2)}) collective-permute-start(bf16[32,1536]{1,0:T(8,128)(2,1)S(1)} %get-tuple-element.22), channel_id=1, source_target_pairs={{0,4},{1,5},{2,6},{3,7},{4,0},{5,1},{6,2},{7,3},{8,12},{9,13},{10,... | collective-permute-start | bytes 294920 | tf_op jit(solution)/shard_map/ppermute | solution.py:157
  51.8 9.8 %collective-permute-start.27 = (bf16[32,1536]{1,0:T(8,128)(2,1)S(1)}, bf16[32,1536]{1,0:T(8,128)(2,1)S(1)}, u32[]{:S(2)}, u32[]{:S(2)}) collective-permute-start(bf16[32,1536]{1,0:T(8,128)(2,1)S(1)} %get-tuple-element.22), channel_id=1, source_target_pairs={{0,8},{1,9},{2,10},{3,11},{4,12},{5,13},{6,14},{7,15},{8,0},{9,1},... | collective-permute-start | bytes 294920 | tf_op jit(solution)/shard_map/ppermute | solution.py:157
  53.1 10.0 %collective-permute-start.28 = (bf16[32,1536]{1,0:T(8,128)(2,1)S(1)}, bf16[32,1536]{1,0:T(8,128)(2,1)S(1)}, u32[]{:S(2)}, u32[]{:S(2)}) collective-permute-start(bf16[32,1536]{1,0:T(8,128)(2,1)S(1)} %get-tuple-element.22), channel_id=1, source_target_pairs={{0,12},{1,13},{2,14},{3,15},{4,8},{5,9},{6,10},{7,11},{8,4},{9,5},... | collective-permute-start | bytes 294920 | tf_op jit(solution)/shard_map/ppermute | solution.py:157
  55.6 42.8 %collective-permute-start.10 = (bf16[256,1536]{1,0:T(8,128)(2,1)S(1)}, bf16[256,1536]{1,0:T(8,128)(2,1)S(1)}, u32[]{:S(2)}, u32[]{:S(2)}) collective-permute-start(bf16[256,1536]{1,0:T(8,128)(2,1)S(1)} %get-tuple-element.18), channel_id=1, source_target_pairs={{0,1},{1,0},{2,3},{3,2},{4,5},{5,4},{6,7},{7,6},{8,9},{9,8},{10,11... | collective-permute-start | bytes 2359304 | tf_op jit(solution)/shard_map/ppermute | solution.py:157
  61.6 20.9 %collective-permute-start.38 = (bf16[128,1536]{1,0:T(8,128)(2,1)S(1)}, bf16[128,1536]{1,0:T(8,128)(2,1)S(1)}, u32[]{:S(2)}, u32[]{:S(2)}) collective-permute-start(bf16[128,1536]{1,0:T(8,128)(2,1)S(1)} %pad_maximum_fusion.1.a_ref), channel_id=1, source_target_pairs={{0,2},{1,3},{2,0},{3,1},{4,6},{5,7},{6,4},{7,5},{8,10},{9,11},{10,... | collective-permute-start | bytes 1179656 | tf_op jit(solution)/shard_map/ppermute | solution.py:157
  63.2 4.7 %collective-permute-start.29 = (bf16[32,1536]{1,0:T(8,128)(2,1)S(1)}, bf16[32,1536]{1,0:T(8,128)(2,1)S(1)}, u32[]{:S(2)}, u32[]{:S(2)}) collective-permute-start(bf16[32,1536]{1,0:T(8,128)(2,1)S(1)} %get-tuple-element.23), channel_id=1, source_target_pairs={{0,4},{1,5},{2,6},{3,7},{4,0},{5,1},{6,2},{7,3},{8,12},{9,13},{10,... | collective-permute-start | bytes 294920 | tf_op jit(solution)/shard_map/ppermute | solution.py:157
  67.9 8.2 %collective-permute-start.30 = (bf16[32,1536]{1,0:T(8,128)(2,1)S(1)}, bf16[32,1536]{1,0:T(8,128)(2,1)S(1)}, u32[]{:S(2)}, u32[]{:S(2)}) collective-permute-start(bf16[32,1536]{1,0:T(8,128)(2,1)S(1)} %get-tuple-element.23), channel_id=1, source_target_pairs={{0,8},{1,9},{2,10},{3,11},{4,12},{5,13},{6,14},{7,15},{8,0},{9,1},... | collective-permute-start | bytes 294920 | tf_op jit(solution)/shard_map/ppermute | solution.py:157
  76.1 6.4 %collective-permute-start.31 = (bf16[32,1536]{1,0:T(8,128)(2,1)S(1)}, bf16[32,1536]{1,0:T(8,128)(2,1)S(1)}, u32[]{:S(2)}, u32[]{:S(2)}) collective-permute-start(bf16[32,1536]{1,0:T(8,128)(2,1)S(1)} %get-tuple-element.23), channel_id=1, source_target_pairs={{0,12},{1,13},{2,14},{3,15},{4,8},{5,9},{6,10},{7,11},{8,4},{9,5},... | collective-permute-start | bytes 294920 | tf_op jit(solution)/shard_map/ppermute | solution.py:157
  82.5 8.1 %collective-permute-start.36 = (bf16[128,1536]{1,0:T(8,128)(2,1)S(1)}, bf16[128,1536]{1,0:T(8,128)(2,1)S(1)}, u32[]{:S(2)}, u32[]{:S(2)}) collective-permute-start(bf16[128,1536]{1,0:T(8,128)(2,1)S(1)} %get-tuple-element.42.a_ref), channel_id=1, source_target_pairs={{0,2},{1,3},{2,0},{3,1},{4,6},{5,7},{6,4},{7,5},{8,10},{9,11},{10,... | collective-permute-start | bytes 1179656 | tf_op jit(solution)/shard_map/ppermute | solution.py:157
  82.5 13.2 %collective-permute-start.34 = (bf16[128,1536]{1,0:T(8,128)(2,1)S(1)}, bf16[128,1536]{1,0:T(8,128)(2,1)S(1)}, u32[]{:S(2)}, u32[]{:S(2)}) collective-permute-start(bf16[128,1536]{1,0:T(8,128)(2,1)S(1)} %get-tuple-element.50.a_ref), channel_id=1, source_target_pairs={{0,2},{1,3},{2,0},{3,1},{4,6},{5,7},{6,4},{7,5},{8,10},{9,11},{10,... | collective-permute-start | bytes 1179656 | tf_op jit(solution)/shard_map/ppermute | solution.py:157
  90.5 8.1 %collective-permute-start.15 = (bf16[256,1536]{1,0:T(8,128)(2,1)S(1)}, bf16[256,1536]{1,0:T(8,128)(2,1)S(1)}, u32[]{:S(2)}, u32[]{:S(2)}) collective-permute-start(bf16[256,1536]{1,0:T(8,128)(2,1)S(1)} %get-tuple-element.20), channel_id=1, source_target_pairs={{0,1},{1,0},{2,3},{3,2},{4,5},{5,4},{6,7},{7,6},{8,9},{9,8},{10,11... | collective-permute-start | bytes 2359304 | tf_op jit(solution)/shard_map/ppermute | solution.py:157
  95.7 9.5 %collective-permute-start.32 = (bf16[128,1536]{1,0:T(8,128)(2,1)S(1)}, bf16[128,1536]{1,0:T(8,128)(2,1)S(1)}, u32[]{:S(2)}, u32[]{:S(2)}) collective-permute-start(bf16[128,1536]{1,0:T(8,128)(2,1)S(1)} %get-tuple-element.58.a_ref), channel_id=1, source_target_pairs={{0,2},{1,3},{2,0},{3,1},{4,6},{5,7},{6,4},{7,5},{8,10},{9,11},{10,... | collective-permute-start | bytes 1179656 | tf_op jit(solution)/shard_map/ppermute | solution.py:157
  97.2 42.2 %collective-permute-start.39 = (bf16[256,1536]{1,0:T(8,128)(2,1)S(1)}, bf16[256,1536]{1,0:T(8,128)(2,1)S(1)}, u32[]{:S(2)}, u32[]{:S(2)}) collective-permute-start(bf16[256,1536]{1,0:T(8,128)(2,1)S(1)} %constant_dynamic-update-slice_fusion.27), channel_id=1, source_target_pairs={{0,1},{1,0},{2,3},{3,2},{4,5},{5,4},{6,7},{7,6},{8,9},{9,8},{10,11... | collective-permute-start | bytes 2359304 | tf_op jit(solution)/shard_map/ppermute | solution.py:157
  97.5 77.1 %collective-permute-start.37 = (bf16[256,1536]{1,0:T(8,128)(2,1)S(1)}, bf16[256,1536]{1,0:T(8,128)(2,1)S(1)}, u32[]{:S(2)}, u32[]{:S(2)}) collective-permute-start(bf16[256,1536]{1,0:T(8,128)(2,1)S(1)} %constant_dynamic-update-slice_fusion.22), channel_id=1, source_target_pairs={{0,1},{1,0},{2,3},{3,2},{4,5},{5,4},{6,7},{7,6},{8,9},{9,8},{10,11... | collective-permute-start | bytes 2359304 | tf_op jit(solution)/shard_map/ppermute | solution.py:157
  98.3 81.5 %collective-permute-start.35 = (bf16[256,1536]{1,0:T(8,128)(2,1)S(1)}, bf16[256,1536]{1,0:T(8,128)(2,1)S(1)}, u32[]{:S(2)}, u32[]{:S(2)}) collective-permute-start(bf16[256,1536]{1,0:T(8,128)(2,1)S(1)} %constant_dynamic-update-slice_fusion.13), channel_id=1, source_target_pairs={{0,1},{1,0},{2,3},{3,2},{4,5},{5,4},{6,7},{7,6},{8,9},{9,8},{10,11... | collective-permute-start | bytes 2359304 | tf_op jit(solution)/shard_map/ppermute | solution.py:157
  98.6 14.9 %collective-permute-start.1 = (bf16[128,1536]{1,0:T(8,128)(2,1)S(1)}, bf16[128,1536]{1,0:T(8,128)(2,1)S(1)}, u32[]{:S(2)}, u32[]{:S(2)}) collective-permute-start(bf16[128,1536]{1,0:T(8,128)(2,1)S(1)} %slice.113), channel_id=1, source_target_pairs={{0,2},{1,3},{2,0},{3,1},{4,6},{5,7},{6,4},{7,5},{8,10},{9,11},{10,... | collective-permute-start | bytes 1179656 | tf_op jit(solution)/shard_map/ppermute | solution.py:157
  105.1 16.9 %collective-permute-start.6 = (bf16[128,1536]{1,0:T(8,128)(2,1)S(1)}, bf16[128,1536]{1,0:T(8,128)(2,1)S(1)}, u32[]{:S(2)}, u32[]{:S(2)}) collective-permute-start(bf16[128,1536]{1,0:T(8,128)(2,1)S(1)} %slice.119), channel_id=1, source_target_pairs={{0,2},{1,3},{2,0},{3,1},{4,6},{5,7},{6,4},{7,5},{8,10},{9,11},{10,... | collective-permute-start | bytes 1179656 | tf_op jit(solution)/shard_map/ppermute | solution.py:157
  107.7 24.6 %copy-start.2 = (bf16[256,1536]{1,0:T(8,128)(2,1)}, bf16[256,1536]{1,0:T(8,128)(2,1)S(1)}, u32[]{:S(2)}) copy-start(bf16[256,1536]{1,0:T(8,128)(2,1)S(1)} %constant_dynamic-update-slice_fusion.4) | copy-start | bytes 2359300
  113.6 16.9 %collective-permute-start.11 = (bf16[128,1536]{1,0:T(8,128)(2,1)S(1)}, bf16[128,1536]{1,0:T(8,128)(2,1)S(1)}, u32[]{:S(2)}, u32[]{:S(2)}) collective-permute-start(bf16[128,1536]{1,0:T(8,128)(2,1)S(1)} %slice.125), channel_id=1, source_target_pairs={{0,2},{1,3},{2,0},{3,1},{4,6},{5,7},{6,4},{7,5},{8,10},{9,11},{10,... | collective-permute-start | bytes 1179656 | tf_op jit(solution)/shard_map/ppermute | solution.py:157
  122.0 15.2 %collective-permute-start.16 = (bf16[128,1536]{1,0:T(8,128)(2,1)S(1)}, bf16[128,1536]{1,0:T(8,128)(2,1)S(1)}, u32[]{:S(2)}, u32[]{:S(2)}) collective-permute-start(bf16[128,1536]{1,0:T(8,128)(2,1)S(1)} %slice.131), channel_id=1, source_target_pairs={{0,2},{1,3},{2,0},{3,1},{4,6},{5,7},{6,4},{7,5},{8,10},{9,11},{10,... | collective-permute-start | bytes 1179656 | tf_op jit(solution)/shard_map/ppermute | solution.py:157
  130.4 15.6 %collective-permute-start.2 = (bf16[32,1536]{1,0:T(8,128)(2,1)S(1)}, bf16[32,1536]{1,0:T(8,128)(2,1)S(1)}, u32[]{:S(2)}, u32[]{:S(2)}) collective-permute-start(bf16[32,1536]{1,0:T(8,128)(2,1)S(1)} %get-tuple-element.29), channel_id=1, source_target_pairs={{0,4},{1,5},{2,6},{3,7},{4,0},{5,1},{6,2},{7,3},{8,12},{9,13},{10,... | collective-permute-start | bytes 294920 | tf_op jit(solution)/shard_map/ppermute | solution.py:157
  137.2 9.3 %collective-permute-start.3 = (bf16[32,1536]{1,0:T(8,128)(2,1)S(1)}, bf16[32,1536]{1,0:T(8,128)(2,1)S(1)}, u32[]{:S(2)}, u32[]{:S(2)}) collective-permute-start(bf16[32,1536]{1,0:T(8,128)(2,1)S(1)} %get-tuple-element.31), channel_id=1, source_target_pairs={{0,8},{1,9},{2,10},{3,11},{4,12},{5,13},{6,14},{7,15},{8,0},{9,1},... | collective-permute-start | bytes 294920 | tf_op jit(solution)/shard_map/ppermute | solution.py:157
  139.4 29.7 %copy-start.3 = (bf16[256,1536]{1,0:T(8,128)(2,1)S(1)}, bf16[256,1536]{1,0:T(8,128)(2,1)}, u32[]{:S(2)}) copy-start(bf16[256,1536]{1,0:T(8,128)(2,1)} %copy-done.2) | copy-start | bytes 2359300
  139.5 9.6 %collective-permute-start.4 = (bf16[32,1536]{1,0:T(8,128)(2,1)S(1)}, bf16[32,1536]{1,0:T(8,128)(2,1)S(1)}, u32[]{:S(2)}, u32[]{:S(2)}) collective-permute-start(bf16[32,1536]{1,0:T(8,128)(2,1)S(1)} %get-tuple-element.30), channel_id=1, source_target_pairs={{0,12},{1,13},{2,14},{3,15},{4,8},{5,9},{6,10},{7,11},{8,4},{9,5},... | collective-permute-start | bytes 294920 | tf_op jit(solution)/shard_map/ppermute | solution.py:157
  146.1 7.9 %collective-permute-start.7 = (bf16[32,1536]{1,0:T(8,128)(2,1)S(1)}, bf16[32,1536]{1,0:T(8,128)(2,1)S(1)}, u32[]{:S(2)}, u32[]{:S(2)}) collective-permute-start(bf16[32,1536]{1,0:T(8,128)(2,1)S(1)} %get-tuple-element.32), channel_id=1, source_target_pairs={{0,4},{1,5},{2,6},{3,7},{4,0},{5,1},{6,2},{7,3},{8,12},{9,13},{10,... | collective-permute-start | bytes 294920 | tf_op jit(solution)/shard_map/ppermute | solution.py:157
  146.4 10.9 %collective-permute-start.8 = (bf16[32,1536]{1,0:T(8,128)(2,1)S(1)}, bf16[32,1536]{1,0:T(8,128)(2,1)S(1)}, u32[]{:S(2)}, u32[]{:S(2)}) collective-permute-start(bf16[32,1536]{1,0:T(8,128)(2,1)S(1)} %get-tuple-element.34), channel_id=1, source_target_pairs={{0,8},{1,9},{2,10},{3,11},{4,12},{5,13},{6,14},{7,15},{8,0},{9,1},... | collective-permute-start | bytes 294920 | tf_op jit(solution)/shard_map/ppermute | solution.py:157
  149.1 8.2 %collective-permute-start.9 = (bf16[32,1536]{1,0:T(8,128)(2,1)S(1)}, bf16[32,1536]{1,0:T(8,128)(2,1)S(1)}, u32[]{:S(2)}, u32[]{:S(2)}) collective-permute-start(bf16[32,1536]{1,0:T(8,128)(2,1)S(1)} %get-tuple-element.33), channel_id=1, source_target_pairs={{0,12},{1,13},{2,14},{3,15},{4,8},{5,9},{6,10},{7,11},{8,4},{9,5},... | collective-permute-start | bytes 294920 | tf_op jit(solution)/shard_map/ppermute | solution.py:157
  154.0 6.2 %collective-permute-start.12 = (bf16[32,1536]{1,0:T(8,128)(2,1)S(1)}, bf16[32,1536]{1,0:T(8,128)(2,1)S(1)}, u32[]{:S(2)}, u32[]{:S(2)}) collective-permute-start(bf16[32,1536]{1,0:T(8,128)(2,1)S(1)} %get-tuple-element.35), channel_id=1, source_target_pairs={{0,4},{1,5},{2,6},{3,7},{4,0},{5,1},{6,2},{7,3},{8,12},{9,13},{10,... | collective-permute-start | bytes 294920 | tf_op jit(solution)/shard_map/ppermute | solution.py:157
  157.3 9.6 %collective-permute-start.13 = (bf16[32,1536]{1,0:T(8,128)(2,1)S(1)}, bf16[32,1536]{1,0:T(8,128)(2,1)S(1)}, u32[]{:S(2)}, u32[]{:S(2)}) collective-permute-start(bf16[32,1536]{1,0:T(8,128)(2,1)S(1)} %get-tuple-element.37), channel_id=1, source_target_pairs={{0,8},{1,9},{2,10},{3,11},{4,12},{5,13},{6,14},{7,15},{8,0},{9,1},... | collective-permute-start | bytes 294920 | tf_op jit(solution)/shard_map/ppermute | solution.py:157
  157.3 9.6 %collective-permute-start.14 = (bf16[32,1536]{1,0:T(8,128)(2,1)S(1)}, bf16[32,1536]{1,0:T(8,128)(2,1)S(1)}, u32[]{:S(2)}, u32[]{:S(2)}) collective-permute-start(bf16[32,1536]{1,0:T(8,128)(2,1)S(1)} %get-tuple-element.36), channel_id=1, source_target_pairs={{0,12},{1,13},{2,14},{3,15},{4,8},{5,9},{6,10},{7,11},{8,4},{9,5},... | collective-permute-start | bytes 294920 | tf_op jit(solution)/shard_map/ppermute | solution.py:157
  160.2 9.0 %collective-permute-start.17 = (bf16[32,1536]{1,0:T(8,128)(2,1)S(1)}, bf16[32,1536]{1,0:T(8,128)(2,1)S(1)}, u32[]{:S(2)}, u32[]{:S(2)}) collective-permute-start(bf16[32,1536]{1,0:T(8,128)(2,1)S(1)} %get-tuple-element.38), channel_id=1, source_target_pairs={{0,4},{1,5},{2,6},{3,7},{4,0},{5,1},{6,2},{7,3},{8,12},{9,13},{10,... | collective-permute-start | bytes 294920 | tf_op jit(solution)/shard_map/ppermute | solution.py:157
  166.9 6.9 %collective-permute-start.18 = (bf16[32,1536]{1,0:T(8,128)(2,1)S(1)}, bf16[32,1536]{1,0:T(8,128)(2,1)S(1)}, u32[]{:S(2)}, u32[]{:S(2)}) collective-permute-start(bf16[32,1536]{1,0:T(8,128)(2,1)S(1)} %get-tuple-element.40), channel_id=1, source_target_pairs={{0,8},{1,9},{2,10},{3,11},{4,12},{5,13},{6,14},{7,15},{8,0},{9,1},... | collective-permute-start | bytes 294920 | tf_op jit(solution)/shard_map/ppermute | solution.py:157
  166.9 6.9 %collective-permute-start.19 = (bf16[32,1536]{1,0:T(8,128)(2,1)S(1)}, bf16[32,1536]{1,0:T(8,128)(2,1)S(1)}, u32[]{:S(2)}, u32[]{:S(2)}) collective-permute-start(bf16[32,1536]{1,0:T(8,128)(2,1)S(1)} %get-tuple-element.39), channel_id=1, source_target_pairs={{0,12},{1,13},{2,14},{3,15},{4,8},{5,9},{6,10},{7,11},{8,4},{9,5},... | collective-permute-start | bytes 294920 | tf_op jit(solution)/shard_map/ppermute | solution.py:157
  169.2 15.8 %collective-permute-start.33 = (bf16[256,1536]{1,0:T(8,128)(2,1)S(1)}, bf16[256,1536]{1,0:T(8,128)(2,1)S(1)}, u32[]{:S(2)}, u32[]{:S(2)}) collective-permute-start(bf16[256,1536]{1,0:T(8,128)(2,1)S(1)} %copy-done.3), channel_id=1, source_target_pairs={{0,1},{1,0},{2,3},{3,2},{4,5},{5,4},{6,7},{7,6},{8,9},{9,8},{10,11... | collective-permute-start | bytes 2359304 | tf_op jit(solution)/shard_map/ppermute | solution.py:157

commit v2 on v0

v2 whole, which is shorter than its diff:
```python
import math

import jax
import jax.numpy as jnp
from jax import lax
from jax.experimental import pallas as pl
from jax.experimental.pallas import tpu as pltpu
from jax.sharding import PartitionSpec as P

RING = 8
PIECES = 4
VMEM_LIMIT = 46 * 1024 * 1024
HIDDEN_LIMIT = 57 * 1024 * 1024
WHOLE = pl.BlockSpec(memory_space=pltpu.VMEM)
OUTSIDE = pl.BlockSpec(memory_space=pltpu.HBM)


def cost(microseconds):
    return pl.CostEstimate(
        flops=int(microseconds * 1.15e9), bytes_accessed=0, transcendentals=0
    )


ANYWHERE = pl.BlockSpec(memory_space=pl.ANY)
SCALAR = pl.BlockSpec(memory_space=pltpu.SMEM)


def gelu_slope(pre):
    coeff = math.sqrt(2.0 / math.pi)
    inner = coeff * (pre + 0.044715 * pre * pre * pre)
    tanh_value = jnp.tanh(inner)
    return 0.5 * (1.0 + tanh_value) + 0.5 * pre * (1.0 - tanh_value * tanh_value) * coeff * (
        1.0 + 3.0 * 0.044715 * pre * pre
    )


def plain(out_grad, pre_act, layer_input, weight):
    slope = gelu_slope(pre_act.astype(jnp.float32))
    grad_hidden = (out_grad.astype(jnp.float32) * slope).astype(jnp.bfloat16)
    local_grad = lax.dot_general(
        lax.all_gather(layer_input, "gx", axis=0, tiled=True),
        grad_hidden,
        (((0,), (0,)), ((), ())),
        preferred_element_type=jnp.float32,
    )
    grad_input = lax.psum_scatter(
        lax.dot_general(
            grad_hidden, weight, (((1,), (1,)), ((), ())), preferred_element_type=jnp.float32
        ),
        "gx",
        scatter_dimension=0,
        tiled=True,
    ).astype(jnp.bfloat16)
    return (grad_input, local_grad.astype(jnp.bfloat16))


def chip_at(place):
    place = place & (RING - 1)
    return jnp.where(place < RING // 2, 2 * place, 2 * (RING - 1 - place) + 1)


def place_of(chip):
    return jnp.where(chip % 2 == 0, chip // 2, RING - 1 - chip // 2)


def ring_pairs():
    path = [2 * p if p < RING // 2 else 2 * (RING - 1 - p) + 1 for p in range(RING)]
    pairs = []
    for place, chip in enumerate(path):
        pairs.append((2 * chip, 2 * path[(place + 1) % RING]))
        pairs.append((2 * chip + 1, 2 * path[(place - 1) % RING] + 1))
    return pairs


def chip_order(me):
    way = jnp.where(me % 2 == 0, 1, -1)
    place = place_of(me // 2)
    steps = [0, -1, -2, -3, 4, 1, 2, 3]
    return [chip_at(place + way * s + RING) for s in steps]


def hidden_kernel(me_ref, og_hbm, pre_hbm, dh_ref, og_ref, pre_ref, sems):
    rows = dh_ref.shape[0] // RING
    copies = []
    for i, chip in enumerate(chip_order(me_ref[0])):
        source = pl.ds(pl.multiple_of(chip * rows, rows), rows)
        block = pl.ds(i * rows, rows)
        pair = (
            pltpu.make_async_copy(og_hbm.at[source, :], og_ref.at[block, :], sems.at[0, i]),
            pltpu.make_async_copy(pre_hbm.at[source, :], pre_ref.at[block, :], sems.at[1, i]),
        )
        for copy in pair:
            copy.start()
        copies.append(pair)
    for i, pair in enumerate(copies):
        for copy in pair:
            copy.wait()
        block = pl.ds(i * rows, rows)
        pre = pre_ref[block, :].astype(jnp.float32)
        og = og_ref[block, :].astype(jnp.float32)
        dh_ref[block, :] = (og * gelu_slope(pre)).astype(jnp.bfloat16)


def hidden(me, out_grad, pre_act):
    shape, dtype = out_grad.shape, out_grad.dtype
    return pl.pallas_call(
        hidden_kernel,
        out_shape=jax.ShapeDtypeStruct(shape, dtype),
        in_specs=[SCALAR, OUTSIDE, OUTSIDE],
        out_specs=WHOLE,
        scratch_shapes=[
            pltpu.VMEM(shape, dtype),
            pltpu.VMEM(shape, dtype),
            pltpu.SemaphoreType.DMA((2, RING)),
        ],
        compiler_params=pltpu.CompilerParams(vmem_limit_bytes=HIDDEN_LIMIT),
        cost_estimate=cost(3),
        name="hidden",
    )(me, out_grad, pre_act)


def prepare_kernel(me_ref, own_ref, twin_ref, mine_ref, other_ref):
    core = me_ref[0] % 2
    rows, half = own_ref.shape[0], mine_ref.shape[1]
    for ref, number in ((mine_ref, core), (other_ref, 1 - core)):
        columns = pl.ds(pl.multiple_of(number * half, half), half)
        ref[pl.ds(pl.multiple_of(core * rows, rows), rows), :] = own_ref[:, columns]
        ref[pl.ds(pl.multiple_of((1 - core) * rows, rows), rows), :] = twin_ref[:, columns]


def prepare(me, own, twin):
    rows, width = own.shape
    out = jax.ShapeDtypeStruct((2 * rows, width // 2), own.dtype)
    return pl.pallas_call(
        prepare_kernel,
        out_shape=(out, out),
        in_specs=[SCALAR, WHOLE, WHOLE],
        out_specs=(WHOLE, WHOLE),
        compiler_params=pltpu.CompilerParams(vmem_limit_bytes=VMEM_LIMIT),
        cost_estimate=cost(1),
        name="prepare",
    )(me, own, twin)


def first_row(me_ref, other, piece, half, wide):
    core = me_ref[0] % 2
    number = 1 - core if other else core
    return pl.multiple_of(number * half + piece * wide, wide)


def input_kernel(me_ref, dh_ref, w_hbm, *refs, other, piece, wide, step):
    outs, (w_ref, part_ref, in_sems, out_sems) = refs[-8:-4], refs[-4:]
    half = outs[0].shape[1]
    row = first_row(me_ref, other, piece, half, wide)
    copies = []
    for i in range(wide // step):
        copy = pltpu.make_async_copy(
            w_hbm.at[pl.ds(pl.multiple_of(row + i * step, step), step), :],
            w_ref.at[pl.ds(i * step, step), :],
            in_sems.at[i],
        )
        copy.start()
        copies.append(copy)
    stores = []
    for i, copy in enumerate(copies):
        copy.wait()
        here = pl.ds(i * step, step)
        part_ref[:, here] = lax.dot_general(
            dh_ref[...], w_ref[here, :], (((1,), (1,)), ((), ())), preferred_element_type=jnp.float32
        ).astype(jnp.bfloat16)
        at = 0
        for j, out in enumerate(outs):
            store = pltpu.make_async_copy(
                part_ref.at[pl.ds(at, out.shape[0]), here],
                out.at[:, pl.ds(piece * wide + i * step, step)],
                out_sems.at[i, j],
            )
            store.start()
            stores.append(store)
            at += out.shape[0]
    for store in stores:
        store.wait()


def input_piece(me, dh, weight, before, other, piece):
    tokens, ff = dh.shape
    half = weight.shape[0] // 2
    wide = half // PIECES
    step = 256
    rows = tokens // RING
    outs = tuple(
        jax.ShapeDtypeStruct((count * rows, half), jnp.bfloat16) for count in (1, 3, 1, 3)
    )
    return pl.pallas_call(
        lambda *refs: input_kernel(*refs, other=other, piece=piece, wide=wide, step=step),
        out_shape=outs,
        in_specs=[SCALAR, WHOLE, OUTSIDE] + [ANYWHERE] * len(before),
        out_specs=(ANYWHERE,) * 4,
        input_output_aliases={3 + i: i for i in range(len(before))},
        scratch_shapes=[
            pltpu.VMEM((wide, ff), jnp.bfloat16),
            pltpu.VMEM((tokens, wide), jnp.bfloat16),
            pltpu.SemaphoreType.DMA((wide // step,)),
            pltpu.SemaphoreType.DMA((wide // step, 4)),
        ],
        compiler_params=pltpu.CompilerParams(vmem_limit_bytes=VMEM_LIMIT),
        cost_estimate=cost(3),
        name="input_piece",
    )(me, dh, weight, *before)


def weight_kernel(me_ref, dh_ref, *refs, other, piece, wide, step):
    blocks, (out_hbm, stage, sems) = refs[:RING], refs[-3:]
    half = blocks[0].shape[1]
    row = first_row(me_ref, other, piece, half, wide)
    x = jnp.concatenate([b[:, pl.ds(piece * wide, wide)] for b in blocks], axis=0)
    copies = []
    for i in range(dh_ref.shape[1] // step):
        columns = pl.ds(i * step, step)
        stage[:, columns] = lax.dot_general(
            x, dh_ref[:, columns], (((0,), (0,)), ((), ())), preferred_element_type=jnp.float32
        ).astype(jnp.bfloat16)
        copy = pltpu.make_async_copy(
            stage.at[:, columns], out_hbm.at[pl.ds(row, wide), columns], sems.at[i]
        )
        copy.start()
        copies.append(copy)
    for copy in copies:
        copy.wait()


def weight_piece(me, dh, blocks, before, other, piece):
    tokens, ff = dh.shape
    half = blocks[0].shape[1]
    wide = half // PIECES
    step = 384
    return pl.pallas_call(
        lambda *refs: weight_kernel(*refs, other=other, piece=piece, wide=wide, step=step),
        out_shape=jax.ShapeDtypeStruct((2 * half, ff), jnp.bfloat16),
        in_specs=[SCALAR, WHOLE] + [WHOLE] * RING + [OUTSIDE] * len(before),
        out_specs=OUTSIDE,
        input_output_aliases={2 + RING: 0} if before else {},
        scratch_shapes=[
            pltpu.VMEM((wide, ff), jnp.bfloat16),
            pltpu.SemaphoreType.DMA((ff // step,)),
        ],
        compiler_params=pltpu.CompilerParams(vmem_limit_bytes=VMEM_LIMIT),
        cost_estimate=cost(3),
        name="weight_piece",
    )(me, dh, *blocks, *before)


def total(*terms):
    result = terms[0].astype(jnp.float32)
    for term in terms[1:]:
        result = result + term.astype(jnp.float32)
    return result.astype(jnp.bfloat16)


def after(x, *others):
    return lax.optimization_barrier((x, *others))[0]


def on_device(out_grad, pre_act, layer_input, weight):
    n = lax.axis_size("gx")
    rows, width = layer_input.shape
    if n != 2 * RING or rows % 16 or width % (2 * PIECES * 256):
        return plain(out_grad, pre_act, layer_input, weight)

    pairs = ring_pairs()
    swaps = [(i, i ^ 1) for i in range(n)]

    def ring(x):
        return lax.ppermute(x, "gx", pairs)

    def swap(x):
        return lax.ppermute(x, "gx", swaps)

    me = lax.axis_index("gx").astype(jnp.int32).reshape(1)
    core = me[0] % 2
    both = 2 * rows

    def block(x, k):
        return x[(k - 1) * both : k * both]

    def product(other, piece, before, *others):
        return input_piece(me, after(dh, *others), weight, before, other, piece)

    m0, o0 = prepare(me, layer_input, swap(layer_input))
    m1 = ring(m0)
    dh = hidden(after(me, m0), out_grad, pre_act)
    o1 = ring(after(o0, dh))
    go = product(True, 0, ())
    m1 = after(m1, go[0])
    m2, sm1 = ring(m1), swap(m1)
    go = product(True, 1, go, m1)
    o1 = after(o1, go[0])
    o2, so1 = ring(o1), swap(o1)
    go = product(True, 2, go, o1)
    m2 = after(m2, go[0])
    m3, sm2 = ring(m2), swap(m2)
    go = product(True, 3, go, m2)
    o2 = after(o2, go[0])
    o3, so2 = ring(o2), swap(o2)
    gm = product(False, 0, (), o2)
    m3 = after(m3, gm[0])
    m4, sm3 = ring(m3), swap(m3)
    own_o, behind_o, opposite_o, ahead_o = go
    from_m, opposite_from = swap(behind_o), swap(opposite_o)
    gm = product(False, 1, gm, m3)
    gm = product(False, 2, gm)
    o3 = after(o3, gm[0])
    so3 = swap(o3)
    gm = product(False, 3, gm, o3, from_m, opposite_from)
    own_m, behind_m, opposite_m, ahead_m = gm
    r4m = ring(total(opposite_m, opposite_from))
    from_o = swap(behind_m)
    m4 = after(m4, gm[0])
    sm4 = swap(m4)
    mine = (m0, m1, m2, m3, m4, so1, so2, so3)
    others = (o0, o1, o2, o3, sm4, sm1, sm2, sm3)

    def gradient(other, piece, before, *ties):
        blocks = others if other else mine
        return weight_piece(me, after(dh, *ties), blocks, before, other, piece)

    def send(ahead, came, k, *ring_terms):
        return ring(total(block(ahead, k), block(came, k), *ring_terms))

    r3o = send(ahead_o, from_o, 3)
    gw = gradient(False, 0, (), from_o)
    r4m = after(r4m, gw)
    r3m = send(ahead_m, from_m, 3, r4m)
    gw = gradient(False, 1, (gw,), r4m)
    r3o = after(r3o, gw)
    r2o = send(ahead_o, from_o, 2, r3o)
    gw = gradient(False, 2, (gw,), r3o)
    r3m = after(r3m, gw)
    r2m = send(ahead_m, from_m, 2, r3m)
    gw = gradient(False, 3, (gw,), r3m)
    r2o = after(r2o, gw)
    r1o = send(ahead_o, from_o, 1, r2o)
    gw = gradient(True, 0, (gw,), r2o)
    r2m = after(r2m, gw)
    r1m = send(ahead_m, from_m, 1, r2m)
    gw = gradient(True, 1, (gw,), r2m)
    gw = gradient(True, 2, (gw,))
    r1o = after(r1o, gw)

    def halves(own, came):
        whole = own.astype(jnp.float32) + came.astype(jnp.float32)
        low, high = whole[:rows], whole[rows:]
        kept = jnp.where(core == 0, low, high)
        return kept, jnp.where(core == 0, high, low).astype(jnp.bfloat16)

    kept_o, sent_o = halves(own_o, r1o)
    came_m = swap(sent_o)
    gw = gradient(True, 3, (gw,), r1o)
    r1m = after(r1m, gw)
    kept_m, sent_m = halves(own_m, r1m)
    came_o = swap(sent_m)
    out_o = (kept_o + came_o.astype(jnp.float32)).astype(jnp.bfloat16)
    out_m = (kept_m + came_m.astype(jnp.float32)).astype(jnp.bfloat16)
    low = jnp.where(core == 0, out_m, out_o)
    high = jnp.where(core == 0, out_o, out_m)
    return (jnp.concatenate([low, high], axis=1), gw)


def solution(mesh):
    placed = (P("group", "gx"), P("group", "gx"), P(("group", "gx"), None), P(None, "gx"))
    return jax.shard_map(
        on_device,
        mesh=mesh,
        in_specs=placed,
        out_specs=(P(("group", "gx"), None), P(None, ("group", "gx"))),
        check_vma=False,
    )
```

time: 222 us -> 127 us (0.57)
  waiting for transfers between devices: 142 us -> 19.5 us
  Pallas kernels: 0 us -> 70.6 us
  matrix products: 38.2 us -> 0 us
  starting transfers between devices: 0.08 us -> 16.9 us
  local copies, waits for them, and re-layouts: 25 us -> 10.7 us
  between operations: 14 us -> 1.14 us
  other arithmetic: 1.92 us -> 6.99 us
    reduce_scatter x1 -> x0, waiting for transfers between devices: 94.3 us -> none  [on_device(): lax.psum_scatter(lax.dot_general(block, weight, (((1,), (1,)), ((), ())),...]
    pallas_call x0 -> x18, Pallas kernels: none -> 70.6 us  [the longest x8 35 us: input_piece(): pl.pallas_call(lambda *refs: input_kernel(*refs, other=other, piece=piece...]
    all_gather x1 -> x0, waiting for transfers between devices: 46.7 us -> none  [on_device(): lax.all_gather(layer_input, 'gx', axis=0, tiled=True)]
    dot_general x2 -> x0, matrix products: 38.2 us -> none  [the longest x1 20.2 us: on_device(): lax.dot_general(block, weight, (((1,), (1,)), ((), ())), preferred_elemen...]
    ppermute x0 -> x27, waiting for transfers between devices: none -> 19.5 us  [the longest x14 16.8 us: ring(): return lax.ppermute(x, 'gx', pairs)]
    ppermute x0 -> x27, starting transfers between devices: none -> 16.9 us  [the longest x14 14.3 us: ring(): return lax.ppermute(x, 'gx', pairs)]
    unnamed x5 -> x50, local copies, waits for them, and re-layouts: 25 us -> 10.7 us
    convert_element_type x1 -> x9, other arithmetic: 1.92 us -> 5.91 us  [the longest x7 5.84 us: total(): return result.astype(jnp.bfloat16)]
  transfers between devices with their start and end apart: 2 -> 27, of which waited for: 2 -> 8; matrix products, arithmetic and copies ran while one was open for 29% -> 4% of each run, Pallas kernels for 0% -> 52%
where the time goes in v2:
time: 127 us; the launch traced here: 126 us
  Pallas kernels  70.6 us (56%)
  waiting for transfers between devices  19.5 us (15%)
  starting transfers between devices  16.9 us (13%)
  local copies, waits for them, and re-layouts  10.7 us (8%)
  other arithmetic  6.99 us (6%)
    pallas_call x8, Pallas kernels, input_piece(): pl.pallas_call(lambda *refs: input_kernel(*refs, other=other, piece=piece...  35 us
    pallas_call x8, Pallas kernels, weight_piece(): pl.pallas_call(lambda *refs: weight_kernel(*refs, other=other, piece=piec...  31.1 us
    ppermute x14, waiting for transfers between devices, ring(): return lax.ppermute(x, 'gx', pairs)  16.8 us
    ppermute x14, starting transfers between devices, ring(): return lax.ppermute(x, 'gx', pairs)  14.3 us
    unnamed x50, local copies, waits for them, and re-layouts  10.7 us
    convert_element_type x7, other arithmetic, total(): return result.astype(jnp.bfloat16)  5.84 us
    pallas_call x1, Pallas kernels, hidden(): pl.pallas_call(hidden_kernel, out_shape=jax.ShapeDtypeStruct(shape, dtype...  4.56 us
    ppermute x13, waiting for transfers between devices, swap(): return lax.ppermute(x, 'gx', swaps)  2.69 us
  transfers between devices with their start and end apart: 27, of which 8 were waited for; matrix products, arithmetic and copies ran while one was open for 4% of the time, Pallas kernels for 52%

profile of v2, /device:TPU:0, one launch (start us, length us, event | category | flops | bytes accessed | tf_op | source)
XLA Modules:
  0.0 125.8 jit_solution(13644809507737058739)
XLA Ops:
  0.6 0.5 collective-permute-start
  1.1 1.6 %collective-permute-done.twin_ref = bf16[32,6144]{1,0:T(8,128)(2,1)S(1)} collective-permute-done((bf16[32,6144]{1,0:T(8,128)(2,1)}, bf16[32,6144]{1,0:T(8,128)(2,1)S(1)}, u32[]{:S(2)}, u32[]{:S(2)}) %collective-permute-start) | collective-permute-done | bytes 393248 | tf_op jit(solution)/shard_map/ppermute | solution.py:277
  2.7 1.0 copy-done.22
  3.8 3.0 %collective-permute-start.2 = (bf16[64,3072]{1,0:T(8,128)(2,1)S(1)}, bf16[64,3072]{1,0:T(8,128)(2,1)S(1)}, u32[]{:S(2)}, u32[]{:S(2)}) collective-permute-start(bf16[64,3072]{1,0:T(8,128)(2,1)S(1)} %get-tuple-element.65.refs_2_), channel_id=1, source_target_pairs={{0,4},{1,3},{4,8},{5,1},{8,12},{9,5},{12,14},{13,9},{14,10},{15,13... | collective-permute-start | bytes 1179656 | tf_op jit(solution)/shard_map/ppermute | solution.py:274
  6.8 4.6 %hidden.1.refs_1_ = bf16[512,1536]{1,0:T(8,128)(2,1)} custom-call(s32[1]{0:T(128)} %bitcast.me_ref.refs_0_, bf16[512,1536]{1,0:T(8,128)(2,1)} %og_hbm.1, bf16[512,1536]{1,0:T(8,128)(2,1)} %pre_hbm.1), custom_call_target="tpu_custom_call" | custom-call | flops 3449999872 | tf_op jit(solution)/shard_map/hidden/pallas_call | solution.py:106
  11.3 1.6 %collective-permute-start.1 = (bf16[64,3072]{1,0:T(8,128)(2,1)S(1)}, bf16[64,3072]{1,0:T(8,128)(2,1)S(1)}, u32[]{:S(2)}, u32[]{:S(2)}) collective-permute-start(bf16[64,3072]{1,0:T(8,128)(2,1)S(1)} %get-tuple-element.68.refs_2_), channel_id=1, source_target_pairs={{0,4},{1,3},{4,8},{5,1},{8,12},{9,5},{12,14},{13,9},{14,10},{15,13... | collective-permute-start | bytes 1179656 | tf_op jit(solution)/shard_map/ppermute | solution.py:274
  13.0 1.4 %copy-done = bf16[512,1536]{1,0:T(8,128)(2,1)S(1)} copy-done((bf16[512,1536]{1,0:T(8,128)(2,1)S(1)}, bf16[512,1536]{1,0:T(8,128)(2,1)}, u32[]{:S(2)}) %copy-start) | copy-done | bytes 1572888
  14.4 4.0 %input_piece.8 = (bf16[64,3072]{1,0:T(8,128)(2,1)S(1)}, bf16[192,3072]{1,0:T(8,128)(2,1)S(1)}, bf16[64,3072]{1,0:T(8,128)(2,1)S(1)}, bf16[192,3072]{1,0:T(8,128)(2,1)S(1)}) custom-call(s32[1]{0:T(128)} %bitcast.me_ref.refs_0_, bf16[512,1536]{1,0:T(8,128)(2,1)S(1)} %copy-done, bf16[6144,1536]{1,0:T(8,128)(2,1)} %refs_2_.15), custom_call_target="tpu_custom_call" | custom-call | flops 3449999872 | tf_op jit(solution)/shard_map/input_piece/pallas_call | solution.py:194
  18.4 1.6 %collective-permute-start.4 = (bf16[64,3072]{1,0:T(8,128)(2,1)S(1)}, bf16[64,3072]{1,0:T(8,128)(2,1)S(1)}, u32[]{:S(2)}, u32[]{:S(2)}) collective-permute-start(bf16[64,3072]{1,0:T(8,128)(2,1)S(1)} %collective-permute-done.2.refs_3_), channel_id=1, source_target_pairs={{0,4},{1,3},{4,8},{5,1},{8,12},{9,5},{12,14},{13,9},{14,10},{15,13... | collective-permute-start | bytes 1179656 | tf_op jit(solution)/shard_map/ppermute | solution.py:274
  20.0 4.0 %input_piece.9 = (bf16[64,3072]{1,0:T(8,128)(2,1)S(1)}, bf16[192,3072]{1,0:T(8,128)(2,1)S(1)}, bf16[64,3072]{1,0:T(8,128)(2,1)S(1)}, bf16[192,3072]{1,0:T(8,128)(2,1)S(1)}) custom-call(s32[1]{0:T(128)} %bitcast.me_ref.refs_0_, bf16[512,1536]{1,0:T(8,128)(2,1)S(1)} %copy-done, ...), custom_call_target="tpu_custom_call", output_to_operand_aliasing={{0}: (3, {}), {1}: (4, {}), {2}: (5, {}), {3}: (6, {})} | custom-call | flops 3449999872 | tf_op jit(solution)/shard_map/input_piece/pallas_call | solution.py:194
  24.0 1.6 %collective-permute-start.3 = (bf16[64,3072]{1,0:T(8,128)(2,1)S(1)}, bf16[64,3072]{1,0:T(8,128)(2,1)}, u32[]{:S(2)}, u32[]{:S(2)}) collective-permute-start(bf16[64,3072]{1,0:T(8,128)(2,1)S(1)} %collective-permute-done.1.refs_3_), channel_id=1, source_target_pairs={{0,4},{1,3},{4,8},{5,1},{8,12},{9,5},{12,14},{13,9},{14,10},{15,13... | collective-permute-start | bytes 1179656 | tf_op jit(solution)/shard_map/ppermute | solution.py:274
  25.6 4.0 %input_piece.10 = (bf16[64,3072]{1,0:T(8,128)(2,1)S(1)}, bf16[192,3072]{1,0:T(8,128)(2,1)S(1)}, bf16[64,3072]{1,0:T(8,128)(2,1)S(1)}, bf16[192,3072]{1,0:T(8,128)(2,1)S(1)}) custom-call(s32[1]{0:T(128)} %bitcast.me_ref.refs_0_, bf16[512,1536]{1,0:T(8,128)(2,1)S(1)} %copy-done, ...), custom_call_target="tpu_custom_call", output_to_operand_aliasing={{0}: (3, {}), {1}: (4, {}), {2}: (5, {}), {3}: (6, {})} | custom-call | flops 3449999872 | tf_op jit(solution)/shard_map/input_piece/pallas_call | solution.py:194
  29.6 4.1 %input_piece.11 = (bf16[64,3072]{1,0:T(8,128)(2,1)S(1)}, bf16[192,3072]{1,0:T(8,128)(2,1)S(1)}, bf16[64,3072]{1,0:T(8,128)(2,1)S(1)}, bf16[192,3072]{1,0:T(8,128)(2,1)S(1)}) custom-call(s32[1]{0:T(128)} %bitcast.me_ref.refs_0_, bf16[512,1536]{1,0:T(8,128)(2,1)S(1)} %copy-done, ...), custom_call_target="tpu_custom_call", output_to_operand_aliasing={{0}: (3, {}), {1}: (4, {}), {2}: (5, {}), {3}: (6, {})} | custom-call | flops 3449999872 | tf_op jit(solution)/shard_map/input_piece/pallas_call | solution.py:194
  33.8 0.7 copy-done.18
  34.5 0.5 collective-permute-start.6
  35.0 0.5 collective-permute-start.5
  35.5 4.6 %input_piece.12 = (bf16[64,3072]{1,0:T(8,128)(2,1)S(1)}, bf16[192,3072]{1,0:T(8,128)(2,1)}, bf16[64,3072]{1,0:T(8,128)(2,1)S(1)}, bf16[192,3072]{1,0:T(8,128)(2,1)S(1)}) custom-call(s32[1]{0:T(128)} %bitcast.me_ref.refs_0_, bf16[512,1536]{1,0:T(8,128)(2,1)S(1)} %copy-done, bf16[6144,1536]{1,0:T(8,128)(2,1)} %refs_2_.15), custom_call_target="tpu_custom_call" | custom-call | flops 3449999872 | tf_op jit(solution)/shard_map/input_piece/pallas_call | solution.py:194
  40.1 2.2 %collective-permute-done.6.refs_5_ = bf16[64,3072]{1,0:T(8,128)(2,1)S(1)} collective-permute-done((bf16[64,3072]{1,0:T(8,128)(2,1)S(1)}, bf16[64,3072]{1,0:T(8,128)(2,1)S(1)}, u32[]{:S(2)}, u32[]{:S(2)}) %collective-permute-start.6) | collective-permute-done | bytes 393248 | tf_op jit(solution)/shard_map/ppermute | solution.py:274
  42.3 4.7 %input_piece.13 = (bf16[64,3072]{1,0:T(8,128)(2,1)S(1)}, bf16[192,3072]{1,0:T(8,128)(2,1)}, bf16[64,3072]{1,0:T(8,128)(2,1)S(1)}, bf16[192,3072]{1,0:T(8,128)(2,1)S(1)}) custom-call(s32[1]{0:T(128)} %bitcast.me_ref.refs_0_, bf16[512,1536]{1,0:T(8,128)(2,1)S(1)} %copy-done, ...), custom_call_target="tpu_custom_call", output_to_operand_aliasing={{0}: (3, {}), {1}: (4, {}), {2}: (5, {}), {3}: (6, {})} | custom-call | flops 3449999872 | tf_op jit(solution)/shard_map/input_piece/pallas_call | solution.py:194
  47.0 4.6 %input_piece.14 = (bf16[64,3072]{1,0:T(8,128)(2,1)S(1)}, bf16[192,3072]{1,0:T(8,128)(2,1)}, bf16[64,3072]{1,0:T(8,128)(2,1)S(1)}, bf16[192,3072]{1,0:T(8,128)(2,1)S(1)}) custom-call(s32[1]{0:T(128)} %bitcast.me_ref.refs_0_, bf16[512,1536]{1,0:T(8,128)(2,1)S(1)} %copy-done, ...), custom_call_target="tpu_custom_call", output_to_operand_aliasing={{0}: (3, {}), {1}: (4, {}), {2}: (5, {}), {3}: (6, {})} | custom-call | flops 3449999872 | tf_op jit(solution)/shard_map/input_piece/pallas_call | solution.py:194
  51.6 5.0 %input_piece.15 = (bf16[64,3072]{1,0:T(8,128)(2,1)S(1)}, bf16[192,3072]{1,0:T(8,128)(2,1)}, bf16[64,3072]{1,0:T(8,128)(2,1)S(1)}, bf16[192,3072]{1,0:T(8,128)(2,1)S(1)}) custom-call(s32[1]{0:T(128)} %bitcast.me_ref.refs_0_, bf16[512,1536]{1,0:T(8,128)(2,1)S(1)} %copy-done, ...), custom_call_target="tpu_custom_call", output_to_operand_aliasing={{0}: (3, {}), {1}: (4, {}), {2}: (5, {}), {3}: (6, {})} | custom-call | flops 3449999872 | tf_op jit(solution)/shard_map/input_piece/pallas_call | solution.py:194
  56.7 1.0 copy-done.2
  57.7 0.7 copy-done.20
  58.5 0.5 collective-permute-start.12
  59.0 0.4 collective-permute-start.11
  59.4 0.3 collective-permute-start.14
  59.7 0.9 add_convert_fusion.6
  60.6 6.2 %collective-permute-done.11.refs_6_ = bf16[64,3072]{1,0:T(8,128)(2,1)S(1)} collective-permute-done((bf16[64,3072]{1,0:T(8,128)(2,1)S(1)}, bf16[64,3072]{1,0:T(8,128)(2,1)S(1)}, u32[]{:S(2)}, u32[]{:S(2)}) %collective-permute-start.11) | collective-permute-done | bytes 393248 | tf_op jit(solution)/shard_map/ppermute | solution.py:274
  66.8 0.7 copy-done.15
  67.5 0.4 collective-permute-start.9
  68.0 0.5 collective-permute-start.21
  68.6 1.0 copy-done.5
  69.6 1.0 copy-done.7
  70.6 1.0 copy-done.10
  71.6 1.0 copy-done.13
  72.5 1.0 copy-done.16
  73.5 4.0 %weight_piece.8.refs_10_ = bf16[6144,1536]{1,0:T(8,128)(2,1)} custom-call(s32[1]{0:T(128)} %bitcast.me_ref.refs_0_, bf16[512,1536]{1,0:T(8,128)(2,1)S(1)} %copy-done.1, bf16[64,3072]{1,0:T(8,128)(2,1)S(1)} %copy-done.5, bf16[64,3072]{1,0:T(8,128)(2,1)S(1)} %copy-done.7, bf16[64,3072]{1,0:T(8,128)(2,1)S(1)} %copy-done.10, bf16[64,3072]{1,0:T(8,128)(2,1)S(1)} %copy-done.13, ...), custom_call_target="tpu_custom_call" | custom-call | flops 3449999872 | tf_op jit(solution)/shard_map/weight_piece/pallas_call | solution.py:237
  77.6 1.2 add_convert_fusion.4
  78.9 0.9 collective-permute-start.16
  79.8 1.1 add_convert_fusion.5
  81.0 0.5 collective-permute-start.15
  81.5 3.9 %weight_piece.9.refs_10_ = bf16[6144,1536]{1,0:T(8,128)(2,1)} custom-call(s32[1]{0:T(128)} %bitcast.me_ref.refs_0_, bf16[512,1536]{1,0:T(8,128)(2,1)S(1)} %copy-done.1, bf16[64,3072]{1,0:T(8,128)(2,1)S(1)} %copy-done.5, bf16[64,3072]{1,0:T(8,128)(2,1)S(1)} %copy-done.8, bf16[64,3072]{1,0:T(8,128)(2,1)S(1)} %copy-done.11, ...), custom_call_target="tpu_custom_call", output_to_operand_aliasing={{}: (10, {})} | custom-call | flops 3449999872 | tf_op jit(solution)/shard_map/weight_piece/pallas_call | solution.py:237
  85.4 1.3 %collective-permute-done.16 = bf16[64,3072]{1,0:T(8,128)(2,1)S(1)} collective-permute-done((bf16[64,3072]{1,0:T(8,128)(2,1)S(1)}, bf16[64,3072]{1,0:T(8,128)(2,1)S(1)}, u32[]{:S(2)}, u32[]{:S(2)}) %collective-permute-start.16) | collective-permute-done | bytes 393248 | tf_op jit(solution)/shard_map/ppermute | solution.py:274
  86.7 3.9 %weight_piece.10.refs_10_ = bf16[6144,1536]{1,0:T(8,128)(2,1)} custom-call(s32[1]{0:T(128)} %bitcast.me_ref.refs_0_, bf16[512,1536]{1,0:T(8,128)(2,1)S(1)} %copy-done.1, bf16[64,3072]{1,0:T(8,128)(2,1)S(1)} %copy-done.5, bf16[64,3072]{1,0:T(8,128)(2,1)S(1)} %copy-done.8, bf16[64,3072]{1,0:T(8,128)(2,1)S(1)} %copy-done.11, ...), custom_call_target="tpu_custom_call", output_to_operand_aliasing={{}: (10, {})} | custom-call | flops 3449999872 | tf_op jit(solution)/shard_map/weight_piece/pallas_call | solution.py:237
  90.6 0.3 collective-permute-done.15
  90.9 1.1 add_convert_fusion.2
  92.1 0.9 collective-permute-start.18
  93.0 0.2 add_convert_fusion.3
  93.1 6.7 %collective-permute-done.18 = bf16[64,3072]{1,0:T(8,128)(2,1)S(1)} collective-permute-done((bf16[64,3072]{1,0:T(8,128)(2,1)S(1)}, bf16[64,3072]{1,0:T(8,128)(2,1)S(1)}, u32[]{:S(2)}, u32[]{:S(2)}) %collective-permute-start.18) | collective-permute-done | bytes 393248 | tf_op jit(solution)/shard_map/ppermute | solution.py:274
  99.9 0.9 collective-permute-start.17
  100.8 3.9 %weight_piece.11.refs_10_ = bf16[6144,1536]{1,0:T(8,128)(2,1)} custom-call(s32[1]{0:T(128)} %bitcast.me_ref.refs_0_, bf16[512,1536]{1,0:T(8,128)(2,1)S(1)} %copy-done.1, bf16[64,3072]{1,0:T(8,128)(2,1)S(1)} %copy-done.5, bf16[64,3072]{1,0:T(8,128)(2,1)S(1)} %copy-done.8, bf16[64,3072]{1,0:T(8,128)(2,1)S(1)} %copy-done.11, ...), custom_call_target="tpu_custom_call", output_to_operand_aliasing={{}: (10, {})} | custom-call | flops 3449999872 | tf_op jit(solution)/shard_map/weight_piece/pallas_call | solution.py:237
  104.7 3.8 %weight_piece.12.refs_10_ = bf16[6144,1536]{1,0:T(8,128)(2,1)} custom-call(s32[1]{0:T(128)} %bitcast.me_ref.refs_0_, bf16[512,1536]{1,0:T(8,128)(2,1)S(1)} %copy-done.1, bf16[64,3072]{1,0:T(8,128)(2,1)S(1)} %get-tuple-element.68.refs_2_, bf16[64,3072]{1,0:T(8,128)(2,1)S(1)} %collective-permute-done.1.refs_3_, ...), custom_call_target="tpu_custom_call", output_to_operand_aliasing={{}: (10, {})} | custom-call | flops 3449999872 | tf_op jit(solution)/shard_map/weight_piece/pallas_call | solution.py:237
  108.5 1.1 add_convert_fusion
  109.7 0.5 collective-permute-start.24
  110.2 0.2 add_convert_fusion.1
  110.3 0.9 collective-permute-start.23
  111.3 3.8 %weight_piece.13.refs_10_ = bf16[6144,1536]{1,0:T(8,128)(2,1)} custom-call(s32[1]{0:T(128)} %bitcast.me_ref.refs_0_, bf16[512,1536]{1,0:T(8,128)(2,1)S(1)} %copy-done.1, bf16[64,3072]{1,0:T(8,128)(2,1)S(1)} %get-tuple-element.68.refs_2_, bf16[64,3072]{1,0:T(8,128)(2,1)S(1)} %collective-permute-done.1.refs_3_, ...), custom_call_target="tpu_custom_call", output_to_operand_aliasing={{}: (10, {})} | custom-call | flops 3449999872 | tf_op jit(solution)/shard_map/weight_piece/pallas_call | solution.py:237
  115.1 3.8 %weight_piece.14.refs_10_ = bf16[6144,1536]{1,0:T(8,128)(2,1)} custom-call(s32[1]{0:T(128)} %bitcast.me_ref.refs_0_, bf16[512,1536]{1,0:T(8,128)(2,1)S(1)} %copy-done.1, bf16[64,3072]{1,0:T(8,128)(2,1)S(1)} %get-tuple-element.68.refs_2_, bf16[64,3072]{1,0:T(8,128)(2,1)S(1)} %collective-permute-done.1.refs_3_, ...), custom_call_target="tpu_custom_call", output_to_operand_aliasing={{}: (10, {})} | custom-call | flops 3449999872 | tf_op jit(solution)/shard_map/weight_piece/pallas_call | solution.py:237
  119.1 3.8 %weight_piece.15 = bf16[6144,1536]{1,0:T(8,128)(2,1)} custom-call(s32[1]{0:T(128)} %bitcast.me_ref.refs_0_, bf16[512,1536]{1,0:T(8,128)(2,1)S(1)} %copy-done.1, bf16[64,3072]{1,0:T(8,128)(2,1)S(1)} %get-tuple-element.68.refs_2_, bf16[64,3072]{1,0:T(8,128)(2,1)S(1)} %collective-permute-done.1.refs_3_, ...), custom_call_target="tpu_custom_call", output_to_operand_aliasing={{}: (10, {})} | custom-call | flops 3449999872 | tf_op jit(solution)/shard_map/weight_piece/pallas_call | solution.py:237
  123.2 0.6 collective-permute-start.25
  123.8 0.8 collective-permute-done.26
  124.6 0.3 collective-permute-done.25
  124.9 0.1 broadcast_select_fusion.1
  125.0 0.8 pad_maximum_fusion
  (72 shorter events, 0.7 us)
Async XLA Ops:
  0.6 2.1 %collective-permute-start = (bf16[32,6144]{1,0:T(8,128)(2,1)}, bf16[32,6144]{1,0:T(8,128)(2,1)S(1)}, u32[]{:S(2)}, u32[]{:S(2)}) collective-permute-start(bf16[32,6144]{1,0:T(8,128)(2,1)} %own_ref.1), channel_id=1, source_target_pairs={{0,1},{1,0},{2,3},{3,2},{4,5},{5,4},{6,7},{7,6},{8,9},{9,8},{10,11... | collective-permute-start | bytes 1179656 | tf_op jit(solution)/shard_map/ppermute | solution.py:277
  2.7 1.0 copy-start.22
  3.8 7.6 %copy-start.4 = (bf16[64,3072]{1,0:T(8,128)(2,1)}, bf16[64,3072]{1,0:T(8,128)(2,1)S(1)}, u32[]{:S(2)}) copy-start(bf16[64,3072]{1,0:T(8,128)(2,1)S(1)} %get-tuple-element.65.refs_2_) | copy-start | bytes 1179652
  3.8 14.6 %collective-permute-start.2 = (bf16[64,3072]{1,0:T(8,128)(2,1)S(1)}, bf16[64,3072]{1,0:T(8,128)(2,1)S(1)}, u32[]{:S(2)}, u32[]{:S(2)}) collective-permute-start(bf16[64,3072]{1,0:T(8,128)(2,1)S(1)} %get-tuple-element.65.refs_2_), channel_id=1, source_target_pairs={{0,4},{1,3},{4,8},{5,1},{8,12},{9,5},{12,14},{13,9},{14,10},{15,13... | collective-permute-start | bytes 1179656 | tf_op jit(solution)/shard_map/ppermute | solution.py:274
  11.3 12.7 %collective-permute-start.1 = (bf16[64,3072]{1,0:T(8,128)(2,1)S(1)}, bf16[64,3072]{1,0:T(8,128)(2,1)S(1)}, u32[]{:S(2)}, u32[]{:S(2)}) collective-permute-start(bf16[64,3072]{1,0:T(8,128)(2,1)S(1)} %get-tuple-element.68.refs_2_), channel_id=1, source_target_pairs={{0,4},{1,3},{4,8},{5,1},{8,12},{9,5},{12,14},{13,9},{14,10},{15,13... | collective-permute-start | bytes 1179656 | tf_op jit(solution)/shard_map/ppermute | solution.py:274
  13.0 1.4 %copy-start = (bf16[512,1536]{1,0:T(8,128)(2,1)S(1)}, bf16[512,1536]{1,0:T(8,128)(2,1)}, u32[]{:S(2)}) copy-start(bf16[512,1536]{1,0:T(8,128)(2,1)} %hidden.1.refs_1_) | copy-start | bytes 4718596
  18.4 5.6 %copy-start.6 = (bf16[64,3072]{1,0:T(8,128)(2,1)}, bf16[64,3072]{1,0:T(8,128)(2,1)S(1)}, u32[]{:S(2)}) copy-start(bf16[64,3072]{1,0:T(8,128)(2,1)S(1)} %collective-permute-done.2.refs_3_) | copy-start | bytes 1179652
  18.4 11.2 %collective-permute-start.4 = (bf16[64,3072]{1,0:T(8,128)(2,1)S(1)}, bf16[64,3072]{1,0:T(8,128)(2,1)S(1)}, u32[]{:S(2)}, u32[]{:S(2)}) collective-permute-start(bf16[64,3072]{1,0:T(8,128)(2,1)S(1)} %collective-permute-done.2.refs_3_), channel_id=1, source_target_pairs={{0,4},{1,3},{4,8},{5,1},{8,12},{9,5},{12,14},{13,9},{14,10},{15,13... | collective-permute-start | bytes 1179656 | tf_op jit(solution)/shard_map/ppermute | solution.py:274
  24.0 10.9 %collective-permute-start.3 = (bf16[64,3072]{1,0:T(8,128)(2,1)S(1)}, bf16[64,3072]{1,0:T(8,128)(2,1)}, u32[]{:S(2)}, u32[]{:S(2)}) collective-permute-start(bf16[64,3072]{1,0:T(8,128)(2,1)S(1)} %collective-permute-done.1.refs_3_), channel_id=1, source_target_pairs={{0,4},{1,3},{4,8},{5,1},{8,12},{9,5},{12,14},{13,9},{14,10},{15,13... | collective-permute-start | bytes 1179656 | tf_op jit(solution)/shard_map/ppermute | solution.py:274
  29.6 4.9 %copy-start.9 = (bf16[64,3072]{1,0:T(8,128)(2,1)}, bf16[64,3072]{1,0:T(8,128)(2,1)S(1)}, u32[]{:S(2)}) copy-start(bf16[64,3072]{1,0:T(8,128)(2,1)S(1)} %collective-permute-done.4.refs_4_) | copy-start | bytes 1179652
  33.8 0.7 copy-start.18
  34.5 17.1 %collective-permute-start.7 = (bf16[192,3072]{1,0:T(8,128)(2,1)S(1)}, bf16[192,3072]{1,0:T(8,128)(2,1)S(1)}, u32[]{:S(2)}, u32[]{:S(2)}) collective-permute-start(bf16[192,3072]{1,0:T(8,128)(2,1)S(1)} %get-tuple-element.102), channel_id=1, source_target_pairs={{0,1},{1,0},{2,3},{3,2},{4,5},{5,4},{6,7},{7,6},{8,9},{9,8},{10,11... | collective-permute-start | bytes 3538952 | tf_op jit(solution)/shard_map/ppermute | solution.py:277
  34.5 7.8 %collective-permute-start.6 = (bf16[64,3072]{1,0:T(8,128)(2,1)S(1)}, bf16[64,3072]{1,0:T(8,128)(2,1)S(1)}, u32[]{:S(2)}, u32[]{:S(2)}) collective-permute-start(bf16[64,3072]{1,0:T(8,128)(2,1)S(1)} %collective-permute-done.4.refs_4_), channel_id=1, source_target_pairs={{0,4},{1,3},{4,8},{5,1},{8,12},{9,5},{12,14},{13,9},{14,10},{15,13... | collective-permute-start | bytes 1179656 | tf_op jit(solution)/shard_map/ppermute | solution.py:274
  35.0 16.6 %collective-permute-start.5 = (bf16[64,3072]{1,0:T(8,128)(2,1)}, bf16[64,3072]{1,0:T(8,128)(2,1)}, u32[]{:S(2)}, u32[]{:S(2)}) collective-permute-start(bf16[64,3072]{1,0:T(8,128)(2,1)} %collective-permute-done.3.refs_4_), channel_id=1, source_target_pairs={{0,4},{1,3},{4,8},{5,1},{8,12},{9,5},{12,14},{13,9},{14,10},{15,13... | collective-permute-start | bytes 1179656 | tf_op jit(solution)/shard_map/ppermute | solution.py:274
  35.4 16.2 %collective-permute-start.8 = (bf16[64,3072]{1,0:T(8,128)(2,1)S(1)}, bf16[64,3072]{1,0:T(8,128)(2,1)S(1)}, u32[]{:S(2)}, u32[]{:S(2)}) collective-permute-start(bf16[64,3072]{1,0:T(8,128)(2,1)S(1)} %get-tuple-element.103), channel_id=1, source_target_pairs={{0,1},{1,0},{2,3},{3,2},{4,5},{5,4},{6,7},{7,6},{8,9},{9,8},{10,11... | collective-permute-start | bytes 1179656 | tf_op jit(solution)/shard_map/ppermute | solution.py:277
  42.3 16.7 %copy-start.12 = (bf16[64,3072]{1,0:T(8,128)(2,1)}, bf16[64,3072]{1,0:T(8,128)(2,1)S(1)}, u32[]{:S(2)}) copy-start(bf16[64,3072]{1,0:T(8,128)(2,1)S(1)} %collective-permute-done.6.refs_5_) | copy-start | bytes 1179652
  51.6 5.1 %copy-start.23 = (bf16[192,3072]{1,0:T(8,128)(2,1)}, bf16[192,3072]{1,0:T(8,128)(2,1)S(1)}, u32[]{:S(2)}) copy-start(bf16[192,3072]{1,0:T(8,128)(2,1)S(1)} %collective-permute-done.7) | copy-start | bytes 3538948
  51.6 16.9 %copy-start.1 = (bf16[512,1536]{1,0:T(8,128)(2,1)S(1)}, bf16[512,1536]{1,0:T(8,128)(2,1)}, u32[]{:S(2)}) copy-start(bf16[512,1536]{1,0:T(8,128)(2,1)} %hidden.1.refs_1_) | copy-start | bytes 4718596
  56.7 1.0 copy-start.2
  57.7 0.7 copy-start.20
  58.5 9.5 %collective-permute-start.10 = (bf16[192,3072]{1,0:T(8,128)(2,1)}, bf16[192,3072]{1,0:T(8,128)(2,1)}, u32[]{:S(2)}, u32[]{:S(2)}) collective-permute-start(bf16[192,3072]{1,0:T(8,128)(2,1)} %get-tuple-element.111), channel_id=1, source_target_pairs={{0,1},{1,0},{2,3},{3,2},{4,5},{5,4},{6,7},{7,6},{8,9},{9,8},{10,11... | collective-permute-start | bytes 3538952 | tf_op jit(solution)/shard_map/ppermute | solution.py:277
  58.5 9.5 %collective-permute-start.12 = (bf16[64,3072]{1,0:T(8,128)(2,1)S(1)}, bf16[64,3072]{1,0:T(8,128)(2,1)}, u32[]{:S(2)}, u32[]{:S(2)}) collective-permute-start(bf16[64,3072]{1,0:T(8,128)(2,1)S(1)} %collective-permute-done.1.refs_3_), channel_id=1, source_target_pairs={{0,1},{1,0},{2,3},{3,2},{4,5},{5,4},{6,7},{7,6},{8,9},{9,8},{10,11... | collective-permute-start | bytes 1179656 | tf_op jit(solution)/shard_map/ppermute | solution.py:277
  59.0 9.5 %collective-permute-start.13 = (bf16[64,3072]{1,0:T(8,128)(2,1)}, bf16[64,3072]{1,0:T(8,128)(2,1)}, u32[]{:S(2)}, u32[]{:S(2)}) collective-permute-start(bf16[64,3072]{1,0:T(8,128)(2,1)} %collective-permute-done.3.refs_4_), channel_id=1, source_target_pairs={{0,1},{1,0},{2,3},{3,2},{4,5},{5,4},{6,7},{7,6},{8,9},{9,8},{10,11... | collective-permute-start | bytes 1179656 | tf_op jit(solution)/shard_map/ppermute | solution.py:277
  59.0 7.8 %collective-permute-start.11 = (bf16[64,3072]{1,0:T(8,128)(2,1)S(1)}, bf16[64,3072]{1,0:T(8,128)(2,1)S(1)}, u32[]{:S(2)}, u32[]{:S(2)}) collective-permute-start(bf16[64,3072]{1,0:T(8,128)(2,1)S(1)} %collective-permute-done.6.refs_5_), channel_id=1, source_target_pairs={{0,4},{1,3},{4,8},{5,1},{8,12},{9,5},{12,14},{13,9},{14,10},{15,13... | collective-permute-start | bytes 1179656 | tf_op jit(solution)/shard_map/ppermute | solution.py:274
  59.4 9.1 %collective-permute-start.14 = (bf16[64,3072]{1,0:T(8,128)(2,1)}, bf16[64,3072]{1,0:T(8,128)(2,1)}, u32[]{:S(2)}, u32[]{:S(2)}) collective-permute-start(bf16[64,3072]{1,0:T(8,128)(2,1)} %collective-permute-done.5.refs_5_), channel_id=1, source_target_pairs={{0,1},{1,0},{2,3},{3,2},{4,5},{5,4},{6,7},{7,6},{8,9},{9,8},{10,11... | collective-permute-start | bytes 1179656 | tf_op jit(solution)/shard_map/ppermute | solution.py:277
  66.8 0.7 copy-start.15
  67.5 10.1 %collective-permute-start.9 = (bf16[64,3072]{1,0:T(8,128)(2,1)}, bf16[64,3072]{1,0:T(8,128)(2,1)}, u32[]{:S(2)}, u32[]{:S(2)}) collective-permute-start(bf16[64,3072]{1,0:T(8,128)(2,1)} %add_convert_fusion.6), channel_id=1, source_target_pairs={{0,4},{1,3},{4,8},{5,1},{8,12},{9,5},{12,14},{13,9},{14,10},{15,13... | collective-permute-start | bytes 1179656 | tf_op jit(solution)/shard_map/ppermute | solution.py:274
  68.0 36.7 %collective-permute-start.20 = (bf16[64,3072]{1,0:T(8,128)(2,1)}, bf16[64,3072]{1,0:T(8,128)(2,1)S(1)}, u32[]{:S(2)}, u32[]{:S(2)}) collective-permute-start(bf16[64,3072]{1,0:T(8,128)(2,1)} %copy-done.6), channel_id=1, source_target_pairs={{0,1},{1,0},{2,3},{3,2},{4,5},{5,4},{6,7},{7,6},{8,9},{9,8},{10,11... | collective-permute-start | bytes 1179656 | tf_op jit(solution)/shard_map/ppermute | solution.py:277
  68.0 36.7 %collective-permute-start.21 = (bf16[64,3072]{1,0:T(8,128)(2,1)}, bf16[64,3072]{1,0:T(8,128)(2,1)S(1)}, u32[]{:S(2)}, u32[]{:S(2)}) collective-permute-start(bf16[64,3072]{1,0:T(8,128)(2,1)} %copy-done.9), channel_id=1, source_target_pairs={{0,1},{1,0},{2,3},{3,2},{4,5},{5,4},{6,7},{7,6},{8,9},{9,8},{10,11... | collective-permute-start | bytes 1179656 | tf_op jit(solution)/shard_map/ppermute | solution.py:277
  68.5 36.2 %collective-permute-start.22 = (bf16[64,3072]{1,0:T(8,128)(2,1)}, bf16[64,3072]{1,0:T(8,128)(2,1)S(1)}, u32[]{:S(2)}, u32[]{:S(2)}) collective-permute-start(bf16[64,3072]{1,0:T(8,128)(2,1)} %copy-done.12), channel_id=1, source_target_pairs={{0,1},{1,0},{2,3},{3,2},{4,5},{5,4},{6,7},{7,6},{8,9},{9,8},{10,11... | collective-permute-start | bytes 1179656 | tf_op jit(solution)/shard_map/ppermute | solution.py:277
  68.6 1.0 copy-start.5
  69.6 1.0 copy-start.7
  70.6 1.0 copy-start.10
  71.6 1.0 copy-start.13
  72.5 1.0 copy-start.16
  73.5 6.3 %copy-start.24 = (bf16[192,3072]{1,0:T(8,128)(2,1)S(1)}, bf16[192,3072]{1,0:T(8,128)(2,1)}, u32[]{:S(2)}) copy-start(bf16[192,3072]{1,0:T(8,128)(2,1)} %copy-done.23) | copy-start | bytes 3538948
  77.6 2.2 %copy-start.3 = (bf16[192,3072]{1,0:T(8,128)(2,1)S(1)}, bf16[192,3072]{1,0:T(8,128)(2,1)}, u32[]{:S(2)}) copy-start(bf16[192,3072]{1,0:T(8,128)(2,1)} %copy-done.2) | copy-start | bytes 3538948
  77.6 3.9 %copy-start.8 = (bf16[64,3072]{1,0:T(8,128)(2,1)S(1)}, bf16[64,3072]{1,0:T(8,128)(2,1)}, u32[]{:S(2)}) copy-start(bf16[64,3072]{1,0:T(8,128)(2,1)} %copy-done.6) | copy-start | bytes 1179652
  77.6 3.9 %copy-start.11 = (bf16[64,3072]{1,0:T(8,128)(2,1)S(1)}, bf16[64,3072]{1,0:T(8,128)(2,1)}, u32[]{:S(2)}) copy-start(bf16[64,3072]{1,0:T(8,128)(2,1)} %copy-done.9) | copy-start | bytes 1179652
  77.6 3.9 %copy-start.14 = (bf16[64,3072]{1,0:T(8,128)(2,1)S(1)}, bf16[64,3072]{1,0:T(8,128)(2,1)}, u32[]{:S(2)}) copy-start(bf16[64,3072]{1,0:T(8,128)(2,1)} %copy-done.12) | copy-start | bytes 1179652
  77.6 3.9 %copy-start.17 = (bf16[64,3072]{1,0:T(8,128)(2,1)S(1)}, bf16[64,3072]{1,0:T(8,128)(2,1)}, u32[]{:S(2)}) copy-start(bf16[64,3072]{1,0:T(8,128)(2,1)} %copy-done.15) | copy-start | bytes 1179652
  78.9 7.8 %collective-permute-start.16 = (bf16[64,3072]{1,0:T(8,128)(2,1)S(1)}, bf16[64,3072]{1,0:T(8,128)(2,1)S(1)}, u32[]{:S(2)}, u32[]{:S(2)}) collective-permute-start(bf16[64,3072]{1,0:T(8,128)(2,1)S(1)} %add_convert_fusion.4), channel_id=1, source_target_pairs={{0,4},{1,3},{4,8},{5,1},{8,12},{9,5},{12,14},{13,9},{14,10},{15,13... | collective-permute-start | bytes 1179656 | tf_op jit(solution)/shard_map/ppermute | solution.py:274
  81.0 10.0 %collective-permute-start.15 = (bf16[64,3072]{1,0:T(8,128)(2,1)S(1)}, bf16[64,3072]{1,0:T(8,128)(2,1)S(1)}, u32[]{:S(2)}, u32[]{:S(2)}) collective-permute-start(bf16[64,3072]{1,0:T(8,128)(2,1)S(1)} %add_convert_fusion.5), channel_id=1, source_target_pairs={{0,4},{1,3},{4,8},{5,1},{8,12},{9,5},{12,14},{13,9},{14,10},{15,13... | collective-permute-start | bytes 1179656 | tf_op jit(solution)/shard_map/ppermute | solution.py:274
  86.7 18.0 %collective-permute-start.19 = (bf16[64,3072]{1,0:T(8,128)(2,1)S(1)}, bf16[64,3072]{1,0:T(8,128)(2,1)S(1)}, u32[]{:S(2)}, u32[]{:S(2)}) collective-permute-start(bf16[64,3072]{1,0:T(8,128)(2,1)S(1)} %copy-done.17), channel_id=1, source_target_pairs={{0,1},{1,0},{2,3},{3,2},{4,5},{5,4},{6,7},{7,6},{8,9},{9,8},{10,11... | collective-permute-start | bytes 1179656 | tf_op jit(solution)/shard_map/ppermute | solution.py:277
  92.1 7.8 %collective-permute-start.18 = (bf16[64,3072]{1,0:T(8,128)(2,1)S(1)}, bf16[64,3072]{1,0:T(8,128)(2,1)S(1)}, u32[]{:S(2)}, u32[]{:S(2)}) collective-permute-start(bf16[64,3072]{1,0:T(8,128)(2,1)S(1)} %add_convert_fusion.2), channel_id=1, source_target_pairs={{0,4},{1,3},{4,8},{5,1},{8,12},{9,5},{12,14},{13,9},{14,10},{15,13... | collective-permute-start | bytes 1179656 | tf_op jit(solution)/shard_map/ppermute | solution.py:274
  99.9 8.7 %collective-permute-start.17 = (bf16[64,3072]{1,0:T(8,128)(2,1)S(1)}, bf16[64,3072]{1,0:T(8,128)(2,1)S(1)}, u32[]{:S(2)}, u32[]{:S(2)}) collective-permute-start(bf16[64,3072]{1,0:T(8,128)(2,1)S(1)} %add_convert_fusion.3), channel_id=1, source_target_pairs={{0,4},{1,3},{4,8},{5,1},{8,12},{9,5},{12,14},{13,9},{14,10},{15,13... | collective-permute-start | bytes 1179656 | tf_op jit(solution)/shard_map/ppermute | solution.py:274
  109.7 9.3 %collective-permute-start.24 = (bf16[64,3072]{1,0:T(8,128)(2,1)S(1)}, bf16[64,3072]{1,0:T(8,128)(2,1)S(1)}, u32[]{:S(2)}, u32[]{:S(2)}) collective-permute-start(bf16[64,3072]{1,0:T(8,128)(2,1)S(1)} %add_convert_fusion), channel_id=1, source_target_pairs={{0,4},{1,3},{4,8},{5,1},{8,12},{9,5},{12,14},{13,9},{14,10},{15,13... | collective-permute-start | bytes 1179656 | tf_op jit(solution)/shard_map/ppermute | solution.py:274
  110.3 12.6 %collective-permute-start.23 = (bf16[64,3072]{1,0:T(8,128)(2,1)S(1)}, bf16[64,3072]{1,0:T(8,128)(2,1)S(1)}, u32[]{:S(2)}, u32[]{:S(2)}) collective-permute-start(bf16[64,3072]{1,0:T(8,128)(2,1)S(1)} %add_convert_fusion.1), channel_id=1, source_target_pairs={{0,4},{1,3},{4,8},{5,1},{8,12},{9,5},{12,14},{13,9},{14,10},{15,13... | collective-permute-start | bytes 1179656 | tf_op jit(solution)/shard_map/ppermute | solution.py:274
  115.1 3.9 %copy-start.19 = (bf16[64,3072]{1,0:T(8,128)(2,1)S(1)}, bf16[64,3072]{1,0:T(8,128)(2,1)}, u32[]{:S(2)}) copy-start(bf16[64,3072]{1,0:T(8,128)(2,1)} %copy-done.18) | copy-start | bytes 1179652
  119.1 3.9 %copy-start.21 = (bf16[64,3072]{1,0:T(8,128)(2,1)S(1)}, bf16[64,3072]{1,0:T(8,128)(2,1)}, u32[]{:S(2)}) copy-start(bf16[64,3072]{1,0:T(8,128)(2,1)} %copy-done.20) | copy-start | bytes 1179652
  123.1 1.5 %collective-permute-start.26 = (bf16[32,3072]{1,0:T(8,128)(2,1)S(1)}, bf16[32,3072]{1,0:T(8,128)(2,1)S(1)}, u32[]{:S(2)}, u32[]{:S(2)}) collective-permute-start(bf16[32,3072]{1,0:T(8,128)(2,1)S(1)} %select_convert_fusion), channel_id=1, source_target_pairs={{0,1},{1,0},{2,3},{3,2},{4,5},{5,4},{6,7},{7,6},{8,9},{9,8},{10,11... | collective-permute-start | bytes 589832 | tf_op jit(solution)/shard_map/ppermute | solution.py:277
  123.2 1.7 %collective-permute-start.25 = (bf16[32,3072]{1,0:T(8,128)(2,1)S(1)}, bf16[32,3072]{1,0:T(8,128)(2,1)S(1)}, u32[]{:S(2)}, u32[]{:S(2)}) collective-permute-start(bf16[32,3072]{1,0:T(8,128)(2,1)S(1)} %select_convert_fusion.1), channel_id=1, source_target_pairs={{0,1},{1,0},{2,3},{3,2},{4,5},{5,4},{6,7},{7,6},{8,9},{9,8},{10,11... | collective-permute-start | bytes 589832 | tf_op jit(solution)/shard_map/ppermute | solution.py:277

commit v3 on v2

--- a/solution.py
+++ b/solution.py
@@ -9,8 +9,7 @@
 
 RING = 8
 PIECES = 4
-VMEM_LIMIT = 46 * 1024 * 1024
-HIDDEN_LIMIT = 57 * 1024 * 1024
+VMEM_LIMIT = 16 * 1024 * 1024
 WHOLE = pl.BlockSpec(memory_space=pltpu.VMEM)
 OUTSIDE = pl.BlockSpec(memory_space=pltpu.HBM)
 
@@ -113,7 +112,7 @@
             pltpu.VMEM(shape, dtype),
             pltpu.SemaphoreType.DMA((2, RING)),
         ],
-        compiler_params=pltpu.CompilerParams(vmem_limit_bytes=HIDDEN_LIMIT),
+        compiler_params=pltpu.CompilerParams(vmem_limit_bytes=VMEM_LIMIT),
         cost_estimate=cost(3),
         name="hidden",
     )(me, out_grad, pre_act)
@@ -165,9 +164,14 @@
     for i, copy in enumerate(copies):
         copy.wait()
         here = pl.ds(i * step, step)
-        part_ref[:, here] = lax.dot_general(
-            dh_ref[...], w_ref[here, :], (((1,), (1,)), ((), ())), preferred_element_type=jnp.float32
-        ).astype(jnp.bfloat16)
+        w = w_ref[here, :]
+        if other:
+            part = lax.dot_general(
+                dh_ref[...], w, (((1,), (1,)), ((), ())), preferred_element_type=jnp.float32
+            )
+        else:
+            part = jnp.dot(dh_ref[...], w.T, preferred_element_type=jnp.float32)
+        part_ref[:, here] = part.astype(jnp.bfloat16)
         at = 0
         for j, out in enumerate(outs):
             store = pltpu.make_async_copy(
@@ -217,9 +221,13 @@
     copies = []
     for i in range(dh_ref.shape[1] // step):
         columns = pl.ds(i * step, step)
-        stage[:, columns] = lax.dot_general(
-            x, dh_ref[:, columns], (((0,), (0,)), ((), ())), preferred_element_type=jnp.float32
-        ).astype(jnp.bfloat16)
+        if other:
+            result = jnp.dot(x.T, dh_ref[:, columns], preferred_element_type=jnp.float32)
+        else:
+            result = lax.dot_general(
+                x, dh_ref[:, columns], (((0,), (0,)), ((), ())), preferred_element_type=jnp.float32
+            )
+        stage[:, columns] = result.astype(jnp.bfloat16)
         copy = pltpu.make_async_copy(
             stage.at[:, columns], out_hbm.at[pl.ds(row, wide), columns], sems.at[i]
         )
@@ -233,7 +241,7 @@
     tokens, ff = dh.shape
     half = blocks[0].shape[1]
     wide = half // PIECES
-    step = 384
+    step = 512 if ff % 512 == 0 else 128
     return pl.pallas_call(
         lambda *refs: weight_kernel(*refs, other=other, piece=piece, wide=wide, step=step),
         out_shape=jax.ShapeDtypeStruct((2 * half, ff), jnp.bfloat16),
@@ -276,6 +284,9 @@
     def swap(x):
         return lax.ppermute(x, "gx", swaps)
 
+    out_grad, pre_act, weight = (
+        pltpu.with_memory_space_constraint(x, pltpu.HBM) for x in (out_grad, pre_act, weight)
+    )
     me = lax.axis_index("gx").astype(jnp.int32).reshape(1)
     core = me[0] % 2
     both = 2 * rows
@@ -286,11 +297,12 @@
     def product(other, piece, before, *others):
         return input_piece(me, after(dh, *others), weight, before, other, piece)
 
-    m0, o0 = prepare(me, layer_input, swap(layer_input))
+    twin = swap(layer_input)
+    dh = hidden(me, out_grad, pre_act)
+    m0, o0 = prepare(me, layer_input, after(twin, dh))
     m1 = ring(m0)
-    dh = hidden(after(me, m0), out_grad, pre_act)
-    o1 = ring(after(o0, dh))
-    go = product(True, 0, ())
+    go = product(True, 0, (), m0)
+    o1 = ring(after(o0, go[0]))
     m1 = after(m1, go[0])
     m2, sm1 = ring(m1), swap(m1)
     go = product(True, 1, go, m1)

time: 127 us -> 121 us (0.953)
  starting transfers between devices: 16.9 us -> 22.7 us
  waiting for transfers between devices: 19.5 us -> 14.9 us
  Pallas kernels: 70.6 us -> 66.6 us
  local copies, waits for them, and re-layouts: 10.7 us -> 7.61 us
    ppermute x14, starting transfers between devices: 14.3 us -> 20 us  [ring(): return lax.ppermute(x, 'gx', pairs)]
    unnamed x50 -> x46, local copies, waits for them, and re-layouts: 10.7 us -> 7.61 us
    ppermute x14, waiting for transfers between devices: 16.8 us -> 13.7 us  [ring(): return lax.ppermute(x, 'gx', pairs)]
    pallas_call x8, Pallas kernels: 31.1 us -> 28.2 us  [weight_piece(): pl.pallas_call(lambda *refs: weight_kernel(*refs, other=other, piece=piec...]
    ppermute x13, waiting for transfers between devices: 2.69 us -> 1.14 us  [swap(): return lax.ppermute(x, 'gx', swaps)]
  transfers between devices with their start and end apart: 27 -> 27, of which waited for: 8 -> 9; matrix products, arithmetic and copies ran while one was open for 4% -> 4% of each run, Pallas kernels for 52% -> 51%
where the time goes in v3:
time: 121 us; the launch traced here: 120 us
  Pallas kernels  66.6 us (55%)
  starting transfers between devices  22.7 us (19%)
  waiting for transfers between devices  14.9 us (12%)
  local copies, waits for them, and re-layouts  7.61 us (6%)
  other arithmetic  7 us (6%)
    pallas_call x8, Pallas kernels, input_piece(): pl.pallas_call(lambda *refs: input_kernel(*refs, other=other, piece=piece...  34.9 us
    pallas_call x8, Pallas kernels, weight_piece(): pl.pallas_call(lambda *refs: weight_kernel(*refs, other=other, piece=piec...  28.2 us
    ppermute x14, starting transfers between devices, ring(): return lax.ppermute(x, 'gx', pairs)  20 us
    ppermute x14, waiting for transfers between devices, ring(): return lax.ppermute(x, 'gx', pairs)  13.7 us
    unnamed x46, local copies, waits for them, and re-layouts  7.61 us
    convert_element_type x7, other arithmetic, total(): return result.astype(jnp.bfloat16)  5.85 us
    pallas_call x1, Pallas kernels, hidden(): pl.pallas_call(hidden_kernel, out_shape=jax.ShapeDtypeStruct(shape, dtype...  3.47 us
    ppermute x13, starting transfers between devices, swap(): return lax.ppermute(x, 'gx', swaps)  2.67 us
  transfers between devices with their start and end apart: 27, of which 9 were waited for; matrix products, arithmetic and copies ran while one was open for 4% of the time, Pallas kernels for 51%

profile of v3, /device:TPU:0, one launch (start us, length us, event | category | flops | bytes accessed | tf_op | source)
XLA Modules:
  0.0 119.9 jit_solution(9852322296614747028)
XLA Ops:
  0.6 0.5 collective-permute-start
  1.1 3.5 %hidden.1.refs_1_ = bf16[512,1536]{1,0:T(8,128)(2,1)S(1)} custom-call(s32[1]{0:T(128)} %bitcast.me_ref.refs_0_, bf16[512,1536]{1,0:T(8,128)(2,1)} %og_hbm.1, bf16[512,1536]{1,0:T(8,128)(2,1)} %pre_hbm.1), custom_call_target="tpu_custom_call" | custom-call | flops 3449999872 | tf_op jit(solution)/shard_map/hidden/pallas_call | solution.py:105
  4.7 2.7 %collective-permute-start.2 = (bf16[64,3072]{1,0:T(8,128)(2,1)S(1)}, bf16[64,3072]{1,0:T(8,128)(2,1)S(1)}, u32[]{:S(2)}, u32[]{:S(2)}) collective-permute-start(bf16[64,3072]{1,0:T(8,128)(2,1)S(1)} %get-tuple-element.68.refs_2_), channel_id=1, source_target_pairs={{0,4},{1,3},{4,8},{5,1},{8,12},{9,5},{12,14},{13,9},{14,10},{15,13... | collective-permute-start | bytes 1179656 | tf_op jit(solution)/shard_map/ppermute | solution.py:282
  7.4 4.0 %input_piece.8 = (bf16[64,3072]{1,0:T(8,128)(2,1)S(1)}, bf16[192,3072]{1,0:T(8,128)(2,1)S(1)}, bf16[64,3072]{1,0:T(8,128)(2,1)S(1)}, bf16[192,3072]{1,0:T(8,128)(2,1)S(1)}) custom-call(s32[1]{0:T(128)} %bitcast.me_ref.refs_0_, bf16[512,1536]{1,0:T(8,128)(2,1)S(1)} %hidden.1.refs_1_, bf16[6144,1536]{1,0:T(8,128)(2,1)} %refs_2_.15), custom_call_target="tpu_custom_call" | custom-call | flops 3449999872 | tf_op jit(solution)/shard_map/input_piece/pallas_call | solution.py:198
  11.4 1.6 %collective-permute-start.1 = (bf16[64,3072]{1,0:T(8,128)(2,1)S(1)}, bf16[64,3072]{1,0:T(8,128)(2,1)S(1)}, u32[]{:S(2)}, u32[]{:S(2)}) collective-permute-start(bf16[64,3072]{1,0:T(8,128)(2,1)S(1)} %get-tuple-element.71.refs_2_), channel_id=1, source_target_pairs={{0,4},{1,3},{4,8},{5,1},{8,12},{9,5},{12,14},{13,9},{14,10},{15,13... | collective-permute-start | bytes 1179656 | tf_op jit(solution)/shard_map/ppermute | solution.py:282
  13.1 2.1 %collective-permute-start.4 = (bf16[64,3072]{1,0:T(8,128)(2,1)S(1)}, bf16[64,3072]{1,0:T(8,128)(2,1)S(1)}, u32[]{:S(2)}, u32[]{:S(2)}) collective-permute-start(bf16[64,3072]{1,0:T(8,128)(2,1)S(1)} %collective-permute-done.2.refs_3_), channel_id=1, source_target_pairs={{0,4},{1,3},{4,8},{5,1},{8,12},{9,5},{12,14},{13,9},{14,10},{15,13... | collective-permute-start | bytes 1179656 | tf_op jit(solution)/shard_map/ppermute | solution.py:282
  15.2 4.0 %input_piece.9 = (bf16[64,3072]{1,0:T(8,128)(2,1)S(1)}, bf16[192,3072]{1,0:T(8,128)(2,1)S(1)}, bf16[64,3072]{1,0:T(8,128)(2,1)S(1)}, bf16[192,3072]{1,0:T(8,128)(2,1)S(1)}) custom-call(s32[1]{0:T(128)} %bitcast.me_ref.refs_0_, bf16[512,1536]{1,0:T(8,128)(2,1)S(1)} %hidden.1.refs_1_, ...), custom_call_target="tpu_custom_call", output_to_operand_aliasing={{0}: (3, {}), {1}: (4, {}), {2}: (5, {}), {3}: (6, {})} | custom-call | flops 3449999872 | tf_op jit(solution)/shard_map/input_piece/pallas_call | solution.py:198
  19.2 1.6 %collective-permute-start.3 = (bf16[64,3072]{1,0:T(8,128)(2,1)S(1)}, bf16[64,3072]{1,0:T(8,128)(2,1)}, u32[]{:S(2)}, u32[]{:S(2)}) collective-permute-start(bf16[64,3072]{1,0:T(8,128)(2,1)S(1)} %collective-permute-done.1.refs_3_), channel_id=1, source_target_pairs={{0,4},{1,3},{4,8},{5,1},{8,12},{9,5},{12,14},{13,9},{14,10},{15,13... | collective-permute-start | bytes 1179656 | tf_op jit(solution)/shard_map/ppermute | solution.py:282
  20.8 4.0 %input_piece.10 = (bf16[64,3072]{1,0:T(8,128)(2,1)S(1)}, bf16[192,3072]{1,0:T(8,128)(2,1)S(1)}, bf16[64,3072]{1,0:T(8,128)(2,1)S(1)}, bf16[192,3072]{1,0:T(8,128)(2,1)S(1)}) custom-call(s32[1]{0:T(128)} %bitcast.me_ref.refs_0_, bf16[512,1536]{1,0:T(8,128)(2,1)S(1)} %hidden.1.refs_1_, ...), custom_call_target="tpu_custom_call", output_to_operand_aliasing={{0}: (3, {}), {1}: (4, {}), {2}: (5, {}), {3}: (6, {})} | custom-call | flops 3449999872 | tf_op jit(solution)/shard_map/input_piece/pallas_call | solution.py:198
  24.8 4.1 %input_piece.11 = (bf16[64,3072]{1,0:T(8,128)(2,1)S(1)}, bf16[192,3072]{1,0:T(8,128)(2,1)S(1)}, bf16[64,3072]{1,0:T(8,128)(2,1)S(1)}, bf16[192,3072]{1,0:T(8,128)(2,1)S(1)}) custom-call(s32[1]{0:T(128)} %bitcast.me_ref.refs_0_, bf16[512,1536]{1,0:T(8,128)(2,1)S(1)} %hidden.1.refs_1_, ...), custom_call_target="tpu_custom_call", output_to_operand_aliasing={{0}: (3, {}), {1}: (4, {}), {2}: (5, {}), {3}: (6, {})} | custom-call | flops 3449999872 | tf_op jit(solution)/shard_map/input_piece/pallas_call | solution.py:198
  29.0 0.7 copy-done.16
  29.7 1.6 %collective-permute-start.6 = (bf16[64,3072]{1,0:T(8,128)(2,1)S(1)}, bf16[64,3072]{1,0:T(8,128)(2,1)S(1)}, u32[]{:S(2)}, u32[]{:S(2)}) collective-permute-start(bf16[64,3072]{1,0:T(8,128)(2,1)S(1)} %collective-permute-done.4.refs_4_), channel_id=1, source_target_pairs={{0,4},{1,3},{4,8},{5,1},{8,12},{9,5},{12,14},{13,9},{14,10},{15,13... | collective-permute-start | bytes 1179656 | tf_op jit(solution)/shard_map/ppermute | solution.py:282
  31.3 1.5 %collective-permute-start.5 = (bf16[64,3072]{1,0:T(8,128)(2,1)}, bf16[64,3072]{1,0:T(8,128)(2,1)}, u32[]{:S(2)}, u32[]{:S(2)}) collective-permute-start(bf16[64,3072]{1,0:T(8,128)(2,1)} %collective-permute-done.3.refs_4_), channel_id=1, source_target_pairs={{0,4},{1,3},{4,8},{5,1},{8,12},{9,5},{12,14},{13,9},{14,10},{15,13... | collective-permute-start | bytes 1179656 | tf_op jit(solution)/shard_map/ppermute | solution.py:282
  32.8 4.5 %input_piece.12 = (bf16[64,3072]{1,0:T(8,128)(2,1)S(1)}, bf16[192,3072]{1,0:T(8,128)(2,1)}, bf16[64,3072]{1,0:T(8,128)(2,1)S(1)}, bf16[192,3072]{1,0:T(8,128)(2,1)S(1)}) custom-call(s32[1]{0:T(128)} %bitcast.me_ref.refs_0_, bf16[512,1536]{1,0:T(8,128)(2,1)S(1)} %hidden.1.refs_1_, bf16[6144,1536]{1,0:T(8,128)(2,1)} %refs_2_.15), custom_call_target="tpu_custom_call" | custom-call | flops 3449999872 | tf_op jit(solution)/shard_map/input_piece/pallas_call | solution.py:198
  37.4 0.1 collective-permute-done.6.refs_5_
  37.5 4.7 %input_piece.13 = (bf16[64,3072]{1,0:T(8,128)(2,1)S(1)}, bf16[192,3072]{1,0:T(8,128)(2,1)}, bf16[64,3072]{1,0:T(8,128)(2,1)S(1)}, bf16[192,3072]{1,0:T(8,128)(2,1)S(1)}) custom-call(s32[1]{0:T(128)} %bitcast.me_ref.refs_0_, bf16[512,1536]{1,0:T(8,128)(2,1)S(1)} %hidden.1.refs_1_, ...), custom_call_target="tpu_custom_call", output_to_operand_aliasing={{0}: (3, {}), {1}: (4, {}), {2}: (5, {}), {3}: (6, {})} | custom-call | flops 3449999872 | tf_op jit(solution)/shard_map/input_piece/pallas_call | solution.py:198
  42.2 4.6 %input_piece.14 = (bf16[64,3072]{1,0:T(8,128)(2,1)S(1)}, bf16[192,3072]{1,0:T(8,128)(2,1)}, bf16[64,3072]{1,0:T(8,128)(2,1)S(1)}, bf16[192,3072]{1,0:T(8,128)(2,1)S(1)}) custom-call(s32[1]{0:T(128)} %bitcast.me_ref.refs_0_, bf16[512,1536]{1,0:T(8,128)(2,1)S(1)} %hidden.1.refs_1_, ...), custom_call_target="tpu_custom_call", output_to_operand_aliasing={{0}: (3, {}), {1}: (4, {}), {2}: (5, {}), {3}: (6, {})} | custom-call | flops 3449999872 | tf_op jit(solution)/shard_map/input_piece/pallas_call | solution.py:198
  46.8 5.0 %input_piece.15 = (bf16[64,3072]{1,0:T(8,128)(2,1)S(1)}, bf16[192,3072]{1,0:T(8,128)(2,1)}, bf16[64,3072]{1,0:T(8,128)(2,1)S(1)}, bf16[192,3072]{1,0:T(8,128)(2,1)S(1)}) custom-call(s32[1]{0:T(128)} %bitcast.me_ref.refs_0_, bf16[512,1536]{1,0:T(8,128)(2,1)S(1)} %hidden.1.refs_1_, ...), custom_call_target="tpu_custom_call", output_to_operand_aliasing={{0}: (3, {}), {1}: (4, {}), {2}: (5, {}), {3}: (6, {})} | custom-call | flops 3449999872 | tf_op jit(solution)/shard_map/input_piece/pallas_call | solution.py:198
  51.8 1.0 copy-done
  52.8 0.4 collective-permute-start.10
  53.3 0.1 collective-permute-start.12
  53.4 0.4 collective-permute-start.13
  53.8 1.1 collective-permute-start.11
  54.9 0.9 add_convert_fusion.6
  55.8 5.8 %collective-permute-done.11.refs_6_ = bf16[64,3072]{1,0:T(8,128)(2,1)S(1)} collective-permute-done((bf16[64,3072]{1,0:T(8,128)(2,1)S(1)}, bf16[64,3072]{1,0:T(8,128)(2,1)S(1)}, u32[]{:S(2)}, u32[]{:S(2)}) %collective-permute-start.11) | collective-permute-done | bytes 393248 | tf_op jit(solution)/shard_map/ppermute | solution.py:282
  61.6 0.8 copy-done.13
  62.4 1.1 collective-permute-start.9
  63.5 0.5 collective-permute-start.21
  64.1 1.0 copy-done.3
  65.1 1.0 copy-done.5
  66.1 1.0 copy-done.8
  67.1 1.0 copy-done.11
  68.1 1.0 copy-done.14
  69.1 3.7 %weight_piece.8.refs_10_ = bf16[6144,1536]{1,0:T(8,128)(2,1)} custom-call(s32[1]{0:T(128)} %bitcast.me_ref.refs_0_, bf16[512,1536]{1,0:T(8,128)(2,1)S(1)} %hidden.1.refs_1_, bf16[64,3072]{1,0:T(8,128)(2,1)S(1)} %copy-done.3, bf16[64,3072]{1,0:T(8,128)(2,1)S(1)} %copy-done.5, bf16[64,3072]{1,0:T(8,128)(2,1)S(1)} %copy-done.8, ...), custom_call_target="tpu_custom_call" | custom-call | flops 3449999872 | tf_op jit(solution)/shard_map/weight_piece/pallas_call | solution.py:245
  72.8 1.2 %add_convert_fusion.4 = bf16[64,3072]{1,0:T(8,128)(2,1)S(1)} fusion(bf16[192,3072]{1,0:T(8,128)(2,1)} %collective-permute-done.10, bf16[192,3072]{1,0:T(8,128)(2,1)S(1)} %get-tuple-element.117), kind=kLoop, calls=%fused_computation.6 | loop fusion | flops 786432 | bytes 1179648 | tf_op jit(solution)/shard_map/convert_element_type | solution.py:265
  74.1 1.6 %collective-permute-start.16 = (bf16[64,3072]{1,0:T(8,128)(2,1)S(1)}, bf16[64,3072]{1,0:T(8,128)(2,1)S(1)}, u32[]{:S(2)}, u32[]{:S(2)}) collective-permute-start(bf16[64,3072]{1,0:T(8,128)(2,1)S(1)} %add_convert_fusion.4), channel_id=1, source_target_pairs={{0,4},{1,3},{4,8},{5,1},{8,12},{9,5},{12,14},{13,9},{14,10},{15,13... | collective-permute-start | bytes 1179656 | tf_op jit(solution)/shard_map/ppermute | solution.py:282
  75.6 1.1 add_convert_fusion.5
  76.8 0.5 collective-permute-start.15
  77.3 3.6 %weight_piece.9.refs_10_ = bf16[6144,1536]{1,0:T(8,128)(2,1)} custom-call(s32[1]{0:T(128)} %bitcast.me_ref.refs_0_, bf16[512,1536]{1,0:T(8,128)(2,1)S(1)} %hidden.1.refs_1_, bf16[64,3072]{1,0:T(8,128)(2,1)S(1)} %copy-done.3, bf16[64,3072]{1,0:T(8,128)(2,1)S(1)} %copy-done.6, bf16[64,3072]{1,0:T(8,128)(2,1)S(1)} %copy-done.9, ...), custom_call_target="tpu_custom_call", output_to_operand_aliasing={{}: (10, {})} | custom-call | flops 3449999872 | tf_op jit(solution)/shard_map/weight_piece/pallas_call | solution.py:245
  80.9 1.0 collective-permute-done.16
  81.9 3.6 %weight_piece.10.refs_10_ = bf16[6144,1536]{1,0:T(8,128)(2,1)} custom-call(s32[1]{0:T(128)} %bitcast.me_ref.refs_0_, bf16[512,1536]{1,0:T(8,128)(2,1)S(1)} %hidden.1.refs_1_, bf16[64,3072]{1,0:T(8,128)(2,1)S(1)} %copy-done.3, bf16[64,3072]{1,0:T(8,128)(2,1)S(1)} %copy-done.6, bf16[64,3072]{1,0:T(8,128)(2,1)S(1)} %copy-done.9, ...), custom_call_target="tpu_custom_call", output_to_operand_aliasing={{}: (10, {})} | custom-call | flops 3449999872 | tf_op jit(solution)/shard_map/weight_piece/pallas_call | solution.py:245
  85.5 0.6 collective-permute-done.15
  86.1 1.1 add_convert_fusion.2
  87.2 1.6 %collective-permute-start.18 = (bf16[64,3072]{1,0:T(8,128)(2,1)S(1)}, bf16[64,3072]{1,0:T(8,128)(2,1)S(1)}, u32[]{:S(2)}, u32[]{:S(2)}) collective-permute-start(bf16[64,3072]{1,0:T(8,128)(2,1)S(1)} %add_convert_fusion.2), channel_id=1, source_target_pairs={{0,4},{1,3},{4,8},{5,1},{8,12},{9,5},{12,14},{13,9},{14,10},{15,13... | collective-permute-start | bytes 1179656 | tf_op jit(solution)/shard_map/ppermute | solution.py:282
  88.8 0.2 add_convert_fusion.3
  89.0 6.1 %collective-permute-done.18 = bf16[64,3072]{1,0:T(8,128)(2,1)S(1)} collective-permute-done((bf16[64,3072]{1,0:T(8,128)(2,1)S(1)}, bf16[64,3072]{1,0:T(8,128)(2,1)S(1)}, u32[]{:S(2)}, u32[]{:S(2)}) %collective-permute-start.18) | collective-permute-done | bytes 393248 | tf_op jit(solution)/shard_map/ppermute | solution.py:282
  95.1 1.5 %collective-permute-start.17 = (bf16[64,3072]{1,0:T(8,128)(2,1)S(1)}, bf16[64,3072]{1,0:T(8,128)(2,1)S(1)}, u32[]{:S(2)}, u32[]{:S(2)}) collective-permute-start(bf16[64,3072]{1,0:T(8,128)(2,1)S(1)} %add_convert_fusion.3), channel_id=1, source_target_pairs={{0,4},{1,3},{4,8},{5,1},{8,12},{9,5},{12,14},{13,9},{14,10},{15,13... | collective-permute-start | bytes 1179656 | tf_op jit(solution)/shard_map/ppermute | solution.py:282
  96.6 3.6 %weight_piece.11.refs_10_ = bf16[6144,1536]{1,0:T(8,128)(2,1)} custom-call(s32[1]{0:T(128)} %bitcast.me_ref.refs_0_, bf16[512,1536]{1,0:T(8,128)(2,1)S(1)} %hidden.1.refs_1_, bf16[64,3072]{1,0:T(8,128)(2,1)S(1)} %copy-done.3, bf16[64,3072]{1,0:T(8,128)(2,1)S(1)} %copy-done.6, bf16[64,3072]{1,0:T(8,128)(2,1)S(1)} %copy-done.9, ...), custom_call_target="tpu_custom_call", output_to_operand_aliasing={{}: (10, {})} | custom-call | flops 3449999872 | tf_op jit(solution)/shard_map/weight_piece/pallas_call | solution.py:245
  100.2 3.4 %weight_piece.12.refs_10_ = bf16[6144,1536]{1,0:T(8,128)(2,1)} custom-call(s32[1]{0:T(128)} %bitcast.me_ref.refs_0_, bf16[512,1536]{1,0:T(8,128)(2,1)S(1)} %hidden.1.refs_1_, bf16[64,3072]{1,0:T(8,128)(2,1)S(1)} %get-tuple-element.71.refs_2_, bf16[64,3072]{1,0:T(8,128)(2,1)S(1)} %collective-permute-done.1.refs_3_, ...), custom_call_target="tpu_custom_call", output_to_operand_aliasing={{}: (10, {})} | custom-call | flops 3449999872 | tf_op jit(solution)/shard_map/weight_piece/pallas_call | solution.py:245
  103.7 1.1 add_convert_fusion
  104.8 0.7 collective-permute-start.24
  105.6 0.2 add_convert_fusion.1
  105.7 0.7 collective-permute-start.23
  106.4 3.4 %weight_piece.13.refs_10_ = bf16[6144,1536]{1,0:T(8,128)(2,1)} custom-call(s32[1]{0:T(128)} %bitcast.me_ref.refs_0_, bf16[512,1536]{1,0:T(8,128)(2,1)S(1)} %hidden.1.refs_1_, bf16[64,3072]{1,0:T(8,128)(2,1)S(1)} %get-tuple-element.71.refs_2_, bf16[64,3072]{1,0:T(8,128)(2,1)S(1)} %collective-permute-done.1.refs_3_, ...), custom_call_target="tpu_custom_call", output_to_operand_aliasing={{}: (10, {})} | custom-call | flops 3449999872 | tf_op jit(solution)/shard_map/weight_piece/pallas_call | solution.py:245
  109.9 3.5 %weight_piece.14.refs_10_ = bf16[6144,1536]{1,0:T(8,128)(2,1)} custom-call(s32[1]{0:T(128)} %bitcast.me_ref.refs_0_, bf16[512,1536]{1,0:T(8,128)(2,1)S(1)} %hidden.1.refs_1_, bf16[64,3072]{1,0:T(8,128)(2,1)S(1)} %get-tuple-element.71.refs_2_, bf16[64,3072]{1,0:T(8,128)(2,1)S(1)} %collective-permute-done.1.refs_3_, ...), custom_call_target="tpu_custom_call", output_to_operand_aliasing={{}: (10, {})} | custom-call | flops 3449999872 | tf_op jit(solution)/shard_map/weight_piece/pallas_call | solution.py:245
  113.4 0.1 convert_add_fusion
  113.5 3.5 %weight_piece.15 = bf16[6144,1536]{1,0:T(8,128)(2,1)} custom-call(s32[1]{0:T(128)} %bitcast.me_ref.refs_0_, bf16[512,1536]{1,0:T(8,128)(2,1)S(1)} %hidden.1.refs_1_, bf16[64,3072]{1,0:T(8,128)(2,1)S(1)} %get-tuple-element.71.refs_2_, bf16[64,3072]{1,0:T(8,128)(2,1)S(1)} %collective-permute-done.1.refs_3_, ...), custom_call_target="tpu_custom_call", output_to_operand_aliasing={{}: (10, {})} | custom-call | flops 3449999872 | tf_op jit(solution)/shard_map/weight_piece/pallas_call | solution.py:245
  117.0 0.1 convert_add_fusion.1
  117.2 0.1 collective-permute-start.26
  117.3 0.6 collective-permute-start.25
  117.8 0.8 collective-permute-done.26
  118.7 0.3 collective-permute-done.25
  119.0 0.1 broadcast_select_fusion.1
  119.1 0.8 pad_maximum_fusion
  (68 shorter events, 0.5 us)
Async XLA Ops:
  0.6 4.0 %collective-permute-start = (bf16[32,6144]{1,0:T(8,128)(2,1)}, bf16[32,6144]{1,0:T(8,128)(2,1)S(1)}, u32[]{:S(2)}, u32[]{:S(2)}) collective-permute-start(bf16[32,6144]{1,0:T(8,128)(2,1)} %own_ref.1), channel_id=1, source_target_pairs={{0,1},{1,0},{2,3},{3,2},{4,5},{5,4},{6,7},{7,6},{8,9},{9,8},{10,11... | collective-permute-start | bytes 1179656 | tf_op jit(solution)/shard_map/ppermute | solution.py:285
  1.1 3.5 %copy-start.20 = (bf16[32,6144]{1,0:T(8,128)(2,1)S(1)}, bf16[32,6144]{1,0:T(8,128)(2,1)}, u32[]{:S(2)}) copy-start(bf16[32,6144]{1,0:T(8,128)(2,1)} %own_ref.1) | copy-start | bytes 1179652
  4.7 6.7 %copy-start.2 = (bf16[64,3072]{1,0:T(8,128)(2,1)}, bf16[64,3072]{1,0:T(8,128)(2,1)S(1)}, u32[]{:S(2)}) copy-start(bf16[64,3072]{1,0:T(8,128)(2,1)S(1)} %get-tuple-element.68.refs_2_) | copy-start | bytes 1179652
  4.7 8.4 %collective-permute-start.2 = (bf16[64,3072]{1,0:T(8,128)(2,1)S(1)}, bf16[64,3072]{1,0:T(8,128)(2,1)S(1)}, u32[]{:S(2)}, u32[]{:S(2)}) collective-permute-start(bf16[64,3072]{1,0:T(8,128)(2,1)S(1)} %get-tuple-element.68.refs_2_), channel_id=1, source_target_pairs={{0,4},{1,3},{4,8},{5,1},{8,12},{9,5},{12,14},{13,9},{14,10},{15,13... | collective-permute-start | bytes 1179656 | tf_op jit(solution)/shard_map/ppermute | solution.py:282
  11.4 7.8 %collective-permute-start.1 = (bf16[64,3072]{1,0:T(8,128)(2,1)S(1)}, bf16[64,3072]{1,0:T(8,128)(2,1)S(1)}, u32[]{:S(2)}, u32[]{:S(2)}) collective-permute-start(bf16[64,3072]{1,0:T(8,128)(2,1)S(1)} %get-tuple-element.71.refs_2_), channel_id=1, source_target_pairs={{0,4},{1,3},{4,8},{5,1},{8,12},{9,5},{12,14},{13,9},{14,10},{15,13... | collective-permute-start | bytes 1179656 | tf_op jit(solution)/shard_map/ppermute | solution.py:282
  13.1 6.1 %copy-start.4 = (bf16[64,3072]{1,0:T(8,128)(2,1)}, bf16[64,3072]{1,0:T(8,128)(2,1)S(1)}, u32[]{:S(2)}) copy-start(bf16[64,3072]{1,0:T(8,128)(2,1)S(1)} %collective-permute-done.2.refs_3_) | copy-start | bytes 1179652
  13.1 11.7 %collective-permute-start.4 = (bf16[64,3072]{1,0:T(8,128)(2,1)S(1)}, bf16[64,3072]{1,0:T(8,128)(2,1)S(1)}, u32[]{:S(2)}, u32[]{:S(2)}) collective-permute-start(bf16[64,3072]{1,0:T(8,128)(2,1)S(1)} %collective-permute-done.2.refs_3_), channel_id=1, source_target_pairs={{0,4},{1,3},{4,8},{5,1},{8,12},{9,5},{12,14},{13,9},{14,10},{15,13... | collective-permute-start | bytes 1179656 | tf_op jit(solution)/shard_map/ppermute | solution.py:282
  19.2 12.1 %collective-permute-start.3 = (bf16[64,3072]{1,0:T(8,128)(2,1)S(1)}, bf16[64,3072]{1,0:T(8,128)(2,1)}, u32[]{:S(2)}, u32[]{:S(2)}) collective-permute-start(bf16[64,3072]{1,0:T(8,128)(2,1)S(1)} %collective-permute-done.1.refs_3_), channel_id=1, source_target_pairs={{0,4},{1,3},{4,8},{5,1},{8,12},{9,5},{12,14},{13,9},{14,10},{15,13... | collective-permute-start | bytes 1179656 | tf_op jit(solution)/shard_map/ppermute | solution.py:282
  24.8 4.9 %copy-start.7 = (bf16[64,3072]{1,0:T(8,128)(2,1)}, bf16[64,3072]{1,0:T(8,128)(2,1)S(1)}, u32[]{:S(2)}) copy-start(bf16[64,3072]{1,0:T(8,128)(2,1)S(1)} %collective-permute-done.4.refs_4_) | copy-start | bytes 1179652
  29.0 0.7 copy-start.16
  29.7 17.1 %collective-permute-start.7 = (bf16[192,3072]{1,0:T(8,128)(2,1)S(1)}, bf16[192,3072]{1,0:T(8,128)(2,1)S(1)}, u32[]{:S(2)}, u32[]{:S(2)}) collective-permute-start(bf16[192,3072]{1,0:T(8,128)(2,1)S(1)} %get-tuple-element.104), channel_id=1, source_target_pairs={{0,1},{1,0},{2,3},{3,2},{4,5},{5,4},{6,7},{7,6},{8,9},{9,8},{10,11... | collective-permute-start | bytes 3538952 | tf_op jit(solution)/shard_map/ppermute | solution.py:285
  29.7 7.8 %collective-permute-start.6 = (bf16[64,3072]{1,0:T(8,128)(2,1)S(1)}, bf16[64,3072]{1,0:T(8,128)(2,1)S(1)}, u32[]{:S(2)}, u32[]{:S(2)}) collective-permute-start(bf16[64,3072]{1,0:T(8,128)(2,1)S(1)} %collective-permute-done.4.refs_4_), channel_id=1, source_target_pairs={{0,4},{1,3},{4,8},{5,1},{8,12},{9,5},{12,14},{13,9},{14,10},{15,13... | collective-permute-start | bytes 1179656 | tf_op jit(solution)/shard_map/ppermute | solution.py:282
  31.3 15.5 %collective-permute-start.5 = (bf16[64,3072]{1,0:T(8,128)(2,1)}, bf16[64,3072]{1,0:T(8,128)(2,1)}, u32[]{:S(2)}, u32[]{:S(2)}) collective-permute-start(bf16[64,3072]{1,0:T(8,128)(2,1)} %collective-permute-done.3.refs_4_), channel_id=1, source_target_pairs={{0,4},{1,3},{4,8},{5,1},{8,12},{9,5},{12,14},{13,9},{14,10},{15,13... | collective-permute-start | bytes 1179656 | tf_op jit(solution)/shard_map/ppermute | solution.py:282
  32.8 14.0 %collective-permute-start.8 = (bf16[64,3072]{1,0:T(8,128)(2,1)S(1)}, bf16[64,3072]{1,0:T(8,128)(2,1)S(1)}, u32[]{:S(2)}, u32[]{:S(2)}) collective-permute-start(bf16[64,3072]{1,0:T(8,128)(2,1)S(1)} %get-tuple-element.105), channel_id=1, source_target_pairs={{0,1},{1,0},{2,3},{3,2},{4,5},{5,4},{6,7},{7,6},{8,9},{9,8},{10,11... | collective-permute-start | bytes 1179656 | tf_op jit(solution)/shard_map/ppermute | solution.py:285
  37.5 16.3 %copy-start.10 = (bf16[64,3072]{1,0:T(8,128)(2,1)}, bf16[64,3072]{1,0:T(8,128)(2,1)S(1)}, u32[]{:S(2)}) copy-start(bf16[64,3072]{1,0:T(8,128)(2,1)S(1)} %collective-permute-done.6.refs_5_) | copy-start | bytes 1179652
  46.8 5.0 %copy-start.21 = (bf16[192,3072]{1,0:T(8,128)(2,1)}, bf16[192,3072]{1,0:T(8,128)(2,1)S(1)}, u32[]{:S(2)}) copy-start(bf16[192,3072]{1,0:T(8,128)(2,1)S(1)} %collective-permute-done.7) | copy-start | bytes 3538948
  51.8 1.0 copy-start
  52.8 8.7 %copy-start.18 = (bf16[64,3072]{1,0:T(8,128)(2,1)}, bf16[64,3072]{1,0:T(8,128)(2,1)S(1)}, u32[]{:S(2)}) copy-start(bf16[64,3072]{1,0:T(8,128)(2,1)S(1)} %get-tuple-element.110) | copy-start | bytes 1179652
  52.8 10.7 %collective-permute-start.10 = (bf16[192,3072]{1,0:T(8,128)(2,1)}, bf16[192,3072]{1,0:T(8,128)(2,1)}, u32[]{:S(2)}, u32[]{:S(2)}) collective-permute-start(bf16[192,3072]{1,0:T(8,128)(2,1)} %get-tuple-element.113), channel_id=1, source_target_pairs={{0,1},{1,0},{2,3},{3,2},{4,5},{5,4},{6,7},{7,6},{8,9},{9,8},{10,11... | collective-permute-start | bytes 3538952 | tf_op jit(solution)/shard_map/ppermute | solution.py:285
  53.3 10.2 %collective-permute-start.12 = (bf16[64,3072]{1,0:T(8,128)(2,1)S(1)}, bf16[64,3072]{1,0:T(8,128)(2,1)}, u32[]{:S(2)}, u32[]{:S(2)}) collective-permute-start(bf16[64,3072]{1,0:T(8,128)(2,1)S(1)} %collective-permute-done.1.refs_3_), channel_id=1, source_target_pairs={{0,1},{1,0},{2,3},{3,2},{4,5},{5,4},{6,7},{7,6},{8,9},{9,8},{10,11... | collective-permute-start | bytes 1179656 | tf_op jit(solution)/shard_map/ppermute | solution.py:285
  53.4 10.7 %collective-permute-start.13 = (bf16[64,3072]{1,0:T(8,128)(2,1)}, bf16[64,3072]{1,0:T(8,128)(2,1)}, u32[]{:S(2)}, u32[]{:S(2)}) collective-permute-start(bf16[64,3072]{1,0:T(8,128)(2,1)} %collective-permute-done.3.refs_4_), channel_id=1, source_target_pairs={{0,1},{1,0},{2,3},{3,2},{4,5},{5,4},{6,7},{7,6},{8,9},{9,8},{10,11... | collective-permute-start | bytes 1179656 | tf_op jit(solution)/shard_map/ppermute | solution.py:285
  53.8 7.8 %collective-permute-start.11 = (bf16[64,3072]{1,0:T(8,128)(2,1)S(1)}, bf16[64,3072]{1,0:T(8,128)(2,1)S(1)}, u32[]{:S(2)}, u32[]{:S(2)}) collective-permute-start(bf16[64,3072]{1,0:T(8,128)(2,1)S(1)} %collective-permute-done.6.refs_5_), channel_id=1, source_target_pairs={{0,4},{1,3},{4,8},{5,1},{8,12},{9,5},{12,14},{13,9},{14,10},{15,13... | collective-permute-start | bytes 1179656 | tf_op jit(solution)/shard_map/ppermute | solution.py:282
  54.9 9.2 %collective-permute-start.14 = (bf16[64,3072]{1,0:T(8,128)(2,1)}, bf16[64,3072]{1,0:T(8,128)(2,1)}, u32[]{:S(2)}, u32[]{:S(2)}) collective-permute-start(bf16[64,3072]{1,0:T(8,128)(2,1)} %collective-permute-done.5.refs_5_), channel_id=1, source_target_pairs={{0,1},{1,0},{2,3},{3,2},{4,5},{5,4},{6,7},{7,6},{8,9},{9,8},{10,11... | collective-permute-start | bytes 1179656 | tf_op jit(solution)/shard_map/ppermute | solution.py:285
  61.6 0.8 copy-start.13
  62.4 10.4 %collective-permute-start.9 = (bf16[64,3072]{1,0:T(8,128)(2,1)}, bf16[64,3072]{1,0:T(8,128)(2,1)}, u32[]{:S(2)}, u32[]{:S(2)}) collective-permute-start(bf16[64,3072]{1,0:T(8,128)(2,1)} %add_convert_fusion.6), channel_id=1, source_target_pairs={{0,4},{1,3},{4,8},{5,1},{8,12},{9,5},{12,14},{13,9},{14,10},{15,13... | collective-permute-start | bytes 1179656 | tf_op jit(solution)/shard_map/ppermute | solution.py:282
  63.5 36.7 %collective-permute-start.20 = (bf16[64,3072]{1,0:T(8,128)(2,1)}, bf16[64,3072]{1,0:T(8,128)(2,1)S(1)}, u32[]{:S(2)}, u32[]{:S(2)}) collective-permute-start(bf16[64,3072]{1,0:T(8,128)(2,1)} %copy-done.4), channel_id=1, source_target_pairs={{0,1},{1,0},{2,3},{3,2},{4,5},{5,4},{6,7},{7,6},{8,9},{9,8},{10,11... | collective-permute-start | bytes 1179656 | tf_op jit(solution)/shard_map/ppermute | solution.py:285
  63.5 36.7 %collective-permute-start.21 = (bf16[64,3072]{1,0:T(8,128)(2,1)}, bf16[64,3072]{1,0:T(8,128)(2,1)S(1)}, u32[]{:S(2)}, u32[]{:S(2)}) collective-permute-start(bf16[64,3072]{1,0:T(8,128)(2,1)} %copy-done.7), channel_id=1, source_target_pairs={{0,1},{1,0},{2,3},{3,2},{4,5},{5,4},{6,7},{7,6},{8,9},{9,8},{10,11... | collective-permute-start | bytes 1179656 | tf_op jit(solution)/shard_map/ppermute | solution.py:285
  64.0 36.2 %collective-permute-start.22 = (bf16[64,3072]{1,0:T(8,128)(2,1)}, bf16[64,3072]{1,0:T(8,128)(2,1)S(1)}, u32[]{:S(2)}, u32[]{:S(2)}) collective-permute-start(bf16[64,3072]{1,0:T(8,128)(2,1)} %copy-done.10), channel_id=1, source_target_pairs={{0,1},{1,0},{2,3},{3,2},{4,5},{5,4},{6,7},{7,6},{8,9},{9,8},{10,11... | collective-permute-start | bytes 1179656 | tf_op jit(solution)/shard_map/ppermute | solution.py:285
  64.1 1.0 copy-start.3
  65.1 1.0 copy-start.5
  66.1 1.0 copy-start.8
  67.1 1.0 copy-start.11
  68.1 1.0 copy-start.14
  69.1 6.5 %copy-start.22 = (bf16[192,3072]{1,0:T(8,128)(2,1)S(1)}, bf16[192,3072]{1,0:T(8,128)(2,1)}, u32[]{:S(2)}) copy-start(bf16[192,3072]{1,0:T(8,128)(2,1)} %copy-done.21) | copy-start | bytes 3538948
  72.8 2.9 %copy-start.1 = (bf16[192,3072]{1,0:T(8,128)(2,1)S(1)}, bf16[192,3072]{1,0:T(8,128)(2,1)}, u32[]{:S(2)}) copy-start(bf16[192,3072]{1,0:T(8,128)(2,1)} %copy-done) | copy-start | bytes 3538948
  72.8 4.5 %copy-start.6 = (bf16[64,3072]{1,0:T(8,128)(2,1)S(1)}, bf16[64,3072]{1,0:T(8,128)(2,1)}, u32[]{:S(2)}) copy-start(bf16[64,3072]{1,0:T(8,128)(2,1)} %copy-done.4) | copy-start | bytes 1179652
  72.8 4.5 %copy-start.9 = (bf16[64,3072]{1,0:T(8,128)(2,1)S(1)}, bf16[64,3072]{1,0:T(8,128)(2,1)}, u32[]{:S(2)}) copy-start(bf16[64,3072]{1,0:T(8,128)(2,1)} %copy-done.7) | copy-start | bytes 1179652
  72.8 4.5 %copy-start.12 = (bf16[64,3072]{1,0:T(8,128)(2,1)S(1)}, bf16[64,3072]{1,0:T(8,128)(2,1)}, u32[]{:S(2)}) copy-start(bf16[64,3072]{1,0:T(8,128)(2,1)} %copy-done.10) | copy-start | bytes 1179652
  72.8 4.5 %copy-start.15 = (bf16[64,3072]{1,0:T(8,128)(2,1)S(1)}, bf16[64,3072]{1,0:T(8,128)(2,1)}, u32[]{:S(2)}) copy-start(bf16[64,3072]{1,0:T(8,128)(2,1)} %copy-done.13) | copy-start | bytes 1179652
  74.1 7.8 %collective-permute-start.16 = (bf16[64,3072]{1,0:T(8,128)(2,1)S(1)}, bf16[64,3072]{1,0:T(8,128)(2,1)S(1)}, u32[]{:S(2)}, u32[]{:S(2)}) collective-permute-start(bf16[64,3072]{1,0:T(8,128)(2,1)S(1)} %add_convert_fusion.4), channel_id=1, source_target_pairs={{0,4},{1,3},{4,8},{5,1},{8,12},{9,5},{12,14},{13,9},{14,10},{15,13... | collective-permute-start | bytes 1179656 | tf_op jit(solution)/shard_map/ppermute | solution.py:282
  76.8 9.3 %collective-permute-start.15 = (bf16[64,3072]{1,0:T(8,128)(2,1)S(1)}, bf16[64,3072]{1,0:T(8,128)(2,1)S(1)}, u32[]{:S(2)}, u32[]{:S(2)}) collective-permute-start(bf16[64,3072]{1,0:T(8,128)(2,1)S(1)} %add_convert_fusion.5), channel_id=1, source_target_pairs={{0,4},{1,3},{4,8},{5,1},{8,12},{9,5},{12,14},{13,9},{14,10},{15,13... | collective-permute-start | bytes 1179656 | tf_op jit(solution)/shard_map/ppermute | solution.py:282
  81.9 18.3 %collective-permute-start.19 = (bf16[64,3072]{1,0:T(8,128)(2,1)S(1)}, bf16[64,3072]{1,0:T(8,128)(2,1)S(1)}, u32[]{:S(2)}, u32[]{:S(2)}) collective-permute-start(bf16[64,3072]{1,0:T(8,128)(2,1)S(1)} %copy-done.15), channel_id=1, source_target_pairs={{0,1},{1,0},{2,3},{3,2},{4,5},{5,4},{6,7},{7,6},{8,9},{9,8},{10,11... | collective-permute-start | bytes 1179656 | tf_op jit(solution)/shard_map/ppermute | solution.py:285
  87.2 7.8 %collective-permute-start.18 = (bf16[64,3072]{1,0:T(8,128)(2,1)S(1)}, bf16[64,3072]{1,0:T(8,128)(2,1)S(1)}, u32[]{:S(2)}, u32[]{:S(2)}) collective-permute-start(bf16[64,3072]{1,0:T(8,128)(2,1)S(1)} %add_convert_fusion.2), channel_id=1, source_target_pairs={{0,4},{1,3},{4,8},{5,1},{8,12},{9,5},{12,14},{13,9},{14,10},{15,13... | collective-permute-start | bytes 1179656 | tf_op jit(solution)/shard_map/ppermute | solution.py:282
  95.1 8.6 %collective-permute-start.17 = (bf16[64,3072]{1,0:T(8,128)(2,1)S(1)}, bf16[64,3072]{1,0:T(8,128)(2,1)S(1)}, u32[]{:S(2)}, u32[]{:S(2)}) collective-permute-start(bf16[64,3072]{1,0:T(8,128)(2,1)S(1)} %add_convert_fusion.3), channel_id=1, source_target_pairs={{0,4},{1,3},{4,8},{5,1},{8,12},{9,5},{12,14},{13,9},{14,10},{15,13... | collective-permute-start | bytes 1179656 | tf_op jit(solution)/shard_map/ppermute | solution.py:282
  104.8 8.6 %collective-permute-start.24 = (bf16[64,3072]{1,0:T(8,128)(2,1)S(1)}, bf16[64,3072]{1,0:T(8,128)(2,1)S(1)}, u32[]{:S(2)}, u32[]{:S(2)}) collective-permute-start(bf16[64,3072]{1,0:T(8,128)(2,1)S(1)} %add_convert_fusion), channel_id=1, source_target_pairs={{0,4},{1,3},{4,8},{5,1},{8,12},{9,5},{12,14},{13,9},{14,10},{15,13... | collective-permute-start | bytes 1179656 | tf_op jit(solution)/shard_map/ppermute | solution.py:282
  105.7 11.3 %collective-permute-start.23 = (bf16[64,3072]{1,0:T(8,128)(2,1)S(1)}, bf16[64,3072]{1,0:T(8,128)(2,1)S(1)}, u32[]{:S(2)}, u32[]{:S(2)}) collective-permute-start(bf16[64,3072]{1,0:T(8,128)(2,1)S(1)} %add_convert_fusion.1), channel_id=1, source_target_pairs={{0,4},{1,3},{4,8},{5,1},{8,12},{9,5},{12,14},{13,9},{14,10},{15,13... | collective-permute-start | bytes 1179656 | tf_op jit(solution)/shard_map/ppermute | solution.py:282
  109.9 3.5 %copy-start.17 = (bf16[64,3072]{1,0:T(8,128)(2,1)S(1)}, bf16[64,3072]{1,0:T(8,128)(2,1)}, u32[]{:S(2)}) copy-start(bf16[64,3072]{1,0:T(8,128)(2,1)} %copy-done.16) | copy-start | bytes 1179652
  113.5 3.5 %copy-start.19 = (bf16[64,3072]{1,0:T(8,128)(2,1)S(1)}, bf16[64,3072]{1,0:T(8,128)(2,1)}, u32[]{:S(2)}) copy-start(bf16[64,3072]{1,0:T(8,128)(2,1)} %copy-done.18) | copy-start | bytes 1179652
  117.2 1.5 %collective-permute-start.26 = (bf16[32,3072]{1,0:T(8,128)(2,1)S(1)}, bf16[32,3072]{1,0:T(8,128)(2,1)S(1)}, u32[]{:S(2)}, u32[]{:S(2)}) collective-permute-start(bf16[32,3072]{1,0:T(8,128)(2,1)S(1)} %select_convert_fusion), channel_id=1, source_target_pairs={{0,1},{1,0},{2,3},{3,2},{4,5},{5,4},{6,7},{7,6},{8,9},{9,8},{10,11... | collective-permute-start | bytes 589832 | tf_op jit(solution)/shard_map/ppermute | solution.py:285
  117.3 1.7 %collective-permute-start.25 = (bf16[32,3072]{1,0:T(8,128)(2,1)S(1)}, bf16[32,3072]{1,0:T(8,128)(2,1)S(1)}, u32[]{:S(2)}, u32[]{:S(2)}) collective-permute-start(bf16[32,3072]{1,0:T(8,128)(2,1)S(1)} %select_convert_fusion.1), channel_id=1, source_target_pairs={{0,1},{1,0},{2,3},{3,2},{4,5},{5,4},{6,7},{7,6},{8,9},{9,8},{10,11... | collective-permute-start | bytes 589832 | tf_op jit(solution)/shard_map/ppermute | solution.py:285

commit v4 on v3

v4 whole, which is shorter than its diff:
```python
import math

import jax
import jax.numpy as jnp
from jax import lax
from jax.experimental import pallas as pl
from jax.experimental.pallas import tpu as pltpu
from jax.sharding import PartitionSpec as P

RING = 8
PIECE_STEPS = 3
PIECES = 4
VMEM_LIMIT = 16 * 1024 * 1024
WHOLE = pl.BlockSpec(memory_space=pltpu.VMEM)
OUTSIDE = pl.BlockSpec(memory_space=pltpu.HBM)


def cost(microseconds):
    return pl.CostEstimate(
        flops=int(microseconds * 1.15e9), bytes_accessed=0, transcendentals=0
    )


ANYWHERE = pl.BlockSpec(memory_space=pl.ANY)
SCALAR = pl.BlockSpec(memory_space=pltpu.SMEM)


def gelu_slope(pre):
    coeff = math.sqrt(2.0 / math.pi)
    inner = coeff * (pre + 0.044715 * pre * pre * pre)
    tanh_value = jnp.tanh(inner)
    return 0.5 * (1.0 + tanh_value) + 0.5 * pre * (1.0 - tanh_value * tanh_value) * coeff * (
        1.0 + 3.0 * 0.044715 * pre * pre
    )


def plain(out_grad, pre_act, layer_input, weight):
    slope = gelu_slope(pre_act.astype(jnp.float32))
    grad_hidden = (out_grad.astype(jnp.float32) * slope).astype(jnp.bfloat16)
    local_grad = lax.dot_general(
        lax.all_gather(layer_input, "gx", axis=0, tiled=True),
        grad_hidden,
        (((0,), (0,)), ((), ())),
        preferred_element_type=jnp.float32,
    )
    grad_input = lax.psum_scatter(
        lax.dot_general(
            grad_hidden, weight, (((1,), (1,)), ((), ())), preferred_element_type=jnp.float32
        ),
        "gx",
        scatter_dimension=0,
        tiled=True,
    ).astype(jnp.bfloat16)
    return (grad_input, local_grad.astype(jnp.bfloat16))


def chip_at(place):
    place = place & (RING - 1)
    return jnp.where(place < RING // 2, 2 * place, 2 * (RING - 1 - place) + 1)


def place_of(chip):
    return jnp.where(chip % 2 == 0, chip // 2, RING - 1 - chip // 2)


def ring_pairs():
    path = [2 * p if p < RING // 2 else 2 * (RING - 1 - p) + 1 for p in range(RING)]
    pairs = []
    for place, chip in enumerate(path):
        pairs.append((2 * chip, 2 * path[(place + 1) % RING]))
        pairs.append((2 * chip + 1, 2 * path[(place - 1) % RING] + 1))
    return pairs


def chip_order(me):
    way = jnp.where(me % 2 == 0, 1, -1)
    place = place_of(me // 2)
    steps = [0, -1, -2, -3, 4, 1, 2, 3]
    return [chip_at(place + way * s + RING) for s in steps]


def hidden_kernel(me_ref, og_hbm, pre_hbm, w_hbm, dh_ref, dht_ref, w_ref, og_ref, pre_ref, sems):
    rows = dh_ref.shape[0] // RING
    copies = []
    for i, chip in enumerate(chip_order(me_ref[0])):
        source = pl.ds(pl.multiple_of(chip * rows, rows), rows)
        block = pl.ds(i * rows, rows)
        pair = (
            pltpu.make_async_copy(og_hbm.at[source, :], og_ref.at[block, :], sems.at[0, i]),
            pltpu.make_async_copy(pre_hbm.at[source, :], pre_ref.at[block, :], sems.at[1, i]),
        )
        for copy in pair:
            copy.start()
        copies.append(pair)
    wide = w_ref.shape[0]
    first = first_row(me_ref, True, 0, w_hbm.shape[0] // 2, wide)
    fetch = pltpu.make_async_copy(w_hbm.at[pl.ds(first, wide), :], w_ref, sems.at[2, 0])
    fetch.start()
    for i, pair in enumerate(copies):
        for copy in pair:
            copy.wait()
        block = pl.ds(i * rows, rows)
        pre = pre_ref[block, :].astype(jnp.float32)
        og = og_ref[block, :].astype(jnp.float32)
        dh_ref[block, :] = (og * gelu_slope(pre)).astype(jnp.bfloat16)
        if i % 2 == 1:
            two = pl.ds((i - 1) * rows, 2 * rows)
            dht_ref[:, two] = dh_ref[two, :].T
    fetch.wait()


def hidden(me, out_grad, pre_act, weight):
    shape, dtype = out_grad.shape, out_grad.dtype
    return pl.pallas_call(
        hidden_kernel,
        out_shape=(
            jax.ShapeDtypeStruct(shape, dtype),
            jax.ShapeDtypeStruct(shape[::-1], dtype),
            jax.ShapeDtypeStruct((weight.shape[0] // (2 * PIECES), shape[1]), dtype),
        ),
        in_specs=[SCALAR, OUTSIDE, OUTSIDE, OUTSIDE],
        out_specs=(WHOLE, WHOLE, WHOLE),
        scratch_shapes=[
            pltpu.VMEM(shape, dtype),
            pltpu.VMEM(shape, dtype),
            pltpu.SemaphoreType.DMA((3, RING)),
        ],
        compiler_params=pltpu.CompilerParams(vmem_limit_bytes=VMEM_LIMIT),
        cost_estimate=cost(1),
        name="hidden",
    )(me, out_grad, pre_act, weight)


def prepare_kernel(me_ref, own_ref, twin_ref, mine_ref, other_ref):
    core = me_ref[0] % 2
    rows, half = own_ref.shape[0], mine_ref.shape[1]
    for ref, number in ((mine_ref, core), (other_ref, 1 - core)):
        columns = pl.ds(pl.multiple_of(number * half, half), half)
        ref[pl.ds(pl.multiple_of(core * rows, rows), rows), :] = own_ref[:, columns]
        ref[pl.ds(pl.multiple_of((1 - core) * rows, rows), rows), :] = twin_ref[:, columns]


def prepare(me, own, twin):
    rows, width = own.shape
    out = jax.ShapeDtypeStruct((2 * rows, width // 2), own.dtype)
    return pl.pallas_call(
        prepare_kernel,
        out_shape=(out, out),
        in_specs=[SCALAR, WHOLE, WHOLE],
        out_specs=(WHOLE, WHOLE),
        compiler_params=pltpu.CompilerParams(vmem_limit_bytes=VMEM_LIMIT),
        cost_estimate=cost(1),
        name="prepare",
    )(me, own, twin)


def first_row(me_ref, other, piece, half, wide):
    core = me_ref[0] % 2
    number = 1 - core if other else core
    return pl.multiple_of(number * half + piece * wide, wide)


def input_kernel(me_ref, dht_ref, w_ref, w_hbm, *refs, other, piece, wide, more):
    outs, part_ref, sems = refs[-7 if more else -6 :][:4], refs[-2], refs[-1]
    half = outs[0].shape[1]
    if more:
        following = (other, piece + 1) if piece + 1 < PIECES else (False, 0)
        fetch = pltpu.make_async_copy(
            w_hbm.at[pl.ds(first_row(me_ref, *following, half, wide), wide), :],
            refs[-3],
            sems.at[PIECE_STEPS, 0],
        )
        fetch.start()
    step = wide // PIECE_STEPS
    stores = []
    for i in range(PIECE_STEPS):
        here = pl.ds(i * step, step)
        part = jnp.dot(w_ref[here, :], dht_ref[...], preferred_element_type=jnp.float32)
        part_ref[:, here] = part.astype(jnp.bfloat16).T
        at = 0
        for j, out in enumerate(outs):
            store = pltpu.make_async_copy(
                part_ref.at[pl.ds(at, out.shape[0]), here],
                out.at[:, pl.ds(piece * wide + i * step, step)],
                sems.at[i, j],
            )
            store.start()
            stores.append(store)
            at += out.shape[0]
    for store in stores:
        store.wait()
    if more:
        fetch.wait()


def input_piece(me, dht, w, weight, before, other, piece):
    ff, tokens = dht.shape
    half = weight.shape[0] // 2
    wide = half // PIECES
    rows = tokens // RING
    more = other or piece + 1 < PIECES
    outs = tuple(
        jax.ShapeDtypeStruct((count * rows, half), jnp.bfloat16) for count in (1, 3, 1, 3)
    )
    following = (jax.ShapeDtypeStruct((wide, ff), jnp.bfloat16),) if more else ()
    result = pl.pallas_call(
        lambda *refs: input_kernel(*refs, other=other, piece=piece, wide=wide, more=more),
        out_shape=outs + following,
        in_specs=[SCALAR, WHOLE, WHOLE, OUTSIDE] + [ANYWHERE] * len(before),
        out_specs=(ANYWHERE,) * 4 + (WHOLE,) * len(following),
        input_output_aliases={4 + i: i for i in range(len(before))},
        scratch_shapes=[
            pltpu.VMEM((tokens, wide), jnp.bfloat16),
            pltpu.SemaphoreType.DMA((PIECE_STEPS + 1, 4)),
        ],
        compiler_params=pltpu.CompilerParams(vmem_limit_bytes=VMEM_LIMIT),
        cost_estimate=cost(1),
        name="input_piece",
    )(me, dht, w, weight, *before)
    return result[:4], (result[4] if more else None)


def weight_kernel(me_ref, dh_ref, *refs, other, piece, wide, step):
    blocks = refs[:RING]
    stage, sems = refs[-2:]
    out_hbm = refs[-3]
    half = blocks[0].shape[1]
    columns = out_hbm.shape[1]
    copies = []
    if piece or other:
        last = (other, piece - 1) if piece else (False, PIECES - 1)
        row = first_row(me_ref, *last, half, wide)
        for i in range(columns // step):
            here = pl.ds(i * step, step)
            copies.append(
                pltpu.make_async_copy(
                    refs[RING].at[:, here], out_hbm.at[pl.ds(row, wide), here], sems.at[0, i]
                )
            )
            copies[-1].start()
    row = first_row(me_ref, other, piece, half, wide)
    x = jnp.concatenate([b[:, pl.ds(piece * wide, wide)] for b in blocks], axis=0).T
    for i in range(columns // step):
        here = pl.ds(i * step, step)
        stage[:, here] = jnp.dot(
            x, dh_ref[:, here], preferred_element_type=jnp.float32
        ).astype(jnp.bfloat16)
        if other and piece == PIECES - 1:
            copies.append(
                pltpu.make_async_copy(
                    stage.at[:, here], out_hbm.at[pl.ds(row, wide), here], sems.at[1, i]
                )
            )
            copies[-1].start()
    for copy in copies:
        copy.wait()


def weight_piece(me, dh, blocks, before, other, piece):
    tokens, ff = dh.shape
    half = blocks[0].shape[1]
    wide = half // PIECES
    step = 512 if ff % 512 == 0 else 128
    return pl.pallas_call(
        lambda *refs: weight_kernel(*refs, other=other, piece=piece, wide=wide, step=step),
        out_shape=(
            jax.ShapeDtypeStruct((2 * half, ff), jnp.bfloat16),
            jax.ShapeDtypeStruct((wide, ff), jnp.bfloat16),
        ),
        in_specs=[SCALAR, WHOLE] + [WHOLE] * RING + ([WHOLE, OUTSIDE] if before else []),
        out_specs=(OUTSIDE, WHOLE),
        input_output_aliases={3 + RING: 0} if before else {},
        scratch_shapes=[pltpu.SemaphoreType.DMA((2, ff // step))],
        compiler_params=pltpu.CompilerParams(vmem_limit_bytes=VMEM_LIMIT),
        cost_estimate=cost(1),
        name="weight_piece",
    )(me, dh, *blocks, *before)


def halves_kernel(me_ref, own_ref, came_ref, kept_ref, sent_ref):
    core = me_ref[0] % 2
    rows = kept_ref.shape[0]
    for ref, number in ((kept_ref, core), (sent_ref, 1 - core)):
        here = pl.ds(pl.multiple_of(number * rows, rows), rows)
        both = own_ref[here, :].astype(jnp.float32) + came_ref[here, :].astype(jnp.float32)
        ref[...] = both.astype(ref.dtype)


def halves(me, own, came):
    shape = (own.shape[0] // 2, own.shape[1])
    return pl.pallas_call(
        halves_kernel,
        out_shape=(
            jax.ShapeDtypeStruct(shape, jnp.float32),
            jax.ShapeDtypeStruct(shape, jnp.bfloat16),
        ),
        in_specs=[SCALAR, WHOLE, WHOLE],
        out_specs=(WHOLE, WHOLE),
        compiler_params=pltpu.CompilerParams(vmem_limit_bytes=VMEM_LIMIT),
        cost_estimate=cost(0.3),
        name="halves",
    )(me, own, came)


def last_kernel(me_ref, mine_ref, mine_came_ref, other_ref, other_came_ref, out_ref):
    core = me_ref[0] % 2
    half = mine_ref.shape[1]
    pairs = ((core, mine_ref, mine_came_ref), (1 - core, other_ref, other_came_ref))
    for number, kept, came in pairs:
        here = pl.ds(pl.multiple_of(number * half, half), half)
        out_ref[:, here] = (kept[...] + came[...].astype(jnp.float32)).astype(out_ref.dtype)


def last(me, mine, mine_came, other, other_came):
    shape = (mine.shape[0], 2 * mine.shape[1])
    return pl.pallas_call(
        last_kernel,
        out_shape=jax.ShapeDtypeStruct(shape, jnp.bfloat16),
        in_specs=[SCALAR] + [WHOLE] * 4,
        out_specs=WHOLE,
        compiler_params=pltpu.CompilerParams(vmem_limit_bytes=VMEM_LIMIT),
        cost_estimate=cost(0.3),
        name="last",
    )(me, mine, mine_came, other, other_came)


def total(*terms):
    result = terms[0].astype(jnp.float32)
    for term in terms[1:]:
        result = result + term.astype(jnp.float32)
    return result.astype(jnp.bfloat16)


def after(x, *others):
    return lax.optimization_barrier((x, *others))[0]


def on_device(out_grad, pre_act, layer_input, weight):
    n = lax.axis_size("gx")
    rows, width = layer_input.shape
    if n != 2 * RING or rows % 16 or width % (2 * PIECES * PIECE_STEPS * 128):
        return plain(out_grad, pre_act, layer_input, weight)

    pairs = ring_pairs()
    swaps = [(i, i ^ 1) for i in range(n)]

    def ring(x):
        return lax.ppermute(x, "gx", pairs)

    def swap(x):
        return lax.ppermute(x, "gx", swaps)

    out_grad, pre_act, weight = (
        pltpu.with_memory_space_constraint(x, pltpu.HBM) for x in (out_grad, pre_act, weight)
    )
    me = lax.axis_index("gx").astype(jnp.int32).reshape(1)
    both = 2 * rows

    def block(x, k):
        return x[(k - 1) * both : k * both]

    def swap_blocks(x):
        return [swap(block(x, k)) for k in (1, 2, 3)]

    twin = swap(layer_input)
    dh, dht, w = hidden(me, out_grad, pre_act, weight)
    m0, o0 = prepare(me, layer_input, after(twin, dh))

    def product(other, piece, w, before, *ties):
        return input_piece(me, after(dht, *ties), w, weight, before, other, piece)

    m1 = ring(m0)
    go, w = product(True, 0, w, (), m0)
    o1 = ring(after(o0, go[0]))
    go, w = product(True, 1, w, go)
    m1 = after(m1, go[0])
    m2, sm1 = ring(m1), swap(m1)
    go, w = product(True, 2, w, go, m1)
    o1 = after(o1, go[0])
    o2, so1 = ring(o1), swap(o1)
    go, w = product(True, 3, w, go, o1)
    m2 = after(m2, go[0])
    m3, sm2 = ring(m2), swap(m2)
    gm, w = product(False, 0, w, (), m2)
    o2 = after(o2, gm[0])
    o3, so2 = ring(o2), swap(o2)
    own_o, behind_o, opposite_o, ahead_o = go
    gm, w = product(False, 1, w, gm, o2, so1)
    m3 = after(m3, gm[0])
    m4, sm3 = ring(m3), swap(m3)
    from_m, opposite_from = swap_blocks(behind_o), swap(opposite_o)
    gm, w = product(False, 2, w, gm, m3, so2)
    o3, m4 = after(o3, gm[0]), after(m4, gm[0])
    so3, sm4 = swap(o3), swap(m4)
    gm, _ = product(False, 3, w, gm, o3, m4, *from_m, opposite_from)
    own_m, behind_m, opposite_m, ahead_m = gm
    r4m = ring(total(opposite_m, opposite_from))
    from_o = swap_blocks(behind_m)
    mine = (m0, m1, m2, m3, m4, so1, so2, so3)
    others = (o0, o1, o2, o3, sm4, sm1, sm2, sm3)

    def gradient(other, piece, before, *ties):
        blocks = others if other else mine
        before = before[::-1]
        return weight_piece(me, after(dh, *ties), blocks, before, other, piece)

    def send(ahead, came, k, *ring_terms):
        return ring(total(block(ahead, k), came[k - 1], *ring_terms))

    r3o = send(ahead_o, from_o, 3)
    gw = gradient(False, 0, (), *from_o)
    r4m = after(r4m, gw[1])
    r3m = send(ahead_m, from_m, 3, r4m)
    gw = gradient(False, 1, gw, r4m)
    r3o = after(r3o, gw[1])
    r2o = send(ahead_o, from_o, 2, r3o)
    gw = gradient(False, 2, gw, r3o)
    r3m = after(r3m, gw[1])
    r2m = send(ahead_m, from_m, 2, r3m)
    gw = gradient(False, 3, gw, r3m)
    r2o = after(r2o, gw[1])
    r1o = send(ahead_o, from_o, 1, r2o)
    gw = gradient(True, 0, gw, r2o)
    r2m = after(r2m, gw[1])
    r1m = send(ahead_m, from_m, 1, r2m)
    gw = gradient(True, 1, gw, r2m)
    gw = gradient(True, 2, gw)
    kept_o, sent_o = halves(me, own_o, after(r1o, gw[1]))
    came_m = swap(sent_o)
    gw = gradient(True, 3, gw, sent_o)
    kept_m, sent_m = halves(me, own_m, after(r1m, gw[1]))
    came_o = swap(sent_m)
    return (last(me, kept_m, came_m, kept_o, came_o), gw[0])


def solution(mesh):
    placed = (P("group", "gx"), P("group", "gx"), P(("group", "gx"), None), P(None, "gx"))
    return jax.shard_map(
        on_device,
        mesh=mesh,
        in_specs=placed,
        out_specs=(P(("group", "gx"), None), P(None, ("group", "gx"))),
        check_vma=False,
    )
```

time: 121 us -> 95.7 us (0.79)
  Pallas kernels: 66.6 us -> 38.6 us
  waiting for transfers between devices: 14.9 us -> 25.5 us
  local copies, waits for them, and re-layouts: 7.61 us -> 0.17 us
  starting transfers between devices: 22.7 us -> 29.4 us
  other arithmetic: 7 us -> 0.91 us
    pallas_call x8, Pallas kernels: 34.9 us -> 17.7 us  [input_piece(): pl.pallas_call(lambda *refs: input_kernel(*refs, other=other, piece=piece...]
    pallas_call x8, Pallas kernels: 28.2 us -> 16.1 us  [weight_piece(): pl.pallas_call(lambda *refs: weight_kernel(*refs, other=other, piece=piec...]
    ppermute x14, waiting for transfers between devices: 13.7 us -> 25.3 us  [ring(): return lax.ppermute(x, 'gx', pairs)]
    unnamed x46 -> x2, local copies, waits for them, and re-layouts: 7.61 us -> 0.01 us
    ppermute x14, starting transfers between devices: 20 us -> 26.1 us  [ring(): return lax.ppermute(x, 'gx', pairs)]
    convert_element_type x7, other arithmetic: 5.85 us -> 0.91 us  [total(): return result.astype(jnp.bfloat16)]
    pallas_call x1 -> x4, Pallas kernels: 3.47 us -> 4.84 us  [the longest x1 3.85 us: hidden(): pl.pallas_call(hidden_kernel, out_shape=(jax.ShapeDtypeStruct(shape, dtyp...]
    ppermute x13 -> x17, starting transfers between devices: 2.67 us -> 3.34 us  [swap(): return lax.ppermute(x, 'gx', swaps)]
  transfers between devices with their start and end apart: 27 -> 31, of which waited for: 9 -> 12; matrix products, arithmetic and copies ran while one was open for 4% -> 1% of each run, Pallas kernels for 51% -> 40%
where the time goes in v4:
time: 95.7 us; the launch traced here: 95.5 us
  Pallas kernels  38.6 us (40%)
  starting transfers between devices  29.4 us (31%)
  waiting for transfers between devices  25.5 us (27%)
    ppermute x14, starting transfers between devices, ring(): return lax.ppermute(x, 'gx', pairs)  26.1 us
    ppermute x14, waiting for transfers between devices, ring(): return lax.ppermute(x, 'gx', pairs)  25.3 us
    pallas_call x8, Pallas kernels, input_piece(): pl.pallas_call(lambda *refs: input_kernel(*refs, other=other, piece=piece...  17.7 us
    pallas_call x8, Pallas kernels, weight_piece(): pl.pallas_call(lambda *refs: weight_kernel(*refs, other=other, piece=piec...  16.1 us
    pallas_call x1, Pallas kernels, hidden(): pl.pallas_call(hidden_kernel, out_shape=(jax.ShapeDtypeStruct(shape, dtyp...  3.85 us
    ppermute x17, starting transfers between devices, swap(): return lax.ppermute(x, 'gx', swaps)  3.34 us
  transfers between devices with their start and end apart: 31, of which 12 were waited for; matrix products, arithmetic and copies ran while one was open for 1% of the time, Pallas kernels for 40%

profile of v4, /device:TPU:0, one launch (start us, length us, event | category | flops | bytes accessed | tf_op | source)
XLA Modules:
  0.0 95.5 jit_solution(14213450228699878399)
XLA Ops:
  0.6 0.5 collective-permute-start
  1.1 3.9 %hidden.1 = (bf16[512,1536]{1,0:T(8,128)(2,1)S(1)}, bf16[1536,512]{1,0:T(8,128)(2,1)S(1)}, bf16[768,1536]{1,0:T(8,128)(2,1)S(1)}) custom-call(s32[1]{0:T(128)} %bitcast.me_ref.refs_0_, bf16[512,1536]{1,0:T(8,128)(2,1)} %og_hbm.1, bf16[512,1536]{1,0:T(8,128)(2,1)} %pre_hbm.1, bf16[6144,1536]{1,0:T(8,128)(2,1)} %refs_3_.15), custom_call_target="tpu_custom_call" | custom-call | flops 1150000000 | tf_op jit(solution)/shard_map/hidden/pallas_call | solution.py:114
  5.0 0.1 prepare.1
  5.1 2.7 %collective-permute-start.2 = (bf16[64,3072]{1,0:T(8,128)(2,1)S(1)}, bf16[64,3072]{1,0:T(8,128)(2,1)S(1)}, u32[]{:S(2)}, u32[]{:S(2)}) collective-permute-start(bf16[64,3072]{1,0:T(8,128)(2,1)S(1)} %get-tuple-element.98.refs_2_), channel_id=1, source_target_pairs={{0,4},{1,3},{4,8},{5,1},{8,12},{9,5},{12,14},{13,9},{14,10},{15,13... | collective-permute-start | bytes 1179656 | tf_op jit(solution)/shard_map/ppermute | solution.py:348
  7.8 2.2 %input_piece.8 = (bf16[64,3072]{1,0:T(8,128)(2,1)S(1)}, bf16[192,3072]{1,0:T(8,128)(2,1)S(1)}, bf16[64,3072]{1,0:T(8,128)(2,1)S(1)}, bf16[192,3072]{1,0:T(8,128)(2,1)S(1)}, bf16[768,1536]{1,0:T(8,128)(2,1)S(1)}) custom-call(s32[1]{0:T(128)} %bitcast.me_ref.refs_0_, bf16[1536,512]{1,0:T(8,128)(2,1)S(1)} %get-tuple-element.144.refs_1_, ...), custom_call_target="tpu_custom_call" | custom-call | flops 1150000000 | tf_op jit(solution)/shard_map/input_piece/pallas_call | solution.py:206
  10.0 1.6 %collective-permute-start.1 = (bf16[64,3072]{1,0:T(8,128)(2,1)S(1)}, bf16[64,3072]{1,0:T(8,128)(2,1)S(1)}, u32[]{:S(2)}, u32[]{:S(2)}) collective-permute-start(bf16[64,3072]{1,0:T(8,128)(2,1)S(1)} %get-tuple-element.102.refs_2_), channel_id=1, source_target_pairs={{0,4},{1,3},{4,8},{5,1},{8,12},{9,5},{12,14},{13,9},{14,10},{15,13... | collective-permute-start | bytes 1179656 | tf_op jit(solution)/shard_map/ppermute | solution.py:348
  11.6 2.2 %input_piece.9 = (bf16[64,3072]{1,0:T(8,128)(2,1)S(1)}, bf16[192,3072]{1,0:T(8,128)(2,1)S(1)}, bf16[64,3072]{1,0:T(8,128)(2,1)S(1)}, bf16[192,3072]{1,0:T(8,128)(2,1)S(1)}, bf16[768,1536]{1,0:T(8,128)(2,1)S(1)}) custom-call(s32[1]{0:T(128)} %bitcast.me_ref.refs_0_, ...), custom_call_target="tpu_custom_call", output_to_operand_aliasing={{0}: (4, {}), {1}: (5, {}), {2}: (6, {}), {3}: (7, {})} | custom-call | flops 1150000000 | tf_op jit(solution)/shard_map/input_piece/pallas_call | solution.py:206
  13.8 1.7 %collective-permute-start.4 = (bf16[64,3072]{1,0:T(8,128)(2,1)S(1)}, bf16[64,3072]{1,0:T(8,128)(2,1)S(1)}, u32[]{:S(2)}, u32[]{:S(2)}) collective-permute-start(bf16[64,3072]{1,0:T(8,128)(2,1)S(1)} %collective-permute-done.2.refs_3_), channel_id=1, source_target_pairs={{0,4},{1,3},{4,8},{5,1},{8,12},{9,5},{12,14},{13,9},{14,10},{15,13... | collective-permute-start | bytes 1179656 | tf_op jit(solution)/shard_map/ppermute | solution.py:348
  15.5 2.2 %input_piece.10 = (bf16[64,3072]{1,0:T(8,128)(2,1)S(1)}, bf16[192,3072]{1,0:T(8,128)(2,1)S(1)}, bf16[64,3072]{1,0:T(8,128)(2,1)S(1)}, bf16[192,3072]{1,0:T(8,128)(2,1)S(1)}, bf16[768,1536]{1,0:T(8,128)(2,1)S(1)}) custom-call(s32[1]{0:T(128)} %bitcast.me_ref.refs_0_, ...), custom_call_target="tpu_custom_call", output_to_operand_aliasing={{0}: (4, {}), {1}: (5, {}), {2}: (6, {}), {3}: (7, {})} | custom-call | flops 1150000000 | tf_op jit(solution)/shard_map/input_piece/pallas_call | solution.py:206
  17.8 1.9 %collective-permute-start.3 = (bf16[64,3072]{1,0:T(8,128)(2,1)S(1)}, bf16[64,3072]{1,0:T(8,128)(2,1)S(1)}, u32[]{:S(2)}, u32[]{:S(2)}) collective-permute-start(bf16[64,3072]{1,0:T(8,128)(2,1)S(1)} %collective-permute-done.1.refs_3_), channel_id=1, source_target_pairs={{0,4},{1,3},{4,8},{5,1},{8,12},{9,5},{12,14},{13,9},{14,10},{15,13... | collective-permute-start | bytes 1179656 | tf_op jit(solution)/shard_map/ppermute | solution.py:348
  19.8 2.2 %input_piece.11 = (bf16[64,3072]{1,0:T(8,128)(2,1)S(1)}, bf16[192,3072]{1,0:T(8,128)(2,1)S(1)}, bf16[64,3072]{1,0:T(8,128)(2,1)S(1)}, bf16[192,3072]{1,0:T(8,128)(2,1)S(1)}, bf16[768,1536]{1,0:T(8,128)(2,1)S(1)}) custom-call(s32[1]{0:T(128)} %bitcast.me_ref.refs_0_, ...), custom_call_target="tpu_custom_call", output_to_operand_aliasing={{0}: (4, {}), {1}: (5, {}), {2}: (6, {}), {3}: (7, {})} | custom-call | flops 1150000000 | tf_op jit(solution)/shard_map/input_piece/pallas_call | solution.py:206
  22.0 1.9 %collective-permute-start.6 = (bf16[64,3072]{1,0:T(8,128)(2,1)S(1)}, bf16[64,3072]{1,0:T(8,128)(2,1)S(1)}, u32[]{:S(2)}, u32[]{:S(2)}) collective-permute-start(bf16[64,3072]{1,0:T(8,128)(2,1)S(1)} %collective-permute-done.4.refs_4_), channel_id=1, source_target_pairs={{0,4},{1,3},{4,8},{5,1},{8,12},{9,5},{12,14},{13,9},{14,10},{15,13... | collective-permute-start | bytes 1179656 | tf_op jit(solution)/shard_map/ppermute | solution.py:348
  24.0 2.2 %input_piece.12 = (bf16[64,3072]{1,0:T(8,128)(2,1)S(1)}, bf16[192,3072]{1,0:T(8,128)(2,1)S(1)}, bf16[64,3072]{1,0:T(8,128)(2,1)S(1)}, bf16[192,3072]{1,0:T(8,128)(2,1)S(1)}, bf16[768,1536]{1,0:T(8,128)(2,1)S(1)}) custom-call(s32[1]{0:T(128)} %bitcast.me_ref.refs_0_, bf16[1536,512]{1,0:T(8,128)(2,1)S(1)} %get-tuple-element.144.refs_1_, ...), custom_call_target="tpu_custom_call" | custom-call | flops 1150000000 | tf_op jit(solution)/shard_map/input_piece/pallas_call | solution.py:206
  26.2 0.1 collective-permute-done.3.refs_4_
  26.2 1.9 %collective-permute-start.5 = (bf16[64,3072]{1,0:T(8,128)(2,1)S(1)}, bf16[64,3072]{1,0:T(8,128)(2,1)S(1)}, u32[]{:S(2)}, u32[]{:S(2)}) collective-permute-start(bf16[64,3072]{1,0:T(8,128)(2,1)S(1)} %collective-permute-done.3.refs_4_), channel_id=1, source_target_pairs={{0,4},{1,3},{4,8},{5,1},{8,12},{9,5},{12,14},{13,9},{14,10},{15,13... | collective-permute-start | bytes 1179656 | tf_op jit(solution)/shard_map/ppermute | solution.py:348
  28.2 0.1 fusion.1
  28.3 0.6 collective-permute-start.10
  28.8 2.2 %input_piece.13 = (bf16[64,3072]{1,0:T(8,128)(2,1)S(1)}, bf16[192,3072]{1,0:T(8,128)(2,1)S(1)}, bf16[64,3072]{1,0:T(8,128)(2,1)S(1)}, bf16[192,3072]{1,0:T(8,128)(2,1)S(1)}, bf16[768,1536]{1,0:T(8,128)(2,1)S(1)}) custom-call(s32[1]{0:T(128)} %bitcast.me_ref.refs_0_, ...), custom_call_target="tpu_custom_call", output_to_operand_aliasing={{0}: (4, {}), {1}: (5, {}), {2}: (6, {}), {3}: (7, {})} | custom-call | flops 1150000000 | tf_op jit(solution)/shard_map/input_piece/pallas_call | solution.py:206
  31.1 1.8 %collective-permute-start.9 = (bf16[64,3072]{1,0:T(8,128)(2,1)S(1)}, bf16[64,3072]{1,0:T(8,128)(2,1)S(1)}, u32[]{:S(2)}, u32[]{:S(2)}) collective-permute-start(bf16[64,3072]{1,0:T(8,128)(2,1)S(1)} %collective-permute-done.6.refs_5_), channel_id=1, source_target_pairs={{0,4},{1,3},{4,8},{5,1},{8,12},{9,5},{12,14},{13,9},{14,10},{15,13... | collective-permute-start | bytes 1179656 | tf_op jit(solution)/shard_map/ppermute | solution.py:348
  32.9 1.8 %collective-permute-done.5.refs_5_ = bf16[64,3072]{1,0:T(8,128)(2,1)S(1)} collective-permute-done((bf16[64,3072]{1,0:T(8,128)(2,1)S(1)}, bf16[64,3072]{1,0:T(8,128)(2,1)S(1)}, u32[]{:S(2)}, u32[]{:S(2)}) %collective-permute-start.5) | collective-permute-done | bytes 393248 | tf_op jit(solution)/shard_map/ppermute | solution.py:348
  34.7 0.5 collective-permute-start.13
  35.2 2.2 %input_piece.14 = (bf16[64,3072]{1,0:T(8,128)(2,1)S(1)}, bf16[192,3072]{1,0:T(8,128)(2,1)S(1)}, bf16[64,3072]{1,0:T(8,128)(2,1)S(1)}, bf16[192,3072]{1,0:T(8,128)(2,1)S(1)}, bf16[768,1536]{1,0:T(8,128)(2,1)S(1)}) custom-call(s32[1]{0:T(128)} %bitcast.me_ref.refs_0_, ...), custom_call_target="tpu_custom_call", output_to_operand_aliasing={{0}: (4, {}), {1}: (5, {}), {2}: (6, {}), {3}: (7, {})} | custom-call | flops 1150000000 | tf_op jit(solution)/shard_map/input_piece/pallas_call | solution.py:206
  37.4 1.7 %collective-permute-done.9.refs_6_ = bf16[64,3072]{1,0:T(8,128)(2,1)S(1)} collective-permute-done((bf16[64,3072]{1,0:T(8,128)(2,1)S(1)}, bf16[64,3072]{1,0:T(8,128)(2,1)S(1)}, u32[]{:S(2)}, u32[]{:S(2)}) %collective-permute-start.9) | collective-permute-done | bytes 393248 | tf_op jit(solution)/shard_map/ppermute | solution.py:348
  39.1 2.2 %input_piece.15 = (bf16[64,3072]{1,0:T(8,128)(2,1)S(1)}, bf16[192,3072]{1,0:T(8,128)(2,1)S(1)}, bf16[64,3072]{1,0:T(8,128)(2,1)S(1)}, bf16[192,3072]{1,0:T(8,128)(2,1)S(1)}) custom-call(s32[1]{0:T(128)} %bitcast.me_ref.refs_0_, ...), custom_call_target="tpu_custom_call", output_to_operand_aliasing={{0}: (4, {}), {1}: (5, {}), {2}: (6, {}), {3}: (7, {})} | custom-call | flops 1150000000 | tf_op jit(solution)/shard_map/input_piece/pallas_call | solution.py:206
  41.3 0.1 fusion
  41.4 0.6 collective-permute-start.15
  42.0 0.1 collective-permute-start.16
  42.1 0.4 collective-permute-start.17
  42.5 0.1 add_convert_fusion.6
  42.6 1.8 %collective-permute-start.14 = (bf16[64,3072]{1,0:T(8,128)(2,1)S(1)}, bf16[64,3072]{1,0:T(8,128)(2,1)S(1)}, u32[]{:S(2)}, u32[]{:S(2)}) collective-permute-start(bf16[64,3072]{1,0:T(8,128)(2,1)S(1)} %add_convert_fusion.6), channel_id=1, source_target_pairs={{0,4},{1,3},{4,8},{5,1},{8,12},{9,5},{12,14},{13,9},{14,10},{15,13... | collective-permute-start | bytes 1179656 | tf_op jit(solution)/shard_map/ppermute | solution.py:348
  44.4 0.1 collective-permute-done.17
  44.5 1.5 %weight_piece.8 = (bf16[6144,1536]{1,0:T(8,128)(2,1)}, bf16[768,1536]{1,0:T(8,128)(2,1)S(1)}) custom-call(s32[1]{0:T(128)} %bitcast.me_ref.refs_0_, bf16[512,1536]{1,0:T(8,128)(2,1)S(1)} %get-tuple-element.183.refs_1_, bf16[64,3072]{1,0:T(8,128)(2,1)S(1)} %get-tuple-element.98.refs_2_, bf16[64,3072]{1,0:T(8,128)(2,1)S(1)} %collective-permute-done.2.refs_3_, ...), custom_call_target="tpu_custom_call" | custom-call | flops 1150000000 | tf_op jit(solution)/shard_map/weight_piece/pallas_call | solution.py:264
  46.0 4.5 %collective-permute-done.14 = bf16[64,3072]{1,0:T(8,128)(2,1)S(1)} collective-permute-done((bf16[64,3072]{1,0:T(8,128)(2,1)S(1)}, bf16[64,3072]{1,0:T(8,128)(2,1)S(1)}, u32[]{:S(2)}, u32[]{:S(2)}) %collective-permute-start.14) | collective-permute-done | bytes 393248 | tf_op jit(solution)/shard_map/ppermute | solution.py:348
  50.4 0.1 add_convert_fusion.4
  50.5 1.8 %collective-permute-start.20 = (bf16[64,3072]{1,0:T(8,128)(2,1)S(1)}, bf16[64,3072]{1,0:T(8,128)(2,1)S(1)}, u32[]{:S(2)}, u32[]{:S(2)}) collective-permute-start(bf16[64,3072]{1,0:T(8,128)(2,1)S(1)} %add_convert_fusion.4), channel_id=1, source_target_pairs={{0,4},{1,3},{4,8},{5,1},{8,12},{9,5},{12,14},{13,9},{14,10},{15,13... | collective-permute-start | bytes 1179656 | tf_op jit(solution)/shard_map/ppermute | solution.py:348
  52.3 0.1 add_convert_fusion.5
  52.5 1.6 %collective-permute-start.19 = (bf16[64,3072]{1,0:T(8,128)(2,1)S(1)}, bf16[64,3072]{1,0:T(8,128)(2,1)S(1)}, u32[]{:S(2)}, u32[]{:S(2)}) collective-permute-start(bf16[64,3072]{1,0:T(8,128)(2,1)S(1)} %add_convert_fusion.5), channel_id=1, source_target_pairs={{0,4},{1,3},{4,8},{5,1},{8,12},{9,5},{12,14},{13,9},{14,10},{15,13... | collective-permute-start | bytes 1179656 | tf_op jit(solution)/shard_map/ppermute | solution.py:348
  54.1 0.5 collective-permute-start.25
  54.6 1.8 %weight_piece.9 = (bf16[6144,1536]{1,0:T(8,128)(2,1)}, bf16[768,1536]{1,0:T(8,128)(2,1)S(1)}) custom-call(s32[1]{0:T(128)} %bitcast.me_ref.refs_0_, bf16[512,1536]{1,0:T(8,128)(2,1)S(1)} %get-tuple-element.183.refs_1_, bf16[64,3072]{1,0:T(8,128)(2,1)S(1)} %get-tuple-element.98.refs_2_, ...), custom_call_target="tpu_custom_call", output_to_operand_aliasing={{0}: (11, {})} | custom-call | flops 1150000000 | tf_op jit(solution)/shard_map/weight_piece/pallas_call | solution.py:264
  56.4 2.0 %collective-permute-done.20 = bf16[64,3072]{1,0:T(8,128)(2,1)S(1)} collective-permute-done((bf16[64,3072]{1,0:T(8,128)(2,1)S(1)}, bf16[64,3072]{1,0:T(8,128)(2,1)S(1)}, u32[]{:S(2)}, u32[]{:S(2)}) %collective-permute-start.20) | collective-permute-done | bytes 393248 | tf_op jit(solution)/shard_map/ppermute | solution.py:348
  58.4 1.8 %weight_piece.10 = (bf16[6144,1536]{1,0:T(8,128)(2,1)}, bf16[768,1536]{1,0:T(8,128)(2,1)S(1)}) custom-call(s32[1]{0:T(128)} %bitcast.me_ref.refs_0_, bf16[512,1536]{1,0:T(8,128)(2,1)S(1)} %get-tuple-element.183.refs_1_, bf16[64,3072]{1,0:T(8,128)(2,1)S(1)} %get-tuple-element.98.refs_2_, ...), custom_call_target="tpu_custom_call", output_to_operand_aliasing={{0}: (11, {})} | custom-call | flops 1150000000 | tf_op jit(solution)/shard_map/weight_piece/pallas_call | solution.py:264
  60.1 2.4 %collective-permute-done.19 = bf16[64,3072]{1,0:T(8,128)(2,1)S(1)} collective-permute-done((bf16[64,3072]{1,0:T(8,128)(2,1)S(1)}, bf16[64,3072]{1,0:T(8,128)(2,1)S(1)}, u32[]{:S(2)}, u32[]{:S(2)}) %collective-permute-start.19) | collective-permute-done | bytes 393248 | tf_op jit(solution)/shard_map/ppermute | solution.py:348
  62.6 0.1 add_convert_fusion.2
  62.7 1.8 %collective-permute-start.22 = (bf16[64,3072]{1,0:T(8,128)(2,1)S(1)}, bf16[64,3072]{1,0:T(8,128)(2,1)S(1)}, u32[]{:S(2)}, u32[]{:S(2)}) collective-permute-start(bf16[64,3072]{1,0:T(8,128)(2,1)S(1)} %add_convert_fusion.2), channel_id=1, source_target_pairs={{0,4},{1,3},{4,8},{5,1},{8,12},{9,5},{12,14},{13,9},{14,10},{15,13... | collective-permute-start | bytes 1179656 | tf_op jit(solution)/shard_map/ppermute | solution.py:348
  64.5 0.1 add_convert_fusion.3
  64.7 5.9 %collective-permute-done.22 = bf16[64,3072]{1,0:T(8,128)(2,1)S(1)} collective-permute-done((bf16[64,3072]{1,0:T(8,128)(2,1)S(1)}, bf16[64,3072]{1,0:T(8,128)(2,1)S(1)}, u32[]{:S(2)}, u32[]{:S(2)}) %collective-permute-start.22) | collective-permute-done | bytes 393248 | tf_op jit(solution)/shard_map/ppermute | solution.py:348
  70.5 1.7 %collective-permute-start.21 = (bf16[64,3072]{1,0:T(8,128)(2,1)S(1)}, bf16[64,3072]{1,0:T(8,128)(2,1)S(1)}, u32[]{:S(2)}, u32[]{:S(2)}) collective-permute-start(bf16[64,3072]{1,0:T(8,128)(2,1)S(1)} %add_convert_fusion.3), channel_id=1, source_target_pairs={{0,4},{1,3},{4,8},{5,1},{8,12},{9,5},{12,14},{13,9},{14,10},{15,13... | collective-permute-start | bytes 1179656 | tf_op jit(solution)/shard_map/ppermute | solution.py:348
  72.3 1.8 %weight_piece.11 = (bf16[6144,1536]{1,0:T(8,128)(2,1)}, bf16[768,1536]{1,0:T(8,128)(2,1)S(1)}) custom-call(s32[1]{0:T(128)} %bitcast.me_ref.refs_0_, bf16[512,1536]{1,0:T(8,128)(2,1)S(1)} %get-tuple-element.183.refs_1_, bf16[64,3072]{1,0:T(8,128)(2,1)S(1)} %get-tuple-element.98.refs_2_, ...), custom_call_target="tpu_custom_call", output_to_operand_aliasing={{0}: (11, {})} | custom-call | flops 1150000000 | tf_op jit(solution)/shard_map/weight_piece/pallas_call | solution.py:264
  74.1 1.8 %weight_piece.12 = (bf16[6144,1536]{1,0:T(8,128)(2,1)}, bf16[768,1536]{1,0:T(8,128)(2,1)S(1)}) custom-call(s32[1]{0:T(128)} %bitcast.me_ref.refs_0_, bf16[512,1536]{1,0:T(8,128)(2,1)S(1)} %get-tuple-element.183.refs_1_, bf16[64,3072]{1,0:T(8,128)(2,1)S(1)} %get-tuple-element.102.refs_2_, ...), custom_call_target="tpu_custom_call", output_to_operand_aliasing={{0}: (11, {})} | custom-call | flops 1150000000 | tf_op jit(solution)/shard_map/weight_piece/pallas_call | solution.py:264
  75.9 2.4 %collective-permute-done.21 = bf16[64,3072]{1,0:T(8,128)(2,1)S(1)} collective-permute-done((bf16[64,3072]{1,0:T(8,128)(2,1)S(1)}, bf16[64,3072]{1,0:T(8,128)(2,1)S(1)}, u32[]{:S(2)}, u32[]{:S(2)}) %collective-permute-start.21) | collective-permute-done | bytes 393248 | tf_op jit(solution)/shard_map/ppermute | solution.py:348
  78.3 0.1 add_convert_fusion
  78.5 1.8 %collective-permute-start.28 = (bf16[64,3072]{1,0:T(8,128)(2,1)S(1)}, bf16[64,3072]{1,0:T(8,128)(2,1)S(1)}, u32[]{:S(2)}, u32[]{:S(2)}) collective-permute-start(bf16[64,3072]{1,0:T(8,128)(2,1)S(1)} %add_convert_fusion), channel_id=1, source_target_pairs={{0,4},{1,3},{4,8},{5,1},{8,12},{9,5},{12,14},{13,9},{14,10},{15,13... | collective-permute-start | bytes 1179656 | tf_op jit(solution)/shard_map/ppermute | solution.py:348
  80.3 0.1 add_convert_fusion.1
  80.4 1.9 %collective-permute-start.27 = (bf16[64,3072]{1,0:T(8,128)(2,1)S(1)}, bf16[64,3072]{1,0:T(8,128)(2,1)S(1)}, u32[]{:S(2)}, u32[]{:S(2)}) collective-permute-start(bf16[64,3072]{1,0:T(8,128)(2,1)S(1)} %add_convert_fusion.1), channel_id=1, source_target_pairs={{0,4},{1,3},{4,8},{5,1},{8,12},{9,5},{12,14},{13,9},{14,10},{15,13... | collective-permute-start | bytes 1179656 | tf_op jit(solution)/shard_map/ppermute | solution.py:348
  82.3 1.8 %weight_piece.13 = (bf16[6144,1536]{1,0:T(8,128)(2,1)}, bf16[768,1536]{1,0:T(8,128)(2,1)S(1)}) custom-call(s32[1]{0:T(128)} %bitcast.me_ref.refs_0_, bf16[512,1536]{1,0:T(8,128)(2,1)S(1)} %get-tuple-element.183.refs_1_, bf16[64,3072]{1,0:T(8,128)(2,1)S(1)} %get-tuple-element.102.refs_2_, ...), custom_call_target="tpu_custom_call", output_to_operand_aliasing={{0}: (11, {})} | custom-call | flops 1150000000 | tf_op jit(solution)/shard_map/weight_piece/pallas_call | solution.py:264
  84.0 1.8 %weight_piece.14 = (bf16[6144,1536]{1,0:T(8,128)(2,1)}, bf16[768,1536]{1,0:T(8,128)(2,1)S(1)}) custom-call(s32[1]{0:T(128)} %bitcast.me_ref.refs_0_, bf16[512,1536]{1,0:T(8,128)(2,1)S(1)} %get-tuple-element.183.refs_1_, bf16[64,3072]{1,0:T(8,128)(2,1)S(1)} %get-tuple-element.102.refs_2_, ...), custom_call_target="tpu_custom_call", output_to_operand_aliasing={{0}: (11, {})} | custom-call | flops 1150000000 | tf_op jit(solution)/shard_map/weight_piece/pallas_call | solution.py:264
  85.8 0.5 collective-permute-done.28.came_ref
  86.3 0.1 halves.3
  86.4 0.1 collective-permute-start.29
  86.5 4.0 %collective-permute-done.27.came_ref = bf16[64,3072]{1,0:T(8,128)(2,1)S(1)} collective-permute-done((bf16[64,3072]{1,0:T(8,128)(2,1)S(1)}, bf16[64,3072]{1,0:T(8,128)(2,1)S(1)}, u32[]{:S(2)}, u32[]{:S(2)}) %collective-permute-start.27) | collective-permute-done | bytes 393248 | tf_op jit(solution)/shard_map/ppermute | solution.py:348
  90.5 0.1 halves.2
  90.6 0.1 collective-permute-start.30
  90.7 4.0 %weight_piece.15 = (bf16[6144,1536]{1,0:T(8,128)(2,1)}, bf16[768,1536]{1,0:T(8,128)(2,1)}) custom-call(s32[1]{0:T(128)} %bitcast.me_ref.refs_0_, bf16[512,1536]{1,0:T(8,128)(2,1)S(1)} %get-tuple-element.183.refs_1_, bf16[64,3072]{1,0:T(8,128)(2,1)S(1)} %get-tuple-element.102.refs_2_, ...), custom_call_target="tpu_custom_call", output_to_operand_aliasing={{0}: (11, {})} | custom-call | flops 1150000000 | tf_op jit(solution)/shard_map/weight_piece/pallas_call | solution.py:264
  94.7 0.8 last.1
  (30 shorter events, 0.2 us)
Async XLA Ops:
  0.6 4.4 %collective-permute-start = (bf16[32,6144]{1,0:T(8,128)(2,1)}, bf16[32,6144]{1,0:T(8,128)(2,1)S(1)}, u32[]{:S(2)}, u32[]{:S(2)}) collective-permute-start(bf16[32,6144]{1,0:T(8,128)(2,1)} %own_ref.1), channel_id=1, source_target_pairs={{0,1},{1,0},{2,3},{3,2},{4,5},{5,4},{6,7},{7,6},{8,9},{9,8},{10,11... | collective-permute-start | bytes 1179656 | tf_op jit(solution)/shard_map/ppermute | solution.py:351
  1.1 3.9 %copy-start = (bf16[32,6144]{1,0:T(8,128)(2,1)S(1)}, bf16[32,6144]{1,0:T(8,128)(2,1)}, u32[]{:S(2)}) copy-start(bf16[32,6144]{1,0:T(8,128)(2,1)} %own_ref.1) | copy-start | bytes 1179652
  5.1 8.7 %collective-permute-start.2 = (bf16[64,3072]{1,0:T(8,128)(2,1)S(1)}, bf16[64,3072]{1,0:T(8,128)(2,1)S(1)}, u32[]{:S(2)}, u32[]{:S(2)}) collective-permute-start(bf16[64,3072]{1,0:T(8,128)(2,1)S(1)} %get-tuple-element.98.refs_2_), channel_id=1, source_target_pairs={{0,4},{1,3},{4,8},{5,1},{8,12},{9,5},{12,14},{13,9},{14,10},{15,13... | collective-permute-start | bytes 1179656 | tf_op jit(solution)/shard_map/ppermute | solution.py:348
  10.0 7.8 %collective-permute-start.1 = (bf16[64,3072]{1,0:T(8,128)(2,1)S(1)}, bf16[64,3072]{1,0:T(8,128)(2,1)S(1)}, u32[]{:S(2)}, u32[]{:S(2)}) collective-permute-start(bf16[64,3072]{1,0:T(8,128)(2,1)S(1)} %get-tuple-element.102.refs_2_), channel_id=1, source_target_pairs={{0,4},{1,3},{4,8},{5,1},{8,12},{9,5},{12,14},{13,9},{14,10},{15,13... | collective-permute-start | bytes 1179656 | tf_op jit(solution)/shard_map/ppermute | solution.py:348
  13.8 8.2 %collective-permute-start.4 = (bf16[64,3072]{1,0:T(8,128)(2,1)S(1)}, bf16[64,3072]{1,0:T(8,128)(2,1)S(1)}, u32[]{:S(2)}, u32[]{:S(2)}) collective-permute-start(bf16[64,3072]{1,0:T(8,128)(2,1)S(1)} %collective-permute-done.2.refs_3_), channel_id=1, source_target_pairs={{0,4},{1,3},{4,8},{5,1},{8,12},{9,5},{12,14},{13,9},{14,10},{15,13... | collective-permute-start | bytes 1179656 | tf_op jit(solution)/shard_map/ppermute | solution.py:348
  17.8 8.4 %collective-permute-start.3 = (bf16[64,3072]{1,0:T(8,128)(2,1)S(1)}, bf16[64,3072]{1,0:T(8,128)(2,1)S(1)}, u32[]{:S(2)}, u32[]{:S(2)}) collective-permute-start(bf16[64,3072]{1,0:T(8,128)(2,1)S(1)} %collective-permute-done.1.refs_3_), channel_id=1, source_target_pairs={{0,4},{1,3},{4,8},{5,1},{8,12},{9,5},{12,14},{13,9},{14,10},{15,13... | collective-permute-start | bytes 1179656 | tf_op jit(solution)/shard_map/ppermute | solution.py:348
  19.8 9.1 %collective-permute-start.7 = (bf16[64,3072]{1,0:T(8,128)(2,1)S(1)}, bf16[64,3072]{1,0:T(8,128)(2,1)S(1)}, u32[]{:S(2)}, u32[]{:S(2)}) collective-permute-start(bf16[64,3072]{1,0:T(8,128)(2,1)S(1)} %collective-permute-done.1.refs_3_), channel_id=1, source_target_pairs={{0,1},{1,0},{2,3},{3,2},{4,5},{5,4},{6,7},{7,6},{8,9},{9,8},{10,11... | collective-permute-start | bytes 1179656 | tf_op jit(solution)/shard_map/ppermute | solution.py:351
  22.0 9.0 %collective-permute-start.6 = (bf16[64,3072]{1,0:T(8,128)(2,1)S(1)}, bf16[64,3072]{1,0:T(8,128)(2,1)S(1)}, u32[]{:S(2)}, u32[]{:S(2)}) collective-permute-start(bf16[64,3072]{1,0:T(8,128)(2,1)S(1)} %collective-permute-done.4.refs_4_), channel_id=1, source_target_pairs={{0,4},{1,3},{4,8},{5,1},{8,12},{9,5},{12,14},{13,9},{14,10},{15,13... | collective-permute-start | bytes 1179656 | tf_op jit(solution)/shard_map/ppermute | solution.py:348
  26.2 8.4 %collective-permute-start.5 = (bf16[64,3072]{1,0:T(8,128)(2,1)S(1)}, bf16[64,3072]{1,0:T(8,128)(2,1)S(1)}, u32[]{:S(2)}, u32[]{:S(2)}) collective-permute-start(bf16[64,3072]{1,0:T(8,128)(2,1)S(1)} %collective-permute-done.3.refs_4_), channel_id=1, source_target_pairs={{0,4},{1,3},{4,8},{5,1},{8,12},{9,5},{12,14},{13,9},{14,10},{15,13... | collective-permute-start | bytes 1179656 | tf_op jit(solution)/shard_map/ppermute | solution.py:348
  28.2 6.5 %collective-permute-start.8 = (bf16[64,3072]{1,0:T(8,128)(2,1)S(1)}, bf16[64,3072]{1,0:T(8,128)(2,1)S(1)}, u32[]{:S(2)}, u32[]{:S(2)}) collective-permute-start(bf16[64,3072]{1,0:T(8,128)(2,1)S(1)} %collective-permute-done.3.refs_4_), channel_id=1, source_target_pairs={{0,1},{1,0},{2,3},{3,2},{4,5},{5,4},{6,7},{7,6},{8,9},{9,8},{10,11... | collective-permute-start | bytes 1179656 | tf_op jit(solution)/shard_map/ppermute | solution.py:351
  28.3 10.8 %collective-permute-start.10 = (bf16[64,3072]{1,0:T(8,128)(2,1)S(1)}, bf16[64,3072]{1,0:T(8,128)(2,1)S(1)}, u32[]{:S(2)}, u32[]{:S(2)}) collective-permute-start(bf16[64,3072]{1,0:T(8,128)(2,1)S(1)} %get-tuple-element.191), channel_id=1, source_target_pairs={{0,1},{1,0},{2,3},{3,2},{4,5},{5,4},{6,7},{7,6},{8,9},{9,8},{10,11... | collective-permute-start | bytes 1179656 | tf_op jit(solution)/shard_map/ppermute | solution.py:351
  31.1 8.0 %collective-permute-start.9 = (bf16[64,3072]{1,0:T(8,128)(2,1)S(1)}, bf16[64,3072]{1,0:T(8,128)(2,1)S(1)}, u32[]{:S(2)}, u32[]{:S(2)}) collective-permute-start(bf16[64,3072]{1,0:T(8,128)(2,1)S(1)} %collective-permute-done.6.refs_5_), channel_id=1, source_target_pairs={{0,4},{1,3},{4,8},{5,1},{8,12},{9,5},{12,14},{13,9},{14,10},{15,13... | collective-permute-start | bytes 1179656 | tf_op jit(solution)/shard_map/ppermute | solution.py:348
  32.9 6.2 %collective-permute-start.11 = (bf16[64,3072]{1,0:T(8,128)(2,1)S(1)}, bf16[64,3072]{1,0:T(8,128)(2,1)S(1)}, u32[]{:S(2)}, u32[]{:S(2)}) collective-permute-start(bf16[64,3072]{1,0:T(8,128)(2,1)S(1)} %get-tuple-element.190), channel_id=1, source_target_pairs={{0,1},{1,0},{2,3},{3,2},{4,5},{5,4},{6,7},{7,6},{8,9},{9,8},{10,11... | collective-permute-start | bytes 1179656 | tf_op jit(solution)/shard_map/ppermute | solution.py:351
  34.7 4.4 %collective-permute-start.12 = (bf16[64,3072]{1,0:T(8,128)(2,1)S(1)}, bf16[64,3072]{1,0:T(8,128)(2,1)S(1)}, u32[]{:S(2)}, u32[]{:S(2)}) collective-permute-start(bf16[64,3072]{1,0:T(8,128)(2,1)S(1)} %get-tuple-element.189), channel_id=1, source_target_pairs={{0,1},{1,0},{2,3},{3,2},{4,5},{5,4},{6,7},{7,6},{8,9},{9,8},{10,11... | collective-permute-start | bytes 1179656 | tf_op jit(solution)/shard_map/ppermute | solution.py:351
  34.7 4.4 %collective-permute-start.13 = (bf16[64,3072]{1,0:T(8,128)(2,1)S(1)}, bf16[64,3072]{1,0:T(8,128)(2,1)S(1)}, u32[]{:S(2)}, u32[]{:S(2)}) collective-permute-start(bf16[64,3072]{1,0:T(8,128)(2,1)S(1)} %get-tuple-element.143), channel_id=1, source_target_pairs={{0,1},{1,0},{2,3},{3,2},{4,5},{5,4},{6,7},{7,6},{8,9},{9,8},{10,11... | collective-permute-start | bytes 1179656 | tf_op jit(solution)/shard_map/ppermute | solution.py:351
  39.1 5.4 %collective-permute-start.18 = (bf16[64,3072]{1,0:T(8,128)(2,1)S(1)}, bf16[64,3072]{1,0:T(8,128)(2,1)S(1)}, u32[]{:S(2)}, u32[]{:S(2)}) collective-permute-start(bf16[64,3072]{1,0:T(8,128)(2,1)S(1)} %collective-permute-done.5.refs_5_), channel_id=1, source_target_pairs={{0,1},{1,0},{2,3},{3,2},{4,5},{5,4},{6,7},{7,6},{8,9},{9,8},{10,11... | collective-permute-start | bytes 1179656 | tf_op jit(solution)/shard_map/ppermute | solution.py:351
  41.4 3.0 %collective-permute-start.15 = (bf16[64,3072]{1,0:T(8,128)(2,1)S(1)}, bf16[64,3072]{1,0:T(8,128)(2,1)S(1)}, u32[]{:S(2)}, u32[]{:S(2)}) collective-permute-start(bf16[64,3072]{1,0:T(8,128)(2,1)S(1)} %get-tuple-element.188), channel_id=1, source_target_pairs={{0,1},{1,0},{2,3},{3,2},{4,5},{5,4},{6,7},{7,6},{8,9},{9,8},{10,11... | collective-permute-start | bytes 1179656 | tf_op jit(solution)/shard_map/ppermute | solution.py:351
  42.0 2.4 %collective-permute-start.16 = (bf16[64,3072]{1,0:T(8,128)(2,1)S(1)}, bf16[64,3072]{1,0:T(8,128)(2,1)S(1)}, u32[]{:S(2)}, u32[]{:S(2)}) collective-permute-start(bf16[64,3072]{1,0:T(8,128)(2,1)S(1)} %get-tuple-element.187), channel_id=1, source_target_pairs={{0,1},{1,0},{2,3},{3,2},{4,5},{5,4},{6,7},{7,6},{8,9},{9,8},{10,11... | collective-permute-start | bytes 1179656 | tf_op jit(solution)/shard_map/ppermute | solution.py:351
  42.1 2.4 %collective-permute-start.17 = (bf16[64,3072]{1,0:T(8,128)(2,1)S(1)}, bf16[64,3072]{1,0:T(8,128)(2,1)S(1)}, u32[]{:S(2)}, u32[]{:S(2)}) collective-permute-start(bf16[64,3072]{1,0:T(8,128)(2,1)S(1)} %get-tuple-element.186), channel_id=1, source_target_pairs={{0,1},{1,0},{2,3},{3,2},{4,5},{5,4},{6,7},{7,6},{8,9},{9,8},{10,11... | collective-permute-start | bytes 1179656 | tf_op jit(solution)/shard_map/ppermute | solution.py:351
  42.6 7.8 %collective-permute-start.14 = (bf16[64,3072]{1,0:T(8,128)(2,1)S(1)}, bf16[64,3072]{1,0:T(8,128)(2,1)S(1)}, u32[]{:S(2)}, u32[]{:S(2)}) collective-permute-start(bf16[64,3072]{1,0:T(8,128)(2,1)S(1)} %add_convert_fusion.6), channel_id=1, source_target_pairs={{0,4},{1,3},{4,8},{5,1},{8,12},{9,5},{12,14},{13,9},{14,10},{15,13... | collective-permute-start | bytes 1179656 | tf_op jit(solution)/shard_map/ppermute | solution.py:348
  50.5 7.8 %collective-permute-start.20 = (bf16[64,3072]{1,0:T(8,128)(2,1)S(1)}, bf16[64,3072]{1,0:T(8,128)(2,1)S(1)}, u32[]{:S(2)}, u32[]{:S(2)}) collective-permute-start(bf16[64,3072]{1,0:T(8,128)(2,1)S(1)} %add_convert_fusion.4), channel_id=1, source_target_pairs={{0,4},{1,3},{4,8},{5,1},{8,12},{9,5},{12,14},{13,9},{14,10},{15,13... | collective-permute-start | bytes 1179656 | tf_op jit(solution)/shard_map/ppermute | solution.py:348
  52.5 10.1 %collective-permute-start.19 = (bf16[64,3072]{1,0:T(8,128)(2,1)S(1)}, bf16[64,3072]{1,0:T(8,128)(2,1)S(1)}, u32[]{:S(2)}, u32[]{:S(2)}) collective-permute-start(bf16[64,3072]{1,0:T(8,128)(2,1)S(1)} %add_convert_fusion.5), channel_id=1, source_target_pairs={{0,4},{1,3},{4,8},{5,1},{8,12},{9,5},{12,14},{13,9},{14,10},{15,13... | collective-permute-start | bytes 1179656 | tf_op jit(solution)/shard_map/ppermute | solution.py:348
  54.1 20.0 %collective-permute-start.24 = (bf16[64,3072]{1,0:T(8,128)(2,1)S(1)}, bf16[64,3072]{1,0:T(8,128)(2,1)S(1)}, u32[]{:S(2)}, u32[]{:S(2)}) collective-permute-start(bf16[64,3072]{1,0:T(8,128)(2,1)S(1)} %collective-permute-done.2.refs_3_), channel_id=1, source_target_pairs={{0,1},{1,0},{2,3},{3,2},{4,5},{5,4},{6,7},{7,6},{8,9},{9,8},{10,11... | collective-permute-start | bytes 1179656 | tf_op jit(solution)/shard_map/ppermute | solution.py:351
  54.1 20.0 %collective-permute-start.25 = (bf16[64,3072]{1,0:T(8,128)(2,1)S(1)}, bf16[64,3072]{1,0:T(8,128)(2,1)S(1)}, u32[]{:S(2)}, u32[]{:S(2)}) collective-permute-start(bf16[64,3072]{1,0:T(8,128)(2,1)S(1)} %collective-permute-done.4.refs_4_), channel_id=1, source_target_pairs={{0,1},{1,0},{2,3},{3,2},{4,5},{5,4},{6,7},{7,6},{8,9},{9,8},{10,11... | collective-permute-start | bytes 1179656 | tf_op jit(solution)/shard_map/ppermute | solution.py:351
  54.6 19.5 %collective-permute-start.26 = (bf16[64,3072]{1,0:T(8,128)(2,1)S(1)}, bf16[64,3072]{1,0:T(8,128)(2,1)S(1)}, u32[]{:S(2)}, u32[]{:S(2)}) collective-permute-start(bf16[64,3072]{1,0:T(8,128)(2,1)S(1)} %collective-permute-done.6.refs_5_), channel_id=1, source_target_pairs={{0,1},{1,0},{2,3},{3,2},{4,5},{5,4},{6,7},{7,6},{8,9},{9,8},{10,11... | collective-permute-start | bytes 1179656 | tf_op jit(solution)/shard_map/ppermute | solution.py:351
  58.4 15.7 %collective-permute-start.23 = (bf16[64,3072]{1,0:T(8,128)(2,1)S(1)}, bf16[64,3072]{1,0:T(8,128)(2,1)S(1)}, u32[]{:S(2)}, u32[]{:S(2)}) collective-permute-start(bf16[64,3072]{1,0:T(8,128)(2,1)S(1)} %collective-permute-done.9.refs_6_), channel_id=1, source_target_pairs={{0,1},{1,0},{2,3},{3,2},{4,5},{5,4},{6,7},{7,6},{8,9},{9,8},{10,11... | collective-permute-start | bytes 1179656 | tf_op jit(solution)/shard_map/ppermute | solution.py:351
  62.7 7.8 %collective-permute-start.22 = (bf16[64,3072]{1,0:T(8,128)(2,1)S(1)}, bf16[64,3072]{1,0:T(8,128)(2,1)S(1)}, u32[]{:S(2)}, u32[]{:S(2)}) collective-permute-start(bf16[64,3072]{1,0:T(8,128)(2,1)S(1)} %add_convert_fusion.2), channel_id=1, source_target_pairs={{0,4},{1,3},{4,8},{5,1},{8,12},{9,5},{12,14},{13,9},{14,10},{15,13... | collective-permute-start | bytes 1179656 | tf_op jit(solution)/shard_map/ppermute | solution.py:348
  70.5 7.8 %collective-permute-start.21 = (bf16[64,3072]{1,0:T(8,128)(2,1)S(1)}, bf16[64,3072]{1,0:T(8,128)(2,1)S(1)}, u32[]{:S(2)}, u32[]{:S(2)}) collective-permute-start(bf16[64,3072]{1,0:T(8,128)(2,1)S(1)} %add_convert_fusion.3), channel_id=1, source_target_pairs={{0,4},{1,3},{4,8},{5,1},{8,12},{9,5},{12,14},{13,9},{14,10},{15,13... | collective-permute-start | bytes 1179656 | tf_op jit(solution)/shard_map/ppermute | solution.py:348
  78.5 7.8 %collective-permute-start.28 = (bf16[64,3072]{1,0:T(8,128)(2,1)S(1)}, bf16[64,3072]{1,0:T(8,128)(2,1)S(1)}, u32[]{:S(2)}, u32[]{:S(2)}) collective-permute-start(bf16[64,3072]{1,0:T(8,128)(2,1)S(1)} %add_convert_fusion), channel_id=1, source_target_pairs={{0,4},{1,3},{4,8},{5,1},{8,12},{9,5},{12,14},{13,9},{14,10},{15,13... | collective-permute-start | bytes 1179656 | tf_op jit(solution)/shard_map/ppermute | solution.py:348
  80.4 10.1 %collective-permute-start.27 = (bf16[64,3072]{1,0:T(8,128)(2,1)S(1)}, bf16[64,3072]{1,0:T(8,128)(2,1)S(1)}, u32[]{:S(2)}, u32[]{:S(2)}) collective-permute-start(bf16[64,3072]{1,0:T(8,128)(2,1)S(1)} %add_convert_fusion.1), channel_id=1, source_target_pairs={{0,4},{1,3},{4,8},{5,1},{8,12},{9,5},{12,14},{13,9},{14,10},{15,13... | collective-permute-start | bytes 1179656 | tf_op jit(solution)/shard_map/ppermute | solution.py:348
  86.4 8.3 %collective-permute-start.29 = (bf16[32,3072]{1,0:T(8,128)(2,1)S(1)}, bf16[32,3072]{1,0:T(8,128)(2,1)S(1)}, u32[]{:S(2)}, u32[]{:S(2)}) collective-permute-start(bf16[32,3072]{1,0:T(8,128)(2,1)S(1)} %get-tuple-element.180), channel_id=1, source_target_pairs={{0,1},{1,0},{2,3},{3,2},{4,5},{5,4},{6,7},{7,6},{8,9},{9,8},{10,11... | collective-permute-start | bytes 589832 | tf_op jit(solution)/shard_map/ppermute | solution.py:351
  90.6 4.1 %collective-permute-start.30 = (bf16[32,3072]{1,0:T(8,128)(2,1)S(1)}, bf16[32,3072]{1,0:T(8,128)(2,1)S(1)}, u32[]{:S(2)}, u32[]{:S(2)}) collective-permute-start(bf16[32,3072]{1,0:T(8,128)(2,1)S(1)} %get-tuple-element.182), channel_id=1, source_target_pairs={{0,1},{1,0},{2,3},{3,2},{4,5},{5,4},{6,7},{7,6},{8,9},{9,8},{10,11... | collective-permute-start | bytes 589832 | tf_op jit(solution)/shard_map/ppermute | solution.py:351

commit v5 on v4

--- a/solution.py
+++ b/solution.py
@@ -140,6 +140,25 @@
         ref[pl.ds(pl.multiple_of((1 - core) * rows, rows), rows), :] = twin_ref[:, columns]
 
 
+def fetch_kernel(own_hbm, own_ref, sem):
+    copy = pltpu.make_async_copy(own_hbm, own_ref, sem)
+    copy.start()
+    copy.wait()
+
+
+def fetch(own):
+    return pl.pallas_call(
+        fetch_kernel,
+        out_shape=jax.ShapeDtypeStruct(own.shape, own.dtype),
+        in_specs=[OUTSIDE],
+        out_specs=WHOLE,
+        scratch_shapes=[pltpu.SemaphoreType.DMA],
+        compiler_params=pltpu.CompilerParams(vmem_limit_bytes=VMEM_LIMIT),
+        cost_estimate=cost(1),
+        name="fetch",
+    )(own)
+
+
 def prepare(me, own, twin):
     rows, width = own.shape
     out = jax.ShapeDtypeStruct((2 * rows, width // 2), own.dtype)
@@ -171,9 +190,10 @@
             sems.at[PIECE_STEPS, 0],
         )
         fetch.start()
-    step = wide // PIECE_STEPS
+    steps = PIECE_STEPS if other else 2
+    step = wide // steps
     stores = []
-    for i in range(PIECE_STEPS):
+    for i in range(steps):
         here = pl.ds(i * step, step)
         part = jnp.dot(w_ref[here, :], dht_ref[...], preferred_element_type=jnp.float32)
         part_ref[:, here] = part.astype(jnp.bfloat16).T
@@ -220,10 +240,19 @@
     return result[:4], (result[4] if more else None)
 
 
-def weight_kernel(me_ref, dh_ref, *refs, other, piece, wide, step):
-    blocks = refs[:RING]
-    stage, sems = refs[-2:]
-    out_hbm = refs[-3]
+def weight_kernel(me_ref, dh_ref, *refs, other, piece, wide, step, terms):
+    blocks, refs = refs[:RING], refs[RING:]
+    if piece or other:
+        before_ref, refs = refs[0], refs[2:]
+    if terms:
+        into = refs[len(terms)]
+        total = None
+        for ref, k in zip(refs, terms):
+            rows = pl.ds(k * into.shape[0], into.shape[0])
+            term = ref[rows, :].astype(jnp.float32)
+            total = term if total is None else total + term
+        into[...] = total.astype(into.dtype)
+    out_hbm, stage, sems = refs[-3:]
     half = blocks[0].shape[1]
     columns = out_hbm.shape[1]
     copies = []
@@ -234,7 +263,7 @@
             here = pl.ds(i * step, step)
             copies.append(
                 pltpu.make_async_copy(
-                    refs[RING].at[:, here], out_hbm.at[pl.ds(row, wide), here], sems.at[0, i]
+                    before_ref.at[:, here], out_hbm.at[pl.ds(row, wide), here], sems.at[0, i]
                 )
             )
             copies[-1].start()
@@ -256,25 +285,33 @@
         copy.wait()
 
 
-def weight_piece(me, dh, blocks, before, other, piece):
+def weight_piece(me, dh, blocks, before, other, piece, terms=()):
     tokens, ff = dh.shape
-    half = blocks[0].shape[1]
+    rows, half = blocks[0].shape
     wide = half // PIECES
     step = 512 if ff % 512 == 0 else 128
-    return pl.pallas_call(
-        lambda *refs: weight_kernel(*refs, other=other, piece=piece, wide=wide, step=step),
-        out_shape=(
+    sums = (jax.ShapeDtypeStruct((rows, half), jnp.bfloat16),) if terms else ()
+    result = pl.pallas_call(
+        lambda *refs: weight_kernel(
+            *refs, other=other, piece=piece, wide=wide, step=step, terms=[k for _, k in terms]
+        ),
+        out_shape=sums
+        + (
             jax.ShapeDtypeStruct((2 * half, ff), jnp.bfloat16),
             jax.ShapeDtypeStruct((wide, ff), jnp.bfloat16),
         ),
-        in_specs=[SCALAR, WHOLE] + [WHOLE] * RING + ([WHOLE, OUTSIDE] if before else []),
-        out_specs=(OUTSIDE, WHOLE),
-        input_output_aliases={3 + RING: 0} if before else {},
+        in_specs=[SCALAR, WHOLE]
+        + [WHOLE] * RING
+        + ([WHOLE, OUTSIDE] if before else [])
+        + [WHOLE] * len(terms),
+        out_specs=(WHOLE,) * len(sums) + (OUTSIDE, WHOLE),
+        input_output_aliases={3 + RING: len(sums)} if before else {},
         scratch_shapes=[pltpu.SemaphoreType.DMA((2, ff // step))],
         compiler_params=pltpu.CompilerParams(vmem_limit_bytes=VMEM_LIMIT),
         cost_estimate=cost(1),
         name="weight_piece",
-    )(me, dh, *blocks, *before)
+    )(me, dh, *blocks, *before, *[x for x, _ in terms])
+    return result[-2:], (result[0] if terms else None)
 
 
 def halves_kernel(me_ref, own_ref, came_ref, kept_ref, sent_ref):
@@ -350,8 +387,9 @@
     def swap(x):
         return lax.ppermute(x, "gx", swaps)
 
-    out_grad, pre_act, weight = (
-        pltpu.with_memory_space_constraint(x, pltpu.HBM) for x in (out_grad, pre_act, weight)
+    out_grad, pre_act, own, weight = (
+        pltpu.with_memory_space_constraint(x, pltpu.HBM)
+        for x in (out_grad, pre_act, layer_input, weight)
     )
     me = lax.axis_index("gx").astype(jnp.int32).reshape(1)
     both = 2 * rows
@@ -363,71 +401,65 @@
         return [swap(block(x, k)) for k in (1, 2, 3)]
 
     twin = swap(layer_input)
-    dh, dht, w = hidden(me, out_grad, pre_act, weight)
-    m0, o0 = prepare(me, layer_input, after(twin, dh))
+    m0, o0 = prepare(me, fetch(own), twin)
 
     def product(other, piece, w, before, *ties):
         return input_piece(me, after(dht, *ties), w, weight, before, other, piece)
 
     m1 = ring(m0)
-    go, w = product(True, 0, w, (), m0)
-    o1 = ring(after(o0, go[0]))
-    go, w = product(True, 1, w, go)
-    m1 = after(m1, go[0])
+    o1 = ring(o0)
+    dh, dht, w = hidden(after(me, o0), out_grad, pre_act, weight)
+    m1 = after(m1, dh)
     m2, sm1 = ring(m1), swap(m1)
-    go, w = product(True, 2, w, go, m1)
+    go, w = product(True, 0, w, (), m1)
     o1 = after(o1, go[0])
     o2, so1 = ring(o1), swap(o1)
-    go, w = product(True, 3, w, go, o1)
+    go, w = product(True, 1, w, go, o1)
     m2 = after(m2, go[0])
     m3, sm2 = ring(m2), swap(m2)
-    gm, w = product(False, 0, w, (), m2)
-    o2 = after(o2, gm[0])
+    go, w = product(True, 2, w, go, m2)
+    o2 = after(o2, go[0])
     o3, so2 = ring(o2), swap(o2)
+    go, w = product(True, 3, w, go, o2)
+    m3 = after(m3, go[0])
+    m4, sm3 = ring(m3), swap(m3)
+    gm, w = product(False, 0, w, (), m3, so1)
     own_o, behind_o, opposite_o, ahead_o = go
-    gm, w = product(False, 1, w, gm, o2, so1)
-    m3 = after(m3, gm[0])
-    m4, sm3 = ring(m3), swap(m3)
     from_m, opposite_from = swap_blocks(behind_o), swap(opposite_o)
-    gm, w = product(False, 2, w, gm, m3, so2)
-    o3, m4 = after(o3, gm[0]), after(m4, gm[0])
-    so3, sm4 = swap(o3), swap(m4)
-    gm, _ = product(False, 3, w, gm, o3, m4, *from_m, opposite_from)
+    gm, w = product(False, 1, w, gm, so2)
+    o3 = after(o3, gm[0])
+    so3 = swap(o3)
+    gm, w = product(False, 2, w, gm, o3)
+    m4 = after(m4, gm[0])
+    sm4 = swap(m4)
+    gm, _ = product(False, 3, w, gm, m4, *from_m, opposite_from)
     own_m, behind_m, opposite_m, ahead_m = gm
     r4m = ring(total(opposite_m, opposite_from))
     from_o = swap_blocks(behind_m)
     mine = (m0, m1, m2, m3, m4, so1, so2, so3)
     others = (o0, o1, o2, o3, sm4, sm1, sm2, sm3)
 
-    def gradient(other, piece, before, *ties):
+    def gradient(other, piece, before, *terms):
         blocks = others if other else mine
         before = before[::-1]
-        return weight_piece(me, after(dh, *ties), blocks, before, other, piece)
-
-    def send(ahead, came, k, *ring_terms):
-        return ring(total(block(ahead, k), came[k - 1], *ring_terms))
-
-    r3o = send(ahead_o, from_o, 3)
-    gw = gradient(False, 0, (), *from_o)
-    r4m = after(r4m, gw[1])
-    r3m = send(ahead_m, from_m, 3, r4m)
-    gw = gradient(False, 1, gw, r4m)
-    r3o = after(r3o, gw[1])
-    r2o = send(ahead_o, from_o, 2, r3o)
-    gw = gradient(False, 2, gw, r3o)
-    r3m = after(r3m, gw[1])
-    r2m = send(ahead_m, from_m, 2, r3m)
-    gw = gradient(False, 3, gw, r3m)
-    r2o = after(r2o, gw[1])
-    r1o = send(ahead_o, from_o, 1, r2o)
-    gw = gradient(True, 0, gw, r2o)
-    r2m = after(r2m, gw[1])
-    r1m = send(ahead_m, from_m, 1, r2m)
-    gw = gradient(True, 1, gw, r2m)
-    gw = gradient(True, 2, gw)
+        return weight_piece(me, dh, blocks, before, other, piece, terms)
+
+    gw, sent = gradient(False, 0, (), (ahead_o, 2), (from_o[2], 0))
+    r3o = ring(sent)
+    gw, sent = gradient(False, 1, gw, (ahead_m, 2), (from_m[2], 0), (r4m, 0))
+    r3m = ring(sent)
+    gw, sent = gradient(False, 2, gw, (ahead_o, 1), (from_o[1], 0), (r3o, 0))
+    r2o = ring(sent)
+    gw, sent = gradient(False, 3, gw, (ahead_m, 1), (from_m[1], 0), (r3m, 0))
+    r2m = ring(sent)
+    gw, sent = gradient(True, 0, gw, (ahead_o, 0), (from_o[0], 0), (r2o, 0))
+    r1o = ring(sent)
+    gw, sent = gradient(True, 1, gw, (ahead_m, 0), (from_m[0], 0), (r2m, 0))
+    r1m = ring(sent)
+    gw, _ = gradient(True, 2, gw)
     kept_o, sent_o = halves(me, own_o, after(r1o, gw[1]))
     came_m = swap(sent_o)
-    gw = gradient(True, 3, gw, sent_o)
+    gw, _ = gradient(True, 3, gw)
     kept_m, sent_m = halves(me, own_m, after(r1m, gw[1]))
     came_o = swap(sent_m)
     return (last(me, kept_m, came_m, kept_o, came_o), gw[0])

time: 95.7 us -> 87.7 us (0.916)
  waiting for transfers between devices: 25.5 us -> 12.2 us
  Pallas kernels: 38.6 us -> 43.1 us
  starting transfers between devices: 29.4 us -> 31 us
    ppermute x14, waiting for transfers between devices: 25.3 us -> 11.6 us  [ring(): return lax.ppermute(x, 'gx', pairs)]
    pallas_call x8, Pallas kernels: 16.1 us -> 20.4 us  [weight_piece(): pl.pallas_call(lambda *refs: weight_kernel(*refs, other=other, piece=piec...]
    ppermute x14, starting transfers between devices: 26.1 us -> 27.7 us  [ring(): return lax.ppermute(x, 'gx', pairs)]
    pallas_call x0 -> x1, Pallas kernels: none -> 1 us  [fetch(): pl.pallas_call(fetch_kernel, out_shape=jax.ShapeDtypeStruct(own.shape, ow...]
  transfers between devices with their start and end apart: 31 -> 31, of which waited for: 12 -> 8; matrix products, arithmetic and copies ran while one was open for 1% -> 0% of each run, Pallas kernels for 40% -> 48%
where the time goes in v5:
time: 87.7 us; the launch traced here: 87.5 us
  Pallas kernels  43.1 us (49%)
  starting transfers between devices  31 us (35%)
  waiting for transfers between devices  12.2 us (14%)
  between operations  0.94 us (1%)
    ppermute x14, starting transfers between devices, ring(): return lax.ppermute(x, 'gx', pairs)  27.7 us
    pallas_call x8, Pallas kernels, weight_piece(): pl.pallas_call(lambda *refs: weight_kernel(*refs, other=other, piece=piec...  20.4 us
    pallas_call x8, Pallas kernels, input_piece(): pl.pallas_call(lambda *refs: input_kernel(*refs, other=other, piece=piece...  16.8 us
    ppermute x14, waiting for transfers between devices, ring(): return lax.ppermute(x, 'gx', pairs)  11.6 us
    pallas_call x1, Pallas kernels, hidden(): pl.pallas_call(hidden_kernel, out_shape=(jax.ShapeDtypeStruct(shape, dtyp...  3.8 us
    ppermute x17, starting transfers between devices, swap(): return lax.ppermute(x, 'gx', swaps)  3.38 us
  transfers between devices with their start and end apart: 31, of which 8 were waited for; matrix products, arithmetic and copies ran while one was open for 0% of the time, Pallas kernels for 48%

profile of v5, /device:TPU:0, one launch (start us, length us, event | category | flops | bytes accessed | tf_op | source)
XLA Modules:
  0.0 87.5 jit_solution(7983105423254758297)
XLA Ops:
  0.6 0.5 collective-permute-start
  1.1 1.0 %fetch.1.own_ref = bf16[32,6144]{1,0:T(8,128)(2,1)S(1)} custom-call(bf16[32,6144]{1,0:T(8,128)(2,1)} %own_hbm.1), custom_call_target="tpu_custom_call" | custom-call | flops 1150000000 | tf_op jit(solution)/shard_map/fetch/pallas_call | solution.py:150
  2.2 0.5 collective-permute-done.twin_ref
  2.7 0.1 prepare.1
  2.8 3.0 %collective-permute-start.1 = (bf16[64,3072]{1,0:T(8,128)(2,1)S(1)}, bf16[64,3072]{1,0:T(8,128)(2,1)S(1)}, u32[]{:S(2)}, u32[]{:S(2)}) collective-permute-start(bf16[64,3072]{1,0:T(8,128)(2,1)S(1)} %get-tuple-element.91.refs_2_), channel_id=1, source_target_pairs={{0,4},{1,3},{4,8},{5,1},{8,12},{9,5},{12,14},{13,9},{14,10},{15,13... | collective-permute-start | bytes 1179656 | tf_op jit(solution)/shard_map/ppermute | solution.py:385
  5.8 1.6 %collective-permute-start.3 = (bf16[64,3072]{1,0:T(8,128)(2,1)S(1)}, bf16[64,3072]{1,0:T(8,128)(2,1)S(1)}, u32[]{:S(2)}, u32[]{:S(2)}) collective-permute-start(bf16[64,3072]{1,0:T(8,128)(2,1)S(1)} %get-tuple-element.88.refs_2_), channel_id=1, source_target_pairs={{0,4},{1,3},{4,8},{5,1},{8,12},{9,5},{12,14},{13,9},{14,10},{15,13... | collective-permute-start | bytes 1179656 | tf_op jit(solution)/shard_map/ppermute | solution.py:385
  7.3 3.8 %hidden.1 = (bf16[512,1536]{1,0:T(8,128)(2,1)S(1)}, bf16[1536,512]{1,0:T(8,128)(2,1)S(1)}, bf16[768,1536]{1,0:T(8,128)(2,1)S(1)}) custom-call(s32[1]{0:T(128)} %bitcast.me_ref.refs_0_, bf16[512,1536]{1,0:T(8,128)(2,1)} %og_hbm.1, bf16[512,1536]{1,0:T(8,128)(2,1)} %pre_hbm.1, bf16[6144,1536]{1,0:T(8,128)(2,1)} %refs_3_.15), custom_call_target="tpu_custom_call" | custom-call | flops 1150000000 | tf_op jit(solution)/shard_map/hidden/pallas_call | solution.py:114
  11.1 0.3 collective-permute-done.1.refs_3_
  11.5 2.1 %collective-permute-start.2 = (bf16[64,3072]{1,0:T(8,128)(2,1)S(1)}, bf16[64,3072]{1,0:T(8,128)(2,1)S(1)}, u32[]{:S(2)}, u32[]{:S(2)}) collective-permute-start(bf16[64,3072]{1,0:T(8,128)(2,1)S(1)} %collective-permute-done.1.refs_3_), channel_id=1, source_target_pairs={{0,4},{1,3},{4,8},{5,1},{8,12},{9,5},{12,14},{13,9},{14,10},{15,13... | collective-permute-start | bytes 1179656 | tf_op jit(solution)/shard_map/ppermute | solution.py:385
  13.5 2.2 %input_piece.8 = (bf16[64,3072]{1,0:T(8,128)(2,1)S(1)}, bf16[192,3072]{1,0:T(8,128)(2,1)S(1)}, bf16[64,3072]{1,0:T(8,128)(2,1)S(1)}, bf16[192,3072]{1,0:T(8,128)(2,1)S(1)}, bf16[768,1536]{1,0:T(8,128)(2,1)S(1)}) custom-call(s32[1]{0:T(128)} %bitcast.me_ref.refs_0_, bf16[1536,512]{1,0:T(8,128)(2,1)S(1)} %get-tuple-element.138.refs_1_, ...), custom_call_target="tpu_custom_call" | custom-call | flops 1150000000 | tf_op jit(solution)/shard_map/input_piece/pallas_call | solution.py:226
  15.8 0.0 collective-permute-done.3.refs_3_
  15.8 2.0 %collective-permute-start.5 = (bf16[64,3072]{1,0:T(8,128)(2,1)S(1)}, bf16[64,3072]{1,0:T(8,128)(2,1)S(1)}, u32[]{:S(2)}, u32[]{:S(2)}) collective-permute-start(bf16[64,3072]{1,0:T(8,128)(2,1)S(1)} %collective-permute-done.3.refs_3_), channel_id=1, source_target_pairs={{0,4},{1,3},{4,8},{5,1},{8,12},{9,5},{12,14},{13,9},{14,10},{15,13... | collective-permute-start | bytes 1179656 | tf_op jit(solution)/shard_map/ppermute | solution.py:385
  17.8 0.0 collective-permute-start.9
  17.8 2.2 %input_piece.9 = (bf16[64,3072]{1,0:T(8,128)(2,1)S(1)}, bf16[192,3072]{1,0:T(8,128)(2,1)S(1)}, bf16[64,3072]{1,0:T(8,128)(2,1)S(1)}, bf16[192,3072]{1,0:T(8,128)(2,1)S(1)}, bf16[768,1536]{1,0:T(8,128)(2,1)S(1)}) custom-call(s32[1]{0:T(128)} %bitcast.me_ref.refs_0_, ...), custom_call_target="tpu_custom_call", output_to_operand_aliasing={{0}: (4, {}), {1}: (5, {}), {2}: (6, {}), {3}: (7, {})} | custom-call | flops 1150000000 | tf_op jit(solution)/shard_map/input_piece/pallas_call | solution.py:226
  20.0 0.0 collective-permute-done.2.refs_4_
  20.0 2.0 %collective-permute-start.4 = (bf16[64,3072]{1,0:T(8,128)(2,1)S(1)}, bf16[64,3072]{1,0:T(8,128)(2,1)S(1)}, u32[]{:S(2)}, u32[]{:S(2)}) collective-permute-start(bf16[64,3072]{1,0:T(8,128)(2,1)S(1)} %collective-permute-done.2.refs_4_), channel_id=1, source_target_pairs={{0,4},{1,3},{4,8},{5,1},{8,12},{9,5},{12,14},{13,9},{14,10},{15,13... | collective-permute-start | bytes 1179656 | tf_op jit(solution)/shard_map/ppermute | solution.py:385
  22.0 2.2 %input_piece.10 = (bf16[64,3072]{1,0:T(8,128)(2,1)S(1)}, bf16[192,3072]{1,0:T(8,128)(2,1)S(1)}, bf16[64,3072]{1,0:T(8,128)(2,1)S(1)}, bf16[192,3072]{1,0:T(8,128)(2,1)S(1)}, bf16[768,1536]{1,0:T(8,128)(2,1)S(1)}) custom-call(s32[1]{0:T(128)} %bitcast.me_ref.refs_0_, ...), custom_call_target="tpu_custom_call", output_to_operand_aliasing={{0}: (4, {}), {1}: (5, {}), {2}: (6, {}), {3}: (7, {})} | custom-call | flops 1150000000 | tf_op jit(solution)/shard_map/input_piece/pallas_call | solution.py:226
  24.2 0.0 collective-permute-done.5.refs_4_
  24.2 0.1 collective-permute-start.8
  24.3 1.9 %collective-permute-start.7 = (bf16[64,3072]{1,0:T(8,128)(2,1)S(1)}, bf16[64,3072]{1,0:T(8,128)(2,1)S(1)}, u32[]{:S(2)}, u32[]{:S(2)}) collective-permute-start(bf16[64,3072]{1,0:T(8,128)(2,1)S(1)} %collective-permute-done.5.refs_4_), channel_id=1, source_target_pairs={{0,4},{1,3},{4,8},{5,1},{8,12},{9,5},{12,14},{13,9},{14,10},{15,13... | collective-permute-start | bytes 1179656 | tf_op jit(solution)/shard_map/ppermute | solution.py:385
  26.2 2.2 %input_piece.11 = (bf16[64,3072]{1,0:T(8,128)(2,1)S(1)}, bf16[192,3072]{1,0:T(8,128)(2,1)S(1)}, bf16[64,3072]{1,0:T(8,128)(2,1)S(1)}, bf16[192,3072]{1,0:T(8,128)(2,1)S(1)}, bf16[768,1536]{1,0:T(8,128)(2,1)S(1)}) custom-call(s32[1]{0:T(128)} %bitcast.me_ref.refs_0_, ...), custom_call_target="tpu_custom_call", output_to_operand_aliasing={{0}: (4, {}), {1}: (5, {}), {2}: (6, {}), {3}: (7, {})} | custom-call | flops 1150000000 | tf_op jit(solution)/shard_map/input_piece/pallas_call | solution.py:226
  28.4 0.1 fusion.1
  28.5 0.2 collective-permute-start.10
  28.7 0.0 collective-permute-done.4.refs_5_
  28.7 1.7 %collective-permute-start.6 = (bf16[64,3072]{1,0:T(8,128)(2,1)S(1)}, bf16[64,3072]{1,0:T(8,128)(2,1)S(1)}, u32[]{:S(2)}, u32[]{:S(2)}) collective-permute-start(bf16[64,3072]{1,0:T(8,128)(2,1)S(1)} %collective-permute-done.4.refs_5_), channel_id=1, source_target_pairs={{0,4},{1,3},{4,8},{5,1},{8,12},{9,5},{12,14},{13,9},{14,10},{15,13... | collective-permute-start | bytes 1179656 | tf_op jit(solution)/shard_map/ppermute | solution.py:385
  30.4 0.5 collective-permute-start.12
  30.9 1.6 %collective-permute-done.7.refs_5_ = bf16[64,3072]{1,0:T(8,128)(2,1)S(1)} collective-permute-done((bf16[64,3072]{1,0:T(8,128)(2,1)S(1)}, bf16[64,3072]{1,0:T(8,128)(2,1)S(1)}, u32[]{:S(2)}, u32[]{:S(2)}) %collective-permute-start.7) | collective-permute-done | bytes 393248 | tf_op jit(solution)/shard_map/ppermute | solution.py:385
  32.5 2.0 %input_piece.12 = (bf16[64,3072]{1,0:T(8,128)(2,1)S(1)}, bf16[192,3072]{1,0:T(8,128)(2,1)S(1)}, bf16[64,3072]{1,0:T(8,128)(2,1)S(1)}, bf16[192,3072]{1,0:T(8,128)(2,1)S(1)}, bf16[768,1536]{1,0:T(8,128)(2,1)S(1)}) custom-call(s32[1]{0:T(128)} %bitcast.me_ref.refs_0_, bf16[1536,512]{1,0:T(8,128)(2,1)S(1)} %get-tuple-element.138.refs_1_, ...), custom_call_target="tpu_custom_call" | custom-call | flops 1150000000 | tf_op jit(solution)/shard_map/input_piece/pallas_call | solution.py:226
  34.5 2.0 %input_piece.13 = (bf16[64,3072]{1,0:T(8,128)(2,1)S(1)}, bf16[192,3072]{1,0:T(8,128)(2,1)S(1)}, bf16[64,3072]{1,0:T(8,128)(2,1)S(1)}, bf16[192,3072]{1,0:T(8,128)(2,1)S(1)}, bf16[768,1536]{1,0:T(8,128)(2,1)S(1)}) custom-call(s32[1]{0:T(128)} %bitcast.me_ref.refs_0_, ...), custom_call_target="tpu_custom_call", output_to_operand_aliasing={{0}: (4, {}), {1}: (5, {}), {2}: (6, {}), {3}: (7, {})} | custom-call | flops 1150000000 | tf_op jit(solution)/shard_map/input_piece/pallas_call | solution.py:226
  36.5 2.0 %input_piece.14 = (bf16[64,3072]{1,0:T(8,128)(2,1)S(1)}, bf16[192,3072]{1,0:T(8,128)(2,1)S(1)}, bf16[64,3072]{1,0:T(8,128)(2,1)S(1)}, bf16[192,3072]{1,0:T(8,128)(2,1)S(1)}, bf16[768,1536]{1,0:T(8,128)(2,1)S(1)}) custom-call(s32[1]{0:T(128)} %bitcast.me_ref.refs_0_, ...), custom_call_target="tpu_custom_call", output_to_operand_aliasing={{0}: (4, {}), {1}: (5, {}), {2}: (6, {}), {3}: (7, {})} | custom-call | flops 1150000000 | tf_op jit(solution)/shard_map/input_piece/pallas_call | solution.py:226
  38.5 0.6 collective-permute-start.18
  39.1 2.0 %input_piece.15 = (bf16[64,3072]{1,0:T(8,128)(2,1)S(1)}, bf16[192,3072]{1,0:T(8,128)(2,1)S(1)}, bf16[64,3072]{1,0:T(8,128)(2,1)S(1)}, bf16[192,3072]{1,0:T(8,128)(2,1)S(1)}) custom-call(s32[1]{0:T(128)} %bitcast.me_ref.refs_0_, ...), custom_call_target="tpu_custom_call", output_to_operand_aliasing={{0}: (4, {}), {1}: (5, {}), {2}: (6, {}), {3}: (7, {})} | custom-call | flops 1150000000 | tf_op jit(solution)/shard_map/input_piece/pallas_call | solution.py:226
  41.1 0.1 fusion
  41.2 0.1 collective-permute-start.19
  41.3 0.1 add_convert_fusion
  41.4 2.1 %collective-permute-start.20 = (bf16[64,3072]{1,0:T(8,128)(2,1)S(1)}, bf16[64,3072]{1,0:T(8,128)(2,1)S(1)}, u32[]{:S(2)}, u32[]{:S(2)}) collective-permute-start(bf16[64,3072]{1,0:T(8,128)(2,1)S(1)} %add_convert_fusion), channel_id=1, source_target_pairs={{0,4},{1,3},{4,8},{5,1},{8,12},{9,5},{12,14},{13,9},{14,10},{15,13... | collective-permute-start | bytes 1179656 | tf_op jit(solution)/shard_map/ppermute | solution.py:385
  43.5 0.1 collective-permute-start.21
  43.7 1.6 %weight_piece.8 = (bf16[64,3072]{1,0:T(8,128)(2,1)S(1)}, bf16[6144,1536]{1,0:T(8,128)(2,1)}, bf16[768,1536]{1,0:T(8,128)(2,1)S(1)}) custom-call(s32[1]{0:T(128)} %bitcast.me_ref.refs_0_, bf16[512,1536]{1,0:T(8,128)(2,1)S(1)} %get-tuple-element.92.refs_1_, bf16[64,3072]{1,0:T(8,128)(2,1)S(1)} %get-tuple-element.91.refs_2_, ...), custom_call_target="tpu_custom_call" | custom-call | flops 1150000000 | tf_op jit(solution)/shard_map/weight_piece/pallas_call | solution.py:294
  45.3 1.5 %collective-permute-start.22 = (bf16[64,3072]{1,0:T(8,128)(2,1)S(1)}, bf16[64,3072]{1,0:T(8,128)(2,1)S(1)}, u32[]{:S(2)}, u32[]{:S(2)}) collective-permute-start(bf16[64,3072]{1,0:T(8,128)(2,1)S(1)} %get-tuple-element.152), channel_id=1, source_target_pairs={{0,4},{1,3},{4,8},{5,1},{8,12},{9,5},{12,14},{13,9},{14,10},{15,13... | collective-permute-start | bytes 1179656 | tf_op jit(solution)/shard_map/ppermute | solution.py:385
  46.8 2.4 %collective-permute-done.20.refs_14_ = bf16[64,3072]{1,0:T(8,128)(2,1)S(1)} collective-permute-done((bf16[64,3072]{1,0:T(8,128)(2,1)S(1)}, bf16[64,3072]{1,0:T(8,128)(2,1)S(1)}, u32[]{:S(2)}, u32[]{:S(2)}) %collective-permute-start.20) | collective-permute-done | bytes 393248 | tf_op jit(solution)/shard_map/ppermute | solution.py:385
  49.2 1.8 %weight_piece.9 = (bf16[64,3072]{1,0:T(8,128)(2,1)S(1)}, bf16[6144,1536]{1,0:T(8,128)(2,1)}, bf16[768,1536]{1,0:T(8,128)(2,1)S(1)}) custom-call(s32[1]{0:T(128)} %bitcast.me_ref.refs_0_, bf16[512,1536]{1,0:T(8,128)(2,1)S(1)} %get-tuple-element.92.refs_1_, bf16[64,3072]{1,0:T(8,128)(2,1)S(1)} %get-tuple-element.91.refs_2_, ...), custom_call_target="tpu_custom_call", output_to_operand_aliasing={{1}: (11, {})} | custom-call | flops 1150000000 | tf_op jit(solution)/shard_map/weight_piece/pallas_call | solution.py:294
  51.0 2.1 %collective-permute-start.23 = (bf16[64,3072]{1,0:T(8,128)(2,1)S(1)}, bf16[64,3072]{1,0:T(8,128)(2,1)S(1)}, u32[]{:S(2)}, u32[]{:S(2)}) collective-permute-start(bf16[64,3072]{1,0:T(8,128)(2,1)S(1)} %get-tuple-element.155), channel_id=1, source_target_pairs={{0,4},{1,3},{4,8},{5,1},{8,12},{9,5},{12,14},{13,9},{14,10},{15,13... | collective-permute-start | bytes 1179656 | tf_op jit(solution)/shard_map/ppermute | solution.py:385
  53.1 0.5 collective-permute-start.17
  53.7 0.1 collective-permute-start.14
  53.7 2.8 %weight_piece.10 = (bf16[64,3072]{1,0:T(8,128)(2,1)S(1)}, bf16[6144,1536]{1,0:T(8,128)(2,1)}, bf16[768,1536]{1,0:T(8,128)(2,1)S(1)}) custom-call(s32[1]{0:T(128)} %bitcast.me_ref.refs_0_, bf16[512,1536]{1,0:T(8,128)(2,1)S(1)} %get-tuple-element.92.refs_1_, bf16[64,3072]{1,0:T(8,128)(2,1)S(1)} %get-tuple-element.91.refs_2_, ...), custom_call_target="tpu_custom_call", output_to_operand_aliasing={{1}: (11, {})} | custom-call | flops 1150000000 | tf_op jit(solution)/shard_map/weight_piece/pallas_call | solution.py:294
  56.6 0.5 collective-permute-start.24
  57.1 1.8 %collective-permute-done.23.refs_14_ = bf16[64,3072]{1,0:T(8,128)(2,1)S(1)} collective-permute-done((bf16[64,3072]{1,0:T(8,128)(2,1)S(1)}, bf16[64,3072]{1,0:T(8,128)(2,1)S(1)}, u32[]{:S(2)}, u32[]{:S(2)}) %collective-permute-start.23) | collective-permute-done | bytes 393248 | tf_op jit(solution)/shard_map/ppermute | solution.py:385
  58.8 2.1 %collective-permute-start.25 = (bf16[64,3072]{1,0:T(8,128)(2,1)S(1)}, bf16[64,3072]{1,0:T(8,128)(2,1)S(1)}, u32[]{:S(2)}, u32[]{:S(2)}) collective-permute-start(bf16[64,3072]{1,0:T(8,128)(2,1)S(1)} %get-tuple-element.158), channel_id=1, source_target_pairs={{0,4},{1,3},{4,8},{5,1},{8,12},{9,5},{12,14},{13,9},{14,10},{15,13... | collective-permute-start | bytes 1179656 | tf_op jit(solution)/shard_map/ppermute | solution.py:385
  60.9 2.8 %weight_piece.11 = (bf16[64,3072]{1,0:T(8,128)(2,1)S(1)}, bf16[6144,1536]{1,0:T(8,128)(2,1)}, bf16[768,1536]{1,0:T(8,128)(2,1)S(1)}) custom-call(s32[1]{0:T(128)} %bitcast.me_ref.refs_0_, bf16[512,1536]{1,0:T(8,128)(2,1)S(1)} %get-tuple-element.92.refs_1_, bf16[64,3072]{1,0:T(8,128)(2,1)S(1)} %get-tuple-element.91.refs_2_, ...), custom_call_target="tpu_custom_call", output_to_operand_aliasing={{1}: (11, {})} | custom-call | flops 1150000000 | tf_op jit(solution)/shard_map/weight_piece/pallas_call | solution.py:294
  63.8 1.8 %collective-permute-start.26 = (bf16[64,3072]{1,0:T(8,128)(2,1)S(1)}, bf16[64,3072]{1,0:T(8,128)(2,1)S(1)}, u32[]{:S(2)}, u32[]{:S(2)}) collective-permute-start(bf16[64,3072]{1,0:T(8,128)(2,1)S(1)} %get-tuple-element.161), channel_id=1, source_target_pairs={{0,4},{1,3},{4,8},{5,1},{8,12},{9,5},{12,14},{13,9},{14,10},{15,13... | collective-permute-start | bytes 1179656 | tf_op jit(solution)/shard_map/ppermute | solution.py:385
  65.6 1.0 %collective-permute-done.25.refs_14_ = bf16[64,3072]{1,0:T(8,128)(2,1)S(1)} collective-permute-done((bf16[64,3072]{1,0:T(8,128)(2,1)S(1)}, bf16[64,3072]{1,0:T(8,128)(2,1)S(1)}, u32[]{:S(2)}, u32[]{:S(2)}) %collective-permute-start.25) | collective-permute-done | bytes 393248 | tf_op jit(solution)/shard_map/ppermute | solution.py:385
  66.6 2.8 %weight_piece.12 = (bf16[64,3072]{1,0:T(8,128)(2,1)S(1)}, bf16[6144,1536]{1,0:T(8,128)(2,1)}, bf16[768,1536]{1,0:T(8,128)(2,1)S(1)}) custom-call(s32[1]{0:T(128)} %bitcast.me_ref.refs_0_, bf16[512,1536]{1,0:T(8,128)(2,1)S(1)} %get-tuple-element.92.refs_1_, bf16[64,3072]{1,0:T(8,128)(2,1)S(1)} %get-tuple-element.88.refs_2_, ...), custom_call_target="tpu_custom_call", output_to_operand_aliasing={{1}: (11, {})} | custom-call | flops 1150000000 | tf_op jit(solution)/shard_map/weight_piece/pallas_call | solution.py:294
  69.5 2.1 %collective-permute-start.28 = (bf16[64,3072]{1,0:T(8,128)(2,1)S(1)}, bf16[64,3072]{1,0:T(8,128)(2,1)S(1)}, u32[]{:S(2)}, u32[]{:S(2)}) collective-permute-start(bf16[64,3072]{1,0:T(8,128)(2,1)S(1)} %get-tuple-element.164), channel_id=1, source_target_pairs={{0,4},{1,3},{4,8},{5,1},{8,12},{9,5},{12,14},{13,9},{14,10},{15,13... | collective-permute-start | bytes 1179656 | tf_op jit(solution)/shard_map/ppermute | solution.py:385
  71.6 0.2 collective-permute-done.26.refs_14_
  71.8 2.8 %weight_piece.13 = (bf16[64,3072]{1,0:T(8,128)(2,1)S(1)}, bf16[6144,1536]{1,0:T(8,128)(2,1)}, bf16[768,1536]{1,0:T(8,128)(2,1)S(1)}) custom-call(s32[1]{0:T(128)} %bitcast.me_ref.refs_0_, bf16[512,1536]{1,0:T(8,128)(2,1)S(1)} %get-tuple-element.92.refs_1_, bf16[64,3072]{1,0:T(8,128)(2,1)S(1)} %get-tuple-element.88.refs_2_, ...), custom_call_target="tpu_custom_call", output_to_operand_aliasing={{1}: (11, {})} | custom-call | flops 1150000000 | tf_op jit(solution)/shard_map/weight_piece/pallas_call | solution.py:294
  74.7 1.6 %collective-permute-start.27 = (bf16[64,3072]{1,0:T(8,128)(2,1)S(1)}, bf16[64,3072]{1,0:T(8,128)(2,1)S(1)}, u32[]{:S(2)}, u32[]{:S(2)}) collective-permute-start(bf16[64,3072]{1,0:T(8,128)(2,1)S(1)} %get-tuple-element.162), channel_id=1, source_target_pairs={{0,4},{1,3},{4,8},{5,1},{8,12},{9,5},{12,14},{13,9},{14,10},{15,13... | collective-permute-start | bytes 1179656 | tf_op jit(solution)/shard_map/ppermute | solution.py:385
  76.3 1.8 %weight_piece.14 = (bf16[6144,1536]{1,0:T(8,128)(2,1)}, bf16[768,1536]{1,0:T(8,128)(2,1)S(1)}) custom-call(s32[1]{0:T(128)} %bitcast.me_ref.refs_0_, bf16[512,1536]{1,0:T(8,128)(2,1)S(1)} %get-tuple-element.92.refs_1_, bf16[64,3072]{1,0:T(8,128)(2,1)S(1)} %get-tuple-element.88.refs_2_, ...), custom_call_target="tpu_custom_call", output_to_operand_aliasing={{0}: (11, {})} | custom-call | flops 1150000000 | tf_op jit(solution)/shard_map/weight_piece/pallas_call | solution.py:294
  78.1 0.1 halves.3
  78.2 0.1 collective-permute-start.29
  78.2 4.2 %collective-permute-done.27.came_ref = bf16[64,3072]{1,0:T(8,128)(2,1)S(1)} collective-permute-done((bf16[64,3072]{1,0:T(8,128)(2,1)S(1)}, bf16[64,3072]{1,0:T(8,128)(2,1)S(1)}, u32[]{:S(2)}, u32[]{:S(2)}) %collective-permute-start.27) | collective-permute-done | bytes 393248 | tf_op jit(solution)/shard_map/ppermute | solution.py:385
  82.5 0.1 halves.2
  82.6 0.1 collective-permute-start.30
  82.7 4.0 %weight_piece.15 = (bf16[6144,1536]{1,0:T(8,128)(2,1)}, bf16[768,1536]{1,0:T(8,128)(2,1)}) custom-call(s32[1]{0:T(128)} %bitcast.me_ref.refs_0_, bf16[512,1536]{1,0:T(8,128)(2,1)S(1)} %get-tuple-element.92.refs_1_, bf16[64,3072]{1,0:T(8,128)(2,1)S(1)} %get-tuple-element.88.refs_2_, ...), custom_call_target="tpu_custom_call", output_to_operand_aliasing={{0}: (11, {})} | custom-call | flops 1150000000 | tf_op jit(solution)/shard_map/weight_piece/pallas_call | solution.py:294
  86.6 0.8 last.1
  (23 shorter events, 0.1 us)
Async XLA Ops:
  0.6 2.1 %collective-permute-start = (bf16[32,6144]{1,0:T(8,128)(2,1)}, bf16[32,6144]{1,0:T(8,128)(2,1)S(1)}, u32[]{:S(2)}, u32[]{:S(2)}) collective-permute-start(bf16[32,6144]{1,0:T(8,128)(2,1)} %own_hbm.1), channel_id=1, source_target_pairs={{0,1},{1,0},{2,3},{3,2},{4,5},{5,4},{6,7},{7,6},{8,9},{9,8},{10,11... | collective-permute-start | bytes 1179656 | tf_op jit(solution)/shard_map/ppermute | solution.py:388
  2.8 8.7 %collective-permute-start.1 = (bf16[64,3072]{1,0:T(8,128)(2,1)S(1)}, bf16[64,3072]{1,0:T(8,128)(2,1)S(1)}, u32[]{:S(2)}, u32[]{:S(2)}) collective-permute-start(bf16[64,3072]{1,0:T(8,128)(2,1)S(1)} %get-tuple-element.91.refs_2_), channel_id=1, source_target_pairs={{0,4},{1,3},{4,8},{5,1},{8,12},{9,5},{12,14},{13,9},{14,10},{15,13... | collective-permute-start | bytes 1179656 | tf_op jit(solution)/shard_map/ppermute | solution.py:385
  5.8 10.0 %collective-permute-start.3 = (bf16[64,3072]{1,0:T(8,128)(2,1)S(1)}, bf16[64,3072]{1,0:T(8,128)(2,1)S(1)}, u32[]{:S(2)}, u32[]{:S(2)}) collective-permute-start(bf16[64,3072]{1,0:T(8,128)(2,1)S(1)} %get-tuple-element.88.refs_2_), channel_id=1, source_target_pairs={{0,4},{1,3},{4,8},{5,1},{8,12},{9,5},{12,14},{13,9},{14,10},{15,13... | collective-permute-start | bytes 1179656 | tf_op jit(solution)/shard_map/ppermute | solution.py:385
  11.5 8.5 %collective-permute-start.2 = (bf16[64,3072]{1,0:T(8,128)(2,1)S(1)}, bf16[64,3072]{1,0:T(8,128)(2,1)S(1)}, u32[]{:S(2)}, u32[]{:S(2)}) collective-permute-start(bf16[64,3072]{1,0:T(8,128)(2,1)S(1)} %collective-permute-done.1.refs_3_), channel_id=1, source_target_pairs={{0,4},{1,3},{4,8},{5,1},{8,12},{9,5},{12,14},{13,9},{14,10},{15,13... | collective-permute-start | bytes 1179656 | tf_op jit(solution)/shard_map/ppermute | solution.py:385
  15.8 8.4 %collective-permute-start.5 = (bf16[64,3072]{1,0:T(8,128)(2,1)S(1)}, bf16[64,3072]{1,0:T(8,128)(2,1)S(1)}, u32[]{:S(2)}, u32[]{:S(2)}) collective-permute-start(bf16[64,3072]{1,0:T(8,128)(2,1)S(1)} %collective-permute-done.3.refs_3_), channel_id=1, source_target_pairs={{0,4},{1,3},{4,8},{5,1},{8,12},{9,5},{12,14},{13,9},{14,10},{15,13... | collective-permute-start | bytes 1179656 | tf_op jit(solution)/shard_map/ppermute | solution.py:385
  17.8 12.6 %collective-permute-start.9 = (bf16[64,3072]{1,0:T(8,128)(2,1)S(1)}, bf16[64,3072]{1,0:T(8,128)(2,1)S(1)}, u32[]{:S(2)}, u32[]{:S(2)}) collective-permute-start(bf16[64,3072]{1,0:T(8,128)(2,1)S(1)} %collective-permute-done.3.refs_3_), channel_id=1, source_target_pairs={{0,1},{1,0},{2,3},{3,2},{4,5},{5,4},{6,7},{7,6},{8,9},{9,8},{10,11... | collective-permute-start | bytes 1179656 | tf_op jit(solution)/shard_map/ppermute | solution.py:388
  20.0 8.7 %collective-permute-start.4 = (bf16[64,3072]{1,0:T(8,128)(2,1)S(1)}, bf16[64,3072]{1,0:T(8,128)(2,1)S(1)}, u32[]{:S(2)}, u32[]{:S(2)}) collective-permute-start(bf16[64,3072]{1,0:T(8,128)(2,1)S(1)} %collective-permute-done.2.refs_4_), channel_id=1, source_target_pairs={{0,4},{1,3},{4,8},{5,1},{8,12},{9,5},{12,14},{13,9},{14,10},{15,13... | collective-permute-start | bytes 1179656 | tf_op jit(solution)/shard_map/ppermute | solution.py:385
  24.2 6.2 %collective-permute-start.8 = (bf16[64,3072]{1,0:T(8,128)(2,1)S(1)}, bf16[64,3072]{1,0:T(8,128)(2,1)S(1)}, u32[]{:S(2)}, u32[]{:S(2)}) collective-permute-start(bf16[64,3072]{1,0:T(8,128)(2,1)S(1)} %collective-permute-done.5.refs_4_), channel_id=1, source_target_pairs={{0,1},{1,0},{2,3},{3,2},{4,5},{5,4},{6,7},{7,6},{8,9},{9,8},{10,11... | collective-permute-start | bytes 1179656 | tf_op jit(solution)/shard_map/ppermute | solution.py:388
  24.3 8.3 %collective-permute-start.7 = (bf16[64,3072]{1,0:T(8,128)(2,1)S(1)}, bf16[64,3072]{1,0:T(8,128)(2,1)S(1)}, u32[]{:S(2)}, u32[]{:S(2)}) collective-permute-start(bf16[64,3072]{1,0:T(8,128)(2,1)S(1)} %collective-permute-done.5.refs_4_), channel_id=1, source_target_pairs={{0,4},{1,3},{4,8},{5,1},{8,12},{9,5},{12,14},{13,9},{14,10},{15,13... | collective-permute-start | bytes 1179656 | tf_op jit(solution)/shard_map/ppermute | solution.py:385
  28.5 10.6 %collective-permute-start.10 = (bf16[64,3072]{1,0:T(8,128)(2,1)S(1)}, bf16[64,3072]{1,0:T(8,128)(2,1)S(1)}, u32[]{:S(2)}, u32[]{:S(2)}) collective-permute-start(bf16[64,3072]{1,0:T(8,128)(2,1)S(1)} %get-tuple-element.179), channel_id=1, source_target_pairs={{0,1},{1,0},{2,3},{3,2},{4,5},{5,4},{6,7},{7,6},{8,9},{9,8},{10,11... | collective-permute-start | bytes 1179656 | tf_op jit(solution)/shard_map/ppermute | solution.py:388
  28.7 9.8 %collective-permute-start.6 = (bf16[64,3072]{1,0:T(8,128)(2,1)S(1)}, bf16[64,3072]{1,0:T(8,128)(2,1)S(1)}, u32[]{:S(2)}, u32[]{:S(2)}) collective-permute-start(bf16[64,3072]{1,0:T(8,128)(2,1)S(1)} %collective-permute-done.4.refs_5_), channel_id=1, source_target_pairs={{0,4},{1,3},{4,8},{5,1},{8,12},{9,5},{12,14},{13,9},{14,10},{15,13... | collective-permute-start | bytes 1179656 | tf_op jit(solution)/shard_map/ppermute | solution.py:385
  30.4 8.7 %collective-permute-start.11 = (bf16[64,3072]{1,0:T(8,128)(2,1)S(1)}, bf16[64,3072]{1,0:T(8,128)(2,1)S(1)}, u32[]{:S(2)}, u32[]{:S(2)}) collective-permute-start(bf16[64,3072]{1,0:T(8,128)(2,1)S(1)} %get-tuple-element.178), channel_id=1, source_target_pairs={{0,1},{1,0},{2,3},{3,2},{4,5},{5,4},{6,7},{7,6},{8,9},{9,8},{10,11... | collective-permute-start | bytes 1179656 | tf_op jit(solution)/shard_map/ppermute | solution.py:388
  30.4 8.7 %collective-permute-start.12 = (bf16[64,3072]{1,0:T(8,128)(2,1)S(1)}, bf16[64,3072]{1,0:T(8,128)(2,1)S(1)}, u32[]{:S(2)}, u32[]{:S(2)}) collective-permute-start(bf16[64,3072]{1,0:T(8,128)(2,1)S(1)} %get-tuple-element.177), channel_id=1, source_target_pairs={{0,1},{1,0},{2,3},{3,2},{4,5},{5,4},{6,7},{7,6},{8,9},{9,8},{10,11... | collective-permute-start | bytes 1179656 | tf_op jit(solution)/shard_map/ppermute | solution.py:388
  32.5 6.6 %collective-permute-start.13 = (bf16[64,3072]{1,0:T(8,128)(2,1)S(1)}, bf16[64,3072]{1,0:T(8,128)(2,1)S(1)}, u32[]{:S(2)}, u32[]{:S(2)}) collective-permute-start(bf16[64,3072]{1,0:T(8,128)(2,1)S(1)} %get-tuple-element.137), channel_id=1, source_target_pairs={{0,1},{1,0},{2,3},{3,2},{4,5},{5,4},{6,7},{7,6},{8,9},{9,8},{10,11... | collective-permute-start | bytes 1179656 | tf_op jit(solution)/shard_map/ppermute | solution.py:388
  38.5 5.1 %collective-permute-start.18 = (bf16[64,3072]{1,0:T(8,128)(2,1)S(1)}, bf16[64,3072]{1,0:T(8,128)(2,1)S(1)}, u32[]{:S(2)}, u32[]{:S(2)}) collective-permute-start(bf16[64,3072]{1,0:T(8,128)(2,1)S(1)} %collective-permute-done.7.refs_5_), channel_id=1, source_target_pairs={{0,1},{1,0},{2,3},{3,2},{4,5},{5,4},{6,7},{7,6},{8,9},{9,8},{10,11... | collective-permute-start | bytes 1179656 | tf_op jit(solution)/shard_map/ppermute | solution.py:388
  41.2 2.5 %collective-permute-start.19 = (bf16[64,3072]{1,0:T(8,128)(2,1)S(1)}, bf16[64,3072]{1,0:T(8,128)(2,1)S(1)}, u32[]{:S(2)}, u32[]{:S(2)}) collective-permute-start(bf16[64,3072]{1,0:T(8,128)(2,1)S(1)} %get-tuple-element.176), channel_id=1, source_target_pairs={{0,1},{1,0},{2,3},{3,2},{4,5},{5,4},{6,7},{7,6},{8,9},{9,8},{10,11... | collective-permute-start | bytes 1179656 | tf_op jit(solution)/shard_map/ppermute | solution.py:388
  41.4 7.8 %collective-permute-start.20 = (bf16[64,3072]{1,0:T(8,128)(2,1)S(1)}, bf16[64,3072]{1,0:T(8,128)(2,1)S(1)}, u32[]{:S(2)}, u32[]{:S(2)}) collective-permute-start(bf16[64,3072]{1,0:T(8,128)(2,1)S(1)} %add_convert_fusion), channel_id=1, source_target_pairs={{0,4},{1,3},{4,8},{5,1},{8,12},{9,5},{12,14},{13,9},{14,10},{15,13... | collective-permute-start | bytes 1179656 | tf_op jit(solution)/shard_map/ppermute | solution.py:385
  43.5 9.6 %collective-permute-start.21 = (bf16[64,3072]{1,0:T(8,128)(2,1)S(1)}, bf16[64,3072]{1,0:T(8,128)(2,1)S(1)}, u32[]{:S(2)}, u32[]{:S(2)}) collective-permute-start(bf16[64,3072]{1,0:T(8,128)(2,1)S(1)} %get-tuple-element.175), channel_id=1, source_target_pairs={{0,1},{1,0},{2,3},{3,2},{4,5},{5,4},{6,7},{7,6},{8,9},{9,8},{10,11... | collective-permute-start | bytes 1179656 | tf_op jit(solution)/shard_map/ppermute | solution.py:388
  45.3 8.4 %collective-permute-start.22 = (bf16[64,3072]{1,0:T(8,128)(2,1)S(1)}, bf16[64,3072]{1,0:T(8,128)(2,1)S(1)}, u32[]{:S(2)}, u32[]{:S(2)}) collective-permute-start(bf16[64,3072]{1,0:T(8,128)(2,1)S(1)} %get-tuple-element.152), channel_id=1, source_target_pairs={{0,4},{1,3},{4,8},{5,1},{8,12},{9,5},{12,14},{13,9},{14,10},{15,13... | collective-permute-start | bytes 1179656 | tf_op jit(solution)/shard_map/ppermute | solution.py:385
  46.8 9.8 %collective-permute-start.15 = (bf16[64,3072]{1,0:T(8,128)(2,1)S(1)}, bf16[64,3072]{1,0:T(8,128)(2,1)S(1)}, u32[]{:S(2)}, u32[]{:S(2)}) collective-permute-start(bf16[64,3072]{1,0:T(8,128)(2,1)S(1)} %collective-permute-done.1.refs_3_), channel_id=1, source_target_pairs={{0,1},{1,0},{2,3},{3,2},{4,5},{5,4},{6,7},{7,6},{8,9},{9,8},{10,11... | collective-permute-start | bytes 1179656 | tf_op jit(solution)/shard_map/ppermute | solution.py:388
  51.0 7.8 %collective-permute-start.23 = (bf16[64,3072]{1,0:T(8,128)(2,1)S(1)}, bf16[64,3072]{1,0:T(8,128)(2,1)S(1)}, u32[]{:S(2)}, u32[]{:S(2)}) collective-permute-start(bf16[64,3072]{1,0:T(8,128)(2,1)S(1)} %get-tuple-element.155), channel_id=1, source_target_pairs={{0,4},{1,3},{4,8},{5,1},{8,12},{9,5},{12,14},{13,9},{14,10},{15,13... | collective-permute-start | bytes 1179656 | tf_op jit(solution)/shard_map/ppermute | solution.py:385
  53.1 10.6 %collective-permute-start.16 = (bf16[64,3072]{1,0:T(8,128)(2,1)S(1)}, bf16[64,3072]{1,0:T(8,128)(2,1)S(1)}, u32[]{:S(2)}, u32[]{:S(2)}) collective-permute-start(bf16[64,3072]{1,0:T(8,128)(2,1)S(1)} %collective-permute-done.2.refs_4_), channel_id=1, source_target_pairs={{0,1},{1,0},{2,3},{3,2},{4,5},{5,4},{6,7},{7,6},{8,9},{9,8},{10,11... | collective-permute-start | bytes 1179656 | tf_op jit(solution)/shard_map/ppermute | solution.py:388
  53.1 12.5 %collective-permute-start.17 = (bf16[64,3072]{1,0:T(8,128)(2,1)S(1)}, bf16[64,3072]{1,0:T(8,128)(2,1)S(1)}, u32[]{:S(2)}, u32[]{:S(2)}) collective-permute-start(bf16[64,3072]{1,0:T(8,128)(2,1)S(1)} %collective-permute-done.4.refs_5_), channel_id=1, source_target_pairs={{0,1},{1,0},{2,3},{3,2},{4,5},{5,4},{6,7},{7,6},{8,9},{9,8},{10,11... | collective-permute-start | bytes 1179656 | tf_op jit(solution)/shard_map/ppermute | solution.py:388
  53.7 12.0 %collective-permute-start.14 = (bf16[64,3072]{1,0:T(8,128)(2,1)S(1)}, bf16[64,3072]{1,0:T(8,128)(2,1)S(1)}, u32[]{:S(2)}, u32[]{:S(2)}) collective-permute-start(bf16[64,3072]{1,0:T(8,128)(2,1)S(1)} %collective-permute-done.6.refs_6_), channel_id=1, source_target_pairs={{0,1},{1,0},{2,3},{3,2},{4,5},{5,4},{6,7},{7,6},{8,9},{9,8},{10,11... | collective-permute-start | bytes 1179656 | tf_op jit(solution)/shard_map/ppermute | solution.py:388
  56.6 9.0 %collective-permute-start.24 = (bf16[64,3072]{1,0:T(8,128)(2,1)S(1)}, bf16[64,3072]{1,0:T(8,128)(2,1)S(1)}, u32[]{:S(2)}, u32[]{:S(2)}) collective-permute-start(bf16[64,3072]{1,0:T(8,128)(2,1)S(1)} %get-tuple-element.174), channel_id=1, source_target_pairs={{0,1},{1,0},{2,3},{3,2},{4,5},{5,4},{6,7},{7,6},{8,9},{9,8},{10,11... | collective-permute-start | bytes 1179656 | tf_op jit(solution)/shard_map/ppermute | solution.py:388
  58.8 7.8 %collective-permute-start.25 = (bf16[64,3072]{1,0:T(8,128)(2,1)S(1)}, bf16[64,3072]{1,0:T(8,128)(2,1)S(1)}, u32[]{:S(2)}, u32[]{:S(2)}) collective-permute-start(bf16[64,3072]{1,0:T(8,128)(2,1)S(1)} %get-tuple-element.158), channel_id=1, source_target_pairs={{0,4},{1,3},{4,8},{5,1},{8,12},{9,5},{12,14},{13,9},{14,10},{15,13... | collective-permute-start | bytes 1179656 | tf_op jit(solution)/shard_map/ppermute | solution.py:385
  63.8 8.0 %collective-permute-start.26 = (bf16[64,3072]{1,0:T(8,128)(2,1)S(1)}, bf16[64,3072]{1,0:T(8,128)(2,1)S(1)}, u32[]{:S(2)}, u32[]{:S(2)}) collective-permute-start(bf16[64,3072]{1,0:T(8,128)(2,1)S(1)} %get-tuple-element.161), channel_id=1, source_target_pairs={{0,4},{1,3},{4,8},{5,1},{8,12},{9,5},{12,14},{13,9},{14,10},{15,13... | collective-permute-start | bytes 1179656 | tf_op jit(solution)/shard_map/ppermute | solution.py:385
  69.5 8.6 %collective-permute-start.28 = (bf16[64,3072]{1,0:T(8,128)(2,1)S(1)}, bf16[64,3072]{1,0:T(8,128)(2,1)S(1)}, u32[]{:S(2)}, u32[]{:S(2)}) collective-permute-start(bf16[64,3072]{1,0:T(8,128)(2,1)S(1)} %get-tuple-element.164), channel_id=1, source_target_pairs={{0,4},{1,3},{4,8},{5,1},{8,12},{9,5},{12,14},{13,9},{14,10},{15,13... | collective-permute-start | bytes 1179656 | tf_op jit(solution)/shard_map/ppermute | solution.py:385
  74.7 7.8 %collective-permute-start.27 = (bf16[64,3072]{1,0:T(8,128)(2,1)S(1)}, bf16[64,3072]{1,0:T(8,128)(2,1)S(1)}, u32[]{:S(2)}, u32[]{:S(2)}) collective-permute-start(bf16[64,3072]{1,0:T(8,128)(2,1)S(1)} %get-tuple-element.162), channel_id=1, source_target_pairs={{0,4},{1,3},{4,8},{5,1},{8,12},{9,5},{12,14},{13,9},{14,10},{15,13... | collective-permute-start | bytes 1179656 | tf_op jit(solution)/shard_map/ppermute | solution.py:385
  78.2 8.5 %collective-permute-start.29 = (bf16[32,3072]{1,0:T(8,128)(2,1)S(1)}, bf16[32,3072]{1,0:T(8,128)(2,1)S(1)}, u32[]{:S(2)}, u32[]{:S(2)}) collective-permute-start(bf16[32,3072]{1,0:T(8,128)(2,1)S(1)} %get-tuple-element.169), channel_id=1, source_target_pairs={{0,1},{1,0},{2,3},{3,2},{4,5},{5,4},{6,7},{7,6},{8,9},{9,8},{10,11... | collective-permute-start | bytes 589832 | tf_op jit(solution)/shard_map/ppermute | solution.py:388
  82.6 4.1 %collective-permute-start.30 = (bf16[32,3072]{1,0:T(8,128)(2,1)S(1)}, bf16[32,3072]{1,0:T(8,128)(2,1)S(1)}, u32[]{:S(2)}, u32[]{:S(2)}) collective-permute-start(bf16[32,3072]{1,0:T(8,128)(2,1)S(1)} %get-tuple-element.171), channel_id=1, source_target_pairs={{0,1},{1,0},{2,3},{3,2},{4,5},{5,4},{6,7},{7,6},{8,9},{9,8},{10,11... | collective-permute-start | bytes 589832 | tf_op jit(solution)/shard_map/ppermute | solution.py:388

commit v6 on v4

v6 whole, which is shorter than its diff:
```python
import math

import jax
import jax.numpy as jnp
from jax import lax
from jax.experimental import pallas as pl
from jax.experimental.pallas import tpu as pltpu
from jax.sharding import PartitionSpec as P

RING = 8
PIECE_STEPS = 2
PIECE_COST = 0.1
PIECES = 4
VMEM_LIMIT = 16 * 1024 * 1024
WHOLE = pl.BlockSpec(memory_space=pltpu.VMEM)
OUTSIDE = pl.BlockSpec(memory_space=pltpu.HBM)


def cost(microseconds):
    return pl.CostEstimate(
        flops=int(microseconds * 1.15e9), bytes_accessed=0, transcendentals=0
    )


ANYWHERE = pl.BlockSpec(memory_space=pl.ANY)
SCALAR = pl.BlockSpec(memory_space=pltpu.SMEM)


def gelu_slope(pre):
    coeff = math.sqrt(2.0 / math.pi)
    square = pre * pre
    tanh_value = jnp.tanh(pre * (coeff + coeff * 0.044715 * square))
    inner_slope = coeff + 3.0 * 0.044715 * coeff * square
    return (0.5 + 0.5 * tanh_value) * (1.0 + pre * (1.0 - tanh_value) * inner_slope)


def plain(out_grad, pre_act, layer_input, weight):
    slope = gelu_slope(pre_act.astype(jnp.float32))
    grad_hidden = (out_grad.astype(jnp.float32) * slope).astype(jnp.bfloat16)
    local_grad = lax.dot_general(
        lax.all_gather(layer_input, "gx", axis=0, tiled=True),
        grad_hidden,
        (((0,), (0,)), ((), ())),
        preferred_element_type=jnp.float32,
    )
    grad_input = lax.psum_scatter(
        lax.dot_general(
            grad_hidden, weight, (((1,), (1,)), ((), ())), preferred_element_type=jnp.float32
        ),
        "gx",
        scatter_dimension=0,
        tiled=True,
    ).astype(jnp.bfloat16)
    return (grad_input, local_grad.astype(jnp.bfloat16))


def chip_at(place):
    place = place & (RING - 1)
    return jnp.where(place < RING // 2, 2 * place, 2 * (RING - 1 - place) + 1)


def place_of(chip):
    return jnp.where(chip % 2 == 0, chip // 2, RING - 1 - chip // 2)


def ring_pairs():
    path = [2 * p if p < RING // 2 else 2 * (RING - 1 - p) + 1 for p in range(RING)]
    along, across = [], []
    for place, chip in enumerate(path):
        ahead, behind = path[(place + 1) % RING], path[(place - 1) % RING]
        along += [(2 * chip, 2 * ahead), (2 * chip + 1, 2 * behind + 1)]
        across += [(2 * chip, 2 * behind + 1), (2 * chip + 1, 2 * ahead)]
    return along, across


def chip_order(me):
    way = jnp.where(me % 2 == 0, 1, -1)
    place = place_of(me // 2)
    steps = [0, -1, -2, -3, 4, 1, 2, 3]
    return [chip_at(place + way * s + RING) for s in steps]


def hidden_kernel(me_ref, og_hbm, pre_hbm, w_hbm, dh_ref, dht_ref, w_ref, og_ref, pre_ref, sems):
    rows = dh_ref.shape[0] // (2 * RING)
    me = me_ref[0]
    copies = []
    for i, chip in enumerate(chip_order(me)):
        for j, core in enumerate((me % 2, 1 - me % 2)):
            source = pl.ds(pl.multiple_of((2 * chip + core) * rows, rows), rows)
            block = pl.ds((2 * i + j) * rows, rows)
            for k, (hbm, ref) in enumerate(((og_hbm, og_ref), (pre_hbm, pre_ref))):
                copy = pltpu.make_async_copy(
                    hbm.at[source, :], ref.at[block, :], sems.at[k, 2 * i + j]
                )
                copy.start()
                copies.append(copy)
    wide = w_ref.shape[0]
    first = first_row(me_ref, True, 0, w_hbm.shape[0] // 2, wide)
    fetch = pltpu.make_async_copy(w_hbm.at[pl.ds(first, wide), :], w_ref, sems.at[2, 0])
    fetch.start()
    for i in range(RING // 2):
        for copy in copies[8 * i : 8 * (i + 1)]:
            copy.wait()
        block = pl.ds(4 * i * rows, 4 * rows)
        pre = pre_ref[block, :].astype(jnp.float32)
        og = og_ref[block, :].astype(jnp.float32)
        dh = (og * gelu_slope(pre)).astype(jnp.bfloat16)
        dh_ref[block, :] = dh
        dht_ref[:, block] = dh.T
    fetch.wait()


def hidden(me, out_grad, pre_act, weight):
    shape, dtype = out_grad.shape, out_grad.dtype
    return pl.pallas_call(
        hidden_kernel,
        out_shape=(
            jax.ShapeDtypeStruct(shape, dtype),
            jax.ShapeDtypeStruct(shape[::-1], dtype),
            jax.ShapeDtypeStruct((weight.shape[0] // (2 * PIECES), shape[1]), dtype),
        ),
        in_specs=[SCALAR, OUTSIDE, OUTSIDE, OUTSIDE],
        out_specs=(WHOLE, WHOLE, WHOLE),
        scratch_shapes=[
            pltpu.VMEM(shape, dtype),
            pltpu.VMEM(shape, dtype),
            pltpu.SemaphoreType.DMA((3, 2 * RING)),
        ],
        compiler_params=pltpu.CompilerParams(vmem_limit_bytes=VMEM_LIMIT),
        cost_estimate=cost(1),
        name="hidden",
    )(me, out_grad, pre_act, weight)


def first_row(me_ref, other, piece, half, wide):
    core = me_ref[0] % 2
    number = 1 - core if other else core
    return pl.multiple_of(number * half + piece * wide, wide)


def input_kernel(me_ref, dht_ref, w_ref, w_hbm, *refs, other, piece, wide, more):
    outs, part_ref, sems = refs[-(RING + 2 + more) :][:RING], refs[-2], refs[-1]
    half = outs[0].shape[1]
    if more:
        following = (other, piece + 1) if piece + 1 < PIECES else (False, 0)
        fetch = pltpu.make_async_copy(
            w_hbm.at[pl.ds(first_row(me_ref, *following, half, wide), wide), :],
            refs[-3],
            sems.at[PIECE_STEPS, 0],
        )
        fetch.start()
    steps = PIECE_STEPS if other else 1
    step = wide // steps
    stores = []
    for i in range(steps):
        here = pl.ds(i * step, step)
        part = jnp.dot(w_ref[here, :], dht_ref[...], preferred_element_type=jnp.float32)
        part_ref[:, here] = part.astype(jnp.bfloat16).T
        for j, out in enumerate(outs):
            rows = out.shape[0]
            store = pltpu.make_async_copy(
                part_ref.at[pl.ds(j * rows, rows), here],
                out.at[:, pl.ds(piece * wide + i * step, step)],
                sems.at[i, j],
            )
            store.start()
            stores.append(store)
    for store in stores:
        store.wait()
    if more:
        fetch.wait()


def input_piece(me, dht, w, weight, before, other, piece):
    ff, tokens = dht.shape
    half = weight.shape[0] // 2
    wide = half // PIECES
    rows = tokens // RING
    more = other or piece + 1 < PIECES
    outs = (jax.ShapeDtypeStruct((rows, half), jnp.bfloat16),) * RING
    following = (jax.ShapeDtypeStruct((wide, ff), jnp.bfloat16),) if more else ()
    result = pl.pallas_call(
        lambda *refs: input_kernel(*refs, other=other, piece=piece, wide=wide, more=more),
        out_shape=outs + following,
        in_specs=[SCALAR, WHOLE, WHOLE, OUTSIDE] + [ANYWHERE] * len(before),
        out_specs=(ANYWHERE,) * RING + (WHOLE,) * len(following),
        input_output_aliases={4 + i: i for i in range(len(before))},
        scratch_shapes=[
            pltpu.VMEM((tokens, wide), jnp.bfloat16),
            pltpu.SemaphoreType.DMA((PIECE_STEPS + 1, RING)),
        ],
        compiler_params=pltpu.CompilerParams(vmem_limit_bytes=VMEM_LIMIT),
        cost_estimate=cost(PIECE_COST),
        name="input_piece",
    )(me, dht, w, weight, *before)
    return result[:RING], (result[RING] if more else None)


def weight_kernel(dh_ref, *refs, piece, wide, step):
    blocks, refs = refs[: 2 * RING], refs[2 * RING :]
    out_hbm, stage, sems = refs[-3:]
    width, columns = out_hbm.shape
    copies = []

    def store(source, number, i):
        here = pl.ds(i * step, step)
        rows = pl.ds(number * wide, wide)
        copy = pltpu.make_async_copy(
            source.at[:, here], out_hbm.at[rows, here], sems.at[piece - number, i]
        )
        copy.start()
        copies.append(copy)

    if piece:
        for i in range(columns // step):
            store(refs[0], piece - 1, i)
    x = jnp.concatenate([b[:, pl.ds(piece * wide, wide)] for b in blocks], axis=0).T
    for i in range(columns // step):
        here = pl.ds(i * step, step)
        stage[:, here] = jnp.dot(
            x, dh_ref[:, here], preferred_element_type=jnp.float32
        ).astype(jnp.bfloat16)
        if (piece + 1) * wide == width:
            store(stage, piece, i)
    for copy in copies:
        copy.wait()


def weight_piece(dh, blocks, before, piece):
    tokens, ff = dh.shape
    width = blocks[0].shape[1]
    wide = width // (2 * PIECES)
    step = 512 if ff % 512 == 0 else 128
    ends = piece == 2 * PIECES - 1
    stage = jax.ShapeDtypeStruct((wide, ff), jnp.bfloat16)
    return pl.pallas_call(
        lambda *refs: weight_kernel(*refs, piece=piece, wide=wide, step=step),
        out_shape=(jax.ShapeDtypeStruct((width, ff), jnp.bfloat16),) + (stage,) * (not ends),
        in_specs=[WHOLE] * (1 + 2 * RING) + ([WHOLE, OUTSIDE] if before else []),
        out_specs=(OUTSIDE,) + (WHOLE,) * (not ends),
        input_output_aliases={2 + 2 * RING: 0} if before else {},
        scratch_shapes=[pltpu.VMEM(stage.shape, stage.dtype)] * ends
        + [pltpu.SemaphoreType.DMA((2, ff // step))],
        compiler_params=pltpu.CompilerParams(vmem_limit_bytes=VMEM_LIMIT),
        cost_estimate=cost(PIECE_COST),
        name="weight_piece",
    )(dh, *blocks, *before)


def total_kernel(part_ref, twin_ref, *refs):
    rows = part_ref.shape[0] // 2
    for here, there in ((pl.ds(0, rows), pl.ds(rows, rows)), (pl.ds(rows, rows), pl.ds(0, rows))):
        total = part_ref[here, :].astype(jnp.float32) + twin_ref[there, :].astype(jnp.float32)
        for ref in refs[:-1]:
            total = total + ref[here, :].astype(jnp.float32)
        refs[-1][here, :] = total.astype(refs[-1].dtype)


def total(*terms):
    return pl.pallas_call(
        total_kernel,
        out_shape=jax.ShapeDtypeStruct(terms[0].shape, terms[0].dtype),
        in_specs=[WHOLE] * len(terms),
        out_specs=WHOLE,
        compiler_params=pltpu.CompilerParams(vmem_limit_bytes=VMEM_LIMIT),
        cost_estimate=cost(0.1),
        name="total",
    )(*terms)


def halves_kernel(own_ref, came_ref, kept_ref, sent_ref):
    rows = kept_ref.shape[0]
    for ref, here in ((kept_ref, pl.ds(0, rows)), (sent_ref, pl.ds(rows, rows))):
        both = own_ref[here, :].astype(jnp.float32) + came_ref[here, :].astype(jnp.float32)
        ref[...] = both.astype(ref.dtype)


def halves(own, came):
    shape = (own.shape[0] // 2, own.shape[1])
    return pl.pallas_call(
        halves_kernel,
        out_shape=(
            jax.ShapeDtypeStruct(shape, jnp.float32),
            jax.ShapeDtypeStruct(shape, jnp.bfloat16),
        ),
        in_specs=[WHOLE, WHOLE],
        out_specs=(WHOLE, WHOLE),
        compiler_params=pltpu.CompilerParams(vmem_limit_bytes=VMEM_LIMIT),
        cost_estimate=cost(0.1),
        name="halves",
    )(own, came)


def last_kernel(me_ref, mine_ref, mine_came_ref, other_ref, other_came_ref, out_ref):
    core = me_ref[0] % 2
    half = mine_ref.shape[1]
    pairs = ((core, mine_ref, mine_came_ref), (1 - core, other_ref, other_came_ref))
    for number, kept, came in pairs:
        here = pl.ds(pl.multiple_of(number * half, half), half)
        out_ref[:, here] = (kept[...] + came[...].astype(jnp.float32)).astype(out_ref.dtype)


def last(me, mine, mine_came, other, other_came):
    shape = (mine.shape[0], 2 * mine.shape[1])
    return pl.pallas_call(
        last_kernel,
        out_shape=jax.ShapeDtypeStruct(shape, jnp.bfloat16),
        in_specs=[SCALAR] + [WHOLE] * 4,
        out_specs=WHOLE,
        compiler_params=pltpu.CompilerParams(vmem_limit_bytes=VMEM_LIMIT),
        cost_estimate=cost(0.3),
        name="last",
    )(me, mine, mine_came, other, other_came)


def after(x, *others):
    return lax.optimization_barrier((x, *others))[0]


def on_device(out_grad, pre_act, layer_input, weight):
    n = lax.axis_size("gx")
    rows, width = layer_input.shape
    if n != 2 * RING or rows % 16 or width % (2 * PIECES * PIECE_STEPS * 128):
        return plain(out_grad, pre_act, layer_input, weight)

    along, across = ring_pairs()
    twins = [(i, i ^ 1) for i in range(n)]

    def ring(x):
        return lax.ppermute(x, "gx", along)

    def swap(x):
        return lax.ppermute(x, "gx", twins)

    out_grad, pre_act, weight = (
        pltpu.with_memory_space_constraint(x, pltpu.HBM) for x in (out_grad, pre_act, weight)
    )
    me = lax.axis_index("gx").astype(jnp.int32).reshape(1)

    a1, b1 = ring(layer_input), lax.ppermute(layer_input, "gx", across)
    twin = swap(layer_input)
    dh, dht, w = hidden(me, out_grad, pre_act, weight)

    def product(other, piece, w, before, *ties):
        return input_piece(me, after(dht, *ties), w, weight, before, other, piece)

    a1 = after(a1, dh)
    a2, sa1 = ring(a1), swap(a1)
    go, w = product(True, 0, w, (), a1, twin)
    b1 = after(b1, go[0])
    b2, sb1 = ring(b1), swap(b1)
    go, w = product(True, 1, w, go, b1, sa1)
    a2 = after(a2, go[0])
    a3, sa2 = ring(a2), swap(a2)
    go, w = product(True, 2, w, go, a2, sb1)
    b2 = after(b2, go[0])
    b3, sb2 = ring(b2), swap(b2)
    go, w = product(True, 3, w, go, b2, sa2)
    a3 = after(a3, go[0])
    a4, sa3 = ring(a3), swap(a3)
    gm, w = product(False, 0, w, (), a3, sb2)
    own_o, behind_o, opposite_o, ahead_o = go[0], go[1:4], go[4], go[5:]
    from_m, opposite_from = [swap(x) for x in behind_o], swap(opposite_o)
    gm, w = product(False, 1, w, gm, sa3)
    b3 = after(b3, gm[0])
    sb3 = swap(b3)
    gm, w = product(False, 2, w, gm, b3, *from_m)
    a4 = after(a4, gm[0])
    sa4 = swap(a4)
    gm, _ = product(False, 3, w, gm, a4, sb3, opposite_from)
    own_m, behind_m, opposite_m, ahead_m = gm[0], gm[1:4], gm[4], gm[5:]
    sent = total(opposite_m, opposite_from)
    r4m = ring(sent)
    from_o = [swap(after(x, sent)) for x in behind_m[::-1]][::-1]
    blocks = (layer_input, twin, a1, b1, a2, b2, a3, b3, a4, sa4, sb1, sa1, sb2, sa2, sb3, sa3)

    def gradient(piece, before, *ties):
        before = before[::-1]
        return weight_piece(after(dh, *ties), blocks, before, piece)

    def send(k, ahead, came, *ring_terms):
        return total(ahead[k - 1], came[k - 1], *ring_terms)

    gw = gradient(0, (), sent, from_o[2])
    sent = send(3, ahead_o, from_o[:2] + [after(from_o[2], gw[1])])
    r3o = ring(sent)
    gw = gradient(1, gw, sent, from_o[1])
    sent = send(3, ahead_m, from_m, after(r4m, gw[1]))
    r3m = ring(sent)
    gw = gradient(2, gw, sent, from_o[0])
    sent = send(2, ahead_o, from_o, after(r3o, gw[1]))
    r2o = ring(sent)
    gw = gradient(3, gw, sent)
    sent = send(2, ahead_m, from_m, after(r3m, gw[1]))
    r2m = ring(sent)
    gw = gradient(4, gw, sent)
    sent = send(1, ahead_o, from_o, after(r2o, gw[1]))
    r1o = ring(sent)
    gw = gradient(5, gw, sent)
    sent = send(1, ahead_m, from_m, after(r2m, gw[1]))
    r1m = ring(sent)
    gw = gradient(6, gw, sent)
    kept_o, sent_o = halves(own_o, after(r1o, gw[1]))
    came_m = swap(sent_o)
    gw = gradient(7, gw, sent_o)
    kept_m, sent_m = halves(own_m, after(r1m, gw[0]))
    came_o = swap(sent_m)
    return (last(me, kept_m, came_m, kept_o, came_o), gw[0])


def solution(mesh):
    placed = (P("group", "gx"), P("group", "gx"), P(("group", "gx"), None), P(None, "gx"))
    return jax.shard_map(
        on_device,
        mesh=mesh,
        in_specs=placed,
        out_specs=(P(("group", "gx"), None), P(None, ("group", "gx"))),
        check_vma=False,
    )
```

time: 95.7 us -> 80.3 us (0.84)
  waiting for transfers between devices: 25.5 us -> 19.4 us
  starting transfers between devices: 29.4 us -> 25.2 us
  Pallas kernels: 38.6 us -> 34.6 us
    ppermute x31, waiting for transfers between devices: 25.5 us -> 19.4 us  [the longest x13 18.2 us: ring(): return lax.ppermute(x, 'gx', along)]
    ppermute x31, starting transfers between devices: 29.4 us -> 25.2 us  [the longest x13 20 us: ring(): return lax.ppermute(x, 'gx', along)]
    pallas_call x9 -> x15, Pallas kernels: 16.1 us -> 14 us  [the longest x8 13.1 us: weight_piece(): pl.pallas_call(lambda *refs: weight_kernel(*refs, piece=piece, wide=wide,...]
    pallas_call x8, Pallas kernels: 17.7 us -> 15.7 us  [input_piece(): pl.pallas_call(lambda *refs: input_kernel(*refs, other=other, piece=piece...]
  transfers between devices with their start and end apart: 31 -> 31, of which waited for: 12 -> 15; matrix products, arithmetic and copies ran while one was open for 1% -> 0% of each run, Pallas kernels for 40% -> 40%
where the time goes in v6:
time: 80.3 us; the launch traced here: 80.1 us
  Pallas kernels  34.6 us (43%)
  starting transfers between devices  25.2 us (31%)
  waiting for transfers between devices  19.4 us (24%)
  between operations  0.87 us (1%)
    ppermute x13, starting transfers between devices, ring(): return lax.ppermute(x, 'gx', along)  20 us
    ppermute x13, waiting for transfers between devices, ring(): return lax.ppermute(x, 'gx', along)  18.2 us
    pallas_call x8, Pallas kernels, input_piece(): pl.pallas_call(lambda *refs: input_kernel(*refs, other=other, piece=piece...  15.7 us
    pallas_call x8, Pallas kernels, weight_piece(): pl.pallas_call(lambda *refs: weight_kernel(*refs, piece=piece, wide=wide,...  13.1 us
    ppermute x17, starting transfers between devices, swap(): return lax.ppermute(x, 'gx', twins)  4.48 us
    pallas_call x1, Pallas kernels, hidden(): pl.pallas_call(hidden_kernel, out_shape=(jax.ShapeDtypeStruct(shape, dtyp...  3.81 us
  transfers between devices with their start and end apart: 31, of which 15 were waited for; matrix products, arithmetic and copies ran while one was open for 0% of the time, Pallas kernels for 40%

profile of v6, /device:TPU:0, one launch (start us, length us, event | category | flops | bytes accessed | tf_op | source)
XLA Modules:
  0.0 80.1 jit_solution(6820073651237808393)
XLA Ops:
  0.6 3.1 %collective-permute-start = (bf16[32,6144]{1,0:T(8,128)(2,1)}, bf16[32,6144]{1,0:T(8,128)(2,1)S(1)}, u32[]{:S(2)}, u32[]{:S(2)}) collective-permute-start(bf16[32,6144]{1,0:T(8,128)(2,1)} %refs_1_.15), channel_id=1, source_target_pairs={{0,4},{1,3},{4,8},{5,1},{8,12},{9,5},{12,14},{13,9},{14,10},{15,13... | collective-permute-start | bytes 1179656 | tf_op jit(solution)/shard_map/ppermute | solution.py:330
  3.7 0.7 collective-permute-start.2
  4.4 3.8 %hidden.1 = (bf16[512,1536]{1,0:T(8,128)(2,1)S(1)}, bf16[1536,512]{1,0:T(8,128)(2,1)S(1)}, bf16[768,1536]{1,0:T(8,128)(2,1)S(1)}) custom-call(s32[1]{0:T(128)} %bitcast.me_ref.refs_0_, bf16[512,1536]{1,0:T(8,128)(2,1)} %og_hbm.1, bf16[512,1536]{1,0:T(8,128)(2,1)} %pre_hbm.1, bf16[6144,1536]{1,0:T(8,128)(2,1)} %refs_3_.15), custom_call_target="tpu_custom_call" | custom-call | flops 1150000000 | tf_op jit(solution)/shard_map/hidden/pallas_call | solution.py:115
  8.2 4.3 %collective-permute-done.refs_3_ = bf16[32,6144]{1,0:T(8,128)(2,1)S(1)} collective-permute-done((bf16[32,6144]{1,0:T(8,128)(2,1)}, bf16[32,6144]{1,0:T(8,128)(2,1)S(1)}, u32[]{:S(2)}, u32[]{:S(2)}) %collective-permute-start) | collective-permute-done | bytes 393248 | tf_op jit(solution)/shard_map/ppermute | solution.py:330
  12.5 2.4 %collective-permute-start.1 = (bf16[32,6144]{1,0:T(8,128)(2,1)S(1)}, bf16[32,6144]{1,0:T(8,128)(2,1)S(1)}, u32[]{:S(2)}, u32[]{:S(2)}) collective-permute-start(bf16[32,6144]{1,0:T(8,128)(2,1)S(1)} %collective-permute-done.refs_3_), channel_id=1, source_target_pairs={{0,4},{1,3},{4,8},{5,1},{8,12},{9,5},{12,14},{13,9},{14,10},{15,13... | collective-permute-start | bytes 1179656 | tf_op jit(solution)/shard_map/ppermute | solution.py:330
  14.9 2.1 %input_piece.8 = (bf16[64,3072]{1,0:T(8,128)(2,1)S(1)}, bf16[64,3072]{1,0:T(8,128)(2,1)S(1)}, bf16[64,3072]{1,0:T(8,128)(2,1)S(1)}, bf16[64,3072]{1,0:T(8,128)(2...) custom-call(s32[1]{0:T(128)} %bitcast.me_ref.refs_0_, ...), custom_call_target="tpu_custom_call" | custom-call | flops 115000000 | tf_op jit(solution)/shard_map/input_piece/pallas_call | solution.py:182
  17.0 0.8 collective-permute-start.7
  17.7 1.0 %collective-permute-start.6 = (bf16[32,6144]{1,0:T(8,128)(2,1)S(1)}, bf16[32,6144]{1,0:T(8,128)(2,1)S(1)}, u32[]{:S(2)}, u32[]{:S(2)}) collective-permute-start(bf16[32,6144]{1,0:T(8,128)(2,1)S(1)} %collective-permute-done.2.refs_4_), channel_id=1, source_target_pairs={{0,4},{1,3},{4,8},{5,1},{8,12},{9,5},{12,14},{13,9},{14,10},{15,13... | collective-permute-start | bytes 1179656 | tf_op jit(solution)/shard_map/ppermute | solution.py:330
  18.7 2.1 %input_piece.9 = (bf16[64,3072]{1,0:T(8,128)(2,1)S(1)}, bf16[64,3072]{1,0:T(8,128)(2,1)S(1)}, bf16[64,3072]{1,0:T(8,128)(2,1)S(1)}, bf16[64,3072]{1,0:T(8,128)(2...) custom-call(s32[1]{0:T(128)} %bitcast.me_ref.refs_0_, ...), custom_call_target="tpu_custom_call", output_to_operand_aliasing={{0}: (4, {}), {1}: (5, {}), {2}: (6, {}), {3}: (7, {}), {4}... | custom-call | flops 115000000 | tf_op jit(solution)/shard_map/input_piece/pallas_call | solution.py:182
  20.8 0.4 collective-permute-done.1.refs_5_
  21.1 0.1 collective-permute-start.8
  21.2 1.4 %collective-permute-start.5 = (bf16[32,6144]{1,0:T(8,128)(2,1)S(1)}, bf16[32,6144]{1,0:T(8,128)(2,1)S(1)}, u32[]{:S(2)}, u32[]{:S(2)}) collective-permute-start(bf16[32,6144]{1,0:T(8,128)(2,1)S(1)} %collective-permute-done.1.refs_5_), channel_id=1, source_target_pairs={{0,4},{1,3},{4,8},{5,1},{8,12},{9,5},{12,14},{13,9},{14,10},{15,13... | collective-permute-start | bytes 1179656 | tf_op jit(solution)/shard_map/ppermute | solution.py:330
  22.7 2.1 %input_piece.10 = (bf16[64,3072]{1,0:T(8,128)(2,1)S(1)}, bf16[64,3072]{1,0:T(8,128)(2,1)S(1)}, bf16[64,3072]{1,0:T(8,128)(2,1)S(1)}, bf16[64,3072]{1,0:T(8,128)(...) custom-call(s32[1]{0:T(128)} %bitcast.me_ref.refs_0_, ...), custom_call_target="tpu_custom_call", output_to_operand_aliasing={{0}: (4, {}), {1}: (5, {}), {2}: (6, {}), {3}: (7, {}), {4}... | custom-call | flops 115000000 | tf_op jit(solution)/shard_map/input_piece/pallas_call | solution.py:182
  24.8 0.8 collective-permute-done.6.refs_6_
  25.5 2.1 %input_piece.11 = (bf16[64,3072]{1,0:T(8,128)(2,1)S(1)}, bf16[64,3072]{1,0:T(8,128)(2,1)S(1)}, bf16[64,3072]{1,0:T(8,128)(2,1)S(1)}, bf16[64,3072]{1,0:T(8,128)(...) custom-call(s32[1]{0:T(128)} %bitcast.me_ref.refs_0_, ...), custom_call_target="tpu_custom_call", output_to_operand_aliasing={{0}: (4, {}), {1}: (5, {}), {2}: (6, {}), {3}: (7, {}), {4}... | custom-call | flops 115000000 | tf_op jit(solution)/shard_map/input_piece/pallas_call | solution.py:182
  27.6 2.1 %collective-permute-done.5.refs_7_ = bf16[32,6144]{1,0:T(8,128)(2,1)S(1)} collective-permute-done((bf16[32,6144]{1,0:T(8,128)(2,1)S(1)}, bf16[32,6144]{1,0:T(8,128)(2,1)S(1)}, u32[]{:S(2)}, u32[]{:S(2)}) %collective-permute-start.5) | collective-permute-done | bytes 393248 | tf_op jit(solution)/shard_map/ppermute | solution.py:330
  29.7 1.4 %collective-permute-start.10 = (bf16[32,6144]{1,0:T(8,128)(2,1)S(1)}, bf16[32,6144]{1,0:T(8,128)(2,1)S(1)}, u32[]{:S(2)}, u32[]{:S(2)}) collective-permute-start(bf16[32,6144]{1,0:T(8,128)(2,1)S(1)} %collective-permute-done.6.refs_6_), channel_id=1, source_target_pairs={{0,4},{1,3},{4,8},{5,1},{8,12},{9,5},{12,14},{13,9},{14,10},{15,13... | collective-permute-start | bytes 1179656 | tf_op jit(solution)/shard_map/ppermute | solution.py:330
  31.1 0.7 collective-permute-start.13
  31.8 0.9 %collective-permute-start.9 = (bf16[32,6144]{1,0:T(8,128)(2,1)S(1)}, bf16[32,6144]{1,0:T(8,128)(2,1)S(1)}, u32[]{:S(2)}, u32[]{:S(2)}) collective-permute-start(bf16[32,6144]{1,0:T(8,128)(2,1)S(1)} %collective-permute-done.5.refs_7_), channel_id=1, source_target_pairs={{0,4},{1,3},{4,8},{5,1},{8,12},{9,5},{12,14},{13,9},{14,10},{15,13... | collective-permute-start | bytes 1179656 | tf_op jit(solution)/shard_map/ppermute | solution.py:330
  32.7 0.4 collective-permute-start.14
  33.1 1.9 %input_piece.12 = (bf16[64,3072]{1,0:T(8,128)(2,1)S(1)}, bf16[64,3072]{1,0:T(8,128)(2,1)S(1)}, bf16[64,3072]{1,0:T(8,128)(2,1)S(1)}, bf16[64,3072]{1,0:T(8,128)(...) custom-call(s32[1]{0:T(128)} %bitcast.me_ref.refs_0_, ...), custom_call_target="tpu_custom_call" | custom-call | flops 115000000 | tf_op jit(solution)/shard_map/input_piece/pallas_call | solution.py:182
  35.0 0.2 collective-permute-start.15
  35.2 1.9 %input_piece.13 = (bf16[64,3072]{1,0:T(8,128)(2,1)S(1)}, bf16[64,3072]{1,0:T(8,128)(2,1)S(1)}, bf16[64,3072]{1,0:T(8,128)(2,1)S(1)}, bf16[64,3072]{1,0:T(8,128)(...) custom-call(s32[1]{0:T(128)} %bitcast.me_ref.refs_0_, ...), custom_call_target="tpu_custom_call", output_to_operand_aliasing={{0}: (4, {}), {1}: (5, {}), {2}: (6, {}), {3}: (7, {}), {4}... | custom-call | flops 115000000 | tf_op jit(solution)/shard_map/input_piece/pallas_call | solution.py:182
  37.1 0.4 collective-permute-done.10.refs_8_
  37.6 0.4 collective-permute-start.16
  38.0 1.9 %input_piece.14 = (bf16[64,3072]{1,0:T(8,128)(2,1)S(1)}, bf16[64,3072]{1,0:T(8,128)(2,1)S(1)}, bf16[64,3072]{1,0:T(8,128)(2,1)S(1)}, bf16[64,3072]{1,0:T(8,128)(...) custom-call(s32[1]{0:T(128)} %bitcast.me_ref.refs_0_, ...), custom_call_target="tpu_custom_call", output_to_operand_aliasing={{0}: (4, {}), {1}: (5, {}), {2}: (6, {}), {3}: (7, {}), {4}... | custom-call | flops 115000000 | tf_op jit(solution)/shard_map/input_piece/pallas_call | solution.py:182
  39.9 1.8 %collective-permute-done.9.refs_9_ = bf16[32,6144]{1,0:T(8,128)(2,1)S(1)} collective-permute-done((bf16[32,6144]{1,0:T(8,128)(2,1)S(1)}, bf16[32,6144]{1,0:T(8,128)(2,1)S(1)}, u32[]{:S(2)}, u32[]{:S(2)}) %collective-permute-start.9) | collective-permute-done | bytes 393248 | tf_op jit(solution)/shard_map/ppermute | solution.py:330
  41.7 1.8 %input_piece.15 = (bf16[64,3072]{1,0:T(8,128)(2,1)S(1)}, bf16[64,3072]{1,0:T(8,128)(2,1)S(1)}, bf16[64,3072]{1,0:T(8,128)(2,1)S(1)}, bf16[64,3072]{1,0:T(8,128)(...) custom-call(s32[1]{0:T(128)} %bitcast.me_ref.refs_0_, ...), custom_call_target="tpu_custom_call", output_to_operand_aliasing={{0}: (4, {}), {1}: (5, {}), {2}: (6, {}), {3}: (7, {}), {4}... | custom-call | flops 115000000 | tf_op jit(solution)/shard_map/input_piece/pallas_call | solution.py:182
  43.5 0.1 total.7
  43.7 0.5 collective-permute-start.20
  44.3 1.4 %collective-permute-start.18 = (bf16[64,3072]{1,0:T(8,128)(2,1)S(1)}, bf16[64,3072]{1,0:T(8,128)(2,1)S(1)}, u32[]{:S(2)}, u32[]{:S(2)}) collective-permute-start(bf16[64,3072]{1,0:T(8,128)(2,1)S(1)} %total.7), channel_id=1, source_target_pairs={{0,4},{1,3},{4,8},{5,1},{8,12},{9,5},{12,14},{13,9},{14,10},{15,13... | collective-permute-start | bytes 1179656 | tf_op jit(solution)/shard_map/ppermute | solution.py:330
  45.7 0.6 collective-permute-start.24
  46.3 1.5 %weight_piece.8 = (bf16[6144,1536]{1,0:T(8,128)(2,1)}, bf16[768,1536]{1,0:T(8,128)(2,1)S(1)}) custom-call(bf16[512,1536]{1,0:T(8,128)(2,1)S(1)} %get-tuple-element.248.refs_0_, bf16[32,6144]{1,0:T(8,128)(2,1)S(1)} %copy-done, bf16[32,6144]{1,0:T(8,128)(2,1)S(1)} %collective-permute-done.3.refs_2_, bf16[32,6144]{1,0:T(8,128)(2,1)S(1)} %collective-permute-done.refs_3_, ...), custom_call_target="tpu_custom_call" | custom-call | flops 115000000 | tf_op jit(solution)/shard_map/weight_piece/pallas_call | solution.py:236
  47.8 0.1 total.8
  47.9 1.1 %collective-permute-start.23 = (bf16[64,3072]{1,0:T(8,128)(2,1)S(1)}, bf16[64,3072]{1,0:T(8,128)(2,1)S(1)}, u32[]{:S(2)}, u32[]{:S(2)}) collective-permute-start(bf16[64,3072]{1,0:T(8,128)(2,1)S(1)} %total.8), channel_id=1, source_target_pairs={{0,4},{1,3},{4,8},{5,1},{8,12},{9,5},{12,14},{13,9},{14,10},{15,13... | collective-permute-start | bytes 1179656 | tf_op jit(solution)/shard_map/ppermute | solution.py:330
  49.0 1.5 %weight_piece.9 = (bf16[6144,1536]{1,0:T(8,128)(2,1)}, bf16[768,1536]{1,0:T(8,128)(2,1)S(1)}) custom-call(bf16[512,1536]{1,0:T(8,128)(2,1)S(1)} %get-tuple-element.248.refs_0_, bf16[32,6144]{1,0:T(8,128)(2,1)S(1)} %copy-done, bf16[32,6144]{1,0:T(8,128)(2,1)S(1)} %collective-permute-done.3.refs_2_, ...), custom_call_target="tpu_custom_call", output_to_operand_aliasing={{0}: (18, {})} | custom-call | flops 115000000 | tf_op jit(solution)/shard_map/weight_piece/pallas_call | solution.py:236
  50.5 1.6 %collective-permute-done.18.refs_0_ = bf16[64,3072]{1,0:T(8,128)(2,1)S(1)} collective-permute-done((bf16[64,3072]{1,0:T(8,128)(2,1)S(1)}, bf16[64,3072]{1,0:T(8,128)(2,1)S(1)}, u32[]{:S(2)}, u32[]{:S(2)}) %collective-permute-start.18) | collective-permute-done | bytes 393248 | tf_op jit(solution)/shard_map/ppermute | solution.py:330
  52.1 0.1 total.9
  52.2 1.4 %collective-permute-start.22 = (bf16[64,3072]{1,0:T(8,128)(2,1)S(1)}, bf16[64,3072]{1,0:T(8,128)(2,1)S(1)}, u32[]{:S(2)}, u32[]{:S(2)}) collective-permute-start(bf16[64,3072]{1,0:T(8,128)(2,1)S(1)} %total.9), channel_id=1, source_target_pairs={{0,4},{1,3},{4,8},{5,1},{8,12},{9,5},{12,14},{13,9},{14,10},{15,13... | collective-permute-start | bytes 1179656 | tf_op jit(solution)/shard_map/ppermute | solution.py:330
  53.7 1.5 %weight_piece.10 = (bf16[6144,1536]{1,0:T(8,128)(2,1)}, bf16[768,1536]{1,0:T(8,128)(2,1)S(1)}) custom-call(bf16[512,1536]{1,0:T(8,128)(2,1)S(1)} %get-tuple-element.248.refs_0_, bf16[32,6144]{1,0:T(8,128)(2,1)S(1)} %copy-done, bf16[32,6144]{1,0:T(8,128)(2,1)S(1)} %collective-permute-done.3.refs_2_, ...), custom_call_target="tpu_custom_call", output_to_operand_aliasing={{0}: (18, {})} | custom-call | flops 115000000 | tf_op jit(solution)/shard_map/weight_piece/pallas_call | solution.py:236
  55.2 1.1 %collective-permute-done.23.refs_0_ = bf16[64,3072]{1,0:T(8,128)(2,1)S(1)} collective-permute-done((bf16[64,3072]{1,0:T(8,128)(2,1)S(1)}, bf16[64,3072]{1,0:T(8,128)(2,1)S(1)}, u32[]{:S(2)}, u32[]{:S(2)}) %collective-permute-start.23) | collective-permute-done | bytes 393248 | tf_op jit(solution)/shard_map/ppermute | solution.py:330
  56.3 0.1 total.10
  56.4 1.4 %collective-permute-start.26 = (bf16[64,3072]{1,0:T(8,128)(2,1)S(1)}, bf16[64,3072]{1,0:T(8,128)(2,1)S(1)}, u32[]{:S(2)}, u32[]{:S(2)}) collective-permute-start(bf16[64,3072]{1,0:T(8,128)(2,1)S(1)} %total.10), channel_id=1, source_target_pairs={{0,4},{1,3},{4,8},{5,1},{8,12},{9,5},{12,14},{13,9},{14,10},{15,13... | collective-permute-start | bytes 1179656 | tf_op jit(solution)/shard_map/ppermute | solution.py:330
  57.9 1.5 %weight_piece.11 = (bf16[6144,1536]{1,0:T(8,128)(2,1)}, bf16[768,1536]{1,0:T(8,128)(2,1)S(1)}) custom-call(bf16[512,1536]{1,0:T(8,128)(2,1)S(1)} %get-tuple-element.248.refs_0_, bf16[32,6144]{1,0:T(8,128)(2,1)S(1)} %copy-done, bf16[32,6144]{1,0:T(8,128)(2,1)S(1)} %collective-permute-done.3.refs_2_, ...), custom_call_target="tpu_custom_call", output_to_operand_aliasing={{0}: (18, {})} | custom-call | flops 115000000 | tf_op jit(solution)/shard_map/weight_piece/pallas_call | solution.py:236
  59.4 1.1 %collective-permute-done.22.refs_0_ = bf16[64,3072]{1,0:T(8,128)(2,1)S(1)} collective-permute-done((bf16[64,3072]{1,0:T(8,128)(2,1)S(1)}, bf16[64,3072]{1,0:T(8,128)(2,1)S(1)}, u32[]{:S(2)}, u32[]{:S(2)}) %collective-permute-start.22) | collective-permute-done | bytes 393248 | tf_op jit(solution)/shard_map/ppermute | solution.py:330
  60.5 0.1 total.11
  60.7 1.4 %collective-permute-start.25 = (bf16[64,3072]{1,0:T(8,128)(2,1)S(1)}, bf16[64,3072]{1,0:T(8,128)(2,1)S(1)}, u32[]{:S(2)}, u32[]{:S(2)}) collective-permute-start(bf16[64,3072]{1,0:T(8,128)(2,1)S(1)} %total.11), channel_id=1, source_target_pairs={{0,4},{1,3},{4,8},{5,1},{8,12},{9,5},{12,14},{13,9},{14,10},{15,13... | collective-permute-start | bytes 1179656 | tf_op jit(solution)/shard_map/ppermute | solution.py:330
  62.1 1.5 %weight_piece.12 = (bf16[6144,1536]{1,0:T(8,128)(2,1)}, bf16[768,1536]{1,0:T(8,128)(2,1)S(1)}) custom-call(bf16[512,1536]{1,0:T(8,128)(2,1)S(1)} %get-tuple-element.248.refs_0_, bf16[32,6144]{1,0:T(8,128)(2,1)S(1)} %copy-done, bf16[32,6144]{1,0:T(8,128)(2,1)S(1)} %collective-permute-done.3.refs_2_, ...), custom_call_target="tpu_custom_call", output_to_operand_aliasing={{0}: (18, {})} | custom-call | flops 115000000 | tf_op jit(solution)/shard_map/weight_piece/pallas_call | solution.py:236
  63.6 1.1 %collective-permute-done.26.refs_0_ = bf16[64,3072]{1,0:T(8,128)(2,1)S(1)} collective-permute-done((bf16[64,3072]{1,0:T(8,128)(2,1)S(1)}, bf16[64,3072]{1,0:T(8,128)(2,1)S(1)}, u32[]{:S(2)}, u32[]{:S(2)}) %collective-permute-start.26) | collective-permute-done | bytes 393248 | tf_op jit(solution)/shard_map/ppermute | solution.py:330
  64.7 0.1 total.12
  64.9 1.4 %collective-permute-start.28 = (bf16[64,3072]{1,0:T(8,128)(2,1)S(1)}, bf16[64,3072]{1,0:T(8,128)(2,1)S(1)}, u32[]{:S(2)}, u32[]{:S(2)}) collective-permute-start(bf16[64,3072]{1,0:T(8,128)(2,1)S(1)} %total.12), channel_id=1, source_target_pairs={{0,4},{1,3},{4,8},{5,1},{8,12},{9,5},{12,14},{13,9},{14,10},{15,13... | collective-permute-start | bytes 1179656 | tf_op jit(solution)/shard_map/ppermute | solution.py:330
  66.3 1.5 %weight_piece.13 = (bf16[6144,1536]{1,0:T(8,128)(2,1)}, bf16[768,1536]{1,0:T(8,128)(2,1)S(1)}) custom-call(bf16[512,1536]{1,0:T(8,128)(2,1)S(1)} %get-tuple-element.248.refs_0_, bf16[32,6144]{1,0:T(8,128)(2,1)S(1)} %copy-done, bf16[32,6144]{1,0:T(8,128)(2,1)S(1)} %collective-permute-done.3.refs_2_, ...), custom_call_target="tpu_custom_call", output_to_operand_aliasing={{0}: (18, {})} | custom-call | flops 115000000 | tf_op jit(solution)/shard_map/weight_piece/pallas_call | solution.py:236
  67.8 1.1 %collective-permute-done.25.refs_0_ = bf16[64,3072]{1,0:T(8,128)(2,1)S(1)} collective-permute-done((bf16[64,3072]{1,0:T(8,128)(2,1)S(1)}, bf16[64,3072]{1,0:T(8,128)(2,1)S(1)}, u32[]{:S(2)}, u32[]{:S(2)}) %collective-permute-start.25) | collective-permute-done | bytes 393248 | tf_op jit(solution)/shard_map/ppermute | solution.py:330
  68.9 0.1 total.13
  69.1 1.7 %collective-permute-start.27 = (bf16[64,3072]{1,0:T(8,128)(2,1)S(1)}, bf16[64,3072]{1,0:T(8,128)(2,1)S(1)}, u32[]{:S(2)}, u32[]{:S(2)}) collective-permute-start(bf16[64,3072]{1,0:T(8,128)(2,1)S(1)} %total.13), channel_id=1, source_target_pairs={{0,4},{1,3},{4,8},{5,1},{8,12},{9,5},{12,14},{13,9},{14,10},{15,13... | collective-permute-start | bytes 1179656 | tf_op jit(solution)/shard_map/ppermute | solution.py:330
  70.7 1.5 %weight_piece.14 = (bf16[6144,1536]{1,0:T(8,128)(2,1)}, bf16[768,1536]{1,0:T(8,128)(2,1)S(1)}) custom-call(bf16[512,1536]{1,0:T(8,128)(2,1)S(1)} %get-tuple-element.248.refs_0_, bf16[32,6144]{1,0:T(8,128)(2,1)S(1)} %copy-done, bf16[32,6144]{1,0:T(8,128)(2,1)S(1)} %collective-permute-done.3.refs_2_, ...), custom_call_target="tpu_custom_call", output_to_operand_aliasing={{0}: (18, {})} | custom-call | flops 115000000 | tf_op jit(solution)/shard_map/weight_piece/pallas_call | solution.py:236
  72.3 0.9 %collective-permute-done.28.came_ref = bf16[64,3072]{1,0:T(8,128)(2,1)S(1)} collective-permute-done((bf16[64,3072]{1,0:T(8,128)(2,1)S(1)}, bf16[64,3072]{1,0:T(8,128)(2,1)S(1)}, u32[]{:S(2)}, u32[]{:S(2)}) %collective-permute-start.28) | collective-permute-done | bytes 393248 | tf_op jit(solution)/shard_map/ppermute | solution.py:330
  73.1 0.1 halves.2
  73.2 2.5 %weight_piece.15 = bf16[6144,1536]{1,0:T(8,128)(2,1)} custom-call(bf16[512,1536]{1,0:T(8,128)(2,1)S(1)} %get-tuple-element.248.refs_0_, bf16[32,6144]{1,0:T(8,128)(2,1)S(1)} %copy-done, bf16[32,6144]{1,0:T(8,128)(2,1)S(1)} %collective-permute-done.3.refs_2_, bf16[32,6144]{1,0:T(8,128)(2,1)S(1)} %collective-permute-done.refs_3_, ...), custom_call_target="tpu_custom_call", output_to_operand_aliasing={{}: (18, {})} | custom-call | flops 115000000 | tf_op jit(solution)/shard_map/weight_piece/pallas_call | solution.py:236
  75.8 1.6 %collective-permute-done.27.came_ref = bf16[64,3072]{1,0:T(8,128)(2,1)S(1)} collective-permute-done((bf16[64,3072]{1,0:T(8,128)(2,1)S(1)}, bf16[64,3072]{1,0:T(8,128)(2,1)S(1)}, u32[]{:S(2)}, u32[]{:S(2)}) %collective-permute-start.27) | collective-permute-done | bytes 393248 | tf_op jit(solution)/shard_map/ppermute | solution.py:330
  77.5 0.5 collective-permute-start.29
  78.0 0.9 %collective-permute-done.30.other_came_ref = bf16[32,3072]{1,0:T(8,128)(2,1)S(1)} collective-permute-done((bf16[32,3072]{1,0:T(8,128)(2,1)S(1)}, bf16[32,3072]{1,0:T(8,128)(2,1)S(1)}, u32[]{:S(2)}, u32[]{:S(2)}) %collective-permute-start.30) | collective-permute-done | bytes 196640 | tf_op jit(solution)/shard_map/ppermute | solution.py:333
  79.0 0.3 collective-permute-done.29.mine_came_ref
  79.2 0.8 %last.1 = bf16[32,6144]{1,0:T(8,128)(2,1)} custom-call(s32[1]{0:T(128)} %bitcast.me_ref.refs_0_, f32[32,3072]{1,0:T(8,128)S(1)} %get-tuple-element.251.mine_ref, bf16[32,3072]{1,0:T(8,128)(2,1)S(1)} %collective-permute-done.29.mine_came_ref, f32[32,3072]{1,0:T(8,128)S(1)} %get-tuple-element.252.other_ref, ...), custom_call_target="tpu_custom_call" | custom-call | flops 345000000 | tf_op jit(solution)/shard_map/last/pallas_call | solution.py:305
  (27 shorter events, 0.4 us)
Async XLA Ops:
  0.6 11.9 %collective-permute-start = (bf16[32,6144]{1,0:T(8,128)(2,1)}, bf16[32,6144]{1,0:T(8,128)(2,1)S(1)}, u32[]{:S(2)}, u32[]{:S(2)}) collective-permute-start(bf16[32,6144]{1,0:T(8,128)(2,1)} %refs_1_.15), channel_id=1, source_target_pairs={{0,4},{1,3},{4,8},{5,1},{8,12},{9,5},{12,14},{13,9},{14,10},{15,13... | collective-permute-start | bytes 1179656 | tf_op jit(solution)/shard_map/ppermute | solution.py:330
  3.7 11.2 %collective-permute-start.3 = (bf16[32,6144]{1,0:T(8,128)(2,1)}, bf16[32,6144]{1,0:T(8,128)(2,1)S(1)}, u32[]{:S(2)}, u32[]{:S(2)}) collective-permute-start(bf16[32,6144]{1,0:T(8,128)(2,1)} %refs_1_.15), channel_id=1, source_target_pairs={{0,1},{1,0},{2,3},{3,2},{4,5},{5,4},{6,7},{7,6},{8,9},{9,8},{10,11... | collective-permute-start | bytes 1179656 | tf_op jit(solution)/shard_map/ppermute | solution.py:333
  3.7 13.3 %collective-permute-start.2 = (bf16[32,6144]{1,0:T(8,128)(2,1)}, bf16[32,6144]{1,0:T(8,128)(2,1)S(1)}, u32[]{:S(2)}, u32[]{:S(2)}) collective-permute-start(bf16[32,6144]{1,0:T(8,128)(2,1)} %refs_1_.15), channel_id=1, source_target_pairs={{0,3},{1,4},{4,1},{5,8},{8,5},{9,12},{12,9},{13,14},{14,13},{15,10... | collective-permute-start | bytes 1179656 | tf_op jit(solution)/shard_map/ppermute | solution.py:340
  12.5 6.2 %collective-permute-start.4 = (bf16[32,6144]{1,0:T(8,128)(2,1)S(1)}, bf16[32,6144]{1,0:T(8,128)(2,1)S(1)}, u32[]{:S(2)}, u32[]{:S(2)}) collective-permute-start(bf16[32,6144]{1,0:T(8,128)(2,1)S(1)} %collective-permute-done.refs_3_), channel_id=1, source_target_pairs={{0,1},{1,0},{2,3},{3,2},{4,5},{5,4},{6,7},{7,6},{8,9},{9,8},{10,11... | collective-permute-start | bytes 1179656 | tf_op jit(solution)/shard_map/ppermute | solution.py:333
  12.5 8.6 %collective-permute-start.1 = (bf16[32,6144]{1,0:T(8,128)(2,1)S(1)}, bf16[32,6144]{1,0:T(8,128)(2,1)S(1)}, u32[]{:S(2)}, u32[]{:S(2)}) collective-permute-start(bf16[32,6144]{1,0:T(8,128)(2,1)S(1)} %collective-permute-done.refs_3_), channel_id=1, source_target_pairs={{0,4},{1,3},{4,8},{5,1},{8,12},{9,5},{12,14},{13,9},{14,10},{15,13... | collective-permute-start | bytes 1179656 | tf_op jit(solution)/shard_map/ppermute | solution.py:330
  17.0 5.7 %collective-permute-start.7 = (bf16[32,6144]{1,0:T(8,128)(2,1)S(1)}, bf16[32,6144]{1,0:T(8,128)(2,1)S(1)}, u32[]{:S(2)}, u32[]{:S(2)}) collective-permute-start(bf16[32,6144]{1,0:T(8,128)(2,1)S(1)} %collective-permute-done.2.refs_4_), channel_id=1, source_target_pairs={{0,1},{1,0},{2,3},{3,2},{4,5},{5,4},{6,7},{7,6},{8,9},{9,8},{10,11... | collective-permute-start | bytes 1179656 | tf_op jit(solution)/shard_map/ppermute | solution.py:333
  17.7 7.8 %collective-permute-start.6 = (bf16[32,6144]{1,0:T(8,128)(2,1)S(1)}, bf16[32,6144]{1,0:T(8,128)(2,1)S(1)}, u32[]{:S(2)}, u32[]{:S(2)}) collective-permute-start(bf16[32,6144]{1,0:T(8,128)(2,1)S(1)} %collective-permute-done.2.refs_4_), channel_id=1, source_target_pairs={{0,4},{1,3},{4,8},{5,1},{8,12},{9,5},{12,14},{13,9},{14,10},{15,13... | collective-permute-start | bytes 1179656 | tf_op jit(solution)/shard_map/ppermute | solution.py:330
  21.1 4.4 %collective-permute-start.8 = (bf16[32,6144]{1,0:T(8,128)(2,1)S(1)}, bf16[32,6144]{1,0:T(8,128)(2,1)S(1)}, u32[]{:S(2)}, u32[]{:S(2)}) collective-permute-start(bf16[32,6144]{1,0:T(8,128)(2,1)S(1)} %collective-permute-done.1.refs_5_), channel_id=1, source_target_pairs={{0,1},{1,0},{2,3},{3,2},{4,5},{5,4},{6,7},{7,6},{8,9},{9,8},{10,11... | collective-permute-start | bytes 1179656 | tf_op jit(solution)/shard_map/ppermute | solution.py:333
  21.2 8.5 %collective-permute-start.5 = (bf16[32,6144]{1,0:T(8,128)(2,1)S(1)}, bf16[32,6144]{1,0:T(8,128)(2,1)S(1)}, u32[]{:S(2)}, u32[]{:S(2)}) collective-permute-start(bf16[32,6144]{1,0:T(8,128)(2,1)S(1)} %collective-permute-done.1.refs_5_), channel_id=1, source_target_pairs={{0,4},{1,3},{4,8},{5,1},{8,12},{9,5},{12,14},{13,9},{14,10},{15,13... | collective-permute-start | bytes 1179656 | tf_op jit(solution)/shard_map/ppermute | solution.py:330
  25.5 7.2 %collective-permute-start.12 = (bf16[32,6144]{1,0:T(8,128)(2,1)S(1)}, bf16[32,6144]{1,0:T(8,128)(2,1)S(1)}, u32[]{:S(2)}, u32[]{:S(2)}) collective-permute-start(bf16[32,6144]{1,0:T(8,128)(2,1)S(1)} %collective-permute-done.6.refs_6_), channel_id=1, source_target_pairs={{0,1},{1,0},{2,3},{3,2},{4,5},{5,4},{6,7},{7,6},{8,9},{9,8},{10,11... | collective-permute-start | bytes 1179656 | tf_op jit(solution)/shard_map/ppermute | solution.py:333
  29.7 5.3 %collective-permute-start.11 = (bf16[32,6144]{1,0:T(8,128)(2,1)S(1)}, bf16[32,6144]{1,0:T(8,128)(2,1)S(1)}, u32[]{:S(2)}, u32[]{:S(2)}) collective-permute-start(bf16[32,6144]{1,0:T(8,128)(2,1)S(1)} %collective-permute-done.5.refs_7_), channel_id=1, source_target_pairs={{0,1},{1,0},{2,3},{3,2},{4,5},{5,4},{6,7},{7,6},{8,9},{9,8},{10,11... | collective-permute-start | bytes 1179656 | tf_op jit(solution)/shard_map/ppermute | solution.py:333
  29.7 7.8 %collective-permute-start.10 = (bf16[32,6144]{1,0:T(8,128)(2,1)S(1)}, bf16[32,6144]{1,0:T(8,128)(2,1)S(1)}, u32[]{:S(2)}, u32[]{:S(2)}) collective-permute-start(bf16[32,6144]{1,0:T(8,128)(2,1)S(1)} %collective-permute-done.6.refs_6_), channel_id=1, source_target_pairs={{0,4},{1,3},{4,8},{5,1},{8,12},{9,5},{12,14},{13,9},{14,10},{15,13... | collective-permute-start | bytes 1179656 | tf_op jit(solution)/shard_map/ppermute | solution.py:330
  31.1 6.5 %collective-permute-start.13 = (bf16[64,3072]{1,0:T(8,128)(2,1)S(1)}, bf16[64,3072]{1,0:T(8,128)(2,1)S(1)}, u32[]{:S(2)}, u32[]{:S(2)}) collective-permute-start(bf16[64,3072]{1,0:T(8,128)(2,1)S(1)} %get-tuple-element.182), channel_id=1, source_target_pairs={{0,1},{1,0},{2,3},{3,2},{4,5},{5,4},{6,7},{7,6},{8,9},{9,8},{10,11... | collective-permute-start | bytes 1179656 | tf_op jit(solution)/shard_map/ppermute | solution.py:333
  31.8 9.9 %collective-permute-start.9 = (bf16[32,6144]{1,0:T(8,128)(2,1)S(1)}, bf16[32,6144]{1,0:T(8,128)(2,1)S(1)}, u32[]{:S(2)}, u32[]{:S(2)}) collective-permute-start(bf16[32,6144]{1,0:T(8,128)(2,1)S(1)} %collective-permute-done.5.refs_7_), channel_id=1, source_target_pairs={{0,4},{1,3},{4,8},{5,1},{8,12},{9,5},{12,14},{13,9},{14,10},{15,13... | collective-permute-start | bytes 1179656 | tf_op jit(solution)/shard_map/ppermute | solution.py:330
  32.7 5.3 %collective-permute-start.14 = (bf16[64,3072]{1,0:T(8,128)(2,1)S(1)}, bf16[64,3072]{1,0:T(8,128)(2,1)S(1)}, u32[]{:S(2)}, u32[]{:S(2)}) collective-permute-start(bf16[64,3072]{1,0:T(8,128)(2,1)S(1)} %get-tuple-element.183), channel_id=1, source_target_pairs={{0,1},{1,0},{2,3},{3,2},{4,5},{5,4},{6,7},{7,6},{8,9},{9,8},{10,11... | collective-permute-start | bytes 1179656 | tf_op jit(solution)/shard_map/ppermute | solution.py:333
  35.0 3.0 %collective-permute-start.15 = (bf16[64,3072]{1,0:T(8,128)(2,1)S(1)}, bf16[64,3072]{1,0:T(8,128)(2,1)S(1)}, u32[]{:S(2)}, u32[]{:S(2)}) collective-permute-start(bf16[64,3072]{1,0:T(8,128)(2,1)S(1)} %get-tuple-element.184), channel_id=1, source_target_pairs={{0,1},{1,0},{2,3},{3,2},{4,5},{5,4},{6,7},{7,6},{8,9},{9,8},{10,11... | collective-permute-start | bytes 1179656 | tf_op jit(solution)/shard_map/ppermute | solution.py:333
  37.5 4.2 %collective-permute-start.17 = (bf16[64,3072]{1,0:T(8,128)(2,1)S(1)}, bf16[64,3072]{1,0:T(8,128)(2,1)S(1)}, u32[]{:S(2)}, u32[]{:S(2)}) collective-permute-start(bf16[64,3072]{1,0:T(8,128)(2,1)S(1)} %get-tuple-element.196), channel_id=1, source_target_pairs={{0,1},{1,0},{2,3},{3,2},{4,5},{5,4},{6,7},{7,6},{8,9},{9,8},{10,11... | collective-permute-start | bytes 1179656 | tf_op jit(solution)/shard_map/ppermute | solution.py:333
  37.6 4.1 %collective-permute-start.16 = (bf16[32,6144]{1,0:T(8,128)(2,1)S(1)}, bf16[32,6144]{1,0:T(8,128)(2,1)S(1)}, u32[]{:S(2)}, u32[]{:S(2)}) collective-permute-start(bf16[32,6144]{1,0:T(8,128)(2,1)S(1)} %collective-permute-done.10.refs_8_), channel_id=1, source_target_pairs={{0,1},{1,0},{2,3},{3,2},{4,5},{5,4},{6,7},{7,6},{8,9},{9,8},{10,11... | collective-permute-start | bytes 1179656 | tf_op jit(solution)/shard_map/ppermute | solution.py:333
  41.7 4.6 %copy-start = (bf16[32,6144]{1,0:T(8,128)(2,1)S(1)}, bf16[32,6144]{1,0:T(8,128)(2,1)}, u32[]{:S(2)}) copy-start(bf16[32,6144]{1,0:T(8,128)(2,1)} %refs_1_.15) | copy-start | bytes 1179652
  43.6 2.7 %collective-permute-start.19 = (bf16[64,3072]{1,0:T(8,128)(2,1)S(1)}, bf16[64,3072]{1,0:T(8,128)(2,1)S(1)}, u32[]{:S(2)}, u32[]{:S(2)}) collective-permute-start(bf16[64,3072]{1,0:T(8,128)(2,1)S(1)} %get-tuple-element.213), channel_id=1, source_target_pairs={{0,1},{1,0},{2,3},{3,2},{4,5},{5,4},{6,7},{7,6},{8,9},{9,8},{10,11... | collective-permute-start | bytes 1179656 | tf_op jit(solution)/shard_map/ppermute | solution.py:333
  43.7 2.6 %collective-permute-start.20 = (bf16[32,6144]{1,0:T(8,128)(2,1)S(1)}, bf16[32,6144]{1,0:T(8,128)(2,1)S(1)}, u32[]{:S(2)}, u32[]{:S(2)}) collective-permute-start(bf16[32,6144]{1,0:T(8,128)(2,1)S(1)} %collective-permute-done.9.refs_9_), channel_id=1, source_target_pairs={{0,1},{1,0},{2,3},{3,2},{4,5},{5,4},{6,7},{7,6},{8,9},{9,8},{10,11... | collective-permute-start | bytes 1179656 | tf_op jit(solution)/shard_map/ppermute | solution.py:333
  44.2 4.8 %collective-permute-start.21 = (bf16[64,3072]{1,0:T(8,128)(2,1)S(1)}, bf16[64,3072]{1,0:T(8,128)(2,1)S(1)}, u32[]{:S(2)}, u32[]{:S(2)}) collective-permute-start(bf16[64,3072]{1,0:T(8,128)(2,1)S(1)} %get-tuple-element.218), channel_id=1, source_target_pairs={{0,1},{1,0},{2,3},{3,2},{4,5},{5,4},{6,7},{7,6},{8,9},{9,8},{10,11... | collective-permute-start | bytes 1179656 | tf_op jit(solution)/shard_map/ppermute | solution.py:333
  44.3 7.8 %collective-permute-start.18 = (bf16[64,3072]{1,0:T(8,128)(2,1)S(1)}, bf16[64,3072]{1,0:T(8,128)(2,1)S(1)}, u32[]{:S(2)}, u32[]{:S(2)}) collective-permute-start(bf16[64,3072]{1,0:T(8,128)(2,1)S(1)} %total.7), channel_id=1, source_target_pairs={{0,4},{1,3},{4,8},{5,1},{8,12},{9,5},{12,14},{13,9},{14,10},{15,13... | collective-permute-start | bytes 1179656 | tf_op jit(solution)/shard_map/ppermute | solution.py:330
  45.7 8.0 %collective-permute-start.24 = (bf16[64,3072]{1,0:T(8,128)(2,1)S(1)}, bf16[64,3072]{1,0:T(8,128)(2,1)S(1)}, u32[]{:S(2)}, u32[]{:S(2)}) collective-permute-start(bf16[64,3072]{1,0:T(8,128)(2,1)S(1)} %get-tuple-element.225), channel_id=1, source_target_pairs={{0,1},{1,0},{2,3},{3,2},{4,5},{5,4},{6,7},{7,6},{8,9},{9,8},{10,11... | collective-permute-start | bytes 1179656 | tf_op jit(solution)/shard_map/ppermute | solution.py:333
  47.9 8.4 %collective-permute-start.23 = (bf16[64,3072]{1,0:T(8,128)(2,1)S(1)}, bf16[64,3072]{1,0:T(8,128)(2,1)S(1)}, u32[]{:S(2)}, u32[]{:S(2)}) collective-permute-start(bf16[64,3072]{1,0:T(8,128)(2,1)S(1)} %total.8), channel_id=1, source_target_pairs={{0,4},{1,3},{4,8},{5,1},{8,12},{9,5},{12,14},{13,9},{14,10},{15,13... | collective-permute-start | bytes 1179656 | tf_op jit(solution)/shard_map/ppermute | solution.py:330
  52.2 8.3 %collective-permute-start.22 = (bf16[64,3072]{1,0:T(8,128)(2,1)S(1)}, bf16[64,3072]{1,0:T(8,128)(2,1)S(1)}, u32[]{:S(2)}, u32[]{:S(2)}) collective-permute-start(bf16[64,3072]{1,0:T(8,128)(2,1)S(1)} %total.9), channel_id=1, source_target_pairs={{0,4},{1,3},{4,8},{5,1},{8,12},{9,5},{12,14},{13,9},{14,10},{15,13... | collective-permute-start | bytes 1179656 | tf_op jit(solution)/shard_map/ppermute | solution.py:330
  56.4 8.3 %collective-permute-start.26 = (bf16[64,3072]{1,0:T(8,128)(2,1)S(1)}, bf16[64,3072]{1,0:T(8,128)(2,1)S(1)}, u32[]{:S(2)}, u32[]{:S(2)}) collective-permute-start(bf16[64,3072]{1,0:T(8,128)(2,1)S(1)} %total.10), channel_id=1, source_target_pairs={{0,4},{1,3},{4,8},{5,1},{8,12},{9,5},{12,14},{13,9},{14,10},{15,13... | collective-permute-start | bytes 1179656 | tf_op jit(solution)/shard_map/ppermute | solution.py:330
  60.7 8.3 %collective-permute-start.25 = (bf16[64,3072]{1,0:T(8,128)(2,1)S(1)}, bf16[64,3072]{1,0:T(8,128)(2,1)S(1)}, u32[]{:S(2)}, u32[]{:S(2)}) collective-permute-start(bf16[64,3072]{1,0:T(8,128)(2,1)S(1)} %total.11), channel_id=1, source_target_pairs={{0,4},{1,3},{4,8},{5,1},{8,12},{9,5},{12,14},{13,9},{14,10},{15,13... | collective-permute-start | bytes 1179656 | tf_op jit(solution)/shard_map/ppermute | solution.py:330
  64.9 8.3 %collective-permute-start.28 = (bf16[64,3072]{1,0:T(8,128)(2,1)S(1)}, bf16[64,3072]{1,0:T(8,128)(2,1)S(1)}, u32[]{:S(2)}, u32[]{:S(2)}) collective-permute-start(bf16[64,3072]{1,0:T(8,128)(2,1)S(1)} %total.12), channel_id=1, source_target_pairs={{0,4},{1,3},{4,8},{5,1},{8,12},{9,5},{12,14},{13,9},{14,10},{15,13... | collective-permute-start | bytes 1179656 | tf_op jit(solution)/shard_map/ppermute | solution.py:330
  69.1 8.3 %collective-permute-start.27 = (bf16[64,3072]{1,0:T(8,128)(2,1)S(1)}, bf16[64,3072]{1,0:T(8,128)(2,1)S(1)}, u32[]{:S(2)}, u32[]{:S(2)}) collective-permute-start(bf16[64,3072]{1,0:T(8,128)(2,1)S(1)} %total.13), channel_id=1, source_target_pairs={{0,4},{1,3},{4,8},{5,1},{8,12},{9,5},{12,14},{13,9},{14,10},{15,13... | collective-permute-start | bytes 1179656 | tf_op jit(solution)/shard_map/ppermute | solution.py:330
  77.4 1.5 %collective-permute-start.30 = (bf16[32,3072]{1,0:T(8,128)(2,1)S(1)}, bf16[32,3072]{1,0:T(8,128)(2,1)S(1)}, u32[]{:S(2)}, u32[]{:S(2)}) collective-permute-start(bf16[32,3072]{1,0:T(8,128)(2,1)S(1)} %get-tuple-element.253), channel_id=1, source_target_pairs={{0,1},{1,0},{2,3},{3,2},{4,5},{5,4},{6,7},{7,6},{8,9},{9,8},{10,11... | collective-permute-start | bytes 589832 | tf_op jit(solution)/shard_map/ppermute | solution.py:333
  77.5 1.7 %collective-permute-start.29 = (bf16[32,3072]{1,0:T(8,128)(2,1)S(1)}, bf16[32,3072]{1,0:T(8,128)(2,1)S(1)}, u32[]{:S(2)}, u32[]{:S(2)}) collective-permute-start(bf16[32,3072]{1,0:T(8,128)(2,1)S(1)} %get-tuple-element.247), channel_id=1, source_target_pairs={{0,1},{1,0},{2,3},{3,2},{4,5},{5,4},{6,7},{7,6},{8,9},{9,8},{10,11... | collective-permute-start | bytes 589832 | tf_op jit(solution)/shard_map/ppermute | solution.py:333

commit v7 on v6

--- a/solution.py
+++ b/solution.py
@@ -8,7 +8,7 @@
 from jax.sharding import PartitionSpec as P
 
 RING = 8
-PIECE_STEPS = 2
+PIECE_STEPS = 1
 PIECE_COST = 0.1
 PIECES = 4
 VMEM_LIMIT = 16 * 1024 * 1024
@@ -149,10 +149,9 @@
             sems.at[PIECE_STEPS, 0],
         )
         fetch.start()
-    steps = PIECE_STEPS if other else 1
-    step = wide // steps
+    step = wide // PIECE_STEPS
     stores = []
-    for i in range(steps):
+    for i in range(PIECE_STEPS):
         here = pl.ds(i * step, step)
         part = jnp.dot(w_ref[here, :], dht_ref[...], preferred_element_type=jnp.float32)
         part_ref[:, here] = part.astype(jnp.bfloat16).T
@@ -337,42 +336,40 @@
     )
     me = lax.axis_index("gx").astype(jnp.int32).reshape(1)
 
-    a1, b1 = ring(layer_input), lax.ppermute(layer_input, "gx", across)
-    twin = swap(layer_input)
+    a1, twin = ring(layer_input), swap(layer_input)
     dh, dht, w = hidden(me, out_grad, pre_act, weight)
+    b1 = lax.ppermute(after(layer_input, dh), "gx", across)
 
     def product(other, piece, w, before, *ties):
         return input_piece(me, after(dht, *ties), w, weight, before, other, piece)
 
-    a1 = after(a1, dh)
+    go, w = product(True, 0, w, ())
+    a1 = after(a1, go[0])
     a2, sa1 = ring(a1), swap(a1)
-    go, w = product(True, 0, w, (), a1, twin)
+    go, w = product(True, 1, w, go, a1, twin)
     b1 = after(b1, go[0])
     b2, sb1 = ring(b1), swap(b1)
-    go, w = product(True, 1, w, go, b1, sa1)
+    go, w = product(True, 2, w, go, b1, sa1)
     a2 = after(a2, go[0])
     a3, sa2 = ring(a2), swap(a2)
-    go, w = product(True, 2, w, go, a2, sb1)
+    go, w = product(True, 3, w, go, a2, sb1)
     b2 = after(b2, go[0])
     b3, sb2 = ring(b2), swap(b2)
-    go, w = product(True, 3, w, go, b2, sa2)
-    a3 = after(a3, go[0])
+    gm, w = product(False, 0, w, (), b2, sa2)
+    a3 = after(a3, gm[0])
     a4, sa3 = ring(a3), swap(a3)
-    gm, w = product(False, 0, w, (), a3, sb2)
     own_o, behind_o, opposite_o, ahead_o = go[0], go[1:4], go[4], go[5:]
-    from_m, opposite_from = [swap(x) for x in behind_o], swap(opposite_o)
-    gm, w = product(False, 1, w, gm, sa3)
-    b3 = after(b3, gm[0])
-    sb3 = swap(b3)
-    gm, w = product(False, 2, w, gm, b3, *from_m)
-    a4 = after(a4, gm[0])
-    sa4 = swap(a4)
-    gm, _ = product(False, 3, w, gm, a4, sb3, opposite_from)
+    opposite_from = swap(opposite_o)
+    gm, w = product(False, 1, w, gm, a3, sb2)
+    gm, w = product(False, 2, w, gm, sa3, opposite_from)
+    gm, _ = product(False, 3, w, gm, b3)
     own_m, behind_m, opposite_m, ahead_m = gm[0], gm[1:4], gm[4], gm[5:]
     sent = total(opposite_m, opposite_from)
     r4m = ring(sent)
-    from_o = [swap(after(x, sent)) for x in behind_m[::-1]][::-1]
-    blocks = (layer_input, twin, a1, b1, a2, b2, a3, b3, a4, sa4, sb1, sa1, sb2, sa2, sb3, sa3)
+    a4 = after(a4, sent)
+    sa4 = swap(a4)
+    from_o, from_m = [None] * 3, [None] * 3
+    from_o[2], from_m[2] = swap(after(behind_m[2], sent)), swap(after(behind_o[2], sent))
 
     def gradient(piece, before, *ties):
         before = before[::-1]
@@ -381,28 +378,32 @@
     def send(k, ahead, came, *ring_terms):
         return total(ahead[k - 1], came[k - 1], *ring_terms)
 
-    gw = gradient(0, (), sent, from_o[2])
-    sent = send(3, ahead_o, from_o[:2] + [after(from_o[2], gw[1])])
+    sent = send(3, ahead_o, from_o)
     r3o = ring(sent)
-    gw = gradient(1, gw, sent, from_o[1])
+    sb3 = swap(after(b3, sent))
+    blocks = (layer_input, twin, a1, b1, a2, b2, a3, b3, a4, sa4, sb1, sa1, sb2, sa2, sb3, sa3)
+    from_o[1], from_m[1] = swap(after(behind_m[1], sent)), swap(after(behind_o[1], sent))
+    gw = gradient(0, (), sent)
     sent = send(3, ahead_m, from_m, after(r4m, gw[1]))
     r3m = ring(sent)
-    gw = gradient(2, gw, sent, from_o[0])
+    from_o[0], from_m[0] = swap(after(behind_m[0], sent)), swap(after(behind_o[0], sent))
+    gw = gradient(1, gw, sent, from_o[1], from_m[1])
     sent = send(2, ahead_o, from_o, after(r3o, gw[1]))
     r2o = ring(sent)
-    gw = gradient(3, gw, sent)
+    gw = gradient(2, gw, sent, from_o[0], from_m[0])
     sent = send(2, ahead_m, from_m, after(r3m, gw[1]))
     r2m = ring(sent)
-    gw = gradient(4, gw, sent)
+    gw = gradient(3, gw, sent)
     sent = send(1, ahead_o, from_o, after(r2o, gw[1]))
     r1o = ring(sent)
-    gw = gradient(5, gw, sent)
+    gw = gradient(4, gw, sent)
     sent = send(1, ahead_m, from_m, after(r2m, gw[1]))
     r1m = ring(sent)
-    gw = gradient(6, gw, sent)
+    gw = gradient(5, gw, sent)
     kept_o, sent_o = halves(own_o, after(r1o, gw[1]))
     came_m = swap(sent_o)
-    gw = gradient(7, gw, sent_o)
+    gw = gradient(6, gw, sent_o)
+    gw = gradient(7, gw, came_m)
     kept_m, sent_m = halves(own_m, after(r1m, gw[0]))
     came_o = swap(sent_m)
     return (last(me, kept_m, came_m, kept_o, came_o), gw[0])

time: 80.3 us -> 77.7 us (0.968)
  waiting for transfers between devices: 19.4 us -> 13.5 us
  Pallas kernels: 34.6 us -> 38.3 us
    ppermute x13, waiting for transfers between devices: 18.2 us -> 11.2 us  [ring(): return lax.ppermute(x, 'gx', along)]
    pallas_call x8, Pallas kernels: 15.7 us -> 19.5 us  [input_piece(): pl.pallas_call(lambda *refs: input_kernel(*refs, other=other, piece=piece...]
    ppermute x17, waiting for transfers between devices: 1.25 us -> 2.32 us  [swap(): return lax.ppermute(x, 'gx', twins)]
  transfers between devices with their start and end apart: 31 -> 31, of which waited for: 15 -> 9; matrix products, arithmetic and copies ran while one was open for 0% -> 0% of each run, Pallas kernels for 40% -> 48%
where the time goes in v7:
time: 77.7 us; the launch traced here: 77.4 us
  Pallas kernels  38.3 us (49%)
  starting transfers between devices  24.6 us (32%)
  waiting for transfers between devices  13.5 us (17%)
  between operations  0.96 us (1%)
    ppermute x13, starting transfers between devices, ring(): return lax.ppermute(x, 'gx', along)  19.6 us
    pallas_call x8, Pallas kernels, input_piece(): pl.pallas_call(lambda *refs: input_kernel(*refs, other=other, piece=piece...  19.5 us
    pallas_call x8, Pallas kernels, weight_piece(): pl.pallas_call(lambda *refs: weight_kernel(*refs, piece=piece, wide=wide,...  13.1 us
    ppermute x13, waiting for transfers between devices, ring(): return lax.ppermute(x, 'gx', along)  11.2 us
    ppermute x17, starting transfers between devices, swap(): return lax.ppermute(x, 'gx', twins)  4.27 us
    pallas_call x1, Pallas kernels, hidden(): pl.pallas_call(hidden_kernel, out_shape=(jax.ShapeDtypeStruct(shape, dtyp...  3.85 us
    ppermute x17, waiting for transfers between devices, swap(): return lax.ppermute(x, 'gx', twins)  2.32 us
  transfers between devices with their start and end apart: 31, of which 9 were waited for; matrix products, arithmetic and copies ran while one was open for 0% of the time, Pallas kernels for 48%

profile of v7, /device:TPU:0, one launch (start us, length us, event | category | flops | bytes accessed | tf_op | source)
XLA Modules:
  0.0 77.4 jit_solution(14934711667155462379)
XLA Ops:
  0.6 3.1 %collective-permute-start.1 = (bf16[32,6144]{1,0:T(8,128)(2,1)}, bf16[32,6144]{1,0:T(8,128)(2,1)S(1)}, u32[]{:S(2)}, u32[]{:S(2)}) collective-permute-start(bf16[32,6144]{1,0:T(8,128)(2,1)} %refs_1_.15), channel_id=1, source_target_pairs={{0,4},{1,3},{4,8},{5,1},{8,12},{9,5},{12,14},{13,9},{14,10},{15,13... | collective-permute-start | bytes 1179656 | tf_op jit(solution)/shard_map/ppermute | solution.py:329
  3.7 3.9 %hidden.1 = (bf16[512,1536]{1,0:T(8,128)(2,1)S(1)}, bf16[1536,512]{1,0:T(8,128)(2,1)S(1)}, bf16[768,1536]{1,0:T(8,128)(2,1)S(1)}) custom-call(s32[1]{0:T(128)} %bitcast.me_ref.refs_0_, bf16[512,1536]{1,0:T(8,128)(2,1)} %og_hbm.1, bf16[512,1536]{1,0:T(8,128)(2,1)} %pre_hbm.1, bf16[6144,1536]{1,0:T(8,128)(2,1)} %refs_3_.15), custom_call_target="tpu_custom_call" | custom-call | flops 1150000000 | tf_op jit(solution)/shard_map/hidden/pallas_call | solution.py:115
  7.6 0.7 collective-permute-start
  8.3 3.1 %input_piece.8 = (bf16[64,3072]{1,0:T(8,128)(2,1)S(1)}, bf16[64,3072]{1,0:T(8,128)(2,1)S(1)}, bf16[64,3072]{1,0:T(8,128)(2,1)S(1)}, bf16[64,3072]{1,0:T(8,128)(2...) custom-call(s32[1]{0:T(128)} %bitcast.me_ref.refs_0_, ...), custom_call_target="tpu_custom_call" | custom-call | flops 115000000 | tf_op jit(solution)/shard_map/input_piece/pallas_call | solution.py:181
  11.4 1.1 %collective-permute-start.5 = (bf16[32,6144]{1,0:T(8,128)(2,1)S(1)}, bf16[32,6144]{1,0:T(8,128)(2,1)S(1)}, u32[]{:S(2)}, u32[]{:S(2)}) collective-permute-start(bf16[32,6144]{1,0:T(8,128)(2,1)S(1)} %collective-permute-done.1.refs_3_), channel_id=1, source_target_pairs={{0,1},{1,0},{2,3},{3,2},{4,5},{5,4},{6,7},{7,6},{8,9},{9,8},{10,11... | collective-permute-start | bytes 1179656 | tf_op jit(solution)/shard_map/ppermute | solution.py:332
  12.5 1.6 %collective-permute-start.4 = (bf16[32,6144]{1,0:T(8,128)(2,1)S(1)}, bf16[32,6144]{1,0:T(8,128)(2,1)S(1)}, u32[]{:S(2)}, u32[]{:S(2)}) collective-permute-start(bf16[32,6144]{1,0:T(8,128)(2,1)S(1)} %collective-permute-done.1.refs_3_), channel_id=1, source_target_pairs={{0,4},{1,3},{4,8},{5,1},{8,12},{9,5},{12,14},{13,9},{14,10},{15,13... | collective-permute-start | bytes 1179656 | tf_op jit(solution)/shard_map/ppermute | solution.py:329
  14.1 3.1 %input_piece.9 = (bf16[64,3072]{1,0:T(8,128)(2,1)S(1)}, bf16[64,3072]{1,0:T(8,128)(2,1)S(1)}, bf16[64,3072]{1,0:T(8,128)(2,1)S(1)}, bf16[64,3072]{1,0:T(8,128)(2...) custom-call(s32[1]{0:T(128)} %bitcast.me_ref.refs_0_, ...), custom_call_target="tpu_custom_call", output_to_operand_aliasing={{0}: (4, {}), {1}: (5, {}), {2}: (6, {}), {3}: (7, {}), {4}... | custom-call | flops 115000000 | tf_op jit(solution)/shard_map/input_piece/pallas_call | solution.py:181
  17.1 0.1 collective-permute-start.6
  17.2 1.6 %collective-permute-start.3 = (bf16[32,6144]{1,0:T(8,128)(2,1)S(1)}, bf16[32,6144]{1,0:T(8,128)(2,1)S(1)}, u32[]{:S(2)}, u32[]{:S(2)}) collective-permute-start(bf16[32,6144]{1,0:T(8,128)(2,1)S(1)} %collective-permute-done.refs_4_), channel_id=1, source_target_pairs={{0,4},{1,3},{4,8},{5,1},{8,12},{9,5},{12,14},{13,9},{14,10},{15,13... | collective-permute-start | bytes 1179656 | tf_op jit(solution)/shard_map/ppermute | solution.py:329
  18.8 3.1 %input_piece.10 = (bf16[64,3072]{1,0:T(8,128)(2,1)S(1)}, bf16[64,3072]{1,0:T(8,128)(2,1)S(1)}, bf16[64,3072]{1,0:T(8,128)(2,1)S(1)}, bf16[64,3072]{1,0:T(8,128)(...) custom-call(s32[1]{0:T(128)} %bitcast.me_ref.refs_0_, ...), custom_call_target="tpu_custom_call", output_to_operand_aliasing={{0}: (4, {}), {1}: (5, {}), {2}: (6, {}), {3}: (7, {}), {4}... | custom-call | flops 115000000 | tf_op jit(solution)/shard_map/input_piece/pallas_call | solution.py:181
  21.9 0.1 collective-permute-start.9
  21.9 0.7 collective-permute-start.8
  22.6 3.1 %input_piece.11 = (bf16[64,3072]{1,0:T(8,128)(2,1)S(1)}, bf16[64,3072]{1,0:T(8,128)(2,1)S(1)}, bf16[64,3072]{1,0:T(8,128)(2,1)S(1)}, bf16[64,3072]{1,0:T(8,128)(...) custom-call(s32[1]{0:T(128)} %bitcast.me_ref.refs_0_, ...), custom_call_target="tpu_custom_call", output_to_operand_aliasing={{0}: (4, {}), {1}: (5, {}), {2}: (6, {}), {3}: (7, {}), {4}... | custom-call | flops 115000000 | tf_op jit(solution)/shard_map/input_piece/pallas_call | solution.py:181
  25.7 1.9 %collective-permute-start.7 = (bf16[32,6144]{1,0:T(8,128)(2,1)S(1)}, bf16[32,6144]{1,0:T(8,128)(2,1)S(1)}, u32[]{:S(2)}, u32[]{:S(2)}) collective-permute-start(bf16[32,6144]{1,0:T(8,128)(2,1)S(1)} %collective-permute-done.3.refs_6_), channel_id=1, source_target_pairs={{0,4},{1,3},{4,8},{5,1},{8,12},{9,5},{12,14},{13,9},{14,10},{15,13... | collective-permute-start | bytes 1179656 | tf_op jit(solution)/shard_map/ppermute | solution.py:329
  27.6 0.5 collective-permute-start.11
  28.1 1.8 %input_piece.12 = (bf16[64,3072]{1,0:T(8,128)(2,1)S(1)}, bf16[64,3072]{1,0:T(8,128)(2,1)S(1)}, bf16[64,3072]{1,0:T(8,128)(2,1)S(1)}, bf16[64,3072]{1,0:T(8,128)(...) custom-call(s32[1]{0:T(128)} %bitcast.me_ref.refs_0_, ...), custom_call_target="tpu_custom_call" | custom-call | flops 115000000 | tf_op jit(solution)/shard_map/input_piece/pallas_call | solution.py:181
  30.0 0.1 collective-permute-start.10
  30.1 0.7 collective-permute-start.16
  30.8 3.2 %collective-permute-done.7.refs_8_ = bf16[32,6144]{1,0:T(8,128)(2,1)S(1)} collective-permute-done((bf16[32,6144]{1,0:T(8,128)(2,1)S(1)}, bf16[32,6144]{1,0:T(8,128)(2,1)S(1)}, u32[]{:S(2)}, u32[]{:S(2)}) %collective-permute-start.7) | collective-permute-done | bytes 393248 | tf_op jit(solution)/shard_map/ppermute | solution.py:329
  34.0 1.8 %input_piece.13 = (bf16[64,3072]{1,0:T(8,128)(2,1)S(1)}, bf16[64,3072]{1,0:T(8,128)(2,1)S(1)}, bf16[64,3072]{1,0:T(8,128)(2,1)S(1)}, bf16[64,3072]{1,0:T(8,128)(...) custom-call(s32[1]{0:T(128)} %bitcast.me_ref.refs_0_, ...), custom_call_target="tpu_custom_call", output_to_operand_aliasing={{0}: (4, {}), {1}: (5, {}), {2}: (6, {}), {3}: (7, {}), {4}... | custom-call | flops 115000000 | tf_op jit(solution)/shard_map/input_piece/pallas_call | solution.py:181
  35.8 1.8 %input_piece.14 = (bf16[64,3072]{1,0:T(8,128)(2,1)S(1)}, bf16[64,3072]{1,0:T(8,128)(2,1)S(1)}, bf16[64,3072]{1,0:T(8,128)(2,1)S(1)}, bf16[64,3072]{1,0:T(8,128)(...) custom-call(s32[1]{0:T(128)} %bitcast.me_ref.refs_0_, ...), custom_call_target="tpu_custom_call", output_to_operand_aliasing={{0}: (4, {}), {1}: (5, {}), {2}: (6, {}), {3}: (7, {}), {4}... | custom-call | flops 115000000 | tf_op jit(solution)/shard_map/input_piece/pallas_call | solution.py:181
  37.7 1.7 %input_piece.15 = (bf16[64,3072]{1,0:T(8,128)(2,1)S(1)}, bf16[64,3072]{1,0:T(8,128)(2,1)S(1)}, bf16[64,3072]{1,0:T(8,128)(2,1)S(1)}, bf16[64,3072]{1,0:T(8,128)(...) custom-call(s32[1]{0:T(128)} %bitcast.me_ref.refs_0_, ...), custom_call_target="tpu_custom_call", output_to_operand_aliasing={{0}: (4, {}), {1}: (5, {}), {2}: (6, {}), {3}: (7, {}), {4}... | custom-call | flops 115000000 | tf_op jit(solution)/shard_map/input_piece/pallas_call | solution.py:181
  39.4 0.1 total.7
  39.6 0.1 collective-permute-start.15
  39.6 0.5 collective-permute-start.17
  40.1 1.2 %collective-permute-done.15.twin_ref = bf16[64,3072]{1,0:T(8,128)(2,1)S(1)} collective-permute-done((bf16[64,3072]{1,0:T(8,128)(2,1)S(1)}, bf16[64,3072]{1,0:T(8,128)(2,1)S(1)}, u32[]{:S(2)}, u32[]{:S(2)}) %collective-permute-start.15) | collective-permute-done | bytes 393248 | tf_op jit(solution)/shard_map/ppermute | solution.py:332
  41.3 0.1 total.8
  41.4 0.2 collective-permute-start.18
  41.6 1.4 %collective-permute-start.14 = (bf16[64,3072]{1,0:T(8,128)(2,1)S(1)}, bf16[64,3072]{1,0:T(8,128)(2,1)S(1)}, u32[]{:S(2)}, u32[]{:S(2)}) collective-permute-start(bf16[64,3072]{1,0:T(8,128)(2,1)S(1)} %total.7), channel_id=1, source_target_pairs={{0,4},{1,3},{4,8},{5,1},{8,12},{9,5},{12,14},{13,9},{14,10},{15,13... | collective-permute-start | bytes 1179656 | tf_op jit(solution)/shard_map/ppermute | solution.py:329
  43.1 0.5 collective-permute-start.20
  43.6 0.0 collective-permute-start.22
  43.6 1.3 %collective-permute-start.23 = (bf16[64,3072]{1,0:T(8,128)(2,1)S(1)}, bf16[64,3072]{1,0:T(8,128)(2,1)S(1)}, u32[]{:S(2)}, u32[]{:S(2)}) collective-permute-start(bf16[64,3072]{1,0:T(8,128)(2,1)S(1)} %total.8), channel_id=1, source_target_pairs={{0,4},{1,3},{4,8},{5,1},{8,12},{9,5},{12,14},{13,9},{14,10},{15,13... | collective-permute-start | bytes 1179656 | tf_op jit(solution)/shard_map/ppermute | solution.py:329
  44.9 1.5 %weight_piece.8 = (bf16[6144,1536]{1,0:T(8,128)(2,1)}, bf16[768,1536]{1,0:T(8,128)(2,1)S(1)}) custom-call(bf16[512,1536]{1,0:T(8,128)(2,1)S(1)} %get-tuple-element.250.refs_0_, bf16[32,6144]{1,0:T(8,128)(2,1)S(1)} %copy-done, bf16[32,6144]{1,0:T(8,128)(2,1)S(1)} %collective-permute-done.2.refs_2_, bf16[32,6144]{1,0:T(8,128)(2,1)S(1)} %collective-permute-done.1.refs_3_, ...), custom_call_target="tpu_custom_call" | custom-call | flops 115000000 | tf_op jit(solution)/shard_map/weight_piece/pallas_call | solution.py:235
  46.4 3.0 %collective-permute-done.14.refs_0_ = bf16[64,3072]{1,0:T(8,128)(2,1)S(1)} collective-permute-done((bf16[64,3072]{1,0:T(8,128)(2,1)S(1)}, bf16[64,3072]{1,0:T(8,128)(2,1)S(1)}, u32[]{:S(2)}, u32[]{:S(2)}) %collective-permute-start.14) | collective-permute-done | bytes 393248 | tf_op jit(solution)/shard_map/ppermute | solution.py:329
  49.4 0.1 total.9
  49.6 0.1 collective-permute-start.19
  49.6 0.5 collective-permute-start.24
  50.1 1.4 %collective-permute-start.21 = (bf16[64,3072]{1,0:T(8,128)(2,1)S(1)}, bf16[64,3072]{1,0:T(8,128)(2,1)S(1)}, u32[]{:S(2)}, u32[]{:S(2)}) collective-permute-start(bf16[64,3072]{1,0:T(8,128)(2,1)S(1)} %total.9), channel_id=1, source_target_pairs={{0,4},{1,3},{4,8},{5,1},{8,12},{9,5},{12,14},{13,9},{14,10},{15,13... | collective-permute-start | bytes 1179656 | tf_op jit(solution)/shard_map/ppermute | solution.py:329
  51.6 1.5 %weight_piece.9 = (bf16[6144,1536]{1,0:T(8,128)(2,1)}, bf16[768,1536]{1,0:T(8,128)(2,1)S(1)}) custom-call(bf16[512,1536]{1,0:T(8,128)(2,1)S(1)} %get-tuple-element.250.refs_0_, bf16[32,6144]{1,0:T(8,128)(2,1)S(1)} %copy-done, bf16[32,6144]{1,0:T(8,128)(2,1)S(1)} %collective-permute-done.2.refs_2_, ...), custom_call_target="tpu_custom_call", output_to_operand_aliasing={{0}: (18, {})} | custom-call | flops 115000000 | tf_op jit(solution)/shard_map/weight_piece/pallas_call | solution.py:235
  53.1 0.6 collective-permute-done.23.refs_0_
  53.6 0.1 total.10
  53.8 1.5 %collective-permute-start.26 = (bf16[64,3072]{1,0:T(8,128)(2,1)S(1)}, bf16[64,3072]{1,0:T(8,128)(2,1)S(1)}, u32[]{:S(2)}, u32[]{:S(2)}) collective-permute-start(bf16[64,3072]{1,0:T(8,128)(2,1)S(1)} %total.10), channel_id=1, source_target_pairs={{0,4},{1,3},{4,8},{5,1},{8,12},{9,5},{12,14},{13,9},{14,10},{15,13... | collective-permute-start | bytes 1179656 | tf_op jit(solution)/shard_map/ppermute | solution.py:329
  55.3 1.5 %weight_piece.10 = (bf16[6144,1536]{1,0:T(8,128)(2,1)}, bf16[768,1536]{1,0:T(8,128)(2,1)S(1)}) custom-call(bf16[512,1536]{1,0:T(8,128)(2,1)S(1)} %get-tuple-element.250.refs_0_, bf16[32,6144]{1,0:T(8,128)(2,1)S(1)} %copy-done, bf16[32,6144]{1,0:T(8,128)(2,1)S(1)} %collective-permute-done.2.refs_2_, ...), custom_call_target="tpu_custom_call", output_to_operand_aliasing={{0}: (18, {})} | custom-call | flops 115000000 | tf_op jit(solution)/shard_map/weight_piece/pallas_call | solution.py:235
  56.8 1.1 %collective-permute-done.21.refs_0_ = bf16[64,3072]{1,0:T(8,128)(2,1)S(1)} collective-permute-done((bf16[64,3072]{1,0:T(8,128)(2,1)S(1)}, bf16[64,3072]{1,0:T(8,128)(2,1)S(1)}, u32[]{:S(2)}, u32[]{:S(2)}) %collective-permute-start.21) | collective-permute-done | bytes 393248 | tf_op jit(solution)/shard_map/ppermute | solution.py:329
  57.9 0.1 total.11
  58.1 1.5 %collective-permute-start.25 = (bf16[64,3072]{1,0:T(8,128)(2,1)S(1)}, bf16[64,3072]{1,0:T(8,128)(2,1)S(1)}, u32[]{:S(2)}, u32[]{:S(2)}) collective-permute-start(bf16[64,3072]{1,0:T(8,128)(2,1)S(1)} %total.11), channel_id=1, source_target_pairs={{0,4},{1,3},{4,8},{5,1},{8,12},{9,5},{12,14},{13,9},{14,10},{15,13... | collective-permute-start | bytes 1179656 | tf_op jit(solution)/shard_map/ppermute | solution.py:329
  59.5 1.5 %weight_piece.11 = (bf16[6144,1536]{1,0:T(8,128)(2,1)}, bf16[768,1536]{1,0:T(8,128)(2,1)S(1)}) custom-call(bf16[512,1536]{1,0:T(8,128)(2,1)S(1)} %get-tuple-element.250.refs_0_, bf16[32,6144]{1,0:T(8,128)(2,1)S(1)} %copy-done, bf16[32,6144]{1,0:T(8,128)(2,1)S(1)} %collective-permute-done.2.refs_2_, ...), custom_call_target="tpu_custom_call", output_to_operand_aliasing={{0}: (18, {})} | custom-call | flops 115000000 | tf_op jit(solution)/shard_map/weight_piece/pallas_call | solution.py:235
  61.1 1.1 %collective-permute-done.26.refs_0_ = bf16[64,3072]{1,0:T(8,128)(2,1)S(1)} collective-permute-done((bf16[64,3072]{1,0:T(8,128)(2,1)S(1)}, bf16[64,3072]{1,0:T(8,128)(2,1)S(1)}, u32[]{:S(2)}, u32[]{:S(2)}) %collective-permute-start.26) | collective-permute-done | bytes 393248 | tf_op jit(solution)/shard_map/ppermute | solution.py:329
  62.1 0.1 total.12
  62.3 1.5 %collective-permute-start.28 = (bf16[64,3072]{1,0:T(8,128)(2,1)S(1)}, bf16[64,3072]{1,0:T(8,128)(2,1)S(1)}, u32[]{:S(2)}, u32[]{:S(2)}) collective-permute-start(bf16[64,3072]{1,0:T(8,128)(2,1)S(1)} %total.12), channel_id=1, source_target_pairs={{0,4},{1,3},{4,8},{5,1},{8,12},{9,5},{12,14},{13,9},{14,10},{15,13... | collective-permute-start | bytes 1179656 | tf_op jit(solution)/shard_map/ppermute | solution.py:329
  63.8 1.5 %weight_piece.12 = (bf16[6144,1536]{1,0:T(8,128)(2,1)}, bf16[768,1536]{1,0:T(8,128)(2,1)S(1)}) custom-call(bf16[512,1536]{1,0:T(8,128)(2,1)S(1)} %get-tuple-element.250.refs_0_, bf16[32,6144]{1,0:T(8,128)(2,1)S(1)} %copy-done, bf16[32,6144]{1,0:T(8,128)(2,1)S(1)} %collective-permute-done.2.refs_2_, ...), custom_call_target="tpu_custom_call", output_to_operand_aliasing={{0}: (18, {})} | custom-call | flops 115000000 | tf_op jit(solution)/shard_map/weight_piece/pallas_call | solution.py:235
  65.3 1.1 %collective-permute-done.25.refs_0_ = bf16[64,3072]{1,0:T(8,128)(2,1)S(1)} collective-permute-done((bf16[64,3072]{1,0:T(8,128)(2,1)S(1)}, bf16[64,3072]{1,0:T(8,128)(2,1)S(1)}, u32[]{:S(2)}, u32[]{:S(2)}) %collective-permute-start.25) | collective-permute-done | bytes 393248 | tf_op jit(solution)/shard_map/ppermute | solution.py:329
  66.3 0.1 total.13
  66.5 1.5 %collective-permute-start.27 = (bf16[64,3072]{1,0:T(8,128)(2,1)S(1)}, bf16[64,3072]{1,0:T(8,128)(2,1)S(1)}, u32[]{:S(2)}, u32[]{:S(2)}) collective-permute-start(bf16[64,3072]{1,0:T(8,128)(2,1)S(1)} %total.13), channel_id=1, source_target_pairs={{0,4},{1,3},{4,8},{5,1},{8,12},{9,5},{12,14},{13,9},{14,10},{15,13... | collective-permute-start | bytes 1179656 | tf_op jit(solution)/shard_map/ppermute | solution.py:329
  68.0 1.5 %weight_piece.13 = (bf16[6144,1536]{1,0:T(8,128)(2,1)}, bf16[768,1536]{1,0:T(8,128)(2,1)S(1)}) custom-call(bf16[512,1536]{1,0:T(8,128)(2,1)S(1)} %get-tuple-element.250.refs_0_, bf16[32,6144]{1,0:T(8,128)(2,1)S(1)} %copy-done, bf16[32,6144]{1,0:T(8,128)(2,1)S(1)} %collective-permute-done.2.refs_2_, ...), custom_call_target="tpu_custom_call", output_to_operand_aliasing={{0}: (18, {})} | custom-call | flops 115000000 | tf_op jit(solution)/shard_map/weight_piece/pallas_call | solution.py:235
  69.5 1.1 %collective-permute-done.28.came_ref = bf16[64,3072]{1,0:T(8,128)(2,1)S(1)} collective-permute-done((bf16[64,3072]{1,0:T(8,128)(2,1)S(1)}, bf16[64,3072]{1,0:T(8,128)(2,1)S(1)}, u32[]{:S(2)}, u32[]{:S(2)}) %collective-permute-start.28) | collective-permute-done | bytes 393248 | tf_op jit(solution)/shard_map/ppermute | solution.py:329
  70.6 0.1 halves.2
  70.7 0.1 collective-permute-start.29
  70.7 1.5 %weight_piece.14 = (bf16[6144,1536]{1,0:T(8,128)(2,1)}, bf16[768,1536]{1,0:T(8,128)(2,1)S(1)}) custom-call(bf16[512,1536]{1,0:T(8,128)(2,1)S(1)} %get-tuple-element.250.refs_0_, bf16[32,6144]{1,0:T(8,128)(2,1)S(1)} %copy-done, bf16[32,6144]{1,0:T(8,128)(2,1)S(1)} %collective-permute-done.2.refs_2_, ...), custom_call_target="tpu_custom_call", output_to_operand_aliasing={{0}: (18, {})} | custom-call | flops 115000000 | tf_op jit(solution)/shard_map/weight_piece/pallas_call | solution.py:235
  72.3 2.5 %weight_piece.15 = bf16[6144,1536]{1,0:T(8,128)(2,1)} custom-call(bf16[512,1536]{1,0:T(8,128)(2,1)S(1)} %get-tuple-element.250.refs_0_, bf16[32,6144]{1,0:T(8,128)(2,1)S(1)} %copy-done, bf16[32,6144]{1,0:T(8,128)(2,1)S(1)} %collective-permute-done.2.refs_2_, bf16[32,6144]{1,0:T(8,128)(2,1)S(1)} %collective-permute-done.1.refs_3_, ...), custom_call_target="tpu_custom_call", output_to_operand_aliasing={{}: (18, {})} | custom-call | flops 115000000 | tf_op jit(solution)/shard_map/weight_piece/pallas_call | solution.py:235
  74.8 0.1 halves.3
  74.9 0.6 collective-permute-start.30
  75.5 1.1 %collective-permute-done.30.other_came_ref = bf16[32,3072]{1,0:T(8,128)(2,1)S(1)} collective-permute-done((bf16[32,3072]{1,0:T(8,128)(2,1)S(1)}, bf16[32,3072]{1,0:T(8,128)(2,1)S(1)}, u32[]{:S(2)}, u32[]{:S(2)}) %collective-permute-start.30) | collective-permute-done | bytes 196640 | tf_op jit(solution)/shard_map/ppermute | solution.py:332
  76.6 0.8 %last.1 = bf16[32,6144]{1,0:T(8,128)(2,1)} custom-call(s32[1]{0:T(128)} %bitcast.me_ref.refs_0_, f32[32,3072]{1,0:T(8,128)S(1)} %get-tuple-element.255.mine_ref, bf16[32,3072]{1,0:T(8,128)(2,1)S(1)} %collective-permute-done.29.mine_came_ref, f32[32,3072]{1,0:T(8,128)S(1)} %get-tuple-element.256.other_ref, ...), custom_call_target="tpu_custom_call" | custom-call | flops 345000000 | tf_op jit(solution)/shard_map/last/pallas_call | solution.py:304
  (27 shorter events, 0.1 us)
Async XLA Ops:
  0.6 10.8 %collective-permute-start.1 = (bf16[32,6144]{1,0:T(8,128)(2,1)}, bf16[32,6144]{1,0:T(8,128)(2,1)S(1)}, u32[]{:S(2)}, u32[]{:S(2)}) collective-permute-start(bf16[32,6144]{1,0:T(8,128)(2,1)} %refs_1_.15), channel_id=1, source_target_pairs={{0,4},{1,3},{4,8},{5,1},{8,12},{9,5},{12,14},{13,9},{14,10},{15,13... | collective-permute-start | bytes 1179656 | tf_op jit(solution)/shard_map/ppermute | solution.py:329
  3.7 10.4 %collective-permute-start.2 = (bf16[32,6144]{1,0:T(8,128)(2,1)}, bf16[32,6144]{1,0:T(8,128)(2,1)S(1)}, u32[]{:S(2)}, u32[]{:S(2)}) collective-permute-start(bf16[32,6144]{1,0:T(8,128)(2,1)} %refs_1_.15), channel_id=1, source_target_pairs={{0,1},{1,0},{2,3},{3,2},{4,5},{5,4},{6,7},{7,6},{8,9},{9,8},{10,11... | collective-permute-start | bytes 1179656 | tf_op jit(solution)/shard_map/ppermute | solution.py:332
  3.7 3.9 %copy-start = (bf16[32,6144]{1,0:T(8,128)(2,1)S(1)}, bf16[32,6144]{1,0:T(8,128)(2,1)}, u32[]{:S(2)}) copy-start(bf16[32,6144]{1,0:T(8,128)(2,1)} %refs_1_.15) | copy-start | bytes 1179652
  7.6 9.5 %collective-permute-start = (bf16[32,6144]{1,0:T(8,128)(2,1)S(1)}, bf16[32,6144]{1,0:T(8,128)(2,1)S(1)}, u32[]{:S(2)}, u32[]{:S(2)}) collective-permute-start(bf16[32,6144]{1,0:T(8,128)(2,1)S(1)} %copy-done), channel_id=1, source_target_pairs={{0,3},{1,4},{4,1},{5,8},{8,5},{9,12},{12,9},{13,14},{14,13},{15,10... | collective-permute-start | bytes 1179656 | tf_op jit(solution)/shard_map/ppermute | solution.py:341
  11.4 7.4 %collective-permute-start.5 = (bf16[32,6144]{1,0:T(8,128)(2,1)S(1)}, bf16[32,6144]{1,0:T(8,128)(2,1)S(1)}, u32[]{:S(2)}, u32[]{:S(2)}) collective-permute-start(bf16[32,6144]{1,0:T(8,128)(2,1)S(1)} %collective-permute-done.1.refs_3_), channel_id=1, source_target_pairs={{0,1},{1,0},{2,3},{3,2},{4,5},{5,4},{6,7},{7,6},{8,9},{9,8},{10,11... | collective-permute-start | bytes 1179656 | tf_op jit(solution)/shard_map/ppermute | solution.py:332
  12.5 9.4 %collective-permute-start.4 = (bf16[32,6144]{1,0:T(8,128)(2,1)S(1)}, bf16[32,6144]{1,0:T(8,128)(2,1)S(1)}, u32[]{:S(2)}, u32[]{:S(2)}) collective-permute-start(bf16[32,6144]{1,0:T(8,128)(2,1)S(1)} %collective-permute-done.1.refs_3_), channel_id=1, source_target_pairs={{0,4},{1,3},{4,8},{5,1},{8,12},{9,5},{12,14},{13,9},{14,10},{15,13... | collective-permute-start | bytes 1179656 | tf_op jit(solution)/shard_map/ppermute | solution.py:329
  17.1 5.5 %collective-permute-start.6 = (bf16[32,6144]{1,0:T(8,128)(2,1)S(1)}, bf16[32,6144]{1,0:T(8,128)(2,1)S(1)}, u32[]{:S(2)}, u32[]{:S(2)}) collective-permute-start(bf16[32,6144]{1,0:T(8,128)(2,1)S(1)} %collective-permute-done.refs_4_), channel_id=1, source_target_pairs={{0,1},{1,0},{2,3},{3,2},{4,5},{5,4},{6,7},{7,6},{8,9},{9,8},{10,11... | collective-permute-start | bytes 1179656 | tf_op jit(solution)/shard_map/ppermute | solution.py:332
  17.2 8.5 %collective-permute-start.3 = (bf16[32,6144]{1,0:T(8,128)(2,1)S(1)}, bf16[32,6144]{1,0:T(8,128)(2,1)S(1)}, u32[]{:S(2)}, u32[]{:S(2)}) collective-permute-start(bf16[32,6144]{1,0:T(8,128)(2,1)S(1)} %collective-permute-done.refs_4_), channel_id=1, source_target_pairs={{0,4},{1,3},{4,8},{5,1},{8,12},{9,5},{12,14},{13,9},{14,10},{15,13... | collective-permute-start | bytes 1179656 | tf_op jit(solution)/shard_map/ppermute | solution.py:329
  21.9 6.3 %collective-permute-start.9 = (bf16[32,6144]{1,0:T(8,128)(2,1)S(1)}, bf16[32,6144]{1,0:T(8,128)(2,1)S(1)}, u32[]{:S(2)}, u32[]{:S(2)}) collective-permute-start(bf16[32,6144]{1,0:T(8,128)(2,1)S(1)} %collective-permute-done.4.refs_5_), channel_id=1, source_target_pairs={{0,1},{1,0},{2,3},{3,2},{4,5},{5,4},{6,7},{7,6},{8,9},{9,8},{10,11... | collective-permute-start | bytes 1179656 | tf_op jit(solution)/shard_map/ppermute | solution.py:332
  21.9 8.0 %collective-permute-start.8 = (bf16[32,6144]{1,0:T(8,128)(2,1)S(1)}, bf16[32,6144]{1,0:T(8,128)(2,1)S(1)}, u32[]{:S(2)}, u32[]{:S(2)}) collective-permute-start(bf16[32,6144]{1,0:T(8,128)(2,1)S(1)} %collective-permute-done.4.refs_5_), channel_id=1, source_target_pairs={{0,4},{1,3},{4,8},{5,1},{8,12},{9,5},{12,14},{13,9},{14,10},{15,13... | collective-permute-start | bytes 1179656 | tf_op jit(solution)/shard_map/ppermute | solution.py:329
  25.7 8.3 %collective-permute-start.7 = (bf16[32,6144]{1,0:T(8,128)(2,1)S(1)}, bf16[32,6144]{1,0:T(8,128)(2,1)S(1)}, u32[]{:S(2)}, u32[]{:S(2)}) collective-permute-start(bf16[32,6144]{1,0:T(8,128)(2,1)S(1)} %collective-permute-done.3.refs_6_), channel_id=1, source_target_pairs={{0,4},{1,3},{4,8},{5,1},{8,12},{9,5},{12,14},{13,9},{14,10},{15,13... | collective-permute-start | bytes 1179656 | tf_op jit(solution)/shard_map/ppermute | solution.py:329
  27.6 6.4 %collective-permute-start.12 = (bf16[32,6144]{1,0:T(8,128)(2,1)S(1)}, bf16[32,6144]{1,0:T(8,128)(2,1)S(1)}, u32[]{:S(2)}, u32[]{:S(2)}) collective-permute-start(bf16[32,6144]{1,0:T(8,128)(2,1)S(1)} %collective-permute-done.3.refs_6_), channel_id=1, source_target_pairs={{0,1},{1,0},{2,3},{3,2},{4,5},{5,4},{6,7},{7,6},{8,9},{9,8},{10,11... | collective-permute-start | bytes 1179656 | tf_op jit(solution)/shard_map/ppermute | solution.py:332
  27.6 8.2 %collective-permute-start.11 = (bf16[64,3072]{1,0:T(8,128)(2,1)S(1)}, bf16[64,3072]{1,0:T(8,128)(2,1)S(1)}, u32[]{:S(2)}, u32[]{:S(2)}) collective-permute-start(bf16[64,3072]{1,0:T(8,128)(2,1)S(1)} %get-tuple-element.174), channel_id=1, source_target_pairs={{0,1},{1,0},{2,3},{3,2},{4,5},{5,4},{6,7},{7,6},{8,9},{9,8},{10,11... | collective-permute-start | bytes 1179656 | tf_op jit(solution)/shard_map/ppermute | solution.py:332
  30.0 5.8 %collective-permute-start.10 = (bf16[32,6144]{1,0:T(8,128)(2,1)S(1)}, bf16[32,6144]{1,0:T(8,128)(2,1)S(1)}, u32[]{:S(2)}, u32[]{:S(2)}) collective-permute-start(bf16[32,6144]{1,0:T(8,128)(2,1)S(1)} %collective-permute-done.8.refs_7_), channel_id=1, source_target_pairs={{0,1},{1,0},{2,3},{3,2},{4,5},{5,4},{6,7},{7,6},{8,9},{9,8},{10,11... | collective-permute-start | bytes 1179656 | tf_op jit(solution)/shard_map/ppermute | solution.py:332
  30.1 9.6 %collective-permute-start.16 = (bf16[32,6144]{1,0:T(8,128)(2,1)S(1)}, bf16[32,6144]{1,0:T(8,128)(2,1)S(1)}, u32[]{:S(2)}, u32[]{:S(2)}) collective-permute-start(bf16[32,6144]{1,0:T(8,128)(2,1)S(1)} %collective-permute-done.8.refs_7_), channel_id=1, source_target_pairs={{0,4},{1,3},{4,8},{5,1},{8,12},{9,5},{12,14},{13,9},{14,10},{15,13... | collective-permute-start | bytes 1179656 | tf_op jit(solution)/shard_map/ppermute | solution.py:329
  39.6 1.8 %collective-permute-start.15 = (bf16[64,3072]{1,0:T(8,128)(2,1)S(1)}, bf16[64,3072]{1,0:T(8,128)(2,1)S(1)}, u32[]{:S(2)}, u32[]{:S(2)}) collective-permute-start(bf16[64,3072]{1,0:T(8,128)(2,1)S(1)} %get-tuple-element.212), channel_id=1, source_target_pairs={{0,1},{1,0},{2,3},{3,2},{4,5},{5,4},{6,7},{7,6},{8,9},{9,8},{10,11... | collective-permute-start | bytes 1179656 | tf_op jit(solution)/shard_map/ppermute | solution.py:332
  39.6 3.9 %collective-permute-start.17 = (bf16[32,6144]{1,0:T(8,128)(2,1)S(1)}, bf16[32,6144]{1,0:T(8,128)(2,1)S(1)}, u32[]{:S(2)}, u32[]{:S(2)}) collective-permute-start(bf16[32,6144]{1,0:T(8,128)(2,1)S(1)} %collective-permute-done.16.refs_9_), channel_id=1, source_target_pairs={{0,1},{1,0},{2,3},{3,2},{4,5},{5,4},{6,7},{7,6},{8,9},{9,8},{10,11... | collective-permute-start | bytes 1179656 | tf_op jit(solution)/shard_map/ppermute | solution.py:332
  41.4 2.1 %collective-permute-start.18 = (bf16[32,6144]{1,0:T(8,128)(2,1)S(1)}, bf16[32,6144]{1,0:T(8,128)(2,1)S(1)}, u32[]{:S(2)}, u32[]{:S(2)}) collective-permute-start(bf16[32,6144]{1,0:T(8,128)(2,1)S(1)} %collective-permute-done.7.refs_8_), channel_id=1, source_target_pairs={{0,1},{1,0},{2,3},{3,2},{4,5},{5,4},{6,7},{7,6},{8,9},{9,8},{10,11... | collective-permute-start | bytes 1179656 | tf_op jit(solution)/shard_map/ppermute | solution.py:332
  41.6 7.8 %collective-permute-start.14 = (bf16[64,3072]{1,0:T(8,128)(2,1)S(1)}, bf16[64,3072]{1,0:T(8,128)(2,1)S(1)}, u32[]{:S(2)}, u32[]{:S(2)}) collective-permute-start(bf16[64,3072]{1,0:T(8,128)(2,1)S(1)} %total.7), channel_id=1, source_target_pairs={{0,4},{1,3},{4,8},{5,1},{8,12},{9,5},{12,14},{13,9},{14,10},{15,13... | collective-permute-start | bytes 1179656 | tf_op jit(solution)/shard_map/ppermute | solution.py:329
  43.1 6.4 %collective-permute-start.13 = (bf16[64,3072]{1,0:T(8,128)(2,1)S(1)}, bf16[64,3072]{1,0:T(8,128)(2,1)S(1)}, u32[]{:S(2)}, u32[]{:S(2)}) collective-permute-start(bf16[64,3072]{1,0:T(8,128)(2,1)S(1)} %get-tuple-element.209), channel_id=1, source_target_pairs={{0,1},{1,0},{2,3},{3,2},{4,5},{5,4},{6,7},{7,6},{8,9},{9,8},{10,11... | collective-permute-start | bytes 1179656 | tf_op jit(solution)/shard_map/ppermute | solution.py:332
  43.1 7.1 %collective-permute-start.20 = (bf16[64,3072]{1,0:T(8,128)(2,1)S(1)}, bf16[64,3072]{1,0:T(8,128)(2,1)S(1)}, u32[]{:S(2)}, u32[]{:S(2)}) collective-permute-start(bf16[64,3072]{1,0:T(8,128)(2,1)S(1)} %get-tuple-element.221), channel_id=1, source_target_pairs={{0,1},{1,0},{2,3},{3,2},{4,5},{5,4},{6,7},{7,6},{8,9},{9,8},{10,11... | collective-permute-start | bytes 1179656 | tf_op jit(solution)/shard_map/ppermute | solution.py:332
  43.6 8.0 %collective-permute-start.22 = (bf16[64,3072]{1,0:T(8,128)(2,1)S(1)}, bf16[64,3072]{1,0:T(8,128)(2,1)S(1)}, u32[]{:S(2)}, u32[]{:S(2)}) collective-permute-start(bf16[64,3072]{1,0:T(8,128)(2,1)S(1)} %get-tuple-element.224), channel_id=1, source_target_pairs={{0,1},{1,0},{2,3},{3,2},{4,5},{5,4},{6,7},{7,6},{8,9},{9,8},{10,11... | collective-permute-start | bytes 1179656 | tf_op jit(solution)/shard_map/ppermute | solution.py:332
  43.6 10.0 %collective-permute-start.23 = (bf16[64,3072]{1,0:T(8,128)(2,1)S(1)}, bf16[64,3072]{1,0:T(8,128)(2,1)S(1)}, u32[]{:S(2)}, u32[]{:S(2)}) collective-permute-start(bf16[64,3072]{1,0:T(8,128)(2,1)S(1)} %total.8), channel_id=1, source_target_pairs={{0,4},{1,3},{4,8},{5,1},{8,12},{9,5},{12,14},{13,9},{14,10},{15,13... | collective-permute-start | bytes 1179656 | tf_op jit(solution)/shard_map/ppermute | solution.py:329
  49.6 5.7 %collective-permute-start.19 = (bf16[64,3072]{1,0:T(8,128)(2,1)S(1)}, bf16[64,3072]{1,0:T(8,128)(2,1)S(1)}, u32[]{:S(2)}, u32[]{:S(2)}) collective-permute-start(bf16[64,3072]{1,0:T(8,128)(2,1)S(1)} %get-tuple-element.218), channel_id=1, source_target_pairs={{0,1},{1,0},{2,3},{3,2},{4,5},{5,4},{6,7},{7,6},{8,9},{9,8},{10,11... | collective-permute-start | bytes 1179656 | tf_op jit(solution)/shard_map/ppermute | solution.py:332
  49.6 5.6 %collective-permute-start.24 = (bf16[64,3072]{1,0:T(8,128)(2,1)S(1)}, bf16[64,3072]{1,0:T(8,128)(2,1)S(1)}, u32[]{:S(2)}, u32[]{:S(2)}) collective-permute-start(bf16[64,3072]{1,0:T(8,128)(2,1)S(1)} %get-tuple-element.230), channel_id=1, source_target_pairs={{0,1},{1,0},{2,3},{3,2},{4,5},{5,4},{6,7},{7,6},{8,9},{9,8},{10,11... | collective-permute-start | bytes 1179656 | tf_op jit(solution)/shard_map/ppermute | solution.py:332
  50.1 7.8 %collective-permute-start.21 = (bf16[64,3072]{1,0:T(8,128)(2,1)S(1)}, bf16[64,3072]{1,0:T(8,128)(2,1)S(1)}, u32[]{:S(2)}, u32[]{:S(2)}) collective-permute-start(bf16[64,3072]{1,0:T(8,128)(2,1)S(1)} %total.9), channel_id=1, source_target_pairs={{0,4},{1,3},{4,8},{5,1},{8,12},{9,5},{12,14},{13,9},{14,10},{15,13... | collective-permute-start | bytes 1179656 | tf_op jit(solution)/shard_map/ppermute | solution.py:329
  53.8 8.4 %collective-permute-start.26 = (bf16[64,3072]{1,0:T(8,128)(2,1)S(1)}, bf16[64,3072]{1,0:T(8,128)(2,1)S(1)}, u32[]{:S(2)}, u32[]{:S(2)}) collective-permute-start(bf16[64,3072]{1,0:T(8,128)(2,1)S(1)} %total.10), channel_id=1, source_target_pairs={{0,4},{1,3},{4,8},{5,1},{8,12},{9,5},{12,14},{13,9},{14,10},{15,13... | collective-permute-start | bytes 1179656 | tf_op jit(solution)/shard_map/ppermute | solution.py:329
  58.1 8.3 %collective-permute-start.25 = (bf16[64,3072]{1,0:T(8,128)(2,1)S(1)}, bf16[64,3072]{1,0:T(8,128)(2,1)S(1)}, u32[]{:S(2)}, u32[]{:S(2)}) collective-permute-start(bf16[64,3072]{1,0:T(8,128)(2,1)S(1)} %total.11), channel_id=1, source_target_pairs={{0,4},{1,3},{4,8},{5,1},{8,12},{9,5},{12,14},{13,9},{14,10},{15,13... | collective-permute-start | bytes 1179656 | tf_op jit(solution)/shard_map/ppermute | solution.py:329
  62.3 8.3 %collective-permute-start.28 = (bf16[64,3072]{1,0:T(8,128)(2,1)S(1)}, bf16[64,3072]{1,0:T(8,128)(2,1)S(1)}, u32[]{:S(2)}, u32[]{:S(2)}) collective-permute-start(bf16[64,3072]{1,0:T(8,128)(2,1)S(1)} %total.12), channel_id=1, source_target_pairs={{0,4},{1,3},{4,8},{5,1},{8,12},{9,5},{12,14},{13,9},{14,10},{15,13... | collective-permute-start | bytes 1179656 | tf_op jit(solution)/shard_map/ppermute | solution.py:329
  66.5 8.3 %collective-permute-start.27 = (bf16[64,3072]{1,0:T(8,128)(2,1)S(1)}, bf16[64,3072]{1,0:T(8,128)(2,1)S(1)}, u32[]{:S(2)}, u32[]{:S(2)}) collective-permute-start(bf16[64,3072]{1,0:T(8,128)(2,1)S(1)} %total.13), channel_id=1, source_target_pairs={{0,4},{1,3},{4,8},{5,1},{8,12},{9,5},{12,14},{13,9},{14,10},{15,13... | collective-permute-start | bytes 1179656 | tf_op jit(solution)/shard_map/ppermute | solution.py:329
  70.7 1.6 %collective-permute-start.29 = (bf16[32,3072]{1,0:T(8,128)(2,1)S(1)}, bf16[32,3072]{1,0:T(8,128)(2,1)S(1)}, u32[]{:S(2)}, u32[]{:S(2)}) collective-permute-start(bf16[32,3072]{1,0:T(8,128)(2,1)S(1)} %get-tuple-element.248), channel_id=1, source_target_pairs={{0,1},{1,0},{2,3},{3,2},{4,5},{5,4},{6,7},{7,6},{8,9},{9,8},{10,11... | collective-permute-start | bytes 589832 | tf_op jit(solution)/shard_map/ppermute | solution.py:332
  74.9 1.6 %collective-permute-start.30 = (bf16[32,3072]{1,0:T(8,128)(2,1)S(1)}, bf16[32,3072]{1,0:T(8,128)(2,1)S(1)}, u32[]{:S(2)}, u32[]{:S(2)}) collective-permute-start(bf16[32,3072]{1,0:T(8,128)(2,1)S(1)} %get-tuple-element.257), channel_id=1, source_target_pairs={{0,1},{1,0},{2,3},{3,2},{4,5},{5,4},{6,7},{7,6},{8,9},{9,8},{10,11... | collective-permute-start | bytes 589832 | tf_op jit(solution)/shard_map/ppermute | solution.py:332

commit v8 on v7

--- a/solution.py
+++ b/solution.py
@@ -8,7 +8,7 @@
 from jax.sharding import PartitionSpec as P
 
 RING = 8
-PIECE_STEPS = 1
+PIECE_STEPS = 2
 PIECE_COST = 0.1
 PIECES = 4
 VMEM_LIMIT = 16 * 1024 * 1024
@@ -149,9 +149,10 @@
             sems.at[PIECE_STEPS, 0],
         )
         fetch.start()
-    step = wide // PIECE_STEPS
+    steps = PIECE_STEPS if other else 1
+    step = wide // steps
     stores = []
-    for i in range(PIECE_STEPS):
+    for i in range(steps):
         here = pl.ds(i * step, step)
         part = jnp.dot(w_ref[here, :], dht_ref[...], preferred_element_type=jnp.float32)
         part_ref[:, here] = part.astype(jnp.bfloat16).T
@@ -359,10 +360,10 @@
     a3 = after(a3, gm[0])
     a4, sa3 = ring(a3), swap(a3)
     own_o, behind_o, opposite_o, ahead_o = go[0], go[1:4], go[4], go[5:]
-    opposite_from = swap(opposite_o)
+    opposite_from = swap(after(opposite_o, gm[0]))
     gm, w = product(False, 1, w, gm, a3, sb2)
-    gm, w = product(False, 2, w, gm, sa3, opposite_from)
-    gm, _ = product(False, 3, w, gm, b3)
+    gm, w = product(False, 2, w, gm, sa3)
+    gm, _ = product(False, 3, w, gm, b3, opposite_from)
     own_m, behind_m, opposite_m, ahead_m = gm[0], gm[1:4], gm[4], gm[5:]
     sent = total(opposite_m, opposite_from)
     r4m = ring(sent)
@@ -378,32 +379,33 @@
     def send(k, ahead, came, *ring_terms):
         return total(ahead[k - 1], came[k - 1], *ring_terms)
 
+    sb3 = swap(after(b3, sent))
+    blocks = (layer_input, twin, a1, b1, a2, b2, a3, b3, a4, sa4, sb1, sa1, sb2, sa2, sb3, sa3)
+    gw = gradient(0, (), sent, from_o[2])
+    from_o[2] = after(from_o[2], gw[1])
     sent = send(3, ahead_o, from_o)
     r3o = ring(sent)
-    sb3 = swap(after(b3, sent))
-    blocks = (layer_input, twin, a1, b1, a2, b2, a3, b3, a4, sa4, sb1, sa1, sb2, sa2, sb3, sa3)
-    from_o[1], from_m[1] = swap(after(behind_m[1], sent)), swap(after(behind_o[1], sent))
-    gw = gradient(0, (), sent)
+    gw = gradient(1, gw, sent)
     sent = send(3, ahead_m, from_m, after(r4m, gw[1]))
     r3m = ring(sent)
-    from_o[0], from_m[0] = swap(after(behind_m[0], sent)), swap(after(behind_o[0], sent))
-    gw = gradient(1, gw, sent, from_o[1], from_m[1])
+    from_o[1], from_m[1] = swap(after(behind_m[1], sent)), swap(after(behind_o[1], sent))
+    gw = gradient(2, gw, sent)
     sent = send(2, ahead_o, from_o, after(r3o, gw[1]))
     r2o = ring(sent)
-    gw = gradient(2, gw, sent, from_o[0], from_m[0])
+    from_o[0], from_m[0] = swap(after(behind_m[0], sent)), swap(after(behind_o[0], sent))
+    gw = gradient(3, gw, sent, from_m[1])
     sent = send(2, ahead_m, from_m, after(r3m, gw[1]))
     r2m = ring(sent)
-    gw = gradient(3, gw, sent)
+    gw = gradient(4, gw, sent, from_o[0], from_m[0])
     sent = send(1, ahead_o, from_o, after(r2o, gw[1]))
     r1o = ring(sent)
-    gw = gradient(4, gw, sent)
+    gw = gradient(5, gw, sent)
     sent = send(1, ahead_m, from_m, after(r2m, gw[1]))
     r1m = ring(sent)
-    gw = gradient(5, gw, sent)
+    gw = gradient(6, gw, sent)
     kept_o, sent_o = halves(own_o, after(r1o, gw[1]))
     came_m = swap(sent_o)
-    gw = gradient(6, gw, sent_o)
-    gw = gradient(7, gw, came_m)
+    gw = gradient(7, gw, sent_o)
     kept_m, sent_m = halves(own_m, after(r1m, gw[0]))
     came_o = swap(sent_m)
     return (last(me, kept_m, came_m, kept_o, came_o), gw[0])

time: 77.7 us -> 74 us (0.952)
  starting transfers between devices: 24.6 us -> 28.9 us
  waiting for transfers between devices: 13.5 us -> 9.36 us
  Pallas kernels: 38.3 us -> 34.6 us
    ppermute x13, waiting for transfers between devices: 11.2 us -> 7.37 us  [ring(): return lax.ppermute(x, 'gx', along)]
    pallas_call x8, Pallas kernels: 19.5 us -> 15.8 us  [input_piece(): pl.pallas_call(lambda *refs: input_kernel(*refs, other=other, piece=piece...]
    ppermute x13, starting transfers between devices: 19.6 us -> 22.7 us  [ring(): return lax.ppermute(x, 'gx', along)]
    ppermute x17, starting transfers between devices: 4.27 us -> 5.44 us  [swap(): return lax.ppermute(x, 'gx', twins)]
  transfers between devices with their start and end apart: 31 -> 31, of which waited for: 9 -> 15; matrix products, arithmetic and copies ran while one was open for 0% -> 0% of each run, Pallas kernels for 48% -> 46%
where the time goes in v8:
time: 74 us; the launch traced here: 73.8 us
  Pallas kernels  34.6 us (47%)
  starting transfers between devices  28.9 us (39%)
  waiting for transfers between devices  9.36 us (13%)
  between operations  0.9 us (1%)
    ppermute x13, starting transfers between devices, ring(): return lax.ppermute(x, 'gx', along)  22.7 us
    pallas_call x8, Pallas kernels, input_piece(): pl.pallas_call(lambda *refs: input_kernel(*refs, other=other, piece=piece...  15.8 us
    pallas_call x8, Pallas kernels, weight_piece(): pl.pallas_call(lambda *refs: weight_kernel(*refs, piece=piece, wide=wide,...  13.1 us
    ppermute x13, waiting for transfers between devices, ring(): return lax.ppermute(x, 'gx', along)  7.37 us
    ppermute x17, starting transfers between devices, swap(): return lax.ppermute(x, 'gx', twins)  5.44 us
    pallas_call x1, Pallas kernels, hidden(): pl.pallas_call(hidden_kernel, out_shape=(jax.ShapeDtypeStruct(shape, dtyp...  3.85 us
    ppermute x17, waiting for transfers between devices, swap(): return lax.ppermute(x, 'gx', twins)  1.99 us
  transfers between devices with their start and end apart: 31, of which 15 were waited for; matrix products, arithmetic and copies ran while one was open for 0% of the time, Pallas kernels for 46%

profile of v8, /device:TPU:0, one launch (start us, length us, event | category | flops | bytes accessed | tf_op | source)
XLA Modules:
  0.0 73.8 jit_solution(8783848539455105082)
XLA Ops:
  0.6 3.1 %collective-permute-start.1 = (bf16[32,6144]{1,0:T(8,128)(2,1)}, bf16[32,6144]{1,0:T(8,128)(2,1)S(1)}, u32[]{:S(2)}, u32[]{:S(2)}) collective-permute-start(bf16[32,6144]{1,0:T(8,128)(2,1)} %refs_1_.15), channel_id=1, source_target_pairs={{0,4},{1,3},{4,8},{5,1},{8,12},{9,5},{12,14},{13,9},{14,10},{15,13... | collective-permute-start | bytes 1179656 | tf_op jit(solution)/shard_map/ppermute | solution.py:330
  3.7 3.9 %hidden.1 = (bf16[512,1536]{1,0:T(8,128)(2,1)S(1)}, bf16[1536,512]{1,0:T(8,128)(2,1)S(1)}, bf16[768,1536]{1,0:T(8,128)(2,1)S(1)}) custom-call(s32[1]{0:T(128)} %bitcast.me_ref.refs_0_, bf16[512,1536]{1,0:T(8,128)(2,1)} %og_hbm.1, bf16[512,1536]{1,0:T(8,128)(2,1)} %pre_hbm.1, bf16[6144,1536]{1,0:T(8,128)(2,1)} %refs_3_.15), custom_call_target="tpu_custom_call" | custom-call | flops 1150000000 | tf_op jit(solution)/shard_map/hidden/pallas_call | solution.py:115
  7.6 0.7 %collective-permute-start = (bf16[32,6144]{1,0:T(8,128)(2,1)S(1)}, bf16[32,6144]{1,0:T(8,128)(2,1)S(1)}, u32[]{:S(2)}, u32[]{:S(2)}) collective-permute-start(bf16[32,6144]{1,0:T(8,128)(2,1)S(1)} %copy-done), channel_id=1, source_target_pairs={{0,3},{1,4},{4,1},{5,8},{8,5},{9,12},{12,9},{13,14},{14,13},{15,10... | collective-permute-start | bytes 1179656 | tf_op jit(solution)/shard_map/ppermute | solution.py:342
  8.3 2.1 %input_piece.8 = (bf16[64,3072]{1,0:T(8,128)(2,1)S(1)}, bf16[64,3072]{1,0:T(8,128)(2,1)S(1)}, bf16[64,3072]{1,0:T(8,128)(2,1)S(1)}, bf16[64,3072]{1,0:T(8,128)(2...) custom-call(s32[1]{0:T(128)} %bitcast.me_ref.refs_0_, ...), custom_call_target="tpu_custom_call" | custom-call | flops 115000000 | tf_op jit(solution)/shard_map/input_piece/pallas_call | solution.py:182
  10.4 1.1 %collective-permute-start.5 = (bf16[32,6144]{1,0:T(8,128)(2,1)S(1)}, bf16[32,6144]{1,0:T(8,128)(2,1)S(1)}, u32[]{:S(2)}, u32[]{:S(2)}) collective-permute-start(bf16[32,6144]{1,0:T(8,128)(2,1)S(1)} %collective-permute-done.1.refs_3_), channel_id=1, source_target_pairs={{0,1},{1,0},{2,3},{3,2},{4,5},{5,4},{6,7},{7,6},{8,9},{9,8},{10,11... | collective-permute-start | bytes 1179656 | tf_op jit(solution)/shard_map/ppermute | solution.py:333
  11.5 1.6 %collective-permute-start.4 = (bf16[32,6144]{1,0:T(8,128)(2,1)S(1)}, bf16[32,6144]{1,0:T(8,128)(2,1)S(1)}, u32[]{:S(2)}, u32[]{:S(2)}) collective-permute-start(bf16[32,6144]{1,0:T(8,128)(2,1)S(1)} %collective-permute-done.1.refs_3_), channel_id=1, source_target_pairs={{0,4},{1,3},{4,8},{5,1},{8,12},{9,5},{12,14},{13,9},{14,10},{15,13... | collective-permute-start | bytes 1179656 | tf_op jit(solution)/shard_map/ppermute | solution.py:330
  13.1 2.1 %input_piece.9 = (bf16[64,3072]{1,0:T(8,128)(2,1)S(1)}, bf16[64,3072]{1,0:T(8,128)(2,1)S(1)}, bf16[64,3072]{1,0:T(8,128)(2,1)S(1)}, bf16[64,3072]{1,0:T(8,128)(2...) custom-call(s32[1]{0:T(128)} %bitcast.me_ref.refs_0_, ...), custom_call_target="tpu_custom_call", output_to_operand_aliasing={{0}: (4, {}), {1}: (5, {}), {2}: (6, {}), {3}: (7, {}), {4}... | custom-call | flops 115000000 | tf_op jit(solution)/shard_map/input_piece/pallas_call | solution.py:182
  15.1 1.8 %collective-permute-start.6 = (bf16[32,6144]{1,0:T(8,128)(2,1)S(1)}, bf16[32,6144]{1,0:T(8,128)(2,1)S(1)}, u32[]{:S(2)}, u32[]{:S(2)}) collective-permute-start(bf16[32,6144]{1,0:T(8,128)(2,1)S(1)} %collective-permute-done.refs_4_), channel_id=1, source_target_pairs={{0,1},{1,0},{2,3},{3,2},{4,5},{5,4},{6,7},{7,6},{8,9},{9,8},{10,11... | collective-permute-start | bytes 1179656 | tf_op jit(solution)/shard_map/ppermute | solution.py:333
  17.0 1.6 %collective-permute-start.3 = (bf16[32,6144]{1,0:T(8,128)(2,1)S(1)}, bf16[32,6144]{1,0:T(8,128)(2,1)S(1)}, u32[]{:S(2)}, u32[]{:S(2)}) collective-permute-start(bf16[32,6144]{1,0:T(8,128)(2,1)S(1)} %collective-permute-done.refs_4_), channel_id=1, source_target_pairs={{0,4},{1,3},{4,8},{5,1},{8,12},{9,5},{12,14},{13,9},{14,10},{15,13... | collective-permute-start | bytes 1179656 | tf_op jit(solution)/shard_map/ppermute | solution.py:330
  18.6 2.1 %input_piece.10 = (bf16[64,3072]{1,0:T(8,128)(2,1)S(1)}, bf16[64,3072]{1,0:T(8,128)(2,1)S(1)}, bf16[64,3072]{1,0:T(8,128)(2,1)S(1)}, bf16[64,3072]{1,0:T(8,128)(...) custom-call(s32[1]{0:T(128)} %bitcast.me_ref.refs_0_, ...), custom_call_target="tpu_custom_call", output_to_operand_aliasing={{0}: (4, {}), {1}: (5, {}), {2}: (6, {}), {3}: (7, {}), {4}... | custom-call | flops 115000000 | tf_op jit(solution)/shard_map/input_piece/pallas_call | solution.py:182
  20.6 0.1 collective-permute-start.8
  20.7 1.7 %collective-permute-start.10 = (bf16[32,6144]{1,0:T(8,128)(2,1)S(1)}, bf16[32,6144]{1,0:T(8,128)(2,1)S(1)}, u32[]{:S(2)}, u32[]{:S(2)}) collective-permute-start(bf16[32,6144]{1,0:T(8,128)(2,1)S(1)} %collective-permute-done.4.refs_5_), channel_id=1, source_target_pairs={{0,4},{1,3},{4,8},{5,1},{8,12},{9,5},{12,14},{13,9},{14,10},{15,13... | collective-permute-start | bytes 1179656 | tf_op jit(solution)/shard_map/ppermute | solution.py:330
  22.4 2.1 %input_piece.11 = (bf16[64,3072]{1,0:T(8,128)(2,1)S(1)}, bf16[64,3072]{1,0:T(8,128)(2,1)S(1)}, bf16[64,3072]{1,0:T(8,128)(2,1)S(1)}, bf16[64,3072]{1,0:T(8,128)(...) custom-call(s32[1]{0:T(128)} %bitcast.me_ref.refs_0_, ...), custom_call_target="tpu_custom_call", output_to_operand_aliasing={{0}: (4, {}), {1}: (5, {}), {2}: (6, {}), {3}: (7, {}), {4}... | custom-call | flops 115000000 | tf_op jit(solution)/shard_map/input_piece/pallas_call | solution.py:182
  24.5 0.3 collective-permute-done.3.refs_6_
  24.8 1.9 %collective-permute-start.7 = (bf16[32,6144]{1,0:T(8,128)(2,1)S(1)}, bf16[32,6144]{1,0:T(8,128)(2,1)S(1)}, u32[]{:S(2)}, u32[]{:S(2)}) collective-permute-start(bf16[32,6144]{1,0:T(8,128)(2,1)S(1)} %collective-permute-done.3.refs_6_), channel_id=1, source_target_pairs={{0,4},{1,3},{4,8},{5,1},{8,12},{9,5},{12,14},{13,9},{14,10},{15,13... | collective-permute-start | bytes 1179656 | tf_op jit(solution)/shard_map/ppermute | solution.py:330
  26.6 1.9 %input_piece.12 = (bf16[64,3072]{1,0:T(8,128)(2,1)S(1)}, bf16[64,3072]{1,0:T(8,128)(2,1)S(1)}, bf16[64,3072]{1,0:T(8,128)(2,1)S(1)}, bf16[64,3072]{1,0:T(8,128)(...) custom-call(s32[1]{0:T(128)} %bitcast.me_ref.refs_0_, ...), custom_call_target="tpu_custom_call" | custom-call | flops 115000000 | tf_op jit(solution)/shard_map/input_piece/pallas_call | solution.py:182
  28.6 0.3 collective-permute-done.10.refs_7_
  29.0 0.2 collective-permute-start.11
  29.1 1.4 %collective-permute-start.16 = (bf16[32,6144]{1,0:T(8,128)(2,1)S(1)}, bf16[32,6144]{1,0:T(8,128)(2,1)S(1)}, u32[]{:S(2)}, u32[]{:S(2)}) collective-permute-start(bf16[32,6144]{1,0:T(8,128)(2,1)S(1)} %collective-permute-done.10.refs_7_), channel_id=1, source_target_pairs={{0,4},{1,3},{4,8},{5,1},{8,12},{9,5},{12,14},{13,9},{14,10},{15,13... | collective-permute-start | bytes 1179656 | tf_op jit(solution)/shard_map/ppermute | solution.py:330
  30.6 1.9 %input_piece.13 = (bf16[64,3072]{1,0:T(8,128)(2,1)S(1)}, bf16[64,3072]{1,0:T(8,128)(2,1)S(1)}, bf16[64,3072]{1,0:T(8,128)(2,1)S(1)}, bf16[64,3072]{1,0:T(8,128)(...) custom-call(s32[1]{0:T(128)} %bitcast.me_ref.refs_0_, ...), custom_call_target="tpu_custom_call", output_to_operand_aliasing={{0}: (4, {}), {1}: (5, {}), {2}: (6, {}), {3}: (7, {}), {4}... | custom-call | flops 115000000 | tf_op jit(solution)/shard_map/input_piece/pallas_call | solution.py:182
  32.5 0.7 collective-permute-done.7.refs_8_
  33.2 1.9 %input_piece.14 = (bf16[64,3072]{1,0:T(8,128)(2,1)S(1)}, bf16[64,3072]{1,0:T(8,128)(2,1)S(1)}, bf16[64,3072]{1,0:T(8,128)(2,1)S(1)}, bf16[64,3072]{1,0:T(8,128)(...) custom-call(s32[1]{0:T(128)} %bitcast.me_ref.refs_0_, ...), custom_call_target="tpu_custom_call", output_to_operand_aliasing={{0}: (4, {}), {1}: (5, {}), {2}: (6, {}), {3}: (7, {}), {4}... | custom-call | flops 115000000 | tf_op jit(solution)/shard_map/input_piece/pallas_call | solution.py:182
  35.1 1.8 %input_piece.15 = (bf16[64,3072]{1,0:T(8,128)(2,1)S(1)}, bf16[64,3072]{1,0:T(8,128)(2,1)S(1)}, bf16[64,3072]{1,0:T(8,128)(2,1)S(1)}, bf16[64,3072]{1,0:T(8,128)(...) custom-call(s32[1]{0:T(128)} %bitcast.me_ref.refs_0_, ...), custom_call_target="tpu_custom_call", output_to_operand_aliasing={{0}: (4, {}), {1}: (5, {}), {2}: (6, {}), {3}: (7, {}), {4}... | custom-call | flops 115000000 | tf_op jit(solution)/shard_map/input_piece/pallas_call | solution.py:182
  36.9 0.1 total.7
  37.0 0.4 collective-permute-done.16.refs_9_
  37.4 0.5 collective-permute-start.17
  37.9 1.6 %collective-permute-start.14 = (bf16[64,3072]{1,0:T(8,128)(2,1)S(1)}, bf16[64,3072]{1,0:T(8,128)(2,1)S(1)}, u32[]{:S(2)}, u32[]{:S(2)}) collective-permute-start(bf16[64,3072]{1,0:T(8,128)(2,1)S(1)} %total.7), channel_id=1, source_target_pairs={{0,4},{1,3},{4,8},{5,1},{8,12},{9,5},{12,14},{13,9},{14,10},{15,13... | collective-permute-start | bytes 1179656 | tf_op jit(solution)/shard_map/ppermute | solution.py:330
  39.5 0.2 collective-permute-done.17.refs_10_
  39.7 0.6 collective-permute-done.18.refs_15_
  40.2 1.5 %weight_piece.8 = (bf16[6144,1536]{1,0:T(8,128)(2,1)}, bf16[768,1536]{1,0:T(8,128)(2,1)S(1)}) custom-call(bf16[512,1536]{1,0:T(8,128)(2,1)S(1)} %get-tuple-element.256.refs_0_, bf16[32,6144]{1,0:T(8,128)(2,1)S(1)} %copy-done, bf16[32,6144]{1,0:T(8,128)(2,1)S(1)} %collective-permute-done.2.refs_2_, bf16[32,6144]{1,0:T(8,128)(2,1)S(1)} %collective-permute-done.1.refs_3_, ...), custom_call_target="tpu_custom_call" | custom-call | flops 115000000 | tf_op jit(solution)/shard_map/weight_piece/pallas_call | solution.py:236
  41.7 0.1 total.8
  41.8 1.6 %collective-permute-start.20 = (bf16[64,3072]{1,0:T(8,128)(2,1)S(1)}, bf16[64,3072]{1,0:T(8,128)(2,1)S(1)}, u32[]{:S(2)}, u32[]{:S(2)}) collective-permute-start(bf16[64,3072]{1,0:T(8,128)(2,1)S(1)} %total.8), channel_id=1, source_target_pairs={{0,4},{1,3},{4,8},{5,1},{8,12},{9,5},{12,14},{13,9},{14,10},{15,13... | collective-permute-start | bytes 1179656 | tf_op jit(solution)/shard_map/ppermute | solution.py:330
  43.5 1.5 %weight_piece.9 = (bf16[6144,1536]{1,0:T(8,128)(2,1)}, bf16[768,1536]{1,0:T(8,128)(2,1)S(1)}) custom-call(bf16[512,1536]{1,0:T(8,128)(2,1)S(1)} %get-tuple-element.256.refs_0_, bf16[32,6144]{1,0:T(8,128)(2,1)S(1)} %copy-done, bf16[32,6144]{1,0:T(8,128)(2,1)S(1)} %collective-permute-done.2.refs_2_, ...), custom_call_target="tpu_custom_call", output_to_operand_aliasing={{0}: (18, {})} | custom-call | flops 115000000 | tf_op jit(solution)/shard_map/weight_piece/pallas_call | solution.py:236
  45.0 0.7 collective-permute-done.14.refs_0_
  45.7 0.1 total.9
  45.9 0.5 collective-permute-start.22
  46.4 1.6 %collective-permute-start.23 = (bf16[64,3072]{1,0:T(8,128)(2,1)S(1)}, bf16[64,3072]{1,0:T(8,128)(2,1)S(1)}, u32[]{:S(2)}, u32[]{:S(2)}) collective-permute-start(bf16[64,3072]{1,0:T(8,128)(2,1)S(1)} %total.9), channel_id=1, source_target_pairs={{0,4},{1,3},{4,8},{5,1},{8,12},{9,5},{12,14},{13,9},{14,10},{15,13... | collective-permute-start | bytes 1179656 | tf_op jit(solution)/shard_map/ppermute | solution.py:330
  48.0 1.5 %weight_piece.10 = (bf16[6144,1536]{1,0:T(8,128)(2,1)}, bf16[768,1536]{1,0:T(8,128)(2,1)S(1)}) custom-call(bf16[512,1536]{1,0:T(8,128)(2,1)S(1)} %get-tuple-element.256.refs_0_, bf16[32,6144]{1,0:T(8,128)(2,1)S(1)} %copy-done, bf16[32,6144]{1,0:T(8,128)(2,1)S(1)} %collective-permute-done.2.refs_2_, ...), custom_call_target="tpu_custom_call", output_to_operand_aliasing={{0}: (18, {})} | custom-call | flops 115000000 | tf_op jit(solution)/shard_map/weight_piece/pallas_call | solution.py:236
  49.5 0.4 collective-permute-done.20.refs_0_
  49.9 0.1 total.10
  50.1 0.5 collective-permute-start.25
  50.6 1.6 %collective-permute-start.26 = (bf16[64,3072]{1,0:T(8,128)(2,1)S(1)}, bf16[64,3072]{1,0:T(8,128)(2,1)S(1)}, u32[]{:S(2)}, u32[]{:S(2)}) collective-permute-start(bf16[64,3072]{1,0:T(8,128)(2,1)S(1)} %total.10), channel_id=1, source_target_pairs={{0,4},{1,3},{4,8},{5,1},{8,12},{9,5},{12,14},{13,9},{14,10},{15,13... | collective-permute-start | bytes 1179656 | tf_op jit(solution)/shard_map/ppermute | solution.py:330
  52.2 1.5 %weight_piece.11 = (bf16[6144,1536]{1,0:T(8,128)(2,1)}, bf16[768,1536]{1,0:T(8,128)(2,1)S(1)}) custom-call(bf16[512,1536]{1,0:T(8,128)(2,1)S(1)} %get-tuple-element.256.refs_0_, bf16[32,6144]{1,0:T(8,128)(2,1)S(1)} %copy-done, bf16[32,6144]{1,0:T(8,128)(2,1)S(1)} %collective-permute-done.2.refs_2_, ...), custom_call_target="tpu_custom_call", output_to_operand_aliasing={{0}: (18, {})} | custom-call | flops 115000000 | tf_op jit(solution)/shard_map/weight_piece/pallas_call | solution.py:236
  53.7 0.5 collective-permute-done.23.refs_0_
  54.2 0.2 total.11
  54.4 1.6 %collective-permute-start.24 = (bf16[64,3072]{1,0:T(8,128)(2,1)S(1)}, bf16[64,3072]{1,0:T(8,128)(2,1)S(1)}, u32[]{:S(2)}, u32[]{:S(2)}) collective-permute-start(bf16[64,3072]{1,0:T(8,128)(2,1)S(1)} %total.11), channel_id=1, source_target_pairs={{0,4},{1,3},{4,8},{5,1},{8,12},{9,5},{12,14},{13,9},{14,10},{15,13... | collective-permute-start | bytes 1179656 | tf_op jit(solution)/shard_map/ppermute | solution.py:330
  56.0 1.5 %weight_piece.12 = (bf16[6144,1536]{1,0:T(8,128)(2,1)}, bf16[768,1536]{1,0:T(8,128)(2,1)S(1)}) custom-call(bf16[512,1536]{1,0:T(8,128)(2,1)S(1)} %get-tuple-element.256.refs_0_, bf16[32,6144]{1,0:T(8,128)(2,1)S(1)} %copy-done, bf16[32,6144]{1,0:T(8,128)(2,1)S(1)} %collective-permute-done.2.refs_2_, ...), custom_call_target="tpu_custom_call", output_to_operand_aliasing={{0}: (18, {})} | custom-call | flops 115000000 | tf_op jit(solution)/shard_map/weight_piece/pallas_call | solution.py:236
  57.5 0.9 %collective-permute-done.26.refs_0_ = bf16[64,3072]{1,0:T(8,128)(2,1)S(1)} collective-permute-done((bf16[64,3072]{1,0:T(8,128)(2,1)S(1)}, bf16[64,3072]{1,0:T(8,128)(2,1)S(1)}, u32[]{:S(2)}, u32[]{:S(2)}) %collective-permute-start.26) | collective-permute-done | bytes 393248 | tf_op jit(solution)/shard_map/ppermute | solution.py:330
  58.4 0.1 total.12
  58.6 1.6 %collective-permute-start.28 = (bf16[64,3072]{1,0:T(8,128)(2,1)S(1)}, bf16[64,3072]{1,0:T(8,128)(2,1)S(1)}, u32[]{:S(2)}, u32[]{:S(2)}) collective-permute-start(bf16[64,3072]{1,0:T(8,128)(2,1)S(1)} %total.12), channel_id=1, source_target_pairs={{0,4},{1,3},{4,8},{5,1},{8,12},{9,5},{12,14},{13,9},{14,10},{15,13... | collective-permute-start | bytes 1179656 | tf_op jit(solution)/shard_map/ppermute | solution.py:330
  60.2 1.5 %weight_piece.13 = (bf16[6144,1536]{1,0:T(8,128)(2,1)}, bf16[768,1536]{1,0:T(8,128)(2,1)S(1)}) custom-call(bf16[512,1536]{1,0:T(8,128)(2,1)S(1)} %get-tuple-element.256.refs_0_, bf16[32,6144]{1,0:T(8,128)(2,1)S(1)} %copy-done, bf16[32,6144]{1,0:T(8,128)(2,1)S(1)} %collective-permute-done.2.refs_2_, ...), custom_call_target="tpu_custom_call", output_to_operand_aliasing={{0}: (18, {})} | custom-call | flops 115000000 | tf_op jit(solution)/shard_map/weight_piece/pallas_call | solution.py:236
  61.7 0.9 %collective-permute-done.24.refs_0_ = bf16[64,3072]{1,0:T(8,128)(2,1)S(1)} collective-permute-done((bf16[64,3072]{1,0:T(8,128)(2,1)S(1)}, bf16[64,3072]{1,0:T(8,128)(2,1)S(1)}, u32[]{:S(2)}, u32[]{:S(2)}) %collective-permute-start.24) | collective-permute-done | bytes 393248 | tf_op jit(solution)/shard_map/ppermute | solution.py:330
  62.6 0.1 total.13
  62.8 1.9 %collective-permute-start.27 = (bf16[64,3072]{1,0:T(8,128)(2,1)S(1)}, bf16[64,3072]{1,0:T(8,128)(2,1)S(1)}, u32[]{:S(2)}, u32[]{:S(2)}) collective-permute-start(bf16[64,3072]{1,0:T(8,128)(2,1)S(1)} %total.13), channel_id=1, source_target_pairs={{0,4},{1,3},{4,8},{5,1},{8,12},{9,5},{12,14},{13,9},{14,10},{15,13... | collective-permute-start | bytes 1179656 | tf_op jit(solution)/shard_map/ppermute | solution.py:330
  64.6 1.5 %weight_piece.14 = (bf16[6144,1536]{1,0:T(8,128)(2,1)}, bf16[768,1536]{1,0:T(8,128)(2,1)S(1)}) custom-call(bf16[512,1536]{1,0:T(8,128)(2,1)S(1)} %get-tuple-element.256.refs_0_, bf16[32,6144]{1,0:T(8,128)(2,1)S(1)} %copy-done, bf16[32,6144]{1,0:T(8,128)(2,1)S(1)} %collective-permute-done.2.refs_2_, ...), custom_call_target="tpu_custom_call", output_to_operand_aliasing={{0}: (18, {})} | custom-call | flops 115000000 | tf_op jit(solution)/shard_map/weight_piece/pallas_call | solution.py:236
  66.1 0.7 collective-permute-done.28.came_ref
  66.8 0.1 halves.2
  66.9 2.5 %weight_piece.15 = bf16[6144,1536]{1,0:T(8,128)(2,1)} custom-call(bf16[512,1536]{1,0:T(8,128)(2,1)S(1)} %get-tuple-element.256.refs_0_, bf16[32,6144]{1,0:T(8,128)(2,1)S(1)} %copy-done, bf16[32,6144]{1,0:T(8,128)(2,1)S(1)} %collective-permute-done.2.refs_2_, bf16[32,6144]{1,0:T(8,128)(2,1)S(1)} %collective-permute-done.1.refs_3_, ...), custom_call_target="tpu_custom_call", output_to_operand_aliasing={{}: (18, {})} | custom-call | flops 115000000 | tf_op jit(solution)/shard_map/weight_piece/pallas_call | solution.py:236
  69.5 1.6 %collective-permute-done.27.came_ref = bf16[64,3072]{1,0:T(8,128)(2,1)S(1)} collective-permute-done((bf16[64,3072]{1,0:T(8,128)(2,1)S(1)}, bf16[64,3072]{1,0:T(8,128)(2,1)S(1)}, u32[]{:S(2)}, u32[]{:S(2)}) %collective-permute-start.27) | collective-permute-done | bytes 393248 | tf_op jit(solution)/shard_map/ppermute | solution.py:330
  71.0 0.1 halves.3
  71.2 0.5 collective-permute-start.29
  71.7 0.9 %collective-permute-done.30.other_came_ref = bf16[32,3072]{1,0:T(8,128)(2,1)S(1)} collective-permute-done((bf16[32,3072]{1,0:T(8,128)(2,1)S(1)}, bf16[32,3072]{1,0:T(8,128)(2,1)S(1)}, u32[]{:S(2)}, u32[]{:S(2)}) %collective-permute-start.30) | collective-permute-done | bytes 196640 | tf_op jit(solution)/shard_map/ppermute | solution.py:333
  72.6 0.3 collective-permute-done.29.mine_came_ref
  72.9 0.8 %last.1 = bf16[32,6144]{1,0:T(8,128)(2,1)} custom-call(s32[1]{0:T(128)} %bitcast.me_ref.refs_0_, f32[32,3072]{1,0:T(8,128)S(1)} %get-tuple-element.259.mine_ref, bf16[32,3072]{1,0:T(8,128)(2,1)S(1)} %collective-permute-done.29.mine_came_ref, f32[32,3072]{1,0:T(8,128)S(1)} %get-tuple-element.260.other_ref, ...), custom_call_target="tpu_custom_call" | custom-call | flops 345000000 | tf_op jit(solution)/shard_map/last/pallas_call | solution.py:305
  (27 shorter events, 0.3 us)
Async XLA Ops:
  0.6 9.8 %collective-permute-start.1 = (bf16[32,6144]{1,0:T(8,128)(2,1)}, bf16[32,6144]{1,0:T(8,128)(2,1)S(1)}, u32[]{:S(2)}, u32[]{:S(2)}) collective-permute-start(bf16[32,6144]{1,0:T(8,128)(2,1)} %refs_1_.15), channel_id=1, source_target_pairs={{0,4},{1,3},{4,8},{5,1},{8,12},{9,5},{12,14},{13,9},{14,10},{15,13... | collective-permute-start | bytes 1179656 | tf_op jit(solution)/shard_map/ppermute | solution.py:330
  3.7 9.4 %collective-permute-start.2 = (bf16[32,6144]{1,0:T(8,128)(2,1)}, bf16[32,6144]{1,0:T(8,128)(2,1)S(1)}, u32[]{:S(2)}, u32[]{:S(2)}) collective-permute-start(bf16[32,6144]{1,0:T(8,128)(2,1)} %refs_1_.15), channel_id=1, source_target_pairs={{0,1},{1,0},{2,3},{3,2},{4,5},{5,4},{6,7},{7,6},{8,9},{9,8},{10,11... | collective-permute-start | bytes 1179656 | tf_op jit(solution)/shard_map/ppermute | solution.py:333
  3.7 3.9 %copy-start = (bf16[32,6144]{1,0:T(8,128)(2,1)S(1)}, bf16[32,6144]{1,0:T(8,128)(2,1)}, u32[]{:S(2)}) copy-start(bf16[32,6144]{1,0:T(8,128)(2,1)} %refs_1_.15) | copy-start | bytes 1179652
  7.6 7.5 %collective-permute-start = (bf16[32,6144]{1,0:T(8,128)(2,1)S(1)}, bf16[32,6144]{1,0:T(8,128)(2,1)S(1)}, u32[]{:S(2)}, u32[]{:S(2)}) collective-permute-start(bf16[32,6144]{1,0:T(8,128)(2,1)S(1)} %copy-done), channel_id=1, source_target_pairs={{0,3},{1,4},{4,1},{5,8},{8,5},{9,12},{12,9},{13,14},{14,13},{15,10... | collective-permute-start | bytes 1179656 | tf_op jit(solution)/shard_map/ppermute | solution.py:342
  10.4 8.2 %collective-permute-start.5 = (bf16[32,6144]{1,0:T(8,128)(2,1)S(1)}, bf16[32,6144]{1,0:T(8,128)(2,1)S(1)}, u32[]{:S(2)}, u32[]{:S(2)}) collective-permute-start(bf16[32,6144]{1,0:T(8,128)(2,1)S(1)} %collective-permute-done.1.refs_3_), channel_id=1, source_target_pairs={{0,1},{1,0},{2,3},{3,2},{4,5},{5,4},{6,7},{7,6},{8,9},{9,8},{10,11... | collective-permute-start | bytes 1179656 | tf_op jit(solution)/shard_map/ppermute | solution.py:333
  11.5 9.1 %collective-permute-start.4 = (bf16[32,6144]{1,0:T(8,128)(2,1)S(1)}, bf16[32,6144]{1,0:T(8,128)(2,1)S(1)}, u32[]{:S(2)}, u32[]{:S(2)}) collective-permute-start(bf16[32,6144]{1,0:T(8,128)(2,1)S(1)} %collective-permute-done.1.refs_3_), channel_id=1, source_target_pairs={{0,4},{1,3},{4,8},{5,1},{8,12},{9,5},{12,14},{13,9},{14,10},{15,13... | collective-permute-start | bytes 1179656 | tf_op jit(solution)/shard_map/ppermute | solution.py:330
  15.1 7.3 %collective-permute-start.6 = (bf16[32,6144]{1,0:T(8,128)(2,1)S(1)}, bf16[32,6144]{1,0:T(8,128)(2,1)S(1)}, u32[]{:S(2)}, u32[]{:S(2)}) collective-permute-start(bf16[32,6144]{1,0:T(8,128)(2,1)S(1)} %collective-permute-done.refs_4_), channel_id=1, source_target_pairs={{0,1},{1,0},{2,3},{3,2},{4,5},{5,4},{6,7},{7,6},{8,9},{9,8},{10,11... | collective-permute-start | bytes 1179656 | tf_op jit(solution)/shard_map/ppermute | solution.py:333
  17.0 7.8 %collective-permute-start.3 = (bf16[32,6144]{1,0:T(8,128)(2,1)S(1)}, bf16[32,6144]{1,0:T(8,128)(2,1)S(1)}, u32[]{:S(2)}, u32[]{:S(2)}) collective-permute-start(bf16[32,6144]{1,0:T(8,128)(2,1)S(1)} %collective-permute-done.refs_4_), channel_id=1, source_target_pairs={{0,4},{1,3},{4,8},{5,1},{8,12},{9,5},{12,14},{13,9},{14,10},{15,13... | collective-permute-start | bytes 1179656 | tf_op jit(solution)/shard_map/ppermute | solution.py:330
  20.6 6.0 %collective-permute-start.8 = (bf16[32,6144]{1,0:T(8,128)(2,1)S(1)}, bf16[32,6144]{1,0:T(8,128)(2,1)S(1)}, u32[]{:S(2)}, u32[]{:S(2)}) collective-permute-start(bf16[32,6144]{1,0:T(8,128)(2,1)S(1)} %collective-permute-done.4.refs_5_), channel_id=1, source_target_pairs={{0,1},{1,0},{2,3},{3,2},{4,5},{5,4},{6,7},{7,6},{8,9},{9,8},{10,11... | collective-permute-start | bytes 1179656 | tf_op jit(solution)/shard_map/ppermute | solution.py:333
  20.7 8.3 %collective-permute-start.10 = (bf16[32,6144]{1,0:T(8,128)(2,1)S(1)}, bf16[32,6144]{1,0:T(8,128)(2,1)S(1)}, u32[]{:S(2)}, u32[]{:S(2)}) collective-permute-start(bf16[32,6144]{1,0:T(8,128)(2,1)S(1)} %collective-permute-done.4.refs_5_), channel_id=1, source_target_pairs={{0,4},{1,3},{4,8},{5,1},{8,12},{9,5},{12,14},{13,9},{14,10},{15,13... | collective-permute-start | bytes 1179656 | tf_op jit(solution)/shard_map/ppermute | solution.py:330
  24.8 5.8 %collective-permute-start.12 = (bf16[32,6144]{1,0:T(8,128)(2,1)S(1)}, bf16[32,6144]{1,0:T(8,128)(2,1)S(1)}, u32[]{:S(2)}, u32[]{:S(2)}) collective-permute-start(bf16[32,6144]{1,0:T(8,128)(2,1)S(1)} %collective-permute-done.3.refs_6_), channel_id=1, source_target_pairs={{0,1},{1,0},{2,3},{3,2},{4,5},{5,4},{6,7},{7,6},{8,9},{9,8},{10,11... | collective-permute-start | bytes 1179656 | tf_op jit(solution)/shard_map/ppermute | solution.py:333
  24.8 8.4 %collective-permute-start.7 = (bf16[32,6144]{1,0:T(8,128)(2,1)S(1)}, bf16[32,6144]{1,0:T(8,128)(2,1)S(1)}, u32[]{:S(2)}, u32[]{:S(2)}) collective-permute-start(bf16[32,6144]{1,0:T(8,128)(2,1)S(1)} %collective-permute-done.3.refs_6_), channel_id=1, source_target_pairs={{0,4},{1,3},{4,8},{5,1},{8,12},{9,5},{12,14},{13,9},{14,10},{15,13... | collective-permute-start | bytes 1179656 | tf_op jit(solution)/shard_map/ppermute | solution.py:330
  28.5 4.6 %collective-permute-start.9 = (bf16[64,3072]{1,0:T(8,128)(2,1)S(1)}, bf16[64,3072]{1,0:T(8,128)(2,1)S(1)}, u32[]{:S(2)}, u32[]{:S(2)}) collective-permute-start(bf16[64,3072]{1,0:T(8,128)(2,1)S(1)} %get-tuple-element.175), channel_id=1, source_target_pairs={{0,1},{1,0},{2,3},{3,2},{4,5},{5,4},{6,7},{7,6},{8,9},{9,8},{10,11... | collective-permute-start | bytes 1179656 | tf_op jit(solution)/shard_map/ppermute | solution.py:333
  29.0 4.2 %collective-permute-start.11 = (bf16[32,6144]{1,0:T(8,128)(2,1)S(1)}, bf16[32,6144]{1,0:T(8,128)(2,1)S(1)}, u32[]{:S(2)}, u32[]{:S(2)}) collective-permute-start(bf16[32,6144]{1,0:T(8,128)(2,1)S(1)} %collective-permute-done.10.refs_7_), channel_id=1, source_target_pairs={{0,1},{1,0},{2,3},{3,2},{4,5},{5,4},{6,7},{7,6},{8,9},{9,8},{10,11... | collective-permute-start | bytes 1179656 | tf_op jit(solution)/shard_map/ppermute | solution.py:333
  29.1 8.3 %collective-permute-start.16 = (bf16[32,6144]{1,0:T(8,128)(2,1)S(1)}, bf16[32,6144]{1,0:T(8,128)(2,1)S(1)}, u32[]{:S(2)}, u32[]{:S(2)}) collective-permute-start(bf16[32,6144]{1,0:T(8,128)(2,1)S(1)} %collective-permute-done.10.refs_7_), channel_id=1, source_target_pairs={{0,4},{1,3},{4,8},{5,1},{8,12},{9,5},{12,14},{13,9},{14,10},{15,13... | collective-permute-start | bytes 1179656 | tf_op jit(solution)/shard_map/ppermute | solution.py:330
  37.4 2.1 %collective-permute-start.15 = (bf16[64,3072]{1,0:T(8,128)(2,1)S(1)}, bf16[64,3072]{1,0:T(8,128)(2,1)S(1)}, u32[]{:S(2)}, u32[]{:S(2)}) collective-permute-start(bf16[64,3072]{1,0:T(8,128)(2,1)S(1)} %get-tuple-element.217), channel_id=1, source_target_pairs={{0,1},{1,0},{2,3},{3,2},{4,5},{5,4},{6,7},{7,6},{8,9},{9,8},{10,11... | collective-permute-start | bytes 1179656 | tf_op jit(solution)/shard_map/ppermute | solution.py:333
  37.4 2.3 %collective-permute-start.17 = (bf16[32,6144]{1,0:T(8,128)(2,1)S(1)}, bf16[32,6144]{1,0:T(8,128)(2,1)S(1)}, u32[]{:S(2)}, u32[]{:S(2)}) collective-permute-start(bf16[32,6144]{1,0:T(8,128)(2,1)S(1)} %collective-permute-done.16.refs_9_), channel_id=1, source_target_pairs={{0,1},{1,0},{2,3},{3,2},{4,5},{5,4},{6,7},{7,6},{8,9},{9,8},{10,11... | collective-permute-start | bytes 1179656 | tf_op jit(solution)/shard_map/ppermute | solution.py:333
  37.9 2.3 %collective-permute-start.18 = (bf16[32,6144]{1,0:T(8,128)(2,1)S(1)}, bf16[32,6144]{1,0:T(8,128)(2,1)S(1)}, u32[]{:S(2)}, u32[]{:S(2)}) collective-permute-start(bf16[32,6144]{1,0:T(8,128)(2,1)S(1)} %collective-permute-done.7.refs_8_), channel_id=1, source_target_pairs={{0,1},{1,0},{2,3},{3,2},{4,5},{5,4},{6,7},{7,6},{8,9},{9,8},{10,11... | collective-permute-start | bytes 1179656 | tf_op jit(solution)/shard_map/ppermute | solution.py:333
  37.9 7.8 %collective-permute-start.14 = (bf16[64,3072]{1,0:T(8,128)(2,1)S(1)}, bf16[64,3072]{1,0:T(8,128)(2,1)S(1)}, u32[]{:S(2)}, u32[]{:S(2)}) collective-permute-start(bf16[64,3072]{1,0:T(8,128)(2,1)S(1)} %total.7), channel_id=1, source_target_pairs={{0,4},{1,3},{4,8},{5,1},{8,12},{9,5},{12,14},{13,9},{14,10},{15,13... | collective-permute-start | bytes 1179656 | tf_op jit(solution)/shard_map/ppermute | solution.py:330
  39.5 6.2 %collective-permute-start.13 = (bf16[64,3072]{1,0:T(8,128)(2,1)S(1)}, bf16[64,3072]{1,0:T(8,128)(2,1)S(1)}, u32[]{:S(2)}, u32[]{:S(2)}) collective-permute-start(bf16[64,3072]{1,0:T(8,128)(2,1)S(1)} %get-tuple-element.214), channel_id=1, source_target_pairs={{0,1},{1,0},{2,3},{3,2},{4,5},{5,4},{6,7},{7,6},{8,9},{9,8},{10,11... | collective-permute-start | bytes 1179656 | tf_op jit(solution)/shard_map/ppermute | solution.py:333
  41.8 8.1 %collective-permute-start.20 = (bf16[64,3072]{1,0:T(8,128)(2,1)S(1)}, bf16[64,3072]{1,0:T(8,128)(2,1)S(1)}, u32[]{:S(2)}, u32[]{:S(2)}) collective-permute-start(bf16[64,3072]{1,0:T(8,128)(2,1)S(1)} %total.8), channel_id=1, source_target_pairs={{0,4},{1,3},{4,8},{5,1},{8,12},{9,5},{12,14},{13,9},{14,10},{15,13... | collective-permute-start | bytes 1179656 | tf_op jit(solution)/shard_map/ppermute | solution.py:330
  45.8 4.1 %collective-permute-start.19 = (bf16[64,3072]{1,0:T(8,128)(2,1)S(1)}, bf16[64,3072]{1,0:T(8,128)(2,1)S(1)}, u32[]{:S(2)}, u32[]{:S(2)}) collective-permute-start(bf16[64,3072]{1,0:T(8,128)(2,1)S(1)} %get-tuple-element.227), channel_id=1, source_target_pairs={{0,1},{1,0},{2,3},{3,2},{4,5},{5,4},{6,7},{7,6},{8,9},{9,8},{10,11... | collective-permute-start | bytes 1179656 | tf_op jit(solution)/shard_map/ppermute | solution.py:333
  45.9 6.3 %collective-permute-start.22 = (bf16[64,3072]{1,0:T(8,128)(2,1)S(1)}, bf16[64,3072]{1,0:T(8,128)(2,1)S(1)}, u32[]{:S(2)}, u32[]{:S(2)}) collective-permute-start(bf16[64,3072]{1,0:T(8,128)(2,1)S(1)} %get-tuple-element.235), channel_id=1, source_target_pairs={{0,1},{1,0},{2,3},{3,2},{4,5},{5,4},{6,7},{7,6},{8,9},{9,8},{10,11... | collective-permute-start | bytes 1179656 | tf_op jit(solution)/shard_map/ppermute | solution.py:333
  46.4 7.8 %collective-permute-start.23 = (bf16[64,3072]{1,0:T(8,128)(2,1)S(1)}, bf16[64,3072]{1,0:T(8,128)(2,1)S(1)}, u32[]{:S(2)}, u32[]{:S(2)}) collective-permute-start(bf16[64,3072]{1,0:T(8,128)(2,1)S(1)} %total.9), channel_id=1, source_target_pairs={{0,4},{1,3},{4,8},{5,1},{8,12},{9,5},{12,14},{13,9},{14,10},{15,13... | collective-permute-start | bytes 1179656 | tf_op jit(solution)/shard_map/ppermute | solution.py:330
  50.1 5.9 %collective-permute-start.21 = (bf16[64,3072]{1,0:T(8,128)(2,1)S(1)}, bf16[64,3072]{1,0:T(8,128)(2,1)S(1)}, u32[]{:S(2)}, u32[]{:S(2)}) collective-permute-start(bf16[64,3072]{1,0:T(8,128)(2,1)S(1)} %get-tuple-element.232), channel_id=1, source_target_pairs={{0,1},{1,0},{2,3},{3,2},{4,5},{5,4},{6,7},{7,6},{8,9},{9,8},{10,11... | collective-permute-start | bytes 1179656 | tf_op jit(solution)/shard_map/ppermute | solution.py:333
  50.1 5.9 %collective-permute-start.25 = (bf16[64,3072]{1,0:T(8,128)(2,1)S(1)}, bf16[64,3072]{1,0:T(8,128)(2,1)S(1)}, u32[]{:S(2)}, u32[]{:S(2)}) collective-permute-start(bf16[64,3072]{1,0:T(8,128)(2,1)S(1)} %get-tuple-element.242), channel_id=1, source_target_pairs={{0,1},{1,0},{2,3},{3,2},{4,5},{5,4},{6,7},{7,6},{8,9},{9,8},{10,11... | collective-permute-start | bytes 1179656 | tf_op jit(solution)/shard_map/ppermute | solution.py:333
  50.6 7.8 %collective-permute-start.26 = (bf16[64,3072]{1,0:T(8,128)(2,1)S(1)}, bf16[64,3072]{1,0:T(8,128)(2,1)S(1)}, u32[]{:S(2)}, u32[]{:S(2)}) collective-permute-start(bf16[64,3072]{1,0:T(8,128)(2,1)S(1)} %total.10), channel_id=1, source_target_pairs={{0,4},{1,3},{4,8},{5,1},{8,12},{9,5},{12,14},{13,9},{14,10},{15,13... | collective-permute-start | bytes 1179656 | tf_op jit(solution)/shard_map/ppermute | solution.py:330
  54.4 8.3 %collective-permute-start.24 = (bf16[64,3072]{1,0:T(8,128)(2,1)S(1)}, bf16[64,3072]{1,0:T(8,128)(2,1)S(1)}, u32[]{:S(2)}, u32[]{:S(2)}) collective-permute-start(bf16[64,3072]{1,0:T(8,128)(2,1)S(1)} %total.11), channel_id=1, source_target_pairs={{0,4},{1,3},{4,8},{5,1},{8,12},{9,5},{12,14},{13,9},{14,10},{15,13... | collective-permute-start | bytes 1179656 | tf_op jit(solution)/shard_map/ppermute | solution.py:330
  58.6 8.3 %collective-permute-start.28 = (bf16[64,3072]{1,0:T(8,128)(2,1)S(1)}, bf16[64,3072]{1,0:T(8,128)(2,1)S(1)}, u32[]{:S(2)}, u32[]{:S(2)}) collective-permute-start(bf16[64,3072]{1,0:T(8,128)(2,1)S(1)} %total.12), channel_id=1, source_target_pairs={{0,4},{1,3},{4,8},{5,1},{8,12},{9,5},{12,14},{13,9},{14,10},{15,13... | collective-permute-start | bytes 1179656 | tf_op jit(solution)/shard_map/ppermute | solution.py:330
  62.8 8.3 %collective-permute-start.27 = (bf16[64,3072]{1,0:T(8,128)(2,1)S(1)}, bf16[64,3072]{1,0:T(8,128)(2,1)S(1)}, u32[]{:S(2)}, u32[]{:S(2)}) collective-permute-start(bf16[64,3072]{1,0:T(8,128)(2,1)S(1)} %total.13), channel_id=1, source_target_pairs={{0,4},{1,3},{4,8},{5,1},{8,12},{9,5},{12,14},{13,9},{14,10},{15,13... | collective-permute-start | bytes 1179656 | tf_op jit(solution)/shard_map/ppermute | solution.py:330
  71.1 1.5 %collective-permute-start.30 = (bf16[32,3072]{1,0:T(8,128)(2,1)S(1)}, bf16[32,3072]{1,0:T(8,128)(2,1)S(1)}, u32[]{:S(2)}, u32[]{:S(2)}) collective-permute-start(bf16[32,3072]{1,0:T(8,128)(2,1)S(1)} %get-tuple-element.261), channel_id=1, source_target_pairs={{0,1},{1,0},{2,3},{3,2},{4,5},{5,4},{6,7},{7,6},{8,9},{9,8},{10,11... | collective-permute-start | bytes 589832 | tf_op jit(solution)/shard_map/ppermute | solution.py:333
  71.2 1.7 %collective-permute-start.29 = (bf16[32,3072]{1,0:T(8,128)(2,1)S(1)}, bf16[32,3072]{1,0:T(8,128)(2,1)S(1)}, u32[]{:S(2)}, u32[]{:S(2)}) collective-permute-start(bf16[32,3072]{1,0:T(8,128)(2,1)S(1)} %get-tuple-element.255), channel_id=1, source_target_pairs={{0,1},{1,0},{2,3},{3,2},{4,5},{5,4},{6,7},{7,6},{8,9},{9,8},{10,11... | collective-permute-start | bytes 589832 | tf_op jit(solution)/shard_map/ppermute | solution.py:333

commit v9 on v8

--- a/solution.py
+++ b/solution.py
@@ -65,12 +65,13 @@
 
 def ring_pairs():
     path = [2 * p if p < RING // 2 else 2 * (RING - 1 - p) + 1 for p in range(RING)]
-    along, across = [], []
+    along, gather_across, sum_across = [], [], []
     for place, chip in enumerate(path):
         ahead, behind = path[(place + 1) % RING], path[(place - 1) % RING]
         along += [(2 * chip, 2 * ahead), (2 * chip + 1, 2 * behind + 1)]
-        across += [(2 * chip, 2 * behind + 1), (2 * chip + 1, 2 * ahead)]
-    return along, across
+        gather_across += [(2 * chip, 2 * behind + 1), (2 * chip + 1, 2 * ahead)]
+        sum_across += [(2 * chip, 2 * ahead + 1), (2 * chip + 1, 2 * behind)]
+    return along, gather_across, sum_across
 
 
 def chip_order(me):
@@ -139,7 +140,7 @@
 
 
 def input_kernel(me_ref, dht_ref, w_ref, w_hbm, *refs, other, piece, wide, more):
-    outs, part_ref, sems = refs[-(RING + 2 + more) :][:RING], refs[-2], refs[-1]
+    outs, part_ref, sems = refs[-(RING + 3 + more) :][: RING + 1], refs[-2], refs[-1]
     half = outs[0].shape[1]
     if more:
         following = (other, piece + 1) if piece + 1 < PIECES else (False, 0)
@@ -156,15 +157,17 @@
         here = pl.ds(i * step, step)
         part = jnp.dot(w_ref[here, :], dht_ref[...], preferred_element_type=jnp.float32)
         part_ref[:, here] = part.astype(jnp.bfloat16).T
+        at = 0
         for j, out in enumerate(outs):
             rows = out.shape[0]
             store = pltpu.make_async_copy(
-                part_ref.at[pl.ds(j * rows, rows), here],
+                part_ref.at[pl.ds(at, rows), here],
                 out.at[:, pl.ds(piece * wide + i * step, step)],
                 sems.at[i, j],
             )
             store.start()
             stores.append(store)
+            at += rows
     for store in stores:
         store.wait()
     if more:
@@ -177,23 +180,26 @@
     wide = half // PIECES
     rows = tokens // RING
     more = other or piece + 1 < PIECES
-    outs = (jax.ShapeDtypeStruct((rows, half), jnp.bfloat16),) * RING
+    outs = tuple(
+        jax.ShapeDtypeStruct((count, half), jnp.bfloat16)
+        for count in [rows // 2] * 2 + [rows] * (RING - 1)
+    )
     following = (jax.ShapeDtypeStruct((wide, ff), jnp.bfloat16),) if more else ()
     result = pl.pallas_call(
         lambda *refs: input_kernel(*refs, other=other, piece=piece, wide=wide, more=more),
         out_shape=outs + following,
         in_specs=[SCALAR, WHOLE, WHOLE, OUTSIDE] + [ANYWHERE] * len(before),
-        out_specs=(ANYWHERE,) * RING + (WHOLE,) * len(following),
+        out_specs=(ANYWHERE,) * len(outs) + (WHOLE,) * len(following),
         input_output_aliases={4 + i: i for i in range(len(before))},
         scratch_shapes=[
             pltpu.VMEM((tokens, wide), jnp.bfloat16),
-            pltpu.SemaphoreType.DMA((PIECE_STEPS + 1, RING)),
+            pltpu.SemaphoreType.DMA((PIECE_STEPS + 1, len(outs))),
         ],
         compiler_params=pltpu.CompilerParams(vmem_limit_bytes=VMEM_LIMIT),
         cost_estimate=cost(PIECE_COST),
         name="input_piece",
     )(me, dht, w, weight, *before)
-    return result[:RING], (result[RING] if more else None)
+    return result[: len(outs)], (result[-1] if more else None)
 
 
 def weight_kernel(dh_ref, *refs, piece, wide, step):
@@ -247,70 +253,59 @@
     )(dh, *blocks, *before)
 
 
-def total_kernel(part_ref, twin_ref, *refs):
+def total_kernel(part_ref, twin_ref, *refs, count):
     rows = part_ref.shape[0] // 2
-    for here, there in ((pl.ds(0, rows), pl.ds(rows, rows)), (pl.ds(rows, rows), pl.ds(0, rows))):
-        total = part_ref[here, :].astype(jnp.float32) + twin_ref[there, :].astype(jnp.float32)
-        for ref in refs[:-1]:
-            total = total + ref[here, :].astype(jnp.float32)
-        refs[-1][here, :] = total.astype(refs[-1].dtype)
-
-
-def total(*terms):
-    return pl.pallas_call(
-        total_kernel,
-        out_shape=jax.ShapeDtypeStruct(terms[0].shape, terms[0].dtype),
+    came, outs = refs[:-count], refs[-count:]
+    for i in range(2):
+        here, there = pl.ds(i * rows, rows), pl.ds((1 - i) * rows, rows)
+        sums = part_ref[here, :].astype(jnp.float32) + twin_ref[there, :].astype(jnp.float32)
+        for ref in came:
+            sums = sums + ref[here, :].astype(jnp.float32)
+        if count == 1:
+            outs[0][here, :] = sums.astype(outs[0].dtype)
+        else:
+            outs[i][...] = sums.astype(outs[i].dtype)
+
+
+def total(*terms, count=1):
+    rows, half = terms[0].shape
+    out = jax.ShapeDtypeStruct((rows // count, half), terms[0].dtype)
+    result = pl.pallas_call(
+        lambda *refs: total_kernel(*refs, count=count),
+        out_shape=(out,) * count,
         in_specs=[WHOLE] * len(terms),
-        out_specs=WHOLE,
+        out_specs=(WHOLE,) * count,
         compiler_params=pltpu.CompilerParams(vmem_limit_bytes=VMEM_LIMIT),
         cost_estimate=cost(0.1),
         name="total",
     )(*terms)
-
-
-def halves_kernel(own_ref, came_ref, kept_ref, sent_ref):
-    rows = kept_ref.shape[0]
-    for ref, here in ((kept_ref, pl.ds(0, rows)), (sent_ref, pl.ds(rows, rows))):
-        both = own_ref[here, :].astype(jnp.float32) + came_ref[here, :].astype(jnp.float32)
-        ref[...] = both.astype(ref.dtype)
-
-
-def halves(own, came):
-    shape = (own.shape[0] // 2, own.shape[1])
-    return pl.pallas_call(
-        halves_kernel,
-        out_shape=(
-            jax.ShapeDtypeStruct(shape, jnp.float32),
-            jax.ShapeDtypeStruct(shape, jnp.bfloat16),
-        ),
-        in_specs=[WHOLE, WHOLE],
-        out_specs=(WHOLE, WHOLE),
-        compiler_params=pltpu.CompilerParams(vmem_limit_bytes=VMEM_LIMIT),
-        cost_estimate=cost(0.1),
-        name="halves",
-    )(own, came)
-
-
-def last_kernel(me_ref, mine_ref, mine_came_ref, other_ref, other_came_ref, out_ref):
+    return result[0] if count == 1 else result
+
+
+def last_kernel(me_ref, *refs):
+    out_ref = refs[-1]
     core = me_ref[0] % 2
-    half = mine_ref.shape[1]
-    pairs = ((core, mine_ref, mine_came_ref), (1 - core, other_ref, other_came_ref))
-    for number, kept, came in pairs:
+    half = refs[0].shape[1]
+    count = (len(refs) - 1) // 2
+    for number, terms in ((core, refs[:count]), (1 - core, refs[count:-1])):
+        sums = terms[0][...].astype(jnp.float32)
+        for term in terms[1:]:
+            sums = sums + term[...].astype(jnp.float32)
         here = pl.ds(pl.multiple_of(number * half, half), half)
-        out_ref[:, here] = (kept[...] + came[...].astype(jnp.float32)).astype(out_ref.dtype)
-
-
-def last(me, mine, mine_came, other, other_came):
-    shape = (mine.shape[0], 2 * mine.shape[1])
+        out_ref[:, here] = sums.astype(out_ref.dtype)
+
+
+def last(me, mine, other):
+    rows, half = mine[0].shape
     return pl.pallas_call(
         last_kernel,
-        out_shape=jax.ShapeDtypeStruct(shape, jnp.bfloat16),
-        in_specs=[SCALAR] + [WHOLE] * 4,
+        out_shape=jax.ShapeDtypeStruct((rows, 2 * half), jnp.bfloat16),
+        in_specs=[SCALAR] + [WHOLE] * (len(mine) + len(other)),
         out_specs=WHOLE,
         compiler_params=pltpu.CompilerParams(vmem_limit_bytes=VMEM_LIMIT),
         cost_estimate=cost(0.3),
         name="last",
-    )(me, mine, mine_came, other, other_came)
+    )(me, *mine, *other)
 
 
 def after(x, *others):
@@ -323,7 +318,7 @@
     if n != 2 * RING or rows % 16 or width % (2 * PIECES * PIECE_STEPS * 128):
         return plain(out_grad, pre_act, layer_input, weight)
 
-    along, across = ring_pairs()
+    along, gather_across, sum_across = ring_pairs()
     twins = [(i, i ^ 1) for i in range(n)]
 
     def ring(x):
@@ -337,38 +332,38 @@
     )
     me = lax.axis_index("gx").astype(jnp.int32).reshape(1)
 
-    a1, twin = ring(layer_input), swap(layer_input)
     dh, dht, w = hidden(me, out_grad, pre_act, weight)
-    b1 = lax.ppermute(after(layer_input, dh), "gx", across)
+    a1, twin = ring(after(layer_input, dh)), swap(layer_input)
 
     def product(other, piece, w, before, *ties):
         return input_piece(me, after(dht, *ties), w, weight, before, other, piece)
 
     go, w = product(True, 0, w, ())
+    b1 = lax.ppermute(after(layer_input, go[0]), "gx", gather_across)
+    go, w = product(True, 1, w, go)
     a1 = after(a1, go[0])
     a2, sa1 = ring(a1), swap(a1)
-    go, w = product(True, 1, w, go, a1, twin)
+    go, w = product(True, 2, w, go, a1, twin)
     b1 = after(b1, go[0])
     b2, sb1 = ring(b1), swap(b1)
-    go, w = product(True, 2, w, go, b1, sa1)
+    go, w = product(True, 3, w, go, b1, sa1)
     a2 = after(a2, go[0])
     a3, sa2 = ring(a2), swap(a2)
-    go, w = product(True, 3, w, go, a2, sb1)
-    b2 = after(b2, go[0])
+    gm, w = product(False, 0, w, (), a2, sb1)
+    b2 = after(b2, gm[0])
     b3, sb2 = ring(b2), swap(b2)
-    gm, w = product(False, 0, w, (), b2, sa2)
+    gm, w = product(False, 1, w, gm, b2, sa2)
     a3 = after(a3, gm[0])
     a4, sa3 = ring(a3), swap(a3)
-    own_o, behind_o, opposite_o, ahead_o = go[0], go[1:4], go[4], go[5:]
+    own_o, behind_o, opposite_o, ahead_o = go[:2], go[2:5], go[5], go[6:]
     opposite_from = swap(after(opposite_o, gm[0]))
-    gm, w = product(False, 1, w, gm, a3, sb2)
-    gm, w = product(False, 2, w, gm, sa3)
-    gm, _ = product(False, 3, w, gm, b3, opposite_from)
-    own_m, behind_m, opposite_m, ahead_m = gm[0], gm[1:4], gm[4], gm[5:]
+    gm, w = product(False, 2, w, gm, a3, sb2)
+    gm, _ = product(False, 3, w, gm, sa3, b3, opposite_from)
+    own_m, behind_m, opposite_m, ahead_m = gm[:2], gm[2:5], gm[5], gm[6:]
     sent = total(opposite_m, opposite_from)
     r4m = ring(sent)
-    a4 = after(a4, sent)
-    sa4 = swap(a4)
+    a4, b3 = after(a4, sent), after(b3, sent)
+    sa4, sb3 = swap(a4), swap(b3)
     from_o, from_m = [None] * 3, [None] * 3
     from_o[2], from_m[2] = swap(after(behind_m[2], sent)), swap(after(behind_o[2], sent))
 
@@ -379,7 +374,6 @@
     def send(k, ahead, came, *ring_terms):
         return total(ahead[k - 1], came[k - 1], *ring_terms)
 
-    sb3 = swap(after(b3, sent))
     blocks = (layer_input, twin, a1, b1, a2, b2, a3, b3, a4, sa4, sb1, sa1, sb2, sa2, sb3, sa3)
     gw = gradient(0, (), sent, from_o[2])
     from_o[2] = after(from_o[2], gw[1])
@@ -397,18 +391,17 @@
     sent = send(2, ahead_m, from_m, after(r3m, gw[1]))
     r2m = ring(sent)
     gw = gradient(4, gw, sent, from_o[0], from_m[0])
-    sent = send(1, ahead_o, from_o, after(r2o, gw[1]))
-    r1o = ring(sent)
-    gw = gradient(5, gw, sent)
-    sent = send(1, ahead_m, from_m, after(r2m, gw[1]))
-    r1m = ring(sent)
-    gw = gradient(6, gw, sent)
-    kept_o, sent_o = halves(own_o, after(r1o, gw[1]))
-    came_m = swap(sent_o)
-    gw = gradient(7, gw, sent_o)
-    kept_m, sent_m = halves(own_m, after(r1m, gw[0]))
-    came_o = swap(sent_m)
-    return (last(me, kept_m, came_m, kept_o, came_o), gw[0])
+    sent = total(ahead_o[0], from_o[0], after(r2o, gw[1]), count=2)
+    r1o, x1m = ring(sent[0]), lax.ppermute(sent[1], "gx", sum_across)
+    own_from_m, own_from_o = swap(after(own_o[1], sent[0])), swap(after(own_m[1], sent[0]))
+    gw = gradient(5, gw, sent[0])
+    sent = total(ahead_m[0], from_m[0], after(r2m, gw[1]), count=2)
+    r1m, x1o = ring(sent[0]), lax.ppermute(sent[1], "gx", sum_across)
+    gw = gradient(6, gw, sent[0])
+    gw = gradient(7, gw, own_from_m, own_from_o)
+    r1m = after(r1m, gw[0])
+    mine = (own_m[0], own_from_m, r1m, x1m)
+    return (last(me, mine, (own_o[0], own_from_o, r1o, x1o)), gw[0])
 
 
 def solution(mesh):

time: 74 us -> 80.1 us (1.082)
  waiting for transfers between devices: 9.36 us -> 16.1 us
  starting transfers between devices: 28.9 us -> 24.3 us
  Pallas kernels: 34.6 us -> 38.4 us
    ppermute x13, waiting for transfers between devices: 7.37 us -> 14.5 us  [ring(): return lax.ppermute(x, 'gx', along)]
    ppermute x13, starting transfers between devices: 22.7 us -> 17.9 us  [ring(): return lax.ppermute(x, 'gx', along)]
    pallas_call x8, Pallas kernels: 15.8 us -> 19.5 us  [input_piece(): pl.pallas_call(lambda *refs: input_kernel(*refs, other=other, piece=piece...]
    ppermute x1 -> x3, starting transfers between devices: 0.74 us -> 2.49 us  [the longest x1 1.62 us: on_device(): r1o, x1m = (ring(sent[0]), lax.ppermute(sent[1], 'gx', sum_across))]
    ppermute x17, starting transfers between devices: 5.44 us -> 4 us  [swap(): return lax.ppermute(x, 'gx', twins)]
    pallas_call x10 -> x8, Pallas kernels: 1.94 us -> 1.87 us  [the longest x1 0.94 us: last(): pl.pallas_call(last_kernel, out_shape=jax.ShapeDtypeStruct((rows, 2 * hal...]
  transfers between devices with their start and end apart: 31 -> 33, of which waited for: 15 -> 11; matrix products, arithmetic and copies ran while one was open for 0% -> 0% of each run, Pallas kernels for 46% -> 42%
where the time goes in v9:
time: 80.1 us; the launch traced here: 79.8 us
  Pallas kernels  38.4 us (48%)
  starting transfers between devices  24.3 us (30%)
  waiting for transfers between devices  16.1 us (20%)
  between operations  0.96 us (1%)
    pallas_call x8, Pallas kernels, input_piece(): pl.pallas_call(lambda *refs: input_kernel(*refs, other=other, piece=piece...  19.5 us
    ppermute x13, starting transfers between devices, ring(): return lax.ppermute(x, 'gx', along)  17.9 us
    ppermute x13, waiting for transfers between devices, ring(): return lax.ppermute(x, 'gx', along)  14.5 us
    pallas_call x8, Pallas kernels, weight_piece(): pl.pallas_call(lambda *refs: weight_kernel(*refs, piece=piece, wide=wide,...  13.1 us
    ppermute x17, starting transfers between devices, swap(): return lax.ppermute(x, 'gx', twins)  4 us
    pallas_call x1, Pallas kernels, hidden(): pl.pallas_call(hidden_kernel, out_shape=(jax.ShapeDtypeStruct(shape, dtyp...  3.87 us
    ppermute x1, starting transfers between devices, on_device(): r1o, x1m = (ring(sent[0]), lax.ppermute(sent[1], 'gx', sum_across))  1.62 us
  transfers between devices with their start and end apart: 33, of which 11 were waited for; matrix products, arithmetic and copies ran while one was open for 0% of the time, Pallas kernels for 42%

profile of v9, /device:TPU:0, one launch (start us, length us, event | category | flops | bytes accessed | tf_op | source)
XLA Modules:
  0.0 79.8 jit_solution(10283009402468015337)
XLA Ops:
  0.6 3.9 %hidden.1 = (bf16[512,1536]{1,0:T(8,128)(2,1)S(1)}, bf16[1536,512]{1,0:T(8,128)(2,1)S(1)}, bf16[768,1536]{1,0:T(8,128)(2,1)S(1)}) custom-call(s32[1]{0:T(128)} %bitcast.me_ref.refs_0_, bf16[512,1536]{1,0:T(8,128)(2,1)} %og_hbm.1, bf16[512,1536]{1,0:T(8,128)(2,1)} %pre_hbm.1, bf16[6144,1536]{1,0:T(8,128)(2,1)} %refs_3_.15), custom_call_target="tpu_custom_call" | custom-call | flops 1150000000 | tf_op jit(solution)/shard_map/hidden/pallas_call | solution.py:116
  4.5 3.1 %collective-permute-start = (bf16[32,6144]{1,0:T(8,128)(2,1)S(1)}, bf16[32,6144]{1,0:T(8,128)(2,1)S(1)}, u32[]{:S(2)}, u32[]{:S(2)}) collective-permute-start(bf16[32,6144]{1,0:T(8,128)(2,1)S(1)} %copy-done), channel_id=1, source_target_pairs={{0,4},{1,3},{4,8},{5,1},{8,12},{9,5},{12,14},{13,9},{14,10},{15,13... | collective-permute-start | bytes 1179656 | tf_op jit(solution)/shard_map/ppermute | solution.py:325
  7.6 2.1 %input_piece.8 = (bf16[32,3072]{1,0:T(8,128)(2,1)S(1)}, bf16[32,3072]{1,0:T(8,128)(2,1)S(1)}, bf16[64,3072]{1,0:T(8,128)(2,1)S(1)}, bf16[64,3072]{1,0:T(8,128)(2...) custom-call(s32[1]{0:T(128)} %bitcast.me_ref.refs_0_, ...), custom_call_target="tpu_custom_call" | custom-call | flops 115000000 | tf_op jit(solution)/shard_map/input_piece/pallas_call | solution.py:188
  9.7 0.7 collective-permute-start.2
  10.4 2.4 %input_piece.9 = (bf16[32,3072]{1,0:T(8,128)(2,1)S(1)}, bf16[32,3072]{1,0:T(8,128)(2,1)S(1)}, bf16[64,3072]{1,0:T(8,128)(2,1)S(1)}, bf16[64,3072]{1,0:T(8,128)(2...) custom-call(s32[1]{0:T(128)} %bitcast.me_ref.refs_0_, ...), custom_call_target="tpu_custom_call", output_to_operand_aliasing={{0}: (4, {}), {1}: (5, {}), {2}: (6, {}), {3}: (7, {}), {4}... | custom-call | flops 115000000 | tf_op jit(solution)/shard_map/input_piece/pallas_call | solution.py:188
  12.8 1.1 %collective-permute-done.refs_3_ = bf16[32,6144]{1,0:T(8,128)(2,1)S(1)} collective-permute-done((bf16[32,6144]{1,0:T(8,128)(2,1)S(1)}, bf16[32,6144]{1,0:T(8,128)(2,1)S(1)}, u32[]{:S(2)}, u32[]{:S(2)}) %collective-permute-start) | collective-permute-done | bytes 393248 | tf_op jit(solution)/shard_map/ppermute | solution.py:325
  13.9 2.5 %collective-permute-start.1 = (bf16[32,6144]{1,0:T(8,128)(2,1)S(1)}, bf16[32,6144]{1,0:T(8,128)(2,1)S(1)}, u32[]{:S(2)}, u32[]{:S(2)}) collective-permute-start(bf16[32,6144]{1,0:T(8,128)(2,1)S(1)} %collective-permute-done.refs_3_), channel_id=1, source_target_pairs={{0,4},{1,3},{4,8},{5,1},{8,12},{9,5},{12,14},{13,9},{14,10},{15,13... | collective-permute-start | bytes 1179656 | tf_op jit(solution)/shard_map/ppermute | solution.py:325
  16.4 2.4 %input_piece.10 = (bf16[32,3072]{1,0:T(8,128)(2,1)S(1)}, bf16[32,3072]{1,0:T(8,128)(2,1)S(1)}, bf16[64,3072]{1,0:T(8,128)(2,1)S(1)}, bf16[64,3072]{1,0:T(8,128)(...) custom-call(s32[1]{0:T(128)} %bitcast.me_ref.refs_0_, ...), custom_call_target="tpu_custom_call", output_to_operand_aliasing={{0}: (4, {}), {1}: (5, {}), {2}: (6, {}), {3}: (7, {}), {4}... | custom-call | flops 115000000 | tf_op jit(solution)/shard_map/input_piece/pallas_call | solution.py:188
  18.8 0.7 collective-permute-start.7
  19.5 1.0 %collective-permute-start.6 = (bf16[32,6144]{1,0:T(8,128)(2,1)S(1)}, bf16[32,6144]{1,0:T(8,128)(2,1)S(1)}, u32[]{:S(2)}, u32[]{:S(2)}) collective-permute-start(bf16[32,6144]{1,0:T(8,128)(2,1)S(1)} %collective-permute-done.2.refs_4_), channel_id=1, source_target_pairs={{0,4},{1,3},{4,8},{5,1},{8,12},{9,5},{12,14},{13,9},{14,10},{15,13... | collective-permute-start | bytes 1179656 | tf_op jit(solution)/shard_map/ppermute | solution.py:325
  20.5 2.4 %input_piece.11 = (bf16[32,3072]{1,0:T(8,128)(2,1)S(1)}, bf16[32,3072]{1,0:T(8,128)(2,1)S(1)}, bf16[64,3072]{1,0:T(8,128)(2,1)S(1)}, bf16[64,3072]{1,0:T(8,128)(...) custom-call(s32[1]{0:T(128)} %bitcast.me_ref.refs_0_, ...), custom_call_target="tpu_custom_call", output_to_operand_aliasing={{0}: (4, {}), {1}: (5, {}), {2}: (6, {}), {3}: (7, {}), {4}... | custom-call | flops 115000000 | tf_op jit(solution)/shard_map/input_piece/pallas_call | solution.py:188
  22.9 0.4 collective-permute-start.8
  23.3 1.5 %collective-permute-start.5 = (bf16[32,6144]{1,0:T(8,128)(2,1)S(1)}, bf16[32,6144]{1,0:T(8,128)(2,1)S(1)}, u32[]{:S(2)}, u32[]{:S(2)}) collective-permute-start(bf16[32,6144]{1,0:T(8,128)(2,1)S(1)} %collective-permute-done.1.refs_5_), channel_id=1, source_target_pairs={{0,4},{1,3},{4,8},{5,1},{8,12},{9,5},{12,14},{13,9},{14,10},{15,13... | collective-permute-start | bytes 1179656 | tf_op jit(solution)/shard_map/ppermute | solution.py:325
  24.8 2.8 %input_piece.12 = (bf16[32,3072]{1,0:T(8,128)(2,1)S(1)}, bf16[32,3072]{1,0:T(8,128)(2,1)S(1)}, bf16[64,3072]{1,0:T(8,128)(2,1)S(1)}, bf16[64,3072]{1,0:T(8,128)(...) custom-call(s32[1]{0:T(128)} %bitcast.me_ref.refs_0_, ...), custom_call_target="tpu_custom_call" | custom-call | flops 115000000 | tf_op jit(solution)/shard_map/input_piece/pallas_call | solution.py:188
  27.6 0.1 collective-permute-start.12
  27.7 2.5 %collective-permute-start.10 = (bf16[32,6144]{1,0:T(8,128)(2,1)S(1)}, bf16[32,6144]{1,0:T(8,128)(2,1)S(1)}, u32[]{:S(2)}, u32[]{:S(2)}) collective-permute-start(bf16[32,6144]{1,0:T(8,128)(2,1)S(1)} %collective-permute-done.6.refs_6_), channel_id=1, source_target_pairs={{0,4},{1,3},{4,8},{5,1},{8,12},{9,5},{12,14},{13,9},{14,10},{15,13... | collective-permute-start | bytes 1179656 | tf_op jit(solution)/shard_map/ppermute | solution.py:325
  30.2 2.8 %input_piece.13 = (bf16[32,3072]{1,0:T(8,128)(2,1)S(1)}, bf16[32,3072]{1,0:T(8,128)(2,1)S(1)}, bf16[64,3072]{1,0:T(8,128)(2,1)S(1)}, bf16[64,3072]{1,0:T(8,128)(...) custom-call(s32[1]{0:T(128)} %bitcast.me_ref.refs_0_, ...), custom_call_target="tpu_custom_call", output_to_operand_aliasing={{0}: (4, {}), {1}: (5, {}), {2}: (6, {}), {3}: (7, {}), {4}... | custom-call | flops 115000000 | tf_op jit(solution)/shard_map/input_piece/pallas_call | solution.py:188
  33.1 0.1 collective-permute-start.9
  33.1 0.5 collective-permute-start.11
  33.6 0.4 collective-permute-start.16
  34.1 2.8 %input_piece.14 = (bf16[32,3072]{1,0:T(8,128)(2,1)S(1)}, bf16[32,3072]{1,0:T(8,128)(2,1)S(1)}, bf16[64,3072]{1,0:T(8,128)(2,1)S(1)}, bf16[64,3072]{1,0:T(8,128)(...) custom-call(s32[1]{0:T(128)} %bitcast.me_ref.refs_0_, ...), custom_call_target="tpu_custom_call", output_to_operand_aliasing={{0}: (4, {}), {1}: (5, {}), {2}: (6, {}), {3}: (7, {}), {4}... | custom-call | flops 115000000 | tf_op jit(solution)/shard_map/input_piece/pallas_call | solution.py:188
  36.9 1.9 %input_piece.15 = (bf16[32,3072]{1,0:T(8,128)(2,1)S(1)}, bf16[32,3072]{1,0:T(8,128)(2,1)S(1)}, bf16[64,3072]{1,0:T(8,128)(2,1)S(1)}, bf16[64,3072]{1,0:T(8,128)(...) custom-call(s32[1]{0:T(128)} %bitcast.me_ref.refs_0_, ...), custom_call_target="tpu_custom_call", output_to_operand_aliasing={{0}: (4, {}), {1}: (5, {}), {2}: (6, {}), {3}: (7, {}), {4}... | custom-call | flops 115000000 | tf_op jit(solution)/shard_map/input_piece/pallas_call | solution.py:188
  38.8 0.1 total.7
  38.9 2.5 %collective-permute-done.16.refs_9_ = bf16[32,6144]{1,0:T(8,128)(2,1)S(1)} collective-permute-done((bf16[32,6144]{1,0:T(8,128)(2,1)S(1)}, bf16[32,6144]{1,0:T(8,128)(2,1)S(1)}, u32[]{:S(2)}, u32[]{:S(2)}) %collective-permute-start.16) | collective-permute-done | bytes 393248 | tf_op jit(solution)/shard_map/ppermute | solution.py:325
  41.4 0.5 collective-permute-start.18
  41.9 0.8 collective-permute-start.14
  42.7 0.4 collective-permute-done.15.refs_1_
  43.1 0.6 collective-permute-done.18.refs_15_
  43.7 0.6 collective-permute-done.17.refs_10_
  44.3 1.5 %weight_piece.8 = (bf16[6144,1536]{1,0:T(8,128)(2,1)}, bf16[768,1536]{1,0:T(8,128)(2,1)S(1)}) custom-call(bf16[512,1536]{1,0:T(8,128)(2,1)S(1)} %get-tuple-element.273.refs_0_, bf16[32,6144]{1,0:T(8,128)(2,1)S(1)} %copy-done, bf16[32,6144]{1,0:T(8,128)(2,1)S(1)} %collective-permute-done.3.refs_2_, bf16[32,6144]{1,0:T(8,128)(2,1)S(1)} %collective-permute-done.refs_3_, ...), custom_call_target="tpu_custom_call" | custom-call | flops 115000000 | tf_op jit(solution)/shard_map/weight_piece/pallas_call | solution.py:242
  45.7 0.1 total.8
  45.8 0.8 %collective-permute-start.20 = (bf16[64,3072]{1,0:T(8,128)(2,1)S(1)}, bf16[64,3072]{1,0:T(8,128)(2,1)S(1)}, u32[]{:S(2)}, u32[]{:S(2)}) collective-permute-start(bf16[64,3072]{1,0:T(8,128)(2,1)S(1)} %total.8), channel_id=1, source_target_pairs={{0,4},{1,3},{4,8},{5,1},{8,12},{9,5},{12,14},{13,9},{14,10},{15,13... | collective-permute-start | bytes 1179656 | tf_op jit(solution)/shard_map/ppermute | solution.py:325
  46.7 1.5 %weight_piece.9 = (bf16[6144,1536]{1,0:T(8,128)(2,1)}, bf16[768,1536]{1,0:T(8,128)(2,1)S(1)}) custom-call(bf16[512,1536]{1,0:T(8,128)(2,1)S(1)} %get-tuple-element.273.refs_0_, bf16[32,6144]{1,0:T(8,128)(2,1)S(1)} %copy-done, bf16[32,6144]{1,0:T(8,128)(2,1)S(1)} %collective-permute-done.3.refs_2_, ...), custom_call_target="tpu_custom_call", output_to_operand_aliasing={{0}: (18, {})} | custom-call | flops 115000000 | tf_op jit(solution)/shard_map/weight_piece/pallas_call | solution.py:242
  48.2 1.5 %collective-permute-done.14.refs_2_ = bf16[64,3072]{1,0:T(8,128)(2,1)S(1)} collective-permute-done((bf16[64,3072]{1,0:T(8,128)(2,1)S(1)}, bf16[64,3072]{1,0:T(8,128)(2,1)S(1)}, u32[]{:S(2)}, u32[]{:S(2)}) %collective-permute-start.14) | collective-permute-done | bytes 393248 | tf_op jit(solution)/shard_map/ppermute | solution.py:325
  49.7 0.1 total.9
  49.9 0.1 collective-permute-start.19
  49.9 0.5 collective-permute-start.23
  50.4 0.8 collective-permute-start.24
  51.2 1.5 %weight_piece.10 = (bf16[6144,1536]{1,0:T(8,128)(2,1)}, bf16[768,1536]{1,0:T(8,128)(2,1)S(1)}) custom-call(bf16[512,1536]{1,0:T(8,128)(2,1)S(1)} %get-tuple-element.273.refs_0_, bf16[32,6144]{1,0:T(8,128)(2,1)S(1)} %copy-done, bf16[32,6144]{1,0:T(8,128)(2,1)S(1)} %collective-permute-done.3.refs_2_, ...), custom_call_target="tpu_custom_call", output_to_operand_aliasing={{0}: (18, {})} | custom-call | flops 115000000 | tf_op jit(solution)/shard_map/weight_piece/pallas_call | solution.py:242
  52.7 1.2 %collective-permute-done.20.refs_2_ = bf16[64,3072]{1,0:T(8,128)(2,1)S(1)} collective-permute-done((bf16[64,3072]{1,0:T(8,128)(2,1)S(1)}, bf16[64,3072]{1,0:T(8,128)(2,1)S(1)}, u32[]{:S(2)}, u32[]{:S(2)}) %collective-permute-start.20) | collective-permute-done | bytes 393248 | tf_op jit(solution)/shard_map/ppermute | solution.py:325
  53.9 0.1 total.10
  54.1 0.1 collective-permute-start.21
  54.1 0.5 collective-permute-start.25
  54.6 0.8 collective-permute-start.22
  55.4 1.5 %weight_piece.11 = (bf16[6144,1536]{1,0:T(8,128)(2,1)}, bf16[768,1536]{1,0:T(8,128)(2,1)S(1)}) custom-call(bf16[512,1536]{1,0:T(8,128)(2,1)S(1)} %get-tuple-element.273.refs_0_, bf16[32,6144]{1,0:T(8,128)(2,1)S(1)} %copy-done, bf16[32,6144]{1,0:T(8,128)(2,1)S(1)} %collective-permute-done.3.refs_2_, ...), custom_call_target="tpu_custom_call", output_to_operand_aliasing={{0}: (18, {})} | custom-call | flops 115000000 | tf_op jit(solution)/shard_map/weight_piece/pallas_call | solution.py:242
  57.0 1.2 %collective-permute-done.24.refs_2_ = bf16[64,3072]{1,0:T(8,128)(2,1)S(1)} collective-permute-done((bf16[64,3072]{1,0:T(8,128)(2,1)S(1)}, bf16[64,3072]{1,0:T(8,128)(2,1)S(1)}, u32[]{:S(2)}, u32[]{:S(2)}) %collective-permute-start.24) | collective-permute-done | bytes 393248 | tf_op jit(solution)/shard_map/ppermute | solution.py:325
  58.2 0.1 total.11
  58.4 0.8 %collective-permute-start.27 = (bf16[64,3072]{1,0:T(8,128)(2,1)S(1)}, bf16[64,3072]{1,0:T(8,128)(2,1)S(1)}, u32[]{:S(2)}, u32[]{:S(2)}) collective-permute-start(bf16[64,3072]{1,0:T(8,128)(2,1)S(1)} %total.11), channel_id=1, source_target_pairs={{0,4},{1,3},{4,8},{5,1},{8,12},{9,5},{12,14},{13,9},{14,10},{15,13... | collective-permute-start | bytes 1179656 | tf_op jit(solution)/shard_map/ppermute | solution.py:325
  59.2 1.5 %weight_piece.12 = (bf16[6144,1536]{1,0:T(8,128)(2,1)}, bf16[768,1536]{1,0:T(8,128)(2,1)S(1)}) custom-call(bf16[512,1536]{1,0:T(8,128)(2,1)S(1)} %get-tuple-element.273.refs_0_, bf16[32,6144]{1,0:T(8,128)(2,1)S(1)} %copy-done, bf16[32,6144]{1,0:T(8,128)(2,1)S(1)} %collective-permute-done.3.refs_2_, ...), custom_call_target="tpu_custom_call", output_to_operand_aliasing={{0}: (18, {})} | custom-call | flops 115000000 | tf_op jit(solution)/shard_map/weight_piece/pallas_call | solution.py:242
  60.7 1.7 %collective-permute-done.22.refs_2_ = bf16[64,3072]{1,0:T(8,128)(2,1)S(1)} collective-permute-done((bf16[64,3072]{1,0:T(8,128)(2,1)S(1)}, bf16[64,3072]{1,0:T(8,128)(2,1)S(1)}, u32[]{:S(2)}, u32[]{:S(2)}) %collective-permute-start.22) | collective-permute-done | bytes 393248 | tf_op jit(solution)/shard_map/ppermute | solution.py:325
  62.4 0.2 total.12
  62.6 0.1 collective-permute-start.26
  62.7 0.5 collective-permute-start.29
  63.2 1.5 %weight_piece.13 = (bf16[6144,1536]{1,0:T(8,128)(2,1)}, bf16[768,1536]{1,0:T(8,128)(2,1)S(1)}) custom-call(bf16[512,1536]{1,0:T(8,128)(2,1)S(1)} %get-tuple-element.273.refs_0_, bf16[32,6144]{1,0:T(8,128)(2,1)S(1)} %copy-done, bf16[32,6144]{1,0:T(8,128)(2,1)S(1)} %collective-permute-done.3.refs_2_, ...), custom_call_target="tpu_custom_call", output_to_operand_aliasing={{0}: (18, {})} | custom-call | flops 115000000 | tf_op jit(solution)/shard_map/weight_piece/pallas_call | solution.py:242
  64.7 2.0 %collective-permute-done.27.refs_2_ = bf16[64,3072]{1,0:T(8,128)(2,1)S(1)} collective-permute-done((bf16[64,3072]{1,0:T(8,128)(2,1)S(1)}, bf16[64,3072]{1,0:T(8,128)(2,1)S(1)}, u32[]{:S(2)}, u32[]{:S(2)}) %collective-permute-start.27) | collective-permute-done | bytes 393248 | tf_op jit(solution)/shard_map/ppermute | solution.py:325
  66.6 0.1 total.13
  66.8 0.8 %collective-permute-start.28 = (bf16[32,3072]{1,0:T(8,128)(2,1)S(1)}, bf16[32,3072]{1,0:T(8,128)(2,1)S(1)}, u32[]{:S(2)}, u32[]{:S(2)}) collective-permute-start(bf16[32,3072]{1,0:T(8,128)(2,1)S(1)} %get-tuple-element.269), channel_id=1, source_target_pairs={{0,4},{1,3},{4,8},{5,1},{8,12},{9,5},{12,14},{13,9},{14,10},{15,13... | collective-permute-start | bytes 589832 | tf_op jit(solution)/shard_map/ppermute | solution.py:325
  67.6 0.1 collective-permute-start.32
  67.8 1.6 %collective-permute-start.30 = (bf16[32,3072]{1,0:T(8,128)(2,1)S(1)}, bf16[32,3072]{1,0:T(8,128)(2,1)S(1)}, u32[]{:S(2)}, u32[]{:S(2)}) collective-permute-start(bf16[32,3072]{1,0:T(8,128)(2,1)S(1)} %get-tuple-element.278), channel_id=1, source_target_pairs={{0,5},{1,2},{4,9},{5,0},{8,13},{9,4},{12,15},{13,8},{14,11},{15,12... | collective-permute-start | bytes 589832 | tf_op jit(solution)/shard_map/ppermute | solution.py:395
  69.4 1.9 %collective-permute-start.31 = (bf16[32,3072]{1,0:T(8,128)(2,1)S(1)}, bf16[32,3072]{1,0:T(8,128)(2,1)S(1)}, u32[]{:S(2)}, u32[]{:S(2)}) collective-permute-start(bf16[32,3072]{1,0:T(8,128)(2,1)S(1)} %get-tuple-element.262), channel_id=1, source_target_pairs={{0,4},{1,3},{4,8},{5,1},{8,12},{9,5},{12,14},{13,9},{14,10},{15,13... | collective-permute-start | bytes 589832 | tf_op jit(solution)/shard_map/ppermute | solution.py:325
  71.3 1.5 %weight_piece.14 = (bf16[6144,1536]{1,0:T(8,128)(2,1)}, bf16[768,1536]{1,0:T(8,128)(2,1)S(1)}) custom-call(bf16[512,1536]{1,0:T(8,128)(2,1)S(1)} %get-tuple-element.273.refs_0_, bf16[32,6144]{1,0:T(8,128)(2,1)S(1)} %copy-done, bf16[32,6144]{1,0:T(8,128)(2,1)S(1)} %collective-permute-done.3.refs_2_, ...), custom_call_target="tpu_custom_call", output_to_operand_aliasing={{0}: (18, {})} | custom-call | flops 115000000 | tf_op jit(solution)/shard_map/weight_piece/pallas_call | solution.py:242
  72.8 2.5 %weight_piece.15 = bf16[6144,1536]{1,0:T(8,128)(2,1)} custom-call(bf16[512,1536]{1,0:T(8,128)(2,1)S(1)} %get-tuple-element.273.refs_0_, bf16[32,6144]{1,0:T(8,128)(2,1)S(1)} %copy-done, bf16[32,6144]{1,0:T(8,128)(2,1)S(1)} %collective-permute-done.3.refs_2_, bf16[32,6144]{1,0:T(8,128)(2,1)S(1)} %collective-permute-done.refs_3_, ...), custom_call_target="tpu_custom_call", output_to_operand_aliasing={{}: (18, {})} | custom-call | flops 115000000 | tf_op jit(solution)/shard_map/weight_piece/pallas_call | solution.py:242
  75.4 3.4 %collective-permute-done.31.refs_6_ = bf16[32,3072]{1,0:T(8,128)(2,1)S(1)} collective-permute-done((bf16[32,3072]{1,0:T(8,128)(2,1)S(1)}, bf16[32,3072]{1,0:T(8,128)(2,1)S(1)}, u32[]{:S(2)}, u32[]{:S(2)}) %collective-permute-start.31) | collective-permute-done | bytes 196640 | tf_op jit(solution)/shard_map/ppermute | solution.py:325
  78.8 0.9 %last.1 = bf16[32,6144]{1,0:T(8,128)(2,1)} custom-call(s32[1]{0:T(128)} %bitcast.me_ref.refs_0_, bf16[32,3072]{1,0:T(8,128)(2,1)S(1)} %get-tuple-element.221.refs_0_, bf16[32,3072]{1,0:T(8,128)(2,1)S(1)} %collective-permute-done.26.refs_1_, bf16[32,3072]{1,0:T(8,128)(2,1)S(1)} %collective-permute-done.28.refs_2_, ...), custom_call_target="tpu_custom_call" | custom-call | flops 345000000 | tf_op jit(solution)/shard_map/last/pallas_call | solution.py:300
  (29 shorter events, 0.1 us)
Async XLA Ops:
  0.6 3.9 %copy-start = (bf16[32,6144]{1,0:T(8,128)(2,1)S(1)}, bf16[32,6144]{1,0:T(8,128)(2,1)}, u32[]{:S(2)}) copy-start(bf16[32,6144]{1,0:T(8,128)(2,1)} %refs_1_.15) | copy-start | bytes 1179652
  4.5 9.4 %collective-permute-start = (bf16[32,6144]{1,0:T(8,128)(2,1)S(1)}, bf16[32,6144]{1,0:T(8,128)(2,1)S(1)}, u32[]{:S(2)}, u32[]{:S(2)}) collective-permute-start(bf16[32,6144]{1,0:T(8,128)(2,1)S(1)} %copy-done), channel_id=1, source_target_pairs={{0,4},{1,3},{4,8},{5,1},{8,12},{9,5},{12,14},{13,9},{14,10},{15,13... | collective-permute-start | bytes 1179656 | tf_op jit(solution)/shard_map/ppermute | solution.py:325
  7.6 8.8 %collective-permute-start.3 = (bf16[32,6144]{1,0:T(8,128)(2,1)S(1)}, bf16[32,6144]{1,0:T(8,128)(2,1)S(1)}, u32[]{:S(2)}, u32[]{:S(2)}) collective-permute-start(bf16[32,6144]{1,0:T(8,128)(2,1)S(1)} %copy-done), channel_id=1, source_target_pairs={{0,1},{1,0},{2,3},{3,2},{4,5},{5,4},{6,7},{7,6},{8,9},{9,8},{10,11... | collective-permute-start | bytes 1179656 | tf_op jit(solution)/shard_map/ppermute | solution.py:328
  9.7 9.1 %collective-permute-start.2 = (bf16[32,6144]{1,0:T(8,128)(2,1)S(1)}, bf16[32,6144]{1,0:T(8,128)(2,1)S(1)}, u32[]{:S(2)}, u32[]{:S(2)}) collective-permute-start(bf16[32,6144]{1,0:T(8,128)(2,1)S(1)} %copy-done), channel_id=1, source_target_pairs={{0,3},{1,4},{4,1},{5,8},{8,5},{9,12},{12,9},{13,14},{14,13},{15,10... | collective-permute-start | bytes 1179656 | tf_op jit(solution)/shard_map/ppermute | solution.py:342
  13.9 6.6 %collective-permute-start.4 = (bf16[32,6144]{1,0:T(8,128)(2,1)S(1)}, bf16[32,6144]{1,0:T(8,128)(2,1)S(1)}, u32[]{:S(2)}, u32[]{:S(2)}) collective-permute-start(bf16[32,6144]{1,0:T(8,128)(2,1)S(1)} %collective-permute-done.refs_3_), channel_id=1, source_target_pairs={{0,1},{1,0},{2,3},{3,2},{4,5},{5,4},{6,7},{7,6},{8,9},{9,8},{10,11... | collective-permute-start | bytes 1179656 | tf_op jit(solution)/shard_map/ppermute | solution.py:328
  13.9 8.9 %collective-permute-start.1 = (bf16[32,6144]{1,0:T(8,128)(2,1)S(1)}, bf16[32,6144]{1,0:T(8,128)(2,1)S(1)}, u32[]{:S(2)}, u32[]{:S(2)}) collective-permute-start(bf16[32,6144]{1,0:T(8,128)(2,1)S(1)} %collective-permute-done.refs_3_), channel_id=1, source_target_pairs={{0,4},{1,3},{4,8},{5,1},{8,12},{9,5},{12,14},{13,9},{14,10},{15,13... | collective-permute-start | bytes 1179656 | tf_op jit(solution)/shard_map/ppermute | solution.py:325
  18.8 6.0 %collective-permute-start.7 = (bf16[32,6144]{1,0:T(8,128)(2,1)S(1)}, bf16[32,6144]{1,0:T(8,128)(2,1)S(1)}, u32[]{:S(2)}, u32[]{:S(2)}) collective-permute-start(bf16[32,6144]{1,0:T(8,128)(2,1)S(1)} %collective-permute-done.2.refs_4_), channel_id=1, source_target_pairs={{0,1},{1,0},{2,3},{3,2},{4,5},{5,4},{6,7},{7,6},{8,9},{9,8},{10,11... | collective-permute-start | bytes 1179656 | tf_op jit(solution)/shard_map/ppermute | solution.py:328
  19.5 8.1 %collective-permute-start.6 = (bf16[32,6144]{1,0:T(8,128)(2,1)S(1)}, bf16[32,6144]{1,0:T(8,128)(2,1)S(1)}, u32[]{:S(2)}, u32[]{:S(2)}) collective-permute-start(bf16[32,6144]{1,0:T(8,128)(2,1)S(1)} %collective-permute-done.2.refs_4_), channel_id=1, source_target_pairs={{0,4},{1,3},{4,8},{5,1},{8,12},{9,5},{12,14},{13,9},{14,10},{15,13... | collective-permute-start | bytes 1179656 | tf_op jit(solution)/shard_map/ppermute | solution.py:325
  22.9 7.3 %collective-permute-start.8 = (bf16[32,6144]{1,0:T(8,128)(2,1)S(1)}, bf16[32,6144]{1,0:T(8,128)(2,1)S(1)}, u32[]{:S(2)}, u32[]{:S(2)}) collective-permute-start(bf16[32,6144]{1,0:T(8,128)(2,1)S(1)} %collective-permute-done.1.refs_5_), channel_id=1, source_target_pairs={{0,1},{1,0},{2,3},{3,2},{4,5},{5,4},{6,7},{7,6},{8,9},{9,8},{10,11... | collective-permute-start | bytes 1179656 | tf_op jit(solution)/shard_map/ppermute | solution.py:328
  23.3 9.8 %collective-permute-start.5 = (bf16[32,6144]{1,0:T(8,128)(2,1)S(1)}, bf16[32,6144]{1,0:T(8,128)(2,1)S(1)}, u32[]{:S(2)}, u32[]{:S(2)}) collective-permute-start(bf16[32,6144]{1,0:T(8,128)(2,1)S(1)} %collective-permute-done.1.refs_5_), channel_id=1, source_target_pairs={{0,4},{1,3},{4,8},{5,1},{8,12},{9,5},{12,14},{13,9},{14,10},{15,13... | collective-permute-start | bytes 1179656 | tf_op jit(solution)/shard_map/ppermute | solution.py:325
  27.6 6.5 %collective-permute-start.12 = (bf16[32,6144]{1,0:T(8,128)(2,1)S(1)}, bf16[32,6144]{1,0:T(8,128)(2,1)S(1)}, u32[]{:S(2)}, u32[]{:S(2)}) collective-permute-start(bf16[32,6144]{1,0:T(8,128)(2,1)S(1)} %collective-permute-done.6.refs_6_), channel_id=1, source_target_pairs={{0,1},{1,0},{2,3},{3,2},{4,5},{5,4},{6,7},{7,6},{8,9},{9,8},{10,11... | collective-permute-start | bytes 1179656 | tf_op jit(solution)/shard_map/ppermute | solution.py:328
  27.7 9.2 %collective-permute-start.10 = (bf16[32,6144]{1,0:T(8,128)(2,1)S(1)}, bf16[32,6144]{1,0:T(8,128)(2,1)S(1)}, u32[]{:S(2)}, u32[]{:S(2)}) collective-permute-start(bf16[32,6144]{1,0:T(8,128)(2,1)S(1)} %collective-permute-done.6.refs_6_), channel_id=1, source_target_pairs={{0,4},{1,3},{4,8},{5,1},{8,12},{9,5},{12,14},{13,9},{14,10},{15,13... | collective-permute-start | bytes 1179656 | tf_op jit(solution)/shard_map/ppermute | solution.py:325
  33.1 3.9 %collective-permute-start.9 = (bf16[32,6144]{1,0:T(8,128)(2,1)S(1)}, bf16[32,6144]{1,0:T(8,128)(2,1)S(1)}, u32[]{:S(2)}, u32[]{:S(2)}) collective-permute-start(bf16[32,6144]{1,0:T(8,128)(2,1)S(1)} %collective-permute-done.5.refs_7_), channel_id=1, source_target_pairs={{0,1},{1,0},{2,3},{3,2},{4,5},{5,4},{6,7},{7,6},{8,9},{9,8},{10,11... | collective-permute-start | bytes 1179656 | tf_op jit(solution)/shard_map/ppermute | solution.py:328
  33.1 3.8 %collective-permute-start.11 = (bf16[64,3072]{1,0:T(8,128)(2,1)S(1)}, bf16[64,3072]{1,0:T(8,128)(2,1)S(1)}, u32[]{:S(2)}, u32[]{:S(2)}) collective-permute-start(bf16[64,3072]{1,0:T(8,128)(2,1)S(1)} %get-tuple-element.199), channel_id=1, source_target_pairs={{0,1},{1,0},{2,3},{3,2},{4,5},{5,4},{6,7},{7,6},{8,9},{9,8},{10,11... | collective-permute-start | bytes 1179656 | tf_op jit(solution)/shard_map/ppermute | solution.py:328
  33.6 7.8 %collective-permute-start.16 = (bf16[32,6144]{1,0:T(8,128)(2,1)S(1)}, bf16[32,6144]{1,0:T(8,128)(2,1)S(1)}, u32[]{:S(2)}, u32[]{:S(2)}) collective-permute-start(bf16[32,6144]{1,0:T(8,128)(2,1)S(1)} %collective-permute-done.5.refs_7_), channel_id=1, source_target_pairs={{0,4},{1,3},{4,8},{5,1},{8,12},{9,5},{12,14},{13,9},{14,10},{15,13... | collective-permute-start | bytes 1179656 | tf_op jit(solution)/shard_map/ppermute | solution.py:325
  41.4 1.7 %collective-permute-start.15 = (bf16[64,3072]{1,0:T(8,128)(2,1)S(1)}, bf16[64,3072]{1,0:T(8,128)(2,1)S(1)}, u32[]{:S(2)}, u32[]{:S(2)}) collective-permute-start(bf16[64,3072]{1,0:T(8,128)(2,1)S(1)} %get-tuple-element.233), channel_id=1, source_target_pairs={{0,1},{1,0},{2,3},{3,2},{4,5},{5,4},{6,7},{7,6},{8,9},{9,8},{10,11... | collective-permute-start | bytes 1179656 | tf_op jit(solution)/shard_map/ppermute | solution.py:328
  41.4 2.3 %collective-permute-start.18 = (bf16[32,6144]{1,0:T(8,128)(2,1)S(1)}, bf16[32,6144]{1,0:T(8,128)(2,1)S(1)}, u32[]{:S(2)}, u32[]{:S(2)}) collective-permute-start(bf16[32,6144]{1,0:T(8,128)(2,1)S(1)} %collective-permute-done.10.refs_8_), channel_id=1, source_target_pairs={{0,1},{1,0},{2,3},{3,2},{4,5},{5,4},{6,7},{7,6},{8,9},{9,8},{10,11... | collective-permute-start | bytes 1179656 | tf_op jit(solution)/shard_map/ppermute | solution.py:328
  41.9 2.3 %collective-permute-start.17 = (bf16[32,6144]{1,0:T(8,128)(2,1)S(1)}, bf16[32,6144]{1,0:T(8,128)(2,1)S(1)}, u32[]{:S(2)}, u32[]{:S(2)}) collective-permute-start(bf16[32,6144]{1,0:T(8,128)(2,1)S(1)} %collective-permute-done.16.refs_9_), channel_id=1, source_target_pairs={{0,1},{1,0},{2,3},{3,2},{4,5},{5,4},{6,7},{7,6},{8,9},{9,8},{10,11... | collective-permute-start | bytes 1179656 | tf_op jit(solution)/shard_map/ppermute | solution.py:328
  41.9 7.8 %collective-permute-start.14 = (bf16[64,3072]{1,0:T(8,128)(2,1)S(1)}, bf16[64,3072]{1,0:T(8,128)(2,1)S(1)}, u32[]{:S(2)}, u32[]{:S(2)}) collective-permute-start(bf16[64,3072]{1,0:T(8,128)(2,1)S(1)} %total.7), channel_id=1, source_target_pairs={{0,4},{1,3},{4,8},{5,1},{8,12},{9,5},{12,14},{13,9},{14,10},{15,13... | collective-permute-start | bytes 1179656 | tf_op jit(solution)/shard_map/ppermute | solution.py:325
  42.7 7.0 %collective-permute-start.13 = (bf16[64,3072]{1,0:T(8,128)(2,1)S(1)}, bf16[64,3072]{1,0:T(8,128)(2,1)S(1)}, u32[]{:S(2)}, u32[]{:S(2)}) collective-permute-start(bf16[64,3072]{1,0:T(8,128)(2,1)S(1)} %get-tuple-element.230), channel_id=1, source_target_pairs={{0,1},{1,0},{2,3},{3,2},{4,5},{5,4},{6,7},{7,6},{8,9},{9,8},{10,11... | collective-permute-start | bytes 1179656 | tf_op jit(solution)/shard_map/ppermute | solution.py:328
  45.8 8.1 %collective-permute-start.20 = (bf16[64,3072]{1,0:T(8,128)(2,1)S(1)}, bf16[64,3072]{1,0:T(8,128)(2,1)S(1)}, u32[]{:S(2)}, u32[]{:S(2)}) collective-permute-start(bf16[64,3072]{1,0:T(8,128)(2,1)S(1)} %total.8), channel_id=1, source_target_pairs={{0,4},{1,3},{4,8},{5,1},{8,12},{9,5},{12,14},{13,9},{14,10},{15,13... | collective-permute-start | bytes 1179656 | tf_op jit(solution)/shard_map/ppermute | solution.py:325
  49.9 4.1 %collective-permute-start.19 = (bf16[64,3072]{1,0:T(8,128)(2,1)S(1)}, bf16[64,3072]{1,0:T(8,128)(2,1)S(1)}, u32[]{:S(2)}, u32[]{:S(2)}) collective-permute-start(bf16[64,3072]{1,0:T(8,128)(2,1)S(1)} %get-tuple-element.243), channel_id=1, source_target_pairs={{0,1},{1,0},{2,3},{3,2},{4,5},{5,4},{6,7},{7,6},{8,9},{9,8},{10,11... | collective-permute-start | bytes 1179656 | tf_op jit(solution)/shard_map/ppermute | solution.py:328
  49.9 5.5 %collective-permute-start.23 = (bf16[64,3072]{1,0:T(8,128)(2,1)S(1)}, bf16[64,3072]{1,0:T(8,128)(2,1)S(1)}, u32[]{:S(2)}, u32[]{:S(2)}) collective-permute-start(bf16[64,3072]{1,0:T(8,128)(2,1)S(1)} %get-tuple-element.251), channel_id=1, source_target_pairs={{0,1},{1,0},{2,3},{3,2},{4,5},{5,4},{6,7},{7,6},{8,9},{9,8},{10,11... | collective-permute-start | bytes 1179656 | tf_op jit(solution)/shard_map/ppermute | solution.py:328
  50.4 7.8 %collective-permute-start.24 = (bf16[64,3072]{1,0:T(8,128)(2,1)S(1)}, bf16[64,3072]{1,0:T(8,128)(2,1)S(1)}, u32[]{:S(2)}, u32[]{:S(2)}) collective-permute-start(bf16[64,3072]{1,0:T(8,128)(2,1)S(1)} %total.9), channel_id=1, source_target_pairs={{0,4},{1,3},{4,8},{5,1},{8,12},{9,5},{12,14},{13,9},{14,10},{15,13... | collective-permute-start | bytes 1179656 | tf_op jit(solution)/shard_map/ppermute | solution.py:325
  54.1 5.1 %collective-permute-start.21 = (bf16[64,3072]{1,0:T(8,128)(2,1)S(1)}, bf16[64,3072]{1,0:T(8,128)(2,1)S(1)}, u32[]{:S(2)}, u32[]{:S(2)}) collective-permute-start(bf16[64,3072]{1,0:T(8,128)(2,1)S(1)} %get-tuple-element.248), channel_id=1, source_target_pairs={{0,1},{1,0},{2,3},{3,2},{4,5},{5,4},{6,7},{7,6},{8,9},{9,8},{10,11... | collective-permute-start | bytes 1179656 | tf_op jit(solution)/shard_map/ppermute | solution.py:328
  54.1 5.1 %collective-permute-start.25 = (bf16[64,3072]{1,0:T(8,128)(2,1)S(1)}, bf16[64,3072]{1,0:T(8,128)(2,1)S(1)}, u32[]{:S(2)}, u32[]{:S(2)}) collective-permute-start(bf16[64,3072]{1,0:T(8,128)(2,1)S(1)} %get-tuple-element.257), channel_id=1, source_target_pairs={{0,1},{1,0},{2,3},{3,2},{4,5},{5,4},{6,7},{7,6},{8,9},{9,8},{10,11... | collective-permute-start | bytes 1179656 | tf_op jit(solution)/shard_map/ppermute | solution.py:328
  54.6 7.8 %collective-permute-start.22 = (bf16[64,3072]{1,0:T(8,128)(2,1)S(1)}, bf16[64,3072]{1,0:T(8,128)(2,1)S(1)}, u32[]{:S(2)}, u32[]{:S(2)}) collective-permute-start(bf16[64,3072]{1,0:T(8,128)(2,1)S(1)} %total.10), channel_id=1, source_target_pairs={{0,4},{1,3},{4,8},{5,1},{8,12},{9,5},{12,14},{13,9},{14,10},{15,13... | collective-permute-start | bytes 1179656 | tf_op jit(solution)/shard_map/ppermute | solution.py:325
  58.4 8.3 %collective-permute-start.27 = (bf16[64,3072]{1,0:T(8,128)(2,1)S(1)}, bf16[64,3072]{1,0:T(8,128)(2,1)S(1)}, u32[]{:S(2)}, u32[]{:S(2)}) collective-permute-start(bf16[64,3072]{1,0:T(8,128)(2,1)S(1)} %total.11), channel_id=1, source_target_pairs={{0,4},{1,3},{4,8},{5,1},{8,12},{9,5},{12,14},{13,9},{14,10},{15,13... | collective-permute-start | bytes 1179656 | tf_op jit(solution)/shard_map/ppermute | solution.py:325
  62.6 6.8 %collective-permute-start.26 = (bf16[32,3072]{1,0:T(8,128)(2,1)S(1)}, bf16[32,3072]{1,0:T(8,128)(2,1)S(1)}, u32[]{:S(2)}, u32[]{:S(2)}) collective-permute-start(bf16[32,3072]{1,0:T(8,128)(2,1)S(1)} %get-tuple-element.263), channel_id=1, source_target_pairs={{0,1},{1,0},{2,3},{3,2},{4,5},{5,4},{6,7},{7,6},{8,9},{9,8},{10,11... | collective-permute-start | bytes 589832 | tf_op jit(solution)/shard_map/ppermute | solution.py:328
  62.7 10.2 %collective-permute-start.29 = (bf16[32,3072]{1,0:T(8,128)(2,1)S(1)}, bf16[32,3072]{1,0:T(8,128)(2,1)S(1)}, u32[]{:S(2)}, u32[]{:S(2)}) collective-permute-start(bf16[32,3072]{1,0:T(8,128)(2,1)S(1)} %get-tuple-element.271), channel_id=1, source_target_pairs={{0,1},{1,0},{2,3},{3,2},{4,5},{5,4},{6,7},{7,6},{8,9},{9,8},{10,11... | collective-permute-start | bytes 589832 | tf_op jit(solution)/shard_map/ppermute | solution.py:328
  66.8 8.6 %collective-permute-start.28 = (bf16[32,3072]{1,0:T(8,128)(2,1)S(1)}, bf16[32,3072]{1,0:T(8,128)(2,1)S(1)}, u32[]{:S(2)}, u32[]{:S(2)}) collective-permute-start(bf16[32,3072]{1,0:T(8,128)(2,1)S(1)} %get-tuple-element.269), channel_id=1, source_target_pairs={{0,4},{1,3},{4,8},{5,1},{8,12},{9,5},{12,14},{13,9},{14,10},{15,13... | collective-permute-start | bytes 589832 | tf_op jit(solution)/shard_map/ppermute | solution.py:325
  67.6 7.8 %collective-permute-start.32 = (bf16[32,3072]{1,0:T(8,128)(2,1)S(1)}, bf16[32,3072]{1,0:T(8,128)(2,1)S(1)}, u32[]{:S(2)}, u32[]{:S(2)}) collective-permute-start(bf16[32,3072]{1,0:T(8,128)(2,1)S(1)} %get-tuple-element.279), channel_id=1, source_target_pairs={{0,5},{1,2},{4,9},{5,0},{8,13},{9,4},{12,15},{13,8},{14,11},{15,12... | collective-permute-start | bytes 589832 | tf_op jit(solution)/shard_map/ppermute | solution.py:399
  67.8 7.7 %collective-permute-start.30 = (bf16[32,3072]{1,0:T(8,128)(2,1)S(1)}, bf16[32,3072]{1,0:T(8,128)(2,1)S(1)}, u32[]{:S(2)}, u32[]{:S(2)}) collective-permute-start(bf16[32,3072]{1,0:T(8,128)(2,1)S(1)} %get-tuple-element.278), channel_id=1, source_target_pairs={{0,5},{1,2},{4,9},{5,0},{8,13},{9,4},{12,15},{13,8},{14,11},{15,12... | collective-permute-start | bytes 589832 | tf_op jit(solution)/shard_map/ppermute | solution.py:395
  69.4 9.4 %collective-permute-start.31 = (bf16[32,3072]{1,0:T(8,128)(2,1)S(1)}, bf16[32,3072]{1,0:T(8,128)(2,1)S(1)}, u32[]{:S(2)}, u32[]{:S(2)}) collective-permute-start(bf16[32,3072]{1,0:T(8,128)(2,1)S(1)} %get-tuple-element.262), channel_id=1, source_target_pairs={{0,4},{1,3},{4,8},{5,1},{8,12},{9,5},{12,14},{13,9},{14,10},{15,13... | collective-permute-start | bytes 589832 | tf_op jit(solution)/shard_map/ppermute | solution.py:325

commit v10 on v8

--- a/solution.py
+++ b/solution.py
@@ -346,14 +346,14 @@
 
     go, w = product(True, 0, w, ())
     a1 = after(a1, go[0])
-    a2, sa1 = ring(a1), swap(a1)
+    a2 = ring(a1)
     go, w = product(True, 1, w, go, a1, twin)
     b1 = after(b1, go[0])
-    b2, sb1 = ring(b1), swap(b1)
-    go, w = product(True, 2, w, go, b1, sa1)
+    b2 = ring(b1)
+    go, w = product(True, 2, w, go, b1)
     a2 = after(a2, go[0])
     a3, sa2 = ring(a2), swap(a2)
-    go, w = product(True, 3, w, go, a2, sb1)
+    go, w = product(True, 3, w, go, a2)
     b2 = after(b2, go[0])
     b3, sb2 = ring(b2), swap(b2)
     gm, w = product(False, 0, w, (), b2, sa2)
@@ -363,7 +363,8 @@
     opposite_from = swap(after(opposite_o, gm[0]))
     gm, w = product(False, 1, w, gm, a3, sb2)
     gm, w = product(False, 2, w, gm, sa3)
-    gm, _ = product(False, 3, w, gm, b3, opposite_from)
+    sa1, sb1 = swap(a1), swap(b1)
+    gm, _ = product(False, 3, w, gm, b3, opposite_from, sa1, sb1)
     own_m, behind_m, opposite_m, ahead_m = gm[0], gm[1:4], gm[4], gm[5:]
     sent = total(opposite_m, opposite_from)
     r4m = ring(sent)

time: 74 us -> 73.9 us (level)
  starting transfers between devices: 28.9 us -> 20.6 us
  waiting for transfers between devices: 9.36 us -> 17.6 us
    ppermute x13, starting transfers between devices: 22.7 us -> 11.5 us  [ring(): return lax.ppermute(x, 'gx', along)]
    ppermute x13, waiting for transfers between devices: 7.37 us -> 13.4 us  [ring(): return lax.ppermute(x, 'gx', along)]
    ppermute x1, waiting for transfers between devices: 0.01 us -> 2.6 us  [on_device(): b1 = lax.ppermute(after(layer_input, dh), 'gx', across)]
    ppermute x17, starting transfers between devices: 5.44 us -> 7.69 us  [swap(): return lax.ppermute(x, 'gx', twins)]
  transfers between devices with their start and end apart: 31 -> 31, of which waited for: 15 -> 14; matrix products, arithmetic and copies ran while one was open for 0% -> 0% of each run, Pallas kernels for 46% -> 46%
where the time goes in v10:
time: 73.9 us; the launch traced here: 73.7 us
  Pallas kernels  34.6 us (47%)
  starting transfers between devices  20.6 us (28%)
  waiting for transfers between devices  17.6 us (24%)
  between operations  0.9 us (1%)
    pallas_call x8, Pallas kernels, input_piece(): pl.pallas_call(lambda *refs: input_kernel(*refs, other=other, piece=piece...  15.7 us
    ppermute x13, waiting for transfers between devices, ring(): return lax.ppermute(x, 'gx', along)  13.4 us
    pallas_call x8, Pallas kernels, weight_piece(): pl.pallas_call(lambda *refs: weight_kernel(*refs, piece=piece, wide=wide,...  13.1 us
    ppermute x13, starting transfers between devices, ring(): return lax.ppermute(x, 'gx', along)  11.5 us
    ppermute x17, starting transfers between devices, swap(): return lax.ppermute(x, 'gx', twins)  7.69 us
    pallas_call x1, Pallas kernels, hidden(): pl.pallas_call(hidden_kernel, out_shape=(jax.ShapeDtypeStruct(shape, dtyp...  3.85 us
    ppermute x1, waiting for transfers between devices, on_device(): b1 = lax.ppermute(after(layer_input, dh), 'gx', across)  2.6 us
    ppermute x17, waiting for transfers between devices, swap(): return lax.ppermute(x, 'gx', twins)  1.57 us
  transfers between devices with their start and end apart: 31, of which 14 were waited for; matrix products, arithmetic and copies ran while one was open for 0% of the time, Pallas kernels for 46%

profile of v10, /device:TPU:0, one launch (start us, length us, event | category | flops | bytes accessed | tf_op | source)
XLA Modules:
  0.0 73.7 jit_solution(15920269854839257614)
XLA Ops:
  0.6 0.5 collective-permute-start.2
  1.1 2.6 %collective-permute-start.1 = (bf16[32,6144]{1,0:T(8,128)(2,1)}, bf16[32,6144]{1,0:T(8,128)(2,1)S(1)}, u32[]{:S(2)}, u32[]{:S(2)}) collective-permute-start(bf16[32,6144]{1,0:T(8,128)(2,1)} %refs_1_.15), channel_id=1, source_target_pairs={{0,4},{1,3},{4,8},{5,1},{8,12},{9,5},{12,14},{13,9},{14,10},{15,13... | collective-permute-start | bytes 1179656 | tf_op jit(solution)/shard_map/ppermute | solution.py:330
  3.8 3.9 %hidden.1 = (bf16[512,1536]{1,0:T(8,128)(2,1)S(1)}, bf16[1536,512]{1,0:T(8,128)(2,1)S(1)}, bf16[768,1536]{1,0:T(8,128)(2,1)S(1)}) custom-call(s32[1]{0:T(128)} %bitcast.me_ref.refs_0_, bf16[512,1536]{1,0:T(8,128)(2,1)} %og_hbm.1, bf16[512,1536]{1,0:T(8,128)(2,1)} %pre_hbm.1, bf16[6144,1536]{1,0:T(8,128)(2,1)} %refs_3_.15), custom_call_target="tpu_custom_call" | custom-call | flops 1150000000 | tf_op jit(solution)/shard_map/hidden/pallas_call | solution.py:115
  7.7 1.4 %collective-permute-start = (bf16[32,6144]{1,0:T(8,128)(2,1)S(1)}, bf16[32,6144]{1,0:T(8,128)(2,1)S(1)}, u32[]{:S(2)}, u32[]{:S(2)}) collective-permute-start(bf16[32,6144]{1,0:T(8,128)(2,1)S(1)} %copy-done), channel_id=1, source_target_pairs={{0,3},{1,4},{4,1},{5,8},{8,5},{9,12},{12,9},{13,14},{14,13},{15,10... | collective-permute-start | bytes 1179656 | tf_op jit(solution)/shard_map/ppermute | solution.py:342
  9.0 2.1 %input_piece.8 = (bf16[64,3072]{1,0:T(8,128)(2,1)S(1)}, bf16[64,3072]{1,0:T(8,128)(2,1)S(1)}, bf16[64,3072]{1,0:T(8,128)(2,1)S(1)}, bf16[64,3072]{1,0:T(8,128)(2...) custom-call(s32[1]{0:T(128)} %bitcast.me_ref.refs_0_, ...), custom_call_target="tpu_custom_call" | custom-call | flops 115000000 | tf_op jit(solution)/shard_map/input_piece/pallas_call | solution.py:182
  11.1 0.7 collective-permute-start.4
  11.8 2.1 %input_piece.9 = (bf16[64,3072]{1,0:T(8,128)(2,1)S(1)}, bf16[64,3072]{1,0:T(8,128)(2,1)S(1)}, bf16[64,3072]{1,0:T(8,128)(2,1)S(1)}, bf16[64,3072]{1,0:T(8,128)(2...) custom-call(s32[1]{0:T(128)} %bitcast.me_ref.refs_0_, ...), custom_call_target="tpu_custom_call", output_to_operand_aliasing={{0}: (4, {}), {1}: (5, {}), {2}: (6, {}), {3}: (7, {}), {4}... | custom-call | flops 115000000 | tf_op jit(solution)/shard_map/input_piece/pallas_call | solution.py:182
  13.8 2.6 %collective-permute-done.refs_4_ = bf16[32,6144]{1,0:T(8,128)(2,1)S(1)} collective-permute-done((bf16[32,6144]{1,0:T(8,128)(2,1)S(1)}, bf16[32,6144]{1,0:T(8,128)(2,1)S(1)}, u32[]{:S(2)}, u32[]{:S(2)}) %collective-permute-start) | collective-permute-done | bytes 393248 | tf_op jit(solution)/shard_map/ppermute | solution.py:342
  16.4 1.2 %collective-permute-start.3 = (bf16[32,6144]{1,0:T(8,128)(2,1)S(1)}, bf16[32,6144]{1,0:T(8,128)(2,1)S(1)}, u32[]{:S(2)}, u32[]{:S(2)}) collective-permute-start(bf16[32,6144]{1,0:T(8,128)(2,1)S(1)} %collective-permute-done.refs_4_), channel_id=1, source_target_pairs={{0,4},{1,3},{4,8},{5,1},{8,12},{9,5},{12,14},{13,9},{14,10},{15,13... | collective-permute-start | bytes 1179656 | tf_op jit(solution)/shard_map/ppermute | solution.py:330
  17.6 2.1 %input_piece.10 = (bf16[64,3072]{1,0:T(8,128)(2,1)S(1)}, bf16[64,3072]{1,0:T(8,128)(2,1)S(1)}, bf16[64,3072]{1,0:T(8,128)(2,1)S(1)}, bf16[64,3072]{1,0:T(8,128)(...) custom-call(s32[1]{0:T(128)} %bitcast.me_ref.refs_0_, ...), custom_call_target="tpu_custom_call", output_to_operand_aliasing={{0}: (4, {}), {1}: (5, {}), {2}: (6, {}), {3}: (7, {}), {4}... | custom-call | flops 115000000 | tf_op jit(solution)/shard_map/input_piece/pallas_call | solution.py:182
  19.7 1.2 %collective-permute-start.6 = (bf16[32,6144]{1,0:T(8,128)(2,1)S(1)}, bf16[32,6144]{1,0:T(8,128)(2,1)S(1)}, u32[]{:S(2)}, u32[]{:S(2)}) collective-permute-start(bf16[32,6144]{1,0:T(8,128)(2,1)S(1)} %collective-permute-done.4.refs_5_), channel_id=1, source_target_pairs={{0,1},{1,0},{2,3},{3,2},{4,5},{5,4},{6,7},{7,6},{8,9},{9,8},{10,11... | collective-permute-start | bytes 1179656 | tf_op jit(solution)/shard_map/ppermute | solution.py:333
  20.9 0.5 collective-permute-start.10
  21.4 1.3 %collective-permute-start.9 = (bf16[32,6144]{1,0:T(8,128)(2,1)S(1)}, bf16[32,6144]{1,0:T(8,128)(2,1)S(1)}, u32[]{:S(2)}, u32[]{:S(2)}) collective-permute-start(bf16[32,6144]{1,0:T(8,128)(2,1)S(1)} %collective-permute-done.refs_4_), channel_id=1, source_target_pairs={{0,1},{1,0},{2,3},{3,2},{4,5},{5,4},{6,7},{7,6},{8,9},{9,8},{10,11... | collective-permute-start | bytes 1179656 | tf_op jit(solution)/shard_map/ppermute | solution.py:333
  22.7 2.1 %input_piece.11 = (bf16[64,3072]{1,0:T(8,128)(2,1)S(1)}, bf16[64,3072]{1,0:T(8,128)(2,1)S(1)}, bf16[64,3072]{1,0:T(8,128)(2,1)S(1)}, bf16[64,3072]{1,0:T(8,128)(...) custom-call(s32[1]{0:T(128)} %bitcast.me_ref.refs_0_, ...), custom_call_target="tpu_custom_call", output_to_operand_aliasing={{0}: (4, {}), {1}: (5, {}), {2}: (6, {}), {3}: (7, {}), {4}... | custom-call | flops 115000000 | tf_op jit(solution)/shard_map/input_piece/pallas_call | solution.py:182
  24.9 0.5 collective-permute-start.8
  25.4 0.5 collective-permute-start.5
  25.9 1.9 %input_piece.12 = (bf16[64,3072]{1,0:T(8,128)(2,1)S(1)}, bf16[64,3072]{1,0:T(8,128)(2,1)S(1)}, bf16[64,3072]{1,0:T(8,128)(2,1)S(1)}, bf16[64,3072]{1,0:T(8,128)(...) custom-call(s32[1]{0:T(128)} %bitcast.me_ref.refs_0_, ...), custom_call_target="tpu_custom_call" | custom-call | flops 115000000 | tf_op jit(solution)/shard_map/input_piece/pallas_call | solution.py:182
  27.8 0.9 %collective-permute-done.10.refs_7_ = bf16[32,6144]{1,0:T(8,128)(2,1)S(1)} collective-permute-done((bf16[32,6144]{1,0:T(8,128)(2,1)S(1)}, bf16[32,6144]{1,0:T(8,128)(2,1)S(1)}, u32[]{:S(2)}, u32[]{:S(2)}) %collective-permute-start.10) | collective-permute-done | bytes 393248 | tf_op jit(solution)/shard_map/ppermute | solution.py:330
  28.7 0.5 collective-permute-start.11
  29.2 0.9 %collective-permute-start.16 = (bf16[32,6144]{1,0:T(8,128)(2,1)S(1)}, bf16[32,6144]{1,0:T(8,128)(2,1)S(1)}, u32[]{:S(2)}, u32[]{:S(2)}) collective-permute-start(bf16[32,6144]{1,0:T(8,128)(2,1)S(1)} %collective-permute-done.10.refs_7_), channel_id=1, source_target_pairs={{0,4},{1,3},{4,8},{5,1},{8,12},{9,5},{12,14},{13,9},{14,10},{15,13... | collective-permute-start | bytes 1179656 | tf_op jit(solution)/shard_map/ppermute | solution.py:330
  30.1 1.9 %input_piece.13 = (bf16[64,3072]{1,0:T(8,128)(2,1)S(1)}, bf16[64,3072]{1,0:T(8,128)(2,1)S(1)}, bf16[64,3072]{1,0:T(8,128)(2,1)S(1)}, bf16[64,3072]{1,0:T(8,128)(...) custom-call(s32[1]{0:T(128)} %bitcast.me_ref.refs_0_, ...), custom_call_target="tpu_custom_call", output_to_operand_aliasing={{0}: (4, {}), {1}: (5, {}), {2}: (6, {}), {3}: (7, {}), {4}... | custom-call | flops 115000000 | tf_op jit(solution)/shard_map/input_piece/pallas_call | solution.py:182
  32.0 1.1 %collective-permute-done.5.refs_8_ = bf16[32,6144]{1,0:T(8,128)(2,1)S(1)} collective-permute-done((bf16[32,6144]{1,0:T(8,128)(2,1)S(1)}, bf16[32,6144]{1,0:T(8,128)(2,1)S(1)}, u32[]{:S(2)}, u32[]{:S(2)}) %collective-permute-start.5) | collective-permute-done | bytes 393248 | tf_op jit(solution)/shard_map/ppermute | solution.py:330
  33.1 1.9 %input_piece.14 = (bf16[64,3072]{1,0:T(8,128)(2,1)S(1)}, bf16[64,3072]{1,0:T(8,128)(2,1)S(1)}, bf16[64,3072]{1,0:T(8,128)(2,1)S(1)}, bf16[64,3072]{1,0:T(8,128)(...) custom-call(s32[1]{0:T(128)} %bitcast.me_ref.refs_0_, ...), custom_call_target="tpu_custom_call", output_to_operand_aliasing={{0}: (4, {}), {1}: (5, {}), {2}: (6, {}), {3}: (7, {}), {4}... | custom-call | flops 115000000 | tf_op jit(solution)/shard_map/input_piece/pallas_call | solution.py:182
  35.0 1.8 %input_piece.15 = (bf16[64,3072]{1,0:T(8,128)(2,1)S(1)}, bf16[64,3072]{1,0:T(8,128)(2,1)S(1)}, bf16[64,3072]{1,0:T(8,128)(2,1)S(1)}, bf16[64,3072]{1,0:T(8,128)(...) custom-call(s32[1]{0:T(128)} %bitcast.me_ref.refs_0_, ...), custom_call_target="tpu_custom_call", output_to_operand_aliasing={{0}: (4, {}), {1}: (5, {}), {2}: (6, {}), {3}: (7, {}), {4}... | custom-call | flops 115000000 | tf_op jit(solution)/shard_map/input_piece/pallas_call | solution.py:182
  36.9 0.1 total.7
  37.0 0.4 collective-permute-done.16.refs_9_
  37.3 0.5 collective-permute-start.17
  37.9 0.7 collective-permute-start.14
  38.5 1.3 %collective-permute-start.13 = (bf16[64,3072]{1,0:T(8,128)(2,1)S(1)}, bf16[64,3072]{1,0:T(8,128)(2,1)S(1)}, u32[]{:S(2)}, u32[]{:S(2)}) collective-permute-start(bf16[64,3072]{1,0:T(8,128)(2,1)S(1)} %get-tuple-element.214), channel_id=1, source_target_pairs={{0,1},{1,0},{2,3},{3,2},{4,5},{5,4},{6,7},{7,6},{8,9},{9,8},{10,11... | collective-permute-start | bytes 1179656 | tf_op jit(solution)/shard_map/ppermute | solution.py:333
  39.9 0.3 collective-permute-done.18.refs_15_
  40.2 1.5 %weight_piece.8 = (bf16[6144,1536]{1,0:T(8,128)(2,1)}, bf16[768,1536]{1,0:T(8,128)(2,1)S(1)}) custom-call(bf16[512,1536]{1,0:T(8,128)(2,1)S(1)} %get-tuple-element.256.refs_0_, bf16[32,6144]{1,0:T(8,128)(2,1)S(1)} %copy-done, bf16[32,6144]{1,0:T(8,128)(2,1)S(1)} %collective-permute-done.2.refs_2_, bf16[32,6144]{1,0:T(8,128)(2,1)S(1)} %collective-permute-done.1.refs_3_, ...), custom_call_target="tpu_custom_call" | custom-call | flops 115000000 | tf_op jit(solution)/shard_map/weight_piece/pallas_call | solution.py:236
  41.7 0.1 total.8
  41.8 0.7 collective-permute-start.20
  42.5 1.5 %weight_piece.9 = (bf16[6144,1536]{1,0:T(8,128)(2,1)}, bf16[768,1536]{1,0:T(8,128)(2,1)S(1)}) custom-call(bf16[512,1536]{1,0:T(8,128)(2,1)S(1)} %get-tuple-element.256.refs_0_, bf16[32,6144]{1,0:T(8,128)(2,1)S(1)} %copy-done, bf16[32,6144]{1,0:T(8,128)(2,1)S(1)} %collective-permute-done.2.refs_2_, ...), custom_call_target="tpu_custom_call", output_to_operand_aliasing={{0}: (18, {})} | custom-call | flops 115000000 | tf_op jit(solution)/shard_map/weight_piece/pallas_call | solution.py:236
  44.0 1.6 %collective-permute-done.14.refs_0_ = bf16[64,3072]{1,0:T(8,128)(2,1)S(1)} collective-permute-done((bf16[64,3072]{1,0:T(8,128)(2,1)S(1)}, bf16[64,3072]{1,0:T(8,128)(2,1)S(1)}, u32[]{:S(2)}, u32[]{:S(2)}) %collective-permute-start.14) | collective-permute-done | bytes 393248 | tf_op jit(solution)/shard_map/ppermute | solution.py:330
  45.6 0.1 total.9
  45.9 0.5 collective-permute-start.22
  46.4 0.7 collective-permute-start.23
  47.0 1.5 %weight_piece.10 = (bf16[6144,1536]{1,0:T(8,128)(2,1)}, bf16[768,1536]{1,0:T(8,128)(2,1)S(1)}) custom-call(bf16[512,1536]{1,0:T(8,128)(2,1)S(1)} %get-tuple-element.256.refs_0_, bf16[32,6144]{1,0:T(8,128)(2,1)S(1)} %copy-done, bf16[32,6144]{1,0:T(8,128)(2,1)S(1)} %collective-permute-done.2.refs_2_, ...), custom_call_target="tpu_custom_call", output_to_operand_aliasing={{0}: (18, {})} | custom-call | flops 115000000 | tf_op jit(solution)/shard_map/weight_piece/pallas_call | solution.py:236
  48.6 1.3 %collective-permute-done.20.refs_0_ = bf16[64,3072]{1,0:T(8,128)(2,1)S(1)} collective-permute-done((bf16[64,3072]{1,0:T(8,128)(2,1)S(1)}, bf16[64,3072]{1,0:T(8,128)(2,1)S(1)}, u32[]{:S(2)}, u32[]{:S(2)}) %collective-permute-start.20) | collective-permute-done | bytes 393248 | tf_op jit(solution)/shard_map/ppermute | solution.py:330
  49.9 0.1 total.10
  50.1 0.5 collective-permute-start.25
  50.6 0.7 collective-permute-start.26
  51.3 1.5 %weight_piece.11 = (bf16[6144,1536]{1,0:T(8,128)(2,1)}, bf16[768,1536]{1,0:T(8,128)(2,1)S(1)}) custom-call(bf16[512,1536]{1,0:T(8,128)(2,1)S(1)} %get-tuple-element.256.refs_0_, bf16[32,6144]{1,0:T(8,128)(2,1)S(1)} %copy-done, bf16[32,6144]{1,0:T(8,128)(2,1)S(1)} %collective-permute-done.2.refs_2_, ...), custom_call_target="tpu_custom_call", output_to_operand_aliasing={{0}: (18, {})} | custom-call | flops 115000000 | tf_op jit(solution)/shard_map/weight_piece/pallas_call | solution.py:236
  52.8 1.4 %collective-permute-done.23.refs_0_ = bf16[64,3072]{1,0:T(8,128)(2,1)S(1)} collective-permute-done((bf16[64,3072]{1,0:T(8,128)(2,1)S(1)}, bf16[64,3072]{1,0:T(8,128)(2,1)S(1)}, u32[]{:S(2)}, u32[]{:S(2)}) %collective-permute-start.23) | collective-permute-done | bytes 393248 | tf_op jit(solution)/shard_map/ppermute | solution.py:330
  54.1 0.2 total.11
  54.3 0.7 collective-permute-start.24
  55.0 1.5 %weight_piece.12 = (bf16[6144,1536]{1,0:T(8,128)(2,1)}, bf16[768,1536]{1,0:T(8,128)(2,1)S(1)}) custom-call(bf16[512,1536]{1,0:T(8,128)(2,1)S(1)} %get-tuple-element.256.refs_0_, bf16[32,6144]{1,0:T(8,128)(2,1)S(1)} %copy-done, bf16[32,6144]{1,0:T(8,128)(2,1)S(1)} %collective-permute-done.2.refs_2_, ...), custom_call_target="tpu_custom_call", output_to_operand_aliasing={{0}: (18, {})} | custom-call | flops 115000000 | tf_op jit(solution)/shard_map/weight_piece/pallas_call | solution.py:236
  56.6 1.8 %collective-permute-done.26.refs_0_ = bf16[64,3072]{1,0:T(8,128)(2,1)S(1)} collective-permute-done((bf16[64,3072]{1,0:T(8,128)(2,1)S(1)}, bf16[64,3072]{1,0:T(8,128)(2,1)S(1)}, u32[]{:S(2)}, u32[]{:S(2)}) %collective-permute-start.26) | collective-permute-done | bytes 393248 | tf_op jit(solution)/shard_map/ppermute | solution.py:330
  58.4 0.1 total.12
  58.5 0.7 collective-permute-start.28
  59.2 1.5 %weight_piece.13 = (bf16[6144,1536]{1,0:T(8,128)(2,1)}, bf16[768,1536]{1,0:T(8,128)(2,1)S(1)}) custom-call(bf16[512,1536]{1,0:T(8,128)(2,1)S(1)} %get-tuple-element.256.refs_0_, bf16[32,6144]{1,0:T(8,128)(2,1)S(1)} %copy-done, bf16[32,6144]{1,0:T(8,128)(2,1)S(1)} %collective-permute-done.2.refs_2_, ...), custom_call_target="tpu_custom_call", output_to_operand_aliasing={{0}: (18, {})} | custom-call | flops 115000000 | tf_op jit(solution)/shard_map/weight_piece/pallas_call | solution.py:236
  60.7 1.8 %collective-permute-done.24.refs_0_ = bf16[64,3072]{1,0:T(8,128)(2,1)S(1)} collective-permute-done((bf16[64,3072]{1,0:T(8,128)(2,1)S(1)}, bf16[64,3072]{1,0:T(8,128)(2,1)S(1)}, u32[]{:S(2)}, u32[]{:S(2)}) %collective-permute-start.24) | collective-permute-done | bytes 393248 | tf_op jit(solution)/shard_map/ppermute | solution.py:330
  62.6 0.1 total.13
  62.7 0.9 %collective-permute-start.27 = (bf16[64,3072]{1,0:T(8,128)(2,1)S(1)}, bf16[64,3072]{1,0:T(8,128)(2,1)S(1)}, u32[]{:S(2)}, u32[]{:S(2)}) collective-permute-start(bf16[64,3072]{1,0:T(8,128)(2,1)S(1)} %total.13), channel_id=1, source_target_pairs={{0,4},{1,3},{4,8},{5,1},{8,12},{9,5},{12,14},{13,9},{14,10},{15,13... | collective-permute-start | bytes 1179656 | tf_op jit(solution)/shard_map/ppermute | solution.py:330
  63.7 1.5 %weight_piece.14 = (bf16[6144,1536]{1,0:T(8,128)(2,1)}, bf16[768,1536]{1,0:T(8,128)(2,1)S(1)}) custom-call(bf16[512,1536]{1,0:T(8,128)(2,1)S(1)} %get-tuple-element.256.refs_0_, bf16[32,6144]{1,0:T(8,128)(2,1)S(1)} %copy-done, bf16[32,6144]{1,0:T(8,128)(2,1)S(1)} %collective-permute-done.2.refs_2_, ...), custom_call_target="tpu_custom_call", output_to_operand_aliasing={{0}: (18, {})} | custom-call | flops 115000000 | tf_op jit(solution)/shard_map/weight_piece/pallas_call | solution.py:236
  65.2 1.6 %collective-permute-done.28.came_ref = bf16[64,3072]{1,0:T(8,128)(2,1)S(1)} collective-permute-done((bf16[64,3072]{1,0:T(8,128)(2,1)S(1)}, bf16[64,3072]{1,0:T(8,128)(2,1)S(1)}, u32[]{:S(2)}, u32[]{:S(2)}) %collective-permute-start.28) | collective-permute-done | bytes 393248 | tf_op jit(solution)/shard_map/ppermute | solution.py:330
  66.9 2.5 %weight_piece.15 = bf16[6144,1536]{1,0:T(8,128)(2,1)} custom-call(bf16[512,1536]{1,0:T(8,128)(2,1)S(1)} %get-tuple-element.256.refs_0_, bf16[32,6144]{1,0:T(8,128)(2,1)S(1)} %copy-done, bf16[32,6144]{1,0:T(8,128)(2,1)S(1)} %collective-permute-done.2.refs_2_, bf16[32,6144]{1,0:T(8,128)(2,1)S(1)} %collective-permute-done.1.refs_3_, ...), custom_call_target="tpu_custom_call", output_to_operand_aliasing={{}: (18, {})} | custom-call | flops 115000000 | tf_op jit(solution)/shard_map/weight_piece/pallas_call | solution.py:236
  69.4 1.6 %collective-permute-done.27.came_ref = bf16[64,3072]{1,0:T(8,128)(2,1)S(1)} collective-permute-done((bf16[64,3072]{1,0:T(8,128)(2,1)S(1)}, bf16[64,3072]{1,0:T(8,128)(2,1)S(1)}, u32[]{:S(2)}, u32[]{:S(2)}) %collective-permute-start.27) | collective-permute-done | bytes 393248 | tf_op jit(solution)/shard_map/ppermute | solution.py:330
  71.0 0.1 halves.3
  71.2 0.5 collective-permute-start.29
  71.7 0.9 %collective-permute-done.30.other_came_ref = bf16[32,3072]{1,0:T(8,128)(2,1)S(1)} collective-permute-done((bf16[32,3072]{1,0:T(8,128)(2,1)S(1)}, bf16[32,3072]{1,0:T(8,128)(2,1)S(1)}, u32[]{:S(2)}, u32[]{:S(2)}) %collective-permute-start.30) | collective-permute-done | bytes 196640 | tf_op jit(solution)/shard_map/ppermute | solution.py:333
  72.6 0.3 collective-permute-done.29.mine_came_ref
  72.9 0.8 %last.1 = bf16[32,6144]{1,0:T(8,128)(2,1)} custom-call(s32[1]{0:T(128)} %bitcast.me_ref.refs_0_, f32[32,3072]{1,0:T(8,128)S(1)} %get-tuple-element.259.mine_ref, bf16[32,3072]{1,0:T(8,128)(2,1)S(1)} %collective-permute-done.29.mine_came_ref, f32[32,3072]{1,0:T(8,128)S(1)} %get-tuple-element.260.other_ref, ...), custom_call_target="tpu_custom_call" | custom-call | flops 345000000 | tf_op jit(solution)/shard_map/last/pallas_call | solution.py:305
  (27 shorter events, 0.5 us)
Async XLA Ops:
  0.6 11.1 %collective-permute-start.2 = (bf16[32,6144]{1,0:T(8,128)(2,1)}, bf16[32,6144]{1,0:T(8,128)(2,1)S(1)}, u32[]{:S(2)}, u32[]{:S(2)}) collective-permute-start(bf16[32,6144]{1,0:T(8,128)(2,1)} %refs_1_.15), channel_id=1, source_target_pairs={{0,1},{1,0},{2,3},{3,2},{4,5},{5,4},{6,7},{7,6},{8,9},{9,8},{10,11... | collective-permute-start | bytes 1179656 | tf_op jit(solution)/shard_map/ppermute | solution.py:333
  1.1 9.9 %collective-permute-start.1 = (bf16[32,6144]{1,0:T(8,128)(2,1)}, bf16[32,6144]{1,0:T(8,128)(2,1)S(1)}, u32[]{:S(2)}, u32[]{:S(2)}) collective-permute-start(bf16[32,6144]{1,0:T(8,128)(2,1)} %refs_1_.15), channel_id=1, source_target_pairs={{0,4},{1,3},{4,8},{5,1},{8,12},{9,5},{12,14},{13,9},{14,10},{15,13... | collective-permute-start | bytes 1179656 | tf_op jit(solution)/shard_map/ppermute | solution.py:330
  3.8 3.9 %copy-start = (bf16[32,6144]{1,0:T(8,128)(2,1)S(1)}, bf16[32,6144]{1,0:T(8,128)(2,1)}, u32[]{:S(2)}) copy-start(bf16[32,6144]{1,0:T(8,128)(2,1)} %refs_1_.15) | copy-start | bytes 1179652
  7.7 8.8 %collective-permute-start = (bf16[32,6144]{1,0:T(8,128)(2,1)S(1)}, bf16[32,6144]{1,0:T(8,128)(2,1)S(1)}, u32[]{:S(2)}, u32[]{:S(2)}) collective-permute-start(bf16[32,6144]{1,0:T(8,128)(2,1)S(1)} %copy-done), channel_id=1, source_target_pairs={{0,3},{1,4},{4,1},{5,8},{8,5},{9,12},{12,9},{13,14},{14,13},{15,10... | collective-permute-start | bytes 1179656 | tf_op jit(solution)/shard_map/ppermute | solution.py:342
  11.1 8.6 %collective-permute-start.4 = (bf16[32,6144]{1,0:T(8,128)(2,1)S(1)}, bf16[32,6144]{1,0:T(8,128)(2,1)S(1)}, u32[]{:S(2)}, u32[]{:S(2)}) collective-permute-start(bf16[32,6144]{1,0:T(8,128)(2,1)S(1)} %collective-permute-done.1.refs_3_), channel_id=1, source_target_pairs={{0,4},{1,3},{4,8},{5,1},{8,12},{9,5},{12,14},{13,9},{14,10},{15,13... | collective-permute-start | bytes 1179656 | tf_op jit(solution)/shard_map/ppermute | solution.py:330
  16.4 8.3 %collective-permute-start.3 = (bf16[32,6144]{1,0:T(8,128)(2,1)S(1)}, bf16[32,6144]{1,0:T(8,128)(2,1)S(1)}, u32[]{:S(2)}, u32[]{:S(2)}) collective-permute-start(bf16[32,6144]{1,0:T(8,128)(2,1)S(1)} %collective-permute-done.refs_4_), channel_id=1, source_target_pairs={{0,4},{1,3},{4,8},{5,1},{8,12},{9,5},{12,14},{13,9},{14,10},{15,13... | collective-permute-start | bytes 1179656 | tf_op jit(solution)/shard_map/ppermute | solution.py:330
  19.7 5.7 %collective-permute-start.6 = (bf16[32,6144]{1,0:T(8,128)(2,1)S(1)}, bf16[32,6144]{1,0:T(8,128)(2,1)S(1)}, u32[]{:S(2)}, u32[]{:S(2)}) collective-permute-start(bf16[32,6144]{1,0:T(8,128)(2,1)S(1)} %collective-permute-done.4.refs_5_), channel_id=1, source_target_pairs={{0,1},{1,0},{2,3},{3,2},{4,5},{5,4},{6,7},{7,6},{8,9},{9,8},{10,11... | collective-permute-start | bytes 1179656 | tf_op jit(solution)/shard_map/ppermute | solution.py:333
  20.9 7.8 %collective-permute-start.10 = (bf16[32,6144]{1,0:T(8,128)(2,1)S(1)}, bf16[32,6144]{1,0:T(8,128)(2,1)S(1)}, u32[]{:S(2)}, u32[]{:S(2)}) collective-permute-start(bf16[32,6144]{1,0:T(8,128)(2,1)S(1)} %collective-permute-done.4.refs_5_), channel_id=1, source_target_pairs={{0,4},{1,3},{4,8},{5,1},{8,12},{9,5},{12,14},{13,9},{14,10},{15,13... | collective-permute-start | bytes 1179656 | tf_op jit(solution)/shard_map/ppermute | solution.py:330
  21.4 7.3 %collective-permute-start.9 = (bf16[32,6144]{1,0:T(8,128)(2,1)S(1)}, bf16[32,6144]{1,0:T(8,128)(2,1)S(1)}, u32[]{:S(2)}, u32[]{:S(2)}) collective-permute-start(bf16[32,6144]{1,0:T(8,128)(2,1)S(1)} %collective-permute-done.refs_4_), channel_id=1, source_target_pairs={{0,1},{1,0},{2,3},{3,2},{4,5},{5,4},{6,7},{7,6},{8,9},{9,8},{10,11... | collective-permute-start | bytes 1179656 | tf_op jit(solution)/shard_map/ppermute | solution.py:333
  24.8 4.4 %collective-permute-start.12 = (bf16[32,6144]{1,0:T(8,128)(2,1)S(1)}, bf16[32,6144]{1,0:T(8,128)(2,1)S(1)}, u32[]{:S(2)}, u32[]{:S(2)}) collective-permute-start(bf16[32,6144]{1,0:T(8,128)(2,1)S(1)} %collective-permute-done.3.refs_6_), channel_id=1, source_target_pairs={{0,1},{1,0},{2,3},{3,2},{4,5},{5,4},{6,7},{7,6},{8,9},{9,8},{10,11... | collective-permute-start | bytes 1179656 | tf_op jit(solution)/shard_map/ppermute | solution.py:333
  24.9 7.2 %collective-permute-start.8 = (bf16[32,6144]{1,0:T(8,128)(2,1)S(1)}, bf16[32,6144]{1,0:T(8,128)(2,1)S(1)}, u32[]{:S(2)}, u32[]{:S(2)}) collective-permute-start(bf16[32,6144]{1,0:T(8,128)(2,1)S(1)} %collective-permute-done.1.refs_3_), channel_id=1, source_target_pairs={{0,1},{1,0},{2,3},{3,2},{4,5},{5,4},{6,7},{7,6},{8,9},{9,8},{10,11... | collective-permute-start | bytes 1179656 | tf_op jit(solution)/shard_map/ppermute | solution.py:333
  25.4 7.8 %collective-permute-start.5 = (bf16[32,6144]{1,0:T(8,128)(2,1)S(1)}, bf16[32,6144]{1,0:T(8,128)(2,1)S(1)}, u32[]{:S(2)}, u32[]{:S(2)}) collective-permute-start(bf16[32,6144]{1,0:T(8,128)(2,1)S(1)} %collective-permute-done.3.refs_6_), channel_id=1, source_target_pairs={{0,4},{1,3},{4,8},{5,1},{8,12},{9,5},{12,14},{13,9},{14,10},{15,13... | collective-permute-start | bytes 1179656 | tf_op jit(solution)/shard_map/ppermute | solution.py:330
  28.7 4.5 %collective-permute-start.7 = (bf16[64,3072]{1,0:T(8,128)(2,1)S(1)}, bf16[64,3072]{1,0:T(8,128)(2,1)S(1)}, u32[]{:S(2)}, u32[]{:S(2)}) collective-permute-start(bf16[64,3072]{1,0:T(8,128)(2,1)S(1)} %get-tuple-element.175), channel_id=1, source_target_pairs={{0,1},{1,0},{2,3},{3,2},{4,5},{5,4},{6,7},{7,6},{8,9},{9,8},{10,11... | collective-permute-start | bytes 1179656 | tf_op jit(solution)/shard_map/ppermute | solution.py:333
  28.7 4.4 %collective-permute-start.11 = (bf16[32,6144]{1,0:T(8,128)(2,1)S(1)}, bf16[32,6144]{1,0:T(8,128)(2,1)S(1)}, u32[]{:S(2)}, u32[]{:S(2)}) collective-permute-start(bf16[32,6144]{1,0:T(8,128)(2,1)S(1)} %collective-permute-done.10.refs_7_), channel_id=1, source_target_pairs={{0,1},{1,0},{2,3},{3,2},{4,5},{5,4},{6,7},{7,6},{8,9},{9,8},{10,11... | collective-permute-start | bytes 1179656 | tf_op jit(solution)/shard_map/ppermute | solution.py:333
  29.2 8.1 %collective-permute-start.16 = (bf16[32,6144]{1,0:T(8,128)(2,1)S(1)}, bf16[32,6144]{1,0:T(8,128)(2,1)S(1)}, u32[]{:S(2)}, u32[]{:S(2)}) collective-permute-start(bf16[32,6144]{1,0:T(8,128)(2,1)S(1)} %collective-permute-done.10.refs_7_), channel_id=1, source_target_pairs={{0,4},{1,3},{4,8},{5,1},{8,12},{9,5},{12,14},{13,9},{14,10},{15,13... | collective-permute-start | bytes 1179656 | tf_op jit(solution)/shard_map/ppermute | solution.py:330
  37.3 2.5 %collective-permute-start.15 = (bf16[64,3072]{1,0:T(8,128)(2,1)S(1)}, bf16[64,3072]{1,0:T(8,128)(2,1)S(1)}, u32[]{:S(2)}, u32[]{:S(2)}) collective-permute-start(bf16[64,3072]{1,0:T(8,128)(2,1)S(1)} %get-tuple-element.217), channel_id=1, source_target_pairs={{0,1},{1,0},{2,3},{3,2},{4,5},{5,4},{6,7},{7,6},{8,9},{9,8},{10,11... | collective-permute-start | bytes 1179656 | tf_op jit(solution)/shard_map/ppermute | solution.py:333
  37.3 2.5 %collective-permute-start.17 = (bf16[32,6144]{1,0:T(8,128)(2,1)S(1)}, bf16[32,6144]{1,0:T(8,128)(2,1)S(1)}, u32[]{:S(2)}, u32[]{:S(2)}) collective-permute-start(bf16[32,6144]{1,0:T(8,128)(2,1)S(1)} %collective-permute-done.16.refs_9_), channel_id=1, source_target_pairs={{0,1},{1,0},{2,3},{3,2},{4,5},{5,4},{6,7},{7,6},{8,9},{9,8},{10,11... | collective-permute-start | bytes 1179656 | tf_op jit(solution)/shard_map/ppermute | solution.py:333
  37.9 2.3 %collective-permute-start.18 = (bf16[32,6144]{1,0:T(8,128)(2,1)S(1)}, bf16[32,6144]{1,0:T(8,128)(2,1)S(1)}, u32[]{:S(2)}, u32[]{:S(2)}) collective-permute-start(bf16[32,6144]{1,0:T(8,128)(2,1)S(1)} %collective-permute-done.5.refs_8_), channel_id=1, source_target_pairs={{0,1},{1,0},{2,3},{3,2},{4,5},{5,4},{6,7},{7,6},{8,9},{9,8},{10,11... | collective-permute-start | bytes 1179656 | tf_op jit(solution)/shard_map/ppermute | solution.py:333
  37.9 7.8 %collective-permute-start.14 = (bf16[64,3072]{1,0:T(8,128)(2,1)S(1)}, bf16[64,3072]{1,0:T(8,128)(2,1)S(1)}, u32[]{:S(2)}, u32[]{:S(2)}) collective-permute-start(bf16[64,3072]{1,0:T(8,128)(2,1)S(1)} %total.7), channel_id=1, source_target_pairs={{0,4},{1,3},{4,8},{5,1},{8,12},{9,5},{12,14},{13,9},{14,10},{15,13... | collective-permute-start | bytes 1179656 | tf_op jit(solution)/shard_map/ppermute | solution.py:330
  38.5 7.1 %collective-permute-start.13 = (bf16[64,3072]{1,0:T(8,128)(2,1)S(1)}, bf16[64,3072]{1,0:T(8,128)(2,1)S(1)}, u32[]{:S(2)}, u32[]{:S(2)}) collective-permute-start(bf16[64,3072]{1,0:T(8,128)(2,1)S(1)} %get-tuple-element.214), channel_id=1, source_target_pairs={{0,1},{1,0},{2,3},{3,2},{4,5},{5,4},{6,7},{7,6},{8,9},{9,8},{10,11... | collective-permute-start | bytes 1179656 | tf_op jit(solution)/shard_map/ppermute | solution.py:333
  41.8 8.1 %collective-permute-start.20 = (bf16[64,3072]{1,0:T(8,128)(2,1)S(1)}, bf16[64,3072]{1,0:T(8,128)(2,1)S(1)}, u32[]{:S(2)}, u32[]{:S(2)}) collective-permute-start(bf16[64,3072]{1,0:T(8,128)(2,1)S(1)} %total.8), channel_id=1, source_target_pairs={{0,4},{1,3},{4,8},{5,1},{8,12},{9,5},{12,14},{13,9},{14,10},{15,13... | collective-permute-start | bytes 1179656 | tf_op jit(solution)/shard_map/ppermute | solution.py:330
  45.8 4.1 %collective-permute-start.19 = (bf16[64,3072]{1,0:T(8,128)(2,1)S(1)}, bf16[64,3072]{1,0:T(8,128)(2,1)S(1)}, u32[]{:S(2)}, u32[]{:S(2)}) collective-permute-start(bf16[64,3072]{1,0:T(8,128)(2,1)S(1)} %get-tuple-element.227), channel_id=1, source_target_pairs={{0,1},{1,0},{2,3},{3,2},{4,5},{5,4},{6,7},{7,6},{8,9},{9,8},{10,11... | collective-permute-start | bytes 1179656 | tf_op jit(solution)/shard_map/ppermute | solution.py:333
  45.9 5.4 %collective-permute-start.22 = (bf16[64,3072]{1,0:T(8,128)(2,1)S(1)}, bf16[64,3072]{1,0:T(8,128)(2,1)S(1)}, u32[]{:S(2)}, u32[]{:S(2)}) collective-permute-start(bf16[64,3072]{1,0:T(8,128)(2,1)S(1)} %get-tuple-element.235), channel_id=1, source_target_pairs={{0,1},{1,0},{2,3},{3,2},{4,5},{5,4},{6,7},{7,6},{8,9},{9,8},{10,11... | collective-permute-start | bytes 1179656 | tf_op jit(solution)/shard_map/ppermute | solution.py:333
  46.4 7.8 %collective-permute-start.23 = (bf16[64,3072]{1,0:T(8,128)(2,1)S(1)}, bf16[64,3072]{1,0:T(8,128)(2,1)S(1)}, u32[]{:S(2)}, u32[]{:S(2)}) collective-permute-start(bf16[64,3072]{1,0:T(8,128)(2,1)S(1)} %total.9), channel_id=1, source_target_pairs={{0,4},{1,3},{4,8},{5,1},{8,12},{9,5},{12,14},{13,9},{14,10},{15,13... | collective-permute-start | bytes 1179656 | tf_op jit(solution)/shard_map/ppermute | solution.py:330
  50.0 5.0 %collective-permute-start.21 = (bf16[64,3072]{1,0:T(8,128)(2,1)S(1)}, bf16[64,3072]{1,0:T(8,128)(2,1)S(1)}, u32[]{:S(2)}, u32[]{:S(2)}) collective-permute-start(bf16[64,3072]{1,0:T(8,128)(2,1)S(1)} %get-tuple-element.232), channel_id=1, source_target_pairs={{0,1},{1,0},{2,3},{3,2},{4,5},{5,4},{6,7},{7,6},{8,9},{9,8},{10,11... | collective-permute-start | bytes 1179656 | tf_op jit(solution)/shard_map/ppermute | solution.py:333
  50.1 5.0 %collective-permute-start.25 = (bf16[64,3072]{1,0:T(8,128)(2,1)S(1)}, bf16[64,3072]{1,0:T(8,128)(2,1)S(1)}, u32[]{:S(2)}, u32[]{:S(2)}) collective-permute-start(bf16[64,3072]{1,0:T(8,128)(2,1)S(1)} %get-tuple-element.242), channel_id=1, source_target_pairs={{0,1},{1,0},{2,3},{3,2},{4,5},{5,4},{6,7},{7,6},{8,9},{9,8},{10,11... | collective-permute-start | bytes 1179656 | tf_op jit(solution)/shard_map/ppermute | solution.py:333
  50.6 7.8 %collective-permute-start.26 = (bf16[64,3072]{1,0:T(8,128)(2,1)S(1)}, bf16[64,3072]{1,0:T(8,128)(2,1)S(1)}, u32[]{:S(2)}, u32[]{:S(2)}) collective-permute-start(bf16[64,3072]{1,0:T(8,128)(2,1)S(1)} %total.10), channel_id=1, source_target_pairs={{0,4},{1,3},{4,8},{5,1},{8,12},{9,5},{12,14},{13,9},{14,10},{15,13... | collective-permute-start | bytes 1179656 | tf_op jit(solution)/shard_map/ppermute | solution.py:330
  54.3 8.3 %collective-permute-start.24 = (bf16[64,3072]{1,0:T(8,128)(2,1)S(1)}, bf16[64,3072]{1,0:T(8,128)(2,1)S(1)}, u32[]{:S(2)}, u32[]{:S(2)}) collective-permute-start(bf16[64,3072]{1,0:T(8,128)(2,1)S(1)} %total.11), channel_id=1, source_target_pairs={{0,4},{1,3},{4,8},{5,1},{8,12},{9,5},{12,14},{13,9},{14,10},{15,13... | collective-permute-start | bytes 1179656 | tf_op jit(solution)/shard_map/ppermute | solution.py:330
  58.5 8.3 %collective-permute-start.28 = (bf16[64,3072]{1,0:T(8,128)(2,1)S(1)}, bf16[64,3072]{1,0:T(8,128)(2,1)S(1)}, u32[]{:S(2)}, u32[]{:S(2)}) collective-permute-start(bf16[64,3072]{1,0:T(8,128)(2,1)S(1)} %total.12), channel_id=1, source_target_pairs={{0,4},{1,3},{4,8},{5,1},{8,12},{9,5},{12,14},{13,9},{14,10},{15,13... | collective-permute-start | bytes 1179656 | tf_op jit(solution)/shard_map/ppermute | solution.py:330
  62.7 8.3 %collective-permute-start.27 = (bf16[64,3072]{1,0:T(8,128)(2,1)S(1)}, bf16[64,3072]{1,0:T(8,128)(2,1)S(1)}, u32[]{:S(2)}, u32[]{:S(2)}) collective-permute-start(bf16[64,3072]{1,0:T(8,128)(2,1)S(1)} %total.13), channel_id=1, source_target_pairs={{0,4},{1,3},{4,8},{5,1},{8,12},{9,5},{12,14},{13,9},{14,10},{15,13... | collective-permute-start | bytes 1179656 | tf_op jit(solution)/shard_map/ppermute | solution.py:330
  71.1 1.5 %collective-permute-start.30 = (bf16[32,3072]{1,0:T(8,128)(2,1)S(1)}, bf16[32,3072]{1,0:T(8,128)(2,1)S(1)}, u32[]{:S(2)}, u32[]{:S(2)}) collective-permute-start(bf16[32,3072]{1,0:T(8,128)(2,1)S(1)} %get-tuple-element.261), channel_id=1, source_target_pairs={{0,1},{1,0},{2,3},{3,2},{4,5},{5,4},{6,7},{7,6},{8,9},{9,8},{10,11... | collective-permute-start | bytes 589832 | tf_op jit(solution)/shard_map/ppermute | solution.py:333
  71.2 1.7 %collective-permute-start.29 = (bf16[32,3072]{1,0:T(8,128)(2,1)S(1)}, bf16[32,3072]{1,0:T(8,128)(2,1)S(1)}, u32[]{:S(2)}, u32[]{:S(2)}) collective-permute-start(bf16[32,3072]{1,0:T(8,128)(2,1)S(1)} %get-tuple-element.255), channel_id=1, source_target_pairs={{0,1},{1,0},{2,3},{3,2},{4,5},{5,4},{6,7},{7,6},{8,9},{9,8},{10,11... | collective-permute-start | bytes 589832 | tf_op jit(solution)/shard_map/ppermute | solution.py:333

commit v11 on v8

--- a/solution.py
+++ b/solution.py
@@ -97,10 +97,11 @@
     wide = w_ref.shape[0]
     first = first_row(me_ref, True, 0, w_hbm.shape[0] // 2, wide)
     fetch = pltpu.make_async_copy(w_hbm.at[pl.ds(first, wide), :], w_ref, sems.at[2, 0])
-    fetch.start()
     for i in range(RING // 2):
         for copy in copies[8 * i : 8 * (i + 1)]:
             copy.wait()
+        if i == 0:
+            fetch.start()
         block = pl.ds(4 * i * rows, 4 * rows)
         pre = pre_ref[block, :].astype(jnp.float32)
         og = og_ref[block, :].astype(jnp.float32)

time: 74 us -> 74 us (level)
  no operation moved by 1% of the time
where the time goes in v11:
time: 74 us; the launch traced here: 73.8 us
  Pallas kernels  34.6 us (47%)
  starting transfers between devices  28.9 us (39%)
  waiting for transfers between devices  9.36 us (13%)
  between operations  0.9 us (1%)
    ppermute x13, starting transfers between devices, ring(): return lax.ppermute(x, 'gx', along)  22.7 us
    pallas_call x8, Pallas kernels, input_piece(): pl.pallas_call(lambda *refs: input_kernel(*refs, other=other, piece=piece...  15.8 us
    pallas_call x8, Pallas kernels, weight_piece(): pl.pallas_call(lambda *refs: weight_kernel(*refs, piece=piece, wide=wide,...  13.1 us
    ppermute x13, waiting for transfers between devices, ring(): return lax.ppermute(x, 'gx', along)  7.37 us
    ppermute x17, starting transfers between devices, swap(): return lax.ppermute(x, 'gx', twins)  5.44 us
    pallas_call x1, Pallas kernels, hidden(): pl.pallas_call(hidden_kernel, out_shape=(jax.ShapeDtypeStruct(shape, dtyp...  3.85 us
    ppermute x17, waiting for transfers between devices, swap(): return lax.ppermute(x, 'gx', twins)  1.99 us
  transfers between devices with their start and end apart: 31, of which 15 were waited for; matrix products, arithmetic and copies ran while one was open for 0% of the time, Pallas kernels for 46%

profile of v11, /device:TPU:0, one launch (start us, length us, event | category | flops | bytes accessed | tf_op | source)
XLA Modules:
  0.0 73.8 jit_solution(9476027298597177311)
XLA Ops:
  0.6 3.1 %collective-permute-start.1 = (bf16[32,6144]{1,0:T(8,128)(2,1)}, bf16[32,6144]{1,0:T(8,128)(2,1)S(1)}, u32[]{:S(2)}, u32[]{:S(2)}) collective-permute-start(bf16[32,6144]{1,0:T(8,128)(2,1)} %refs_1_.15), channel_id=1, source_target_pairs={{0,4},{1,3},{4,8},{5,1},{8,12},{9,5},{12,14},{13,9},{14,10},{15,13... | collective-permute-start | bytes 1179656 | tf_op jit(solution)/shard_map/ppermute | solution.py:331
  3.7 3.9 %hidden.1 = (bf16[512,1536]{1,0:T(8,128)(2,1)S(1)}, bf16[1536,512]{1,0:T(8,128)(2,1)S(1)}, bf16[768,1536]{1,0:T(8,128)(2,1)S(1)}) custom-call(s32[1]{0:T(128)} %bitcast.me_ref.refs_0_, bf16[512,1536]{1,0:T(8,128)(2,1)} %og_hbm.1, bf16[512,1536]{1,0:T(8,128)(2,1)} %pre_hbm.1, bf16[6144,1536]{1,0:T(8,128)(2,1)} %refs_3_.15), custom_call_target="tpu_custom_call" | custom-call | flops 1150000000 | tf_op jit(solution)/shard_map/hidden/pallas_call | solution.py:116
  7.6 0.7 %collective-permute-start = (bf16[32,6144]{1,0:T(8,128)(2,1)S(1)}, bf16[32,6144]{1,0:T(8,128)(2,1)S(1)}, u32[]{:S(2)}, u32[]{:S(2)}) collective-permute-start(bf16[32,6144]{1,0:T(8,128)(2,1)S(1)} %copy-done), channel_id=1, source_target_pairs={{0,3},{1,4},{4,1},{5,8},{8,5},{9,12},{12,9},{13,14},{14,13},{15,10... | collective-permute-start | bytes 1179656 | tf_op jit(solution)/shard_map/ppermute | solution.py:343
  8.3 2.1 %input_piece.8 = (bf16[64,3072]{1,0:T(8,128)(2,1)S(1)}, bf16[64,3072]{1,0:T(8,128)(2,1)S(1)}, bf16[64,3072]{1,0:T(8,128)(2,1)S(1)}, bf16[64,3072]{1,0:T(8,128)(2...) custom-call(s32[1]{0:T(128)} %bitcast.me_ref.refs_0_, ...), custom_call_target="tpu_custom_call" | custom-call | flops 115000000 | tf_op jit(solution)/shard_map/input_piece/pallas_call | solution.py:183
  10.4 1.1 %collective-permute-start.5 = (bf16[32,6144]{1,0:T(8,128)(2,1)S(1)}, bf16[32,6144]{1,0:T(8,128)(2,1)S(1)}, u32[]{:S(2)}, u32[]{:S(2)}) collective-permute-start(bf16[32,6144]{1,0:T(8,128)(2,1)S(1)} %collective-permute-done.1.refs_3_), channel_id=1, source_target_pairs={{0,1},{1,0},{2,3},{3,2},{4,5},{5,4},{6,7},{7,6},{8,9},{9,8},{10,11... | collective-permute-start | bytes 1179656 | tf_op jit(solution)/shard_map/ppermute | solution.py:334
  11.5 1.6 %collective-permute-start.4 = (bf16[32,6144]{1,0:T(8,128)(2,1)S(1)}, bf16[32,6144]{1,0:T(8,128)(2,1)S(1)}, u32[]{:S(2)}, u32[]{:S(2)}) collective-permute-start(bf16[32,6144]{1,0:T(8,128)(2,1)S(1)} %collective-permute-done.1.refs_3_), channel_id=1, source_target_pairs={{0,4},{1,3},{4,8},{5,1},{8,12},{9,5},{12,14},{13,9},{14,10},{15,13... | collective-permute-start | bytes 1179656 | tf_op jit(solution)/shard_map/ppermute | solution.py:331
  13.1 2.1 %input_piece.9 = (bf16[64,3072]{1,0:T(8,128)(2,1)S(1)}, bf16[64,3072]{1,0:T(8,128)(2,1)S(1)}, bf16[64,3072]{1,0:T(8,128)(2,1)S(1)}, bf16[64,3072]{1,0:T(8,128)(2...) custom-call(s32[1]{0:T(128)} %bitcast.me_ref.refs_0_, ...), custom_call_target="tpu_custom_call", output_to_operand_aliasing={{0}: (4, {}), {1}: (5, {}), {2}: (6, {}), {3}: (7, {}), {4}... | custom-call | flops 115000000 | tf_op jit(solution)/shard_map/input_piece/pallas_call | solution.py:183
  15.1 1.8 %collective-permute-start.6 = (bf16[32,6144]{1,0:T(8,128)(2,1)S(1)}, bf16[32,6144]{1,0:T(8,128)(2,1)S(1)}, u32[]{:S(2)}, u32[]{:S(2)}) collective-permute-start(bf16[32,6144]{1,0:T(8,128)(2,1)S(1)} %collective-permute-done.refs_4_), channel_id=1, source_target_pairs={{0,1},{1,0},{2,3},{3,2},{4,5},{5,4},{6,7},{7,6},{8,9},{9,8},{10,11... | collective-permute-start | bytes 1179656 | tf_op jit(solution)/shard_map/ppermute | solution.py:334
  17.0 1.6 %collective-permute-start.3 = (bf16[32,6144]{1,0:T(8,128)(2,1)S(1)}, bf16[32,6144]{1,0:T(8,128)(2,1)S(1)}, u32[]{:S(2)}, u32[]{:S(2)}) collective-permute-start(bf16[32,6144]{1,0:T(8,128)(2,1)S(1)} %collective-permute-done.refs_4_), channel_id=1, source_target_pairs={{0,4},{1,3},{4,8},{5,1},{8,12},{9,5},{12,14},{13,9},{14,10},{15,13... | collective-permute-start | bytes 1179656 | tf_op jit(solution)/shard_map/ppermute | solution.py:331
  18.6 2.1 %input_piece.10 = (bf16[64,3072]{1,0:T(8,128)(2,1)S(1)}, bf16[64,3072]{1,0:T(8,128)(2,1)S(1)}, bf16[64,3072]{1,0:T(8,128)(2,1)S(1)}, bf16[64,3072]{1,0:T(8,128)(...) custom-call(s32[1]{0:T(128)} %bitcast.me_ref.refs_0_, ...), custom_call_target="tpu_custom_call", output_to_operand_aliasing={{0}: (4, {}), {1}: (5, {}), {2}: (6, {}), {3}: (7, {}), {4}... | custom-call | flops 115000000 | tf_op jit(solution)/shard_map/input_piece/pallas_call | solution.py:183
  20.6 0.1 collective-permute-start.8
  20.7 1.7 %collective-permute-start.10 = (bf16[32,6144]{1,0:T(8,128)(2,1)S(1)}, bf16[32,6144]{1,0:T(8,128)(2,1)S(1)}, u32[]{:S(2)}, u32[]{:S(2)}) collective-permute-start(bf16[32,6144]{1,0:T(8,128)(2,1)S(1)} %collective-permute-done.4.refs_5_), channel_id=1, source_target_pairs={{0,4},{1,3},{4,8},{5,1},{8,12},{9,5},{12,14},{13,9},{14,10},{15,13... | collective-permute-start | bytes 1179656 | tf_op jit(solution)/shard_map/ppermute | solution.py:331
  22.4 2.1 %input_piece.11 = (bf16[64,3072]{1,0:T(8,128)(2,1)S(1)}, bf16[64,3072]{1,0:T(8,128)(2,1)S(1)}, bf16[64,3072]{1,0:T(8,128)(2,1)S(1)}, bf16[64,3072]{1,0:T(8,128)(...) custom-call(s32[1]{0:T(128)} %bitcast.me_ref.refs_0_, ...), custom_call_target="tpu_custom_call", output_to_operand_aliasing={{0}: (4, {}), {1}: (5, {}), {2}: (6, {}), {3}: (7, {}), {4}... | custom-call | flops 115000000 | tf_op jit(solution)/shard_map/input_piece/pallas_call | solution.py:183
  24.5 0.3 collective-permute-done.3.refs_6_
  24.8 1.9 %collective-permute-start.7 = (bf16[32,6144]{1,0:T(8,128)(2,1)S(1)}, bf16[32,6144]{1,0:T(8,128)(2,1)S(1)}, u32[]{:S(2)}, u32[]{:S(2)}) collective-permute-start(bf16[32,6144]{1,0:T(8,128)(2,1)S(1)} %collective-permute-done.3.refs_6_), channel_id=1, source_target_pairs={{0,4},{1,3},{4,8},{5,1},{8,12},{9,5},{12,14},{13,9},{14,10},{15,13... | collective-permute-start | bytes 1179656 | tf_op jit(solution)/shard_map/ppermute | solution.py:331
  26.6 1.9 %input_piece.12 = (bf16[64,3072]{1,0:T(8,128)(2,1)S(1)}, bf16[64,3072]{1,0:T(8,128)(2,1)S(1)}, bf16[64,3072]{1,0:T(8,128)(2,1)S(1)}, bf16[64,3072]{1,0:T(8,128)(...) custom-call(s32[1]{0:T(128)} %bitcast.me_ref.refs_0_, ...), custom_call_target="tpu_custom_call" | custom-call | flops 115000000 | tf_op jit(solution)/shard_map/input_piece/pallas_call | solution.py:183
  28.6 0.3 collective-permute-done.10.refs_7_
  29.0 0.2 collective-permute-start.11
  29.1 1.4 %collective-permute-start.16 = (bf16[32,6144]{1,0:T(8,128)(2,1)S(1)}, bf16[32,6144]{1,0:T(8,128)(2,1)S(1)}, u32[]{:S(2)}, u32[]{:S(2)}) collective-permute-start(bf16[32,6144]{1,0:T(8,128)(2,1)S(1)} %collective-permute-done.10.refs_7_), channel_id=1, source_target_pairs={{0,4},{1,3},{4,8},{5,1},{8,12},{9,5},{12,14},{13,9},{14,10},{15,13... | collective-permute-start | bytes 1179656 | tf_op jit(solution)/shard_map/ppermute | solution.py:331
  30.6 1.9 %input_piece.13 = (bf16[64,3072]{1,0:T(8,128)(2,1)S(1)}, bf16[64,3072]{1,0:T(8,128)(2,1)S(1)}, bf16[64,3072]{1,0:T(8,128)(2,1)S(1)}, bf16[64,3072]{1,0:T(8,128)(...) custom-call(s32[1]{0:T(128)} %bitcast.me_ref.refs_0_, ...), custom_call_target="tpu_custom_call", output_to_operand_aliasing={{0}: (4, {}), {1}: (5, {}), {2}: (6, {}), {3}: (7, {}), {4}... | custom-call | flops 115000000 | tf_op jit(solution)/shard_map/input_piece/pallas_call | solution.py:183
  32.5 0.7 collective-permute-done.7.refs_8_
  33.2 1.9 %input_piece.14 = (bf16[64,3072]{1,0:T(8,128)(2,1)S(1)}, bf16[64,3072]{1,0:T(8,128)(2,1)S(1)}, bf16[64,3072]{1,0:T(8,128)(2,1)S(1)}, bf16[64,3072]{1,0:T(8,128)(...) custom-call(s32[1]{0:T(128)} %bitcast.me_ref.refs_0_, ...), custom_call_target="tpu_custom_call", output_to_operand_aliasing={{0}: (4, {}), {1}: (5, {}), {2}: (6, {}), {3}: (7, {}), {4}... | custom-call | flops 115000000 | tf_op jit(solution)/shard_map/input_piece/pallas_call | solution.py:183
  35.1 1.8 %input_piece.15 = (bf16[64,3072]{1,0:T(8,128)(2,1)S(1)}, bf16[64,3072]{1,0:T(8,128)(2,1)S(1)}, bf16[64,3072]{1,0:T(8,128)(2,1)S(1)}, bf16[64,3072]{1,0:T(8,128)(...) custom-call(s32[1]{0:T(128)} %bitcast.me_ref.refs_0_, ...), custom_call_target="tpu_custom_call", output_to_operand_aliasing={{0}: (4, {}), {1}: (5, {}), {2}: (6, {}), {3}: (7, {}), {4}... | custom-call | flops 115000000 | tf_op jit(solution)/shard_map/input_piece/pallas_call | solution.py:183
  36.9 0.1 total.7
  37.0 0.4 collective-permute-done.16.refs_9_
  37.4 0.5 collective-permute-start.17
  37.9 1.6 %collective-permute-start.14 = (bf16[64,3072]{1,0:T(8,128)(2,1)S(1)}, bf16[64,3072]{1,0:T(8,128)(2,1)S(1)}, u32[]{:S(2)}, u32[]{:S(2)}) collective-permute-start(bf16[64,3072]{1,0:T(8,128)(2,1)S(1)} %total.7), channel_id=1, source_target_pairs={{0,4},{1,3},{4,8},{5,1},{8,12},{9,5},{12,14},{13,9},{14,10},{15,13... | collective-permute-start | bytes 1179656 | tf_op jit(solution)/shard_map/ppermute | solution.py:331
  39.5 0.2 collective-permute-done.17.refs_10_
  39.7 0.6 collective-permute-done.18.refs_15_
  40.2 1.5 %weight_piece.8 = (bf16[6144,1536]{1,0:T(8,128)(2,1)}, bf16[768,1536]{1,0:T(8,128)(2,1)S(1)}) custom-call(bf16[512,1536]{1,0:T(8,128)(2,1)S(1)} %get-tuple-element.256.refs_0_, bf16[32,6144]{1,0:T(8,128)(2,1)S(1)} %copy-done, bf16[32,6144]{1,0:T(8,128)(2,1)S(1)} %collective-permute-done.2.refs_2_, bf16[32,6144]{1,0:T(8,128)(2,1)S(1)} %collective-permute-done.1.refs_3_, ...), custom_call_target="tpu_custom_call" | custom-call | flops 115000000 | tf_op jit(solution)/shard_map/weight_piece/pallas_call | solution.py:237
  41.7 0.1 total.8
  41.8 1.6 %collective-permute-start.20 = (bf16[64,3072]{1,0:T(8,128)(2,1)S(1)}, bf16[64,3072]{1,0:T(8,128)(2,1)S(1)}, u32[]{:S(2)}, u32[]{:S(2)}) collective-permute-start(bf16[64,3072]{1,0:T(8,128)(2,1)S(1)} %total.8), channel_id=1, source_target_pairs={{0,4},{1,3},{4,8},{5,1},{8,12},{9,5},{12,14},{13,9},{14,10},{15,13... | collective-permute-start | bytes 1179656 | tf_op jit(solution)/shard_map/ppermute | solution.py:331
  43.5 1.5 %weight_piece.9 = (bf16[6144,1536]{1,0:T(8,128)(2,1)}, bf16[768,1536]{1,0:T(8,128)(2,1)S(1)}) custom-call(bf16[512,1536]{1,0:T(8,128)(2,1)S(1)} %get-tuple-element.256.refs_0_, bf16[32,6144]{1,0:T(8,128)(2,1)S(1)} %copy-done, bf16[32,6144]{1,0:T(8,128)(2,1)S(1)} %collective-permute-done.2.refs_2_, ...), custom_call_target="tpu_custom_call", output_to_operand_aliasing={{0}: (18, {})} | custom-call | flops 115000000 | tf_op jit(solution)/shard_map/weight_piece/pallas_call | solution.py:237
  45.0 0.7 collective-permute-done.14.refs_0_
  45.7 0.1 total.9
  45.9 0.5 collective-permute-start.22
  46.4 1.6 %collective-permute-start.23 = (bf16[64,3072]{1,0:T(8,128)(2,1)S(1)}, bf16[64,3072]{1,0:T(8,128)(2,1)S(1)}, u32[]{:S(2)}, u32[]{:S(2)}) collective-permute-start(bf16[64,3072]{1,0:T(8,128)(2,1)S(1)} %total.9), channel_id=1, source_target_pairs={{0,4},{1,3},{4,8},{5,1},{8,12},{9,5},{12,14},{13,9},{14,10},{15,13... | collective-permute-start | bytes 1179656 | tf_op jit(solution)/shard_map/ppermute | solution.py:331
  48.0 1.5 %weight_piece.10 = (bf16[6144,1536]{1,0:T(8,128)(2,1)}, bf16[768,1536]{1,0:T(8,128)(2,1)S(1)}) custom-call(bf16[512,1536]{1,0:T(8,128)(2,1)S(1)} %get-tuple-element.256.refs_0_, bf16[32,6144]{1,0:T(8,128)(2,1)S(1)} %copy-done, bf16[32,6144]{1,0:T(8,128)(2,1)S(1)} %collective-permute-done.2.refs_2_, ...), custom_call_target="tpu_custom_call", output_to_operand_aliasing={{0}: (18, {})} | custom-call | flops 115000000 | tf_op jit(solution)/shard_map/weight_piece/pallas_call | solution.py:237
  49.5 0.4 collective-permute-done.20.refs_0_
  49.9 0.1 total.10
  50.1 0.5 collective-permute-start.25
  50.6 1.6 %collective-permute-start.26 = (bf16[64,3072]{1,0:T(8,128)(2,1)S(1)}, bf16[64,3072]{1,0:T(8,128)(2,1)S(1)}, u32[]{:S(2)}, u32[]{:S(2)}) collective-permute-start(bf16[64,3072]{1,0:T(8,128)(2,1)S(1)} %total.10), channel_id=1, source_target_pairs={{0,4},{1,3},{4,8},{5,1},{8,12},{9,5},{12,14},{13,9},{14,10},{15,13... | collective-permute-start | bytes 1179656 | tf_op jit(solution)/shard_map/ppermute | solution.py:331
  52.2 1.5 %weight_piece.11 = (bf16[6144,1536]{1,0:T(8,128)(2,1)}, bf16[768,1536]{1,0:T(8,128)(2,1)S(1)}) custom-call(bf16[512,1536]{1,0:T(8,128)(2,1)S(1)} %get-tuple-element.256.refs_0_, bf16[32,6144]{1,0:T(8,128)(2,1)S(1)} %copy-done, bf16[32,6144]{1,0:T(8,128)(2,1)S(1)} %collective-permute-done.2.refs_2_, ...), custom_call_target="tpu_custom_call", output_to_operand_aliasing={{0}: (18, {})} | custom-call | flops 115000000 | tf_op jit(solution)/shard_map/weight_piece/pallas_call | solution.py:237
  53.7 0.5 collective-permute-done.23.refs_0_
  54.2 0.2 total.11
  54.4 1.6 %collective-permute-start.24 = (bf16[64,3072]{1,0:T(8,128)(2,1)S(1)}, bf16[64,3072]{1,0:T(8,128)(2,1)S(1)}, u32[]{:S(2)}, u32[]{:S(2)}) collective-permute-start(bf16[64,3072]{1,0:T(8,128)(2,1)S(1)} %total.11), channel_id=1, source_target_pairs={{0,4},{1,3},{4,8},{5,1},{8,12},{9,5},{12,14},{13,9},{14,10},{15,13... | collective-permute-start | bytes 1179656 | tf_op jit(solution)/shard_map/ppermute | solution.py:331
  56.0 1.5 %weight_piece.12 = (bf16[6144,1536]{1,0:T(8,128)(2,1)}, bf16[768,1536]{1,0:T(8,128)(2,1)S(1)}) custom-call(bf16[512,1536]{1,0:T(8,128)(2,1)S(1)} %get-tuple-element.256.refs_0_, bf16[32,6144]{1,0:T(8,128)(2,1)S(1)} %copy-done, bf16[32,6144]{1,0:T(8,128)(2,1)S(1)} %collective-permute-done.2.refs_2_, ...), custom_call_target="tpu_custom_call", output_to_operand_aliasing={{0}: (18, {})} | custom-call | flops 115000000 | tf_op jit(solution)/shard_map/weight_piece/pallas_call | solution.py:237
  57.5 0.9 %collective-permute-done.26.refs_0_ = bf16[64,3072]{1,0:T(8,128)(2,1)S(1)} collective-permute-done((bf16[64,3072]{1,0:T(8,128)(2,1)S(1)}, bf16[64,3072]{1,0:T(8,128)(2,1)S(1)}, u32[]{:S(2)}, u32[]{:S(2)}) %collective-permute-start.26) | collective-permute-done | bytes 393248 | tf_op jit(solution)/shard_map/ppermute | solution.py:331
  58.4 0.1 total.12
  58.6 1.6 %collective-permute-start.28 = (bf16[64,3072]{1,0:T(8,128)(2,1)S(1)}, bf16[64,3072]{1,0:T(8,128)(2,1)S(1)}, u32[]{:S(2)}, u32[]{:S(2)}) collective-permute-start(bf16[64,3072]{1,0:T(8,128)(2,1)S(1)} %total.12), channel_id=1, source_target_pairs={{0,4},{1,3},{4,8},{5,1},{8,12},{9,5},{12,14},{13,9},{14,10},{15,13... | collective-permute-start | bytes 1179656 | tf_op jit(solution)/shard_map/ppermute | solution.py:331
  60.2 1.5 %weight_piece.13 = (bf16[6144,1536]{1,0:T(8,128)(2,1)}, bf16[768,1536]{1,0:T(8,128)(2,1)S(1)}) custom-call(bf16[512,1536]{1,0:T(8,128)(2,1)S(1)} %get-tuple-element.256.refs_0_, bf16[32,6144]{1,0:T(8,128)(2,1)S(1)} %copy-done, bf16[32,6144]{1,0:T(8,128)(2,1)S(1)} %collective-permute-done.2.refs_2_, ...), custom_call_target="tpu_custom_call", output_to_operand_aliasing={{0}: (18, {})} | custom-call | flops 115000000 | tf_op jit(solution)/shard_map/weight_piece/pallas_call | solution.py:237
  61.7 0.9 %collective-permute-done.24.refs_0_ = bf16[64,3072]{1,0:T(8,128)(2,1)S(1)} collective-permute-done((bf16[64,3072]{1,0:T(8,128)(2,1)S(1)}, bf16[64,3072]{1,0:T(8,128)(2,1)S(1)}, u32[]{:S(2)}, u32[]{:S(2)}) %collective-permute-start.24) | collective-permute-done | bytes 393248 | tf_op jit(solution)/shard_map/ppermute | solution.py:331
  62.6 0.1 total.13
  62.8 1.9 %collective-permute-start.27 = (bf16[64,3072]{1,0:T(8,128)(2,1)S(1)}, bf16[64,3072]{1,0:T(8,128)(2,1)S(1)}, u32[]{:S(2)}, u32[]{:S(2)}) collective-permute-start(bf16[64,3072]{1,0:T(8,128)(2,1)S(1)} %total.13), channel_id=1, source_target_pairs={{0,4},{1,3},{4,8},{5,1},{8,12},{9,5},{12,14},{13,9},{14,10},{15,13... | collective-permute-start | bytes 1179656 | tf_op jit(solution)/shard_map/ppermute | solution.py:331
  64.6 1.5 %weight_piece.14 = (bf16[6144,1536]{1,0:T(8,128)(2,1)}, bf16[768,1536]{1,0:T(8,128)(2,1)S(1)}) custom-call(bf16[512,1536]{1,0:T(8,128)(2,1)S(1)} %get-tuple-element.256.refs_0_, bf16[32,6144]{1,0:T(8,128)(2,1)S(1)} %copy-done, bf16[32,6144]{1,0:T(8,128)(2,1)S(1)} %collective-permute-done.2.refs_2_, ...), custom_call_target="tpu_custom_call", output_to_operand_aliasing={{0}: (18, {})} | custom-call | flops 115000000 | tf_op jit(solution)/shard_map/weight_piece/pallas_call | solution.py:237
  66.1 0.7 collective-permute-done.28.came_ref
  66.8 0.1 halves.2
  66.9 2.5 %weight_piece.15 = bf16[6144,1536]{1,0:T(8,128)(2,1)} custom-call(bf16[512,1536]{1,0:T(8,128)(2,1)S(1)} %get-tuple-element.256.refs_0_, bf16[32,6144]{1,0:T(8,128)(2,1)S(1)} %copy-done, bf16[32,6144]{1,0:T(8,128)(2,1)S(1)} %collective-permute-done.2.refs_2_, bf16[32,6144]{1,0:T(8,128)(2,1)S(1)} %collective-permute-done.1.refs_3_, ...), custom_call_target="tpu_custom_call", output_to_operand_aliasing={{}: (18, {})} | custom-call | flops 115000000 | tf_op jit(solution)/shard_map/weight_piece/pallas_call | solution.py:237
  69.5 1.6 %collective-permute-done.27.came_ref = bf16[64,3072]{1,0:T(8,128)(2,1)S(1)} collective-permute-done((bf16[64,3072]{1,0:T(8,128)(2,1)S(1)}, bf16[64,3072]{1,0:T(8,128)(2,1)S(1)}, u32[]{:S(2)}, u32[]{:S(2)}) %collective-permute-start.27) | collective-permute-done | bytes 393248 | tf_op jit(solution)/shard_map/ppermute | solution.py:331
  71.0 0.1 halves.3
  71.2 0.5 collective-permute-start.29
  71.7 0.9 %collective-permute-done.30.other_came_ref = bf16[32,3072]{1,0:T(8,128)(2,1)S(1)} collective-permute-done((bf16[32,3072]{1,0:T(8,128)(2,1)S(1)}, bf16[32,3072]{1,0:T(8,128)(2,1)S(1)}, u32[]{:S(2)}, u32[]{:S(2)}) %collective-permute-start.30) | collective-permute-done | bytes 196640 | tf_op jit(solution)/shard_map/ppermute | solution.py:334
  72.6 0.3 collective-permute-done.29.mine_came_ref
  72.9 0.8 %last.1 = bf16[32,6144]{1,0:T(8,128)(2,1)} custom-call(s32[1]{0:T(128)} %bitcast.me_ref.refs_0_, f32[32,3072]{1,0:T(8,128)S(1)} %get-tuple-element.259.mine_ref, bf16[32,3072]{1,0:T(8,128)(2,1)S(1)} %collective-permute-done.29.mine_came_ref, f32[32,3072]{1,0:T(8,128)S(1)} %get-tuple-element.260.other_ref, ...), custom_call_target="tpu_custom_call" | custom-call | flops 345000000 | tf_op jit(solution)/shard_map/last/pallas_call | solution.py:306
  (27 shorter events, 0.3 us)
Async XLA Ops:
  0.6 9.8 %collective-permute-start.1 = (bf16[32,6144]{1,0:T(8,128)(2,1)}, bf16[32,6144]{1,0:T(8,128)(2,1)S(1)}, u32[]{:S(2)}, u32[]{:S(2)}) collective-permute-start(bf16[32,6144]{1,0:T(8,128)(2,1)} %refs_1_.15), channel_id=1, source_target_pairs={{0,4},{1,3},{4,8},{5,1},{8,12},{9,5},{12,14},{13,9},{14,10},{15,13... | collective-permute-start | bytes 1179656 | tf_op jit(solution)/shard_map/ppermute | solution.py:331
  3.7 9.4 %collective-permute-start.2 = (bf16[32,6144]{1,0:T(8,128)(2,1)}, bf16[32,6144]{1,0:T(8,128)(2,1)S(1)}, u32[]{:S(2)}, u32[]{:S(2)}) collective-permute-start(bf16[32,6144]{1,0:T(8,128)(2,1)} %refs_1_.15), channel_id=1, source_target_pairs={{0,1},{1,0},{2,3},{3,2},{4,5},{5,4},{6,7},{7,6},{8,9},{9,8},{10,11... | collective-permute-start | bytes 1179656 | tf_op jit(solution)/shard_map/ppermute | solution.py:334
  3.7 3.9 %copy-start = (bf16[32,6144]{1,0:T(8,128)(2,1)S(1)}, bf16[32,6144]{1,0:T(8,128)(2,1)}, u32[]{:S(2)}) copy-start(bf16[32,6144]{1,0:T(8,128)(2,1)} %refs_1_.15) | copy-start | bytes 1179652
  7.6 7.5 %collective-permute-start = (bf16[32,6144]{1,0:T(8,128)(2,1)S(1)}, bf16[32,6144]{1,0:T(8,128)(2,1)S(1)}, u32[]{:S(2)}, u32[]{:S(2)}) collective-permute-start(bf16[32,6144]{1,0:T(8,128)(2,1)S(1)} %copy-done), channel_id=1, source_target_pairs={{0,3},{1,4},{4,1},{5,8},{8,5},{9,12},{12,9},{13,14},{14,13},{15,10... | collective-permute-start | bytes 1179656 | tf_op jit(solution)/shard_map/ppermute | solution.py:343
  10.4 8.2 %collective-permute-start.5 = (bf16[32,6144]{1,0:T(8,128)(2,1)S(1)}, bf16[32,6144]{1,0:T(8,128)(2,1)S(1)}, u32[]{:S(2)}, u32[]{:S(2)}) collective-permute-start(bf16[32,6144]{1,0:T(8,128)(2,1)S(1)} %collective-permute-done.1.refs_3_), channel_id=1, source_target_pairs={{0,1},{1,0},{2,3},{3,2},{4,5},{5,4},{6,7},{7,6},{8,9},{9,8},{10,11... | collective-permute-start | bytes 1179656 | tf_op jit(solution)/shard_map/ppermute | solution.py:334
  11.5 9.1 %collective-permute-start.4 = (bf16[32,6144]{1,0:T(8,128)(2,1)S(1)}, bf16[32,6144]{1,0:T(8,128)(2,1)S(1)}, u32[]{:S(2)}, u32[]{:S(2)}) collective-permute-start(bf16[32,6144]{1,0:T(8,128)(2,1)S(1)} %collective-permute-done.1.refs_3_), channel_id=1, source_target_pairs={{0,4},{1,3},{4,8},{5,1},{8,12},{9,5},{12,14},{13,9},{14,10},{15,13... | collective-permute-start | bytes 1179656 | tf_op jit(solution)/shard_map/ppermute | solution.py:331
  15.1 7.3 %collective-permute-start.6 = (bf16[32,6144]{1,0:T(8,128)(2,1)S(1)}, bf16[32,6144]{1,0:T(8,128)(2,1)S(1)}, u32[]{:S(2)}, u32[]{:S(2)}) collective-permute-start(bf16[32,6144]{1,0:T(8,128)(2,1)S(1)} %collective-permute-done.refs_4_), channel_id=1, source_target_pairs={{0,1},{1,0},{2,3},{3,2},{4,5},{5,4},{6,7},{7,6},{8,9},{9,8},{10,11... | collective-permute-start | bytes 1179656 | tf_op jit(solution)/shard_map/ppermute | solution.py:334
  17.0 7.8 %collective-permute-start.3 = (bf16[32,6144]{1,0:T(8,128)(2,1)S(1)}, bf16[32,6144]{1,0:T(8,128)(2,1)S(1)}, u32[]{:S(2)}, u32[]{:S(2)}) collective-permute-start(bf16[32,6144]{1,0:T(8,128)(2,1)S(1)} %collective-permute-done.refs_4_), channel_id=1, source_target_pairs={{0,4},{1,3},{4,8},{5,1},{8,12},{9,5},{12,14},{13,9},{14,10},{15,13... | collective-permute-start | bytes 1179656 | tf_op jit(solution)/shard_map/ppermute | solution.py:331
  20.6 6.0 %collective-permute-start.8 = (bf16[32,6144]{1,0:T(8,128)(2,1)S(1)}, bf16[32,6144]{1,0:T(8,128)(2,1)S(1)}, u32[]{:S(2)}, u32[]{:S(2)}) collective-permute-start(bf16[32,6144]{1,0:T(8,128)(2,1)S(1)} %collective-permute-done.4.refs_5_), channel_id=1, source_target_pairs={{0,1},{1,0},{2,3},{3,2},{4,5},{5,4},{6,7},{7,6},{8,9},{9,8},{10,11... | collective-permute-start | bytes 1179656 | tf_op jit(solution)/shard_map/ppermute | solution.py:334
  20.7 8.3 %collective-permute-start.10 = (bf16[32,6144]{1,0:T(8,128)(2,1)S(1)}, bf16[32,6144]{1,0:T(8,128)(2,1)S(1)}, u32[]{:S(2)}, u32[]{:S(2)}) collective-permute-start(bf16[32,6144]{1,0:T(8,128)(2,1)S(1)} %collective-permute-done.4.refs_5_), channel_id=1, source_target_pairs={{0,4},{1,3},{4,8},{5,1},{8,12},{9,5},{12,14},{13,9},{14,10},{15,13... | collective-permute-start | bytes 1179656 | tf_op jit(solution)/shard_map/ppermute | solution.py:331
  24.8 5.8 %collective-permute-start.12 = (bf16[32,6144]{1,0:T(8,128)(2,1)S(1)}, bf16[32,6144]{1,0:T(8,128)(2,1)S(1)}, u32[]{:S(2)}, u32[]{:S(2)}) collective-permute-start(bf16[32,6144]{1,0:T(8,128)(2,1)S(1)} %collective-permute-done.3.refs_6_), channel_id=1, source_target_pairs={{0,1},{1,0},{2,3},{3,2},{4,5},{5,4},{6,7},{7,6},{8,9},{9,8},{10,11... | collective-permute-start | bytes 1179656 | tf_op jit(solution)/shard_map/ppermute | solution.py:334
  24.8 8.4 %collective-permute-start.7 = (bf16[32,6144]{1,0:T(8,128)(2,1)S(1)}, bf16[32,6144]{1,0:T(8,128)(2,1)S(1)}, u32[]{:S(2)}, u32[]{:S(2)}) collective-permute-start(bf16[32,6144]{1,0:T(8,128)(2,1)S(1)} %collective-permute-done.3.refs_6_), channel_id=1, source_target_pairs={{0,4},{1,3},{4,8},{5,1},{8,12},{9,5},{12,14},{13,9},{14,10},{15,13... | collective-permute-start | bytes 1179656 | tf_op jit(solution)/shard_map/ppermute | solution.py:331
  28.5 4.6 %collective-permute-start.9 = (bf16[64,3072]{1,0:T(8,128)(2,1)S(1)}, bf16[64,3072]{1,0:T(8,128)(2,1)S(1)}, u32[]{:S(2)}, u32[]{:S(2)}) collective-permute-start(bf16[64,3072]{1,0:T(8,128)(2,1)S(1)} %get-tuple-element.175), channel_id=1, source_target_pairs={{0,1},{1,0},{2,3},{3,2},{4,5},{5,4},{6,7},{7,6},{8,9},{9,8},{10,11... | collective-permute-start | bytes 1179656 | tf_op jit(solution)/shard_map/ppermute | solution.py:334
  29.0 4.2 %collective-permute-start.11 = (bf16[32,6144]{1,0:T(8,128)(2,1)S(1)}, bf16[32,6144]{1,0:T(8,128)(2,1)S(1)}, u32[]{:S(2)}, u32[]{:S(2)}) collective-permute-start(bf16[32,6144]{1,0:T(8,128)(2,1)S(1)} %collective-permute-done.10.refs_7_), channel_id=1, source_target_pairs={{0,1},{1,0},{2,3},{3,2},{4,5},{5,4},{6,7},{7,6},{8,9},{9,8},{10,11... | collective-permute-start | bytes 1179656 | tf_op jit(solution)/shard_map/ppermute | solution.py:334
  29.1 8.3 %collective-permute-start.16 = (bf16[32,6144]{1,0:T(8,128)(2,1)S(1)}, bf16[32,6144]{1,0:T(8,128)(2,1)S(1)}, u32[]{:S(2)}, u32[]{:S(2)}) collective-permute-start(bf16[32,6144]{1,0:T(8,128)(2,1)S(1)} %collective-permute-done.10.refs_7_), channel_id=1, source_target_pairs={{0,4},{1,3},{4,8},{5,1},{8,12},{9,5},{12,14},{13,9},{14,10},{15,13... | collective-permute-start | bytes 1179656 | tf_op jit(solution)/shard_map/ppermute | solution.py:331
  37.4 2.1 %collective-permute-start.15 = (bf16[64,3072]{1,0:T(8,128)(2,1)S(1)}, bf16[64,3072]{1,0:T(8,128)(2,1)S(1)}, u32[]{:S(2)}, u32[]{:S(2)}) collective-permute-start(bf16[64,3072]{1,0:T(8,128)(2,1)S(1)} %get-tuple-element.217), channel_id=1, source_target_pairs={{0,1},{1,0},{2,3},{3,2},{4,5},{5,4},{6,7},{7,6},{8,9},{9,8},{10,11... | collective-permute-start | bytes 1179656 | tf_op jit(solution)/shard_map/ppermute | solution.py:334
  37.4 2.3 %collective-permute-start.17 = (bf16[32,6144]{1,0:T(8,128)(2,1)S(1)}, bf16[32,6144]{1,0:T(8,128)(2,1)S(1)}, u32[]{:S(2)}, u32[]{:S(2)}) collective-permute-start(bf16[32,6144]{1,0:T(8,128)(2,1)S(1)} %collective-permute-done.16.refs_9_), channel_id=1, source_target_pairs={{0,1},{1,0},{2,3},{3,2},{4,5},{5,4},{6,7},{7,6},{8,9},{9,8},{10,11... | collective-permute-start | bytes 1179656 | tf_op jit(solution)/shard_map/ppermute | solution.py:334
  37.9 2.3 %collective-permute-start.18 = (bf16[32,6144]{1,0:T(8,128)(2,1)S(1)}, bf16[32,6144]{1,0:T(8,128)(2,1)S(1)}, u32[]{:S(2)}, u32[]{:S(2)}) collective-permute-start(bf16[32,6144]{1,0:T(8,128)(2,1)S(1)} %collective-permute-done.7.refs_8_), channel_id=1, source_target_pairs={{0,1},{1,0},{2,3},{3,2},{4,5},{5,4},{6,7},{7,6},{8,9},{9,8},{10,11... | collective-permute-start | bytes 1179656 | tf_op jit(solution)/shard_map/ppermute | solution.py:334
  37.9 7.8 %collective-permute-start.14 = (bf16[64,3072]{1,0:T(8,128)(2,1)S(1)}, bf16[64,3072]{1,0:T(8,128)(2,1)S(1)}, u32[]{:S(2)}, u32[]{:S(2)}) collective-permute-start(bf16[64,3072]{1,0:T(8,128)(2,1)S(1)} %total.7), channel_id=1, source_target_pairs={{0,4},{1,3},{4,8},{5,1},{8,12},{9,5},{12,14},{13,9},{14,10},{15,13... | collective-permute-start | bytes 1179656 | tf_op jit(solution)/shard_map/ppermute | solution.py:331
  39.5 6.2 %collective-permute-start.13 = (bf16[64,3072]{1,0:T(8,128)(2,1)S(1)}, bf16[64,3072]{1,0:T(8,128)(2,1)S(1)}, u32[]{:S(2)}, u32[]{:S(2)}) collective-permute-start(bf16[64,3072]{1,0:T(8,128)(2,1)S(1)} %get-tuple-element.214), channel_id=1, source_target_pairs={{0,1},{1,0},{2,3},{3,2},{4,5},{5,4},{6,7},{7,6},{8,9},{9,8},{10,11... | collective-permute-start | bytes 1179656 | tf_op jit(solution)/shard_map/ppermute | solution.py:334
  41.8 8.1 %collective-permute-start.20 = (bf16[64,3072]{1,0:T(8,128)(2,1)S(1)}, bf16[64,3072]{1,0:T(8,128)(2,1)S(1)}, u32[]{:S(2)}, u32[]{:S(2)}) collective-permute-start(bf16[64,3072]{1,0:T(8,128)(2,1)S(1)} %total.8), channel_id=1, source_target_pairs={{0,4},{1,3},{4,8},{5,1},{8,12},{9,5},{12,14},{13,9},{14,10},{15,13... | collective-permute-start | bytes 1179656 | tf_op jit(solution)/shard_map/ppermute | solution.py:331
  45.8 4.1 %collective-permute-start.19 = (bf16[64,3072]{1,0:T(8,128)(2,1)S(1)}, bf16[64,3072]{1,0:T(8,128)(2,1)S(1)}, u32[]{:S(2)}, u32[]{:S(2)}) collective-permute-start(bf16[64,3072]{1,0:T(8,128)(2,1)S(1)} %get-tuple-element.227), channel_id=1, source_target_pairs={{0,1},{1,0},{2,3},{3,2},{4,5},{5,4},{6,7},{7,6},{8,9},{9,8},{10,11... | collective-permute-start | bytes 1179656 | tf_op jit(solution)/shard_map/ppermute | solution.py:334
  45.9 6.3 %collective-permute-start.22 = (bf16[64,3072]{1,0:T(8,128)(2,1)S(1)}, bf16[64,3072]{1,0:T(8,128)(2,1)S(1)}, u32[]{:S(2)}, u32[]{:S(2)}) collective-permute-start(bf16[64,3072]{1,0:T(8,128)(2,1)S(1)} %get-tuple-element.235), channel_id=1, source_target_pairs={{0,1},{1,0},{2,3},{3,2},{4,5},{5,4},{6,7},{7,6},{8,9},{9,8},{10,11... | collective-permute-start | bytes 1179656 | tf_op jit(solution)/shard_map/ppermute | solution.py:334
  46.4 7.8 %collective-permute-start.23 = (bf16[64,3072]{1,0:T(8,128)(2,1)S(1)}, bf16[64,3072]{1,0:T(8,128)(2,1)S(1)}, u32[]{:S(2)}, u32[]{:S(2)}) collective-permute-start(bf16[64,3072]{1,0:T(8,128)(2,1)S(1)} %total.9), channel_id=1, source_target_pairs={{0,4},{1,3},{4,8},{5,1},{8,12},{9,5},{12,14},{13,9},{14,10},{15,13... | collective-permute-start | bytes 1179656 | tf_op jit(solution)/shard_map/ppermute | solution.py:331
  50.1 5.9 %collective-permute-start.21 = (bf16[64,3072]{1,0:T(8,128)(2,1)S(1)}, bf16[64,3072]{1,0:T(8,128)(2,1)S(1)}, u32[]{:S(2)}, u32[]{:S(2)}) collective-permute-start(bf16[64,3072]{1,0:T(8,128)(2,1)S(1)} %get-tuple-element.232), channel_id=1, source_target_pairs={{0,1},{1,0},{2,3},{3,2},{4,5},{5,4},{6,7},{7,6},{8,9},{9,8},{10,11... | collective-permute-start | bytes 1179656 | tf_op jit(solution)/shard_map/ppermute | solution.py:334
  50.1 5.9 %collective-permute-start.25 = (bf16[64,3072]{1,0:T(8,128)(2,1)S(1)}, bf16[64,3072]{1,0:T(8,128)(2,1)S(1)}, u32[]{:S(2)}, u32[]{:S(2)}) collective-permute-start(bf16[64,3072]{1,0:T(8,128)(2,1)S(1)} %get-tuple-element.242), channel_id=1, source_target_pairs={{0,1},{1,0},{2,3},{3,2},{4,5},{5,4},{6,7},{7,6},{8,9},{9,8},{10,11... | collective-permute-start | bytes 1179656 | tf_op jit(solution)/shard_map/ppermute | solution.py:334
  50.6 7.8 %collective-permute-start.26 = (bf16[64,3072]{1,0:T(8,128)(2,1)S(1)}, bf16[64,3072]{1,0:T(8,128)(2,1)S(1)}, u32[]{:S(2)}, u32[]{:S(2)}) collective-permute-start(bf16[64,3072]{1,0:T(8,128)(2,1)S(1)} %total.10), channel_id=1, source_target_pairs={{0,4},{1,3},{4,8},{5,1},{8,12},{9,5},{12,14},{13,9},{14,10},{15,13... | collective-permute-start | bytes 1179656 | tf_op jit(solution)/shard_map/ppermute | solution.py:331
  54.4 8.3 %collective-permute-start.24 = (bf16[64,3072]{1,0:T(8,128)(2,1)S(1)}, bf16[64,3072]{1,0:T(8,128)(2,1)S(1)}, u32[]{:S(2)}, u32[]{:S(2)}) collective-permute-start(bf16[64,3072]{1,0:T(8,128)(2,1)S(1)} %total.11), channel_id=1, source_target_pairs={{0,4},{1,3},{4,8},{5,1},{8,12},{9,5},{12,14},{13,9},{14,10},{15,13... | collective-permute-start | bytes 1179656 | tf_op jit(solution)/shard_map/ppermute | solution.py:331
  58.6 8.3 %collective-permute-start.28 = (bf16[64,3072]{1,0:T(8,128)(2,1)S(1)}, bf16[64,3072]{1,0:T(8,128)(2,1)S(1)}, u32[]{:S(2)}, u32[]{:S(2)}) collective-permute-start(bf16[64,3072]{1,0:T(8,128)(2,1)S(1)} %total.12), channel_id=1, source_target_pairs={{0,4},{1,3},{4,8},{5,1},{8,12},{9,5},{12,14},{13,9},{14,10},{15,13... | collective-permute-start | bytes 1179656 | tf_op jit(solution)/shard_map/ppermute | solution.py:331
  62.8 8.3 %collective-permute-start.27 = (bf16[64,3072]{1,0:T(8,128)(2,1)S(1)}, bf16[64,3072]{1,0:T(8,128)(2,1)S(1)}, u32[]{:S(2)}, u32[]{:S(2)}) collective-permute-start(bf16[64,3072]{1,0:T(8,128)(2,1)S(1)} %total.13), channel_id=1, source_target_pairs={{0,4},{1,3},{4,8},{5,1},{8,12},{9,5},{12,14},{13,9},{14,10},{15,13... | collective-permute-start | bytes 1179656 | tf_op jit(solution)/shard_map/ppermute | solution.py:331
  71.1 1.5 %collective-permute-start.30 = (bf16[32,3072]{1,0:T(8,128)(2,1)S(1)}, bf16[32,3072]{1,0:T(8,128)(2,1)S(1)}, u32[]{:S(2)}, u32[]{:S(2)}) collective-permute-start(bf16[32,3072]{1,0:T(8,128)(2,1)S(1)} %get-tuple-element.261), channel_id=1, source_target_pairs={{0,1},{1,0},{2,3},{3,2},{4,5},{5,4},{6,7},{7,6},{8,9},{9,8},{10,11... | collective-permute-start | bytes 589832 | tf_op jit(solution)/shard_map/ppermute | solution.py:334
  71.2 1.7 %collective-permute-start.29 = (bf16[32,3072]{1,0:T(8,128)(2,1)S(1)}, bf16[32,3072]{1,0:T(8,128)(2,1)S(1)}, u32[]{:S(2)}, u32[]{:S(2)}) collective-permute-start(bf16[32,3072]{1,0:T(8,128)(2,1)S(1)} %get-tuple-element.255), channel_id=1, source_target_pairs={{0,1},{1,0},{2,3},{3,2},{4,5},{5,4},{6,7},{7,6},{8,9},{9,8},{10,11... | collective-permute-start | bytes 589832 | tf_op jit(solution)/shard_map/ppermute | solution.py:334
